TPU v7x, 32 devices: a whole 2x2x4 slice. The times are simulated.
32 devices in a mesh: rep: 4 (over y, x), shard: 8 (over z, core).
Axes of the slice: x: 2, y: 2, z: 4, core: 2. Of those that a mesh axis runs over, the one named last changes fastest.
Arguments:
- layer_in: bfloat16 [8, 1024, 1024], P('shard', 'rep'), may hold values from -6 to 6
- out_grad: bfloat16 [8, 1024, 1024], P('shard', 'rep'), may hold values from -6 to 6
- attn_norm: bfloat16 [1024], P('shard'), may hold values from 0.099609375 to 1.8984375
- query_weight: bfloat16 [1024, 2048], P('shard'), may hold values from -0.1875 to 0.1875
- key_projection: bfloat16 [1024, 1024], P('shard'), may hold values from -0.1875 to 0.1875
- value_projection: bfloat16 [1024, 1024], P('shard'), may hold values from -0.1875 to 0.1875
- query_norm: bfloat16 [128], P('shard'), may hold values from 1 to 2
- key_norm: bfloat16 [128], P('shard'), may hold values from 1 to 2
- out_weight: bfloat16 [2048, 1024], P('shard'), may hold values from -2 to 2
- mlp_norm: bfloat16 [1024], P('shard'), may hold values from 0.099609375 to 1.8984375
- gate_weight: bfloat16 [1024, 3072], P('shard'), may hold values from -0.1875 to 0.1875
- up_weight: bfloat16 [1024, 3072], P('shard'), may hold values from -0.1875 to 0.1875
- down_weight: bfloat16 [3072, 1024], P('shard'), may hold values from -0.109375 to 0.109375
- picture_starts: int32 [8, 3], P('shard'), may hold values from 0 to 768, as said below
- picture_count: int32 [8], P('shard'), may hold values from 1 to 3
Outputs:
- layer_out: bfloat16 [8, 1024, 1024], P('shard', 'rep')
- in_grad: bfloat16 [8, 1024, 1024], P('shard', 'rep')
- attn_norm_grad: float32 [1024], P('shard')
- query_weight_grad: float32 [1024, 2048], P('shard')
- key_weight_grad: float32 [1024, 1024], P('shard')
- value_weight_grad: float32 [1024, 1024], P('shard')
- query_norm_grad: float32 [128], P('shard')
- key_norm_grad: float32 [128], P('shard')
- out_weight_grad: float32 [2048, 1024], P('shard')
- mlp_norm_grad: float32 [1024], P('shard')
- gate_weight_grad: float32 [1024, 3072], P('shard')
- up_weight_grad: float32 [1024, 3072], P('shard')
- down_weight_grad: float32 [3072, 1024], P('shard')
Inputs may be any that keep to these rules, and one draw needn't show every extreme that they name: `picture_starts`: in row b the entries 0 to picture_count[b] - 1 are distinct multiples of 256 in increasing order; the other entries are ignored.
All inputs are finite; a program needn't handle non-finite values.
Results may differ from a plain program's by a relative error of at most 0.023.
Values may be sent and summed in bfloat16 or wider, within the bound.
No kernel may reach another device: no remote copies, remote signals or barrier semaphores. Data moves between devices by JAX's collectives and lax.ppermute only.
A program may use at most 192 MiB of HBM per device.

v0:
```python
from functools import partial

import jax
import jax.numpy as jnp
from jax import lax
from jax.sharding import PartitionSpec as P

MODEL_WIDTH = 1024
QUERY_HEADS = 16
KEY_VALUE_HEADS = 8
HEAD_SIZE = 128
PIECE = 256


EPSILON = 1e-06
ROPE_BASE = 1000000.0


def root_mean_scale(values, gain_row):
    return (
        values * lax.rsqrt(jnp.mean(values * values, axis=-1, keepdims=True) + EPSILON) * gain_row
    )


def apply_rotary(values, token_positions):
    half_width = values.shape[-1] // 2
    inv_freq = ROPE_BASE ** (-2.0 * jnp.arange(half_width, dtype=jnp.float32) / values.shape[-1])
    angles = token_positions.astype(jnp.float32)[:, None] * inv_freq[None, :]
    cosine = jnp.cos(angles)[:, None, :]
    sine = jnp.sin(angles)[:, None, :]
    front_part = values[..., :half_width]
    back_part = values[..., half_width:]
    return jnp.concatenate(
        [front_part * cosine - back_part * sine, back_part * cosine + front_part * sine], axis=-1
    )


def head_output(token_positions, heads, raw_rows, gain_row):
    shaped = raw_rows.reshape(raw_rows.shape[0], heads, -1)
    return apply_rotary(root_mean_scale(shaped, gain_row), token_positions)


def piece_ids(token_positions, picture_piece_starts, picture_piece_count):
    slot_ids = jnp.arange(picture_piece_starts.shape[0], dtype=jnp.int32)
    inside = (
        (token_positions[:, None] >= picture_piece_starts[None, :])
        & (token_positions[:, None] < picture_piece_starts[None, :] + PIECE)
        & (slot_ids[None, :] < picture_piece_count)
    )
    return jnp.sum(jnp.where(inside, slot_ids[None, :] + 1, 0), axis=1)


def project_inputs(tokens, attention_forward, token_positions):
    total_row_count = tokens.shape[0]
    normed = root_mean_scale(tokens, attention_forward[0].astype(jnp.float32)).astype(jnp.bfloat16)
    query_raw = jnp.dot(normed, attention_forward[1], preferred_element_type=jnp.float32)
    unrotated_key = jnp.dot(normed, attention_forward[2], preferred_element_type=jnp.float32)
    value_row_list = jnp.dot(
        normed, attention_forward[3], preferred_element_type=jnp.float32
    ).astype(jnp.bfloat16)
    rotated_query = head_output(
        token_positions, QUERY_HEADS, query_raw, attention_forward[4].astype(jnp.float32)
    ).astype(jnp.bfloat16)
    rotated_key = (
        head_output(
            token_positions,
            KEY_VALUE_HEADS,
            unrotated_key,
            attention_forward[5].astype(jnp.float32),
        )
        .reshape(total_row_count, KEY_VALUE_HEADS * HEAD_SIZE)
        .astype(jnp.bfloat16)
    )
    return (normed, query_raw, unrotated_key, rotated_query, rotated_key, value_row_list)


def block_scores(grouped_query, key_rows, score_scale):
    return (
        jnp.einsum("sngd,knd->ngsk", grouped_query, key_rows, preferred_element_type=jnp.float32)
        * score_scale
    )


def log_totals(grouped_query, key_block_list, mask_blocks, score_scale):
    head_shape = (grouped_query.shape[1], grouped_query.shape[2], grouped_query.shape[0])
    start_state = (jnp.full(head_shape, -1e30, jnp.float32), jnp.zeros(head_shape, jnp.float32))

    def log_absorb(carried, block_items):
        run_max, run_sum = carried
        key_rows, mask_rows = block_items
        scores = jnp.where(
            mask_rows[None, None], block_scores(grouped_query, key_rows, score_scale), -1e30
        )
        new_max = jnp.maximum(run_max, jnp.max(scores, axis=-1))
        terms = jnp.where(mask_rows[None, None], jnp.exp(scores - new_max[..., None]), 0.0)
        run_sum = run_sum * jnp.exp(run_max - new_max) + jnp.sum(terms, axis=-1)
        return ((new_max, run_sum), None)

    (run_max, run_sum), unused_out = lax.scan(
        log_absorb, start_state, (key_block_list, mask_blocks)
    )
    return run_max + jnp.log(run_sum)


def block_probs(grouped_query, key_rows, mask_rows, log_sum, score_scale):
    scores = block_scores(grouped_query, key_rows, score_scale)
    return jnp.where(mask_rows[None, None], jnp.exp(scores - log_sum[..., None]), 0.0)


def attend_values(
    grouped_query, key_block_list, value_block_list, mask_blocks, log_sum, score_scale
):

    def attend_absorb(carried, block_items):
        key_rows, value_row_list, mask_rows = block_items
        probabilities = block_probs(grouped_query, key_rows, mask_rows, log_sum, score_scale)
        added = jnp.einsum(
            "ngsk,knd->sngd",
            probabilities.astype(jnp.bfloat16),
            value_row_list,
            preferred_element_type=jnp.float32,
        )
        return (carried + added, None)

    start_state = jnp.zeros(grouped_query.shape, jnp.float32)
    attended, unused_out = lax.scan(
        attend_absorb, start_state, (key_block_list, value_block_list, mask_blocks)
    )
    return attended


def attention_back(
    grouped_query,
    key_block_list,
    value_block_list,
    mask_blocks,
    log_sum,
    gradient_groups,
    score_scale,
):

    def measure(row_delta, block_items):
        key_rows, value_row_list, mask_rows = block_items
        probabilities = block_probs(grouped_query, key_rows, mask_rows, log_sum, score_scale)
        dprobs = jnp.einsum(
            "sngd,knd->ngsk", gradient_groups, value_row_list, preferred_element_type=jnp.float32
        )
        return (row_delta + jnp.sum(probabilities * dprobs, axis=-1), None)

    head_shape = (grouped_query.shape[1], grouped_query.shape[2], grouped_query.shape[0])
    row_delta, unused_out = lax.scan(
        measure, jnp.zeros(head_shape, jnp.float32), (key_block_list, value_block_list, mask_blocks)
    )

    def spread(dquery, block_items):
        key_rows, value_row_list, mask_rows = block_items
        probabilities = block_probs(grouped_query, key_rows, mask_rows, log_sum, score_scale)
        dprobs = jnp.einsum(
            "sngd,knd->ngsk", gradient_groups, value_row_list, preferred_element_type=jnp.float32
        )
        dscores = (score_scale * (probabilities * (dprobs - row_delta[..., None]))).astype(
            jnp.bfloat16
        )
        dquery = dquery + jnp.einsum(
            "ngsk,knd->sngd", dscores, key_rows, preferred_element_type=jnp.float32
        )
        key_terms = jnp.einsum(
            "ngsk,sngd->knd", dscores, grouped_query, preferred_element_type=jnp.float32
        )
        dvalues = jnp.einsum(
            "ngsk,sngd->knd",
            probabilities.astype(jnp.bfloat16),
            gradient_groups,
            preferred_element_type=jnp.float32,
        )
        block_len = key_rows.shape[0]
        return (
            dquery,
            jnp.concatenate(
                [key_terms.reshape(block_len, -1), dvalues.reshape(block_len, -1)], axis=1
            ),
        )

    dquery, kv_terms = lax.scan(
        spread,
        jnp.zeros(grouped_query.shape, jnp.float32),
        (key_block_list, value_block_list, mask_blocks),
    )
    return (dquery, kv_terms.reshape(-1, kv_terms.shape[-1]))


def finish_forward(tokens, mixed_head_rows, out_full, mlp_full):
    after_attn = tokens + jnp.dot(mixed_head_rows, out_full, preferred_element_type=jnp.float32)
    mlp_in = root_mean_scale(after_attn, mlp_full[0].astype(jnp.float32)).astype(jnp.bfloat16)
    gate_act = jnp.dot(mlp_in, mlp_full[1], preferred_element_type=jnp.float32)
    up_act = jnp.dot(mlp_in, mlp_full[2], preferred_element_type=jnp.float32)
    hidden = (jax.nn.silu(gate_act) * up_act).astype(jnp.bfloat16)
    result = after_attn + jnp.dot(hidden, mlp_full[3], preferred_element_type=jnp.float32)
    return (after_attn, mlp_in, gate_act, up_act, hidden, result)


def activate(gate_value, up_value):
    return jax.nn.silu(gate_value) * up_value


def split_heads(
    rotated_query,
    key_everything,
    value_everything,
    sequence_count,
    sequences_per_shard,
    block_count,
    block_key,
):
    grouped_query = rotated_query.reshape(
        sequence_count,
        sequences_per_shard,
        KEY_VALUE_HEADS,
        QUERY_HEADS // KEY_VALUE_HEADS,
        HEAD_SIZE,
    )
    key_block_list = key_everything.reshape(
        sequence_count, block_count, block_key, KEY_VALUE_HEADS, HEAD_SIZE
    )
    value_block_list = value_everything.reshape(
        sequence_count, block_count, block_key, KEY_VALUE_HEADS, HEAD_SIZE
    )
    return (grouped_query, key_block_list, value_block_list)


def per_device(
    layer_in,
    out_grad,
    attn_norm,
    query_weight,
    key_projection,
    value_projection,
    query_norm,
    key_norm,
    out_weight,
    mlp_norm,
    gate_weight,
    up_weight,
    down_weight,
    picture_starts,
    picture_count,
):
    replicas = lax.axis_size("rep")
    sequence_count = layer_in.shape[0]
    sequences_per_shard = layer_in.shape[1]
    total_row_count = sequence_count * sequences_per_shard
    seq_len = sequences_per_shard * replicas
    key_group = 1
    while key_group * 2 * sequences_per_shard <= 512 and replicas % (key_group * 2) == 0:
        key_group = key_group * 2
    block_key = key_group * sequences_per_shard
    block_count = seq_len // block_key
    score_scale = HEAD_SIZE ** (-0.5)
    key_value_width = KEY_VALUE_HEADS * HEAD_SIZE
    token_positions = lax.axis_index("rep") * sequences_per_shard + jnp.arange(
        sequences_per_shard, dtype=jnp.int32
    )
    position_per_row = jnp.tile(token_positions, sequence_count)
    key_positions = jnp.arange(seq_len, dtype=jnp.int32)
    seq_item = 0
    query_piece = piece_ids(token_positions, picture_starts[seq_item], picture_count[seq_item])
    key_piece = piece_ids(key_positions, picture_starts[seq_item], picture_count[seq_item])
    allowed = (key_positions[None, :] <= token_positions[:, None]) | (query_piece[:, None] > 0) & (
        query_piece[:, None] == key_piece[None, :]
    )
    mask_list = [allowed.reshape(sequences_per_shard, block_count, block_key).transpose(1, 0, 2)]
    tokens = layer_in.reshape(total_row_count, MODEL_WIDTH).astype(jnp.float32)
    cotangent = out_grad.reshape(total_row_count, MODEL_WIDTH).astype(jnp.float32)
    attention_forward = (
        lax.all_gather(attn_norm, "shard", axis=0, tiled=True),
        lax.all_gather(query_weight, "shard", axis=0, tiled=True),
        lax.all_gather(key_projection, "shard", axis=0, tiled=True),
        lax.all_gather(value_projection, "shard", axis=0, tiled=True),
        lax.all_gather(query_norm, "shard", axis=0, tiled=True),
        lax.all_gather(key_norm, "shard", axis=0, tiled=True),
        lax.all_gather(out_weight, "shard", axis=0, tiled=True),
    )
    mlp_full = (
        lax.all_gather(mlp_norm, "shard", axis=0, tiled=True),
        lax.all_gather(gate_weight, "shard", axis=0, tiled=True),
        lax.all_gather(up_weight, "shard", axis=0, tiled=True),
        lax.all_gather(down_weight, "shard", axis=0, tiled=True),
    )
    normed, query_raw, unrotated_key, rotated_query, rotated_key, value_row_list = project_inputs(
        tokens, attention_forward, position_per_row
    )
    key_everything, value_everything = (
        lax.all_gather(
            rotated_key.reshape(sequence_count, sequences_per_shard, key_value_width),
            "rep",
            axis=1,
            tiled=True,
        ),
        lax.all_gather(
            value_row_list.reshape(sequence_count, sequences_per_shard, key_value_width),
            "rep",
            axis=1,
            tiled=True,
        ),
    )
    grouped_query, key_block_list, value_block_list = split_heads(
        rotated_query,
        key_everything,
        value_everything,
        sequence_count,
        sequences_per_shard,
        block_count,
        block_key,
    )
    attended_list = []
    seq_item = 0
    log_sum = log_totals(
        grouped_query[seq_item], key_block_list[seq_item], mask_list[seq_item], score_scale
    )
    log_list = [log_sum]
    attended_list.append(
        attend_values(
            grouped_query[seq_item],
            key_block_list[seq_item],
            value_block_list[seq_item],
            mask_list[seq_item],
            log_sum,
            score_scale,
        )
    )
    mixed_head_rows = (
        jnp.stack(attended_list)
        .reshape(total_row_count, QUERY_HEADS * HEAD_SIZE)
        .astype(jnp.bfloat16)
    )
    after_attn, mlp_in, gate_act, up_act, hidden, result = finish_forward(
        tokens, mixed_head_rows, attention_forward[6], mlp_full
    )
    layer_out = result.astype(jnp.bfloat16).reshape(
        sequence_count, sequences_per_shard, MODEL_WIDTH
    )
    attention_backward = (
        lax.all_gather(attn_norm, "shard", axis=0, tiled=True),
        lax.all_gather(query_weight, "shard", axis=0, tiled=True),
        lax.all_gather(key_projection, "shard", axis=0, tiled=True),
        lax.all_gather(value_projection, "shard", axis=0, tiled=True),
        lax.all_gather(query_norm, "shard", axis=0, tiled=True),
        lax.all_gather(key_norm, "shard", axis=0, tiled=True),
        lax.all_gather(out_weight, "shard", axis=0, tiled=True),
    )
    mlp_back = (
        lax.all_gather(mlp_norm, "shard", axis=0, tiled=True),
        lax.all_gather(gate_weight, "shard", axis=0, tiled=True),
        lax.all_gather(up_weight, "shard", axis=0, tiled=True),
        lax.all_gather(down_weight, "shard", axis=0, tiled=True),
    )
    normed, query_raw, unrotated_key, rotated_query, rotated_key, value_row_list = project_inputs(
        tokens, attention_backward, position_per_row
    )
    key_again, value_again = (
        lax.all_gather(
            rotated_key.reshape(sequence_count, sequences_per_shard, key_value_width),
            "rep",
            axis=1,
            tiled=True,
        ),
        lax.all_gather(
            value_row_list.reshape(sequence_count, sequences_per_shard, key_value_width),
            "rep",
            axis=1,
            tiled=True,
        ),
    )
    grouped_query, key_block_list, value_block_list = split_heads(
        rotated_query,
        key_again,
        value_again,
        sequence_count,
        sequences_per_shard,
        block_count,
        block_key,
    )
    attended_list = []
    seq_item = 0
    attended_list.append(
        attend_values(
            grouped_query[seq_item],
            key_block_list[seq_item],
            value_block_list[seq_item],
            mask_list[seq_item],
            log_list[seq_item],
            score_scale,
        )
    )
    mixed_head_rows = (
        jnp.stack(attended_list)
        .reshape(total_row_count, QUERY_HEADS * HEAD_SIZE)
        .astype(jnp.bfloat16)
    )
    after_attn, mlp_in, gate_act, up_act, hidden, result_again = finish_forward(
        tokens, mixed_head_rows, attention_backward[6], mlp_back
    )
    down_in = out_grad.reshape(total_row_count, MODEL_WIDTH)
    down_w_grad = jnp.einsum("sf,sd->fd", hidden, down_in, preferred_element_type=jnp.float32)
    hidden_grad = jnp.einsum("sd,fd->sf", down_in, mlp_back[3], preferred_element_type=jnp.float32)
    unused_act, pull_act = jax.vjp(activate, gate_act, up_act)
    gate_grad, up_grad = pull_act(hidden_grad)
    gate_low = gate_grad.astype(jnp.bfloat16)
    up_low = up_grad.astype(jnp.bfloat16)
    gate_w_grad = jnp.einsum("sd,sf->df", mlp_in, gate_low, preferred_element_type=jnp.float32)
    up_w_grad = jnp.einsum("sd,sf->df", mlp_in, up_low, preferred_element_type=jnp.float32)
    mlp_in_grad = jnp.einsum(
        "sf,df->sd", gate_low, mlp_back[1], preferred_element_type=jnp.float32
    ) + jnp.einsum("sf,df->sd", up_low, mlp_back[2], preferred_element_type=jnp.float32)
    unused_norm, pull_norm = jax.vjp(root_mean_scale, after_attn, mlp_back[0].astype(jnp.float32))
    attn_out_grad, mlp_gain_grad = pull_norm(mlp_in_grad)
    residual_grad = cotangent + attn_out_grad
    mlp_shards = (
        lax.psum_scatter(
            mlp_gain_grad.astype(jnp.bfloat16), "shard", scatter_dimension=0, tiled=True
        ).astype(jnp.float32),
        lax.psum_scatter(
            gate_w_grad.astype(jnp.bfloat16), "shard", scatter_dimension=0, tiled=True
        ).astype(jnp.float32),
        lax.psum_scatter(
            up_w_grad.astype(jnp.bfloat16), "shard", scatter_dimension=0, tiled=True
        ).astype(jnp.float32),
        lax.psum_scatter(
            down_w_grad.astype(jnp.bfloat16), "shard", scatter_dimension=0, tiled=True
        ).astype(jnp.float32),
    )
    branch_grad = residual_grad.astype(jnp.bfloat16)
    out_w_grad = jnp.einsum(
        "sm,sd->md", mixed_head_rows, branch_grad, preferred_element_type=jnp.float32
    )
    mixed_gradient = jnp.einsum(
        "sd,md->sm", branch_grad, attention_backward[6], preferred_element_type=jnp.float32
    ).astype(jnp.bfloat16)
    gradient_groups = mixed_gradient.reshape(
        sequence_count,
        sequences_per_shard,
        KEY_VALUE_HEADS,
        QUERY_HEADS // KEY_VALUE_HEADS,
        HEAD_SIZE,
    )
    seq_item = 0
    dquery, kv_terms = attention_back(
        grouped_query[seq_item],
        key_block_list[seq_item],
        value_block_list[seq_item],
        mask_list[seq_item],
        log_list[seq_item],
        gradient_groups[seq_item],
        score_scale,
    )
    dquery_list = [dquery]
    kv_list = [kv_terms]
    query_rot_grad = jnp.stack(dquery_list).reshape(total_row_count, QUERY_HEADS, HEAD_SIZE)
    kv_grad = (
        lax.psum_scatter(
            jnp.stack(kv_list).astype(jnp.bfloat16), "rep", scatter_dimension=1, tiled=True
        )
        .astype(jnp.float32)
        .reshape(total_row_count, 2 * key_value_width)
    )
    rotated_key_gradient = kv_grad[:, :key_value_width]
    value_low = kv_grad[:, key_value_width:].astype(jnp.bfloat16)
    unused_query, pull_query = jax.vjp(
        partial(head_output, position_per_row, QUERY_HEADS),
        query_raw,
        attention_backward[4].astype(jnp.float32),
    )
    query_raw_grad, query_gain_grad = pull_query(query_rot_grad)
    unused_key, gather_key_rows = jax.vjp(
        partial(head_output, position_per_row, KEY_VALUE_HEADS),
        unrotated_key,
        attention_backward[5].astype(jnp.float32),
    )
    unrotated_key_gradient, key_scale_gradient = gather_key_rows(
        rotated_key_gradient.reshape(total_row_count, KEY_VALUE_HEADS, HEAD_SIZE)
    )
    query_low = query_raw_grad.astype(jnp.bfloat16)
    key_low = unrotated_key_gradient.astype(jnp.bfloat16)
    query_w_grad = jnp.einsum("sd,sq->dq", normed, query_low, preferred_element_type=jnp.float32)
    key_w_grad = jnp.einsum("sd,sq->dq", normed, key_low, preferred_element_type=jnp.float32)
    value_w_grad = jnp.einsum("sd,sq->dq", normed, value_low, preferred_element_type=jnp.float32)
    normed_grad = jnp.einsum(
        "sq,dq->sd", query_low, attention_backward[1], preferred_element_type=jnp.float32
    )
    normed_grad = normed_grad + jnp.einsum(
        "sq,dq->sd", key_low, attention_backward[2], preferred_element_type=jnp.float32
    )
    normed_grad = normed_grad + jnp.einsum(
        "sq,dq->sd", value_low, attention_backward[3], preferred_element_type=jnp.float32
    )
    unused_attn, pull_attn = jax.vjp(
        root_mean_scale, tokens, attention_backward[0].astype(jnp.float32)
    )
    token_grad, attn_gain_grad = pull_attn(normed_grad)
    in_grad = (
        (residual_grad + token_grad)
        .astype(jnp.bfloat16)
        .reshape(sequence_count, sequences_per_shard, MODEL_WIDTH)
    )
    attn_shards = (
        lax.psum_scatter(
            attn_gain_grad.astype(jnp.bfloat16), "shard", scatter_dimension=0, tiled=True
        ).astype(jnp.float32),
        lax.psum_scatter(
            query_w_grad.astype(jnp.bfloat16), "shard", scatter_dimension=0, tiled=True
        ).astype(jnp.float32),
        lax.psum_scatter(
            key_w_grad.astype(jnp.bfloat16), "shard", scatter_dimension=0, tiled=True
        ).astype(jnp.float32),
        lax.psum_scatter(
            value_w_grad.astype(jnp.bfloat16), "shard", scatter_dimension=0, tiled=True
        ).astype(jnp.float32),
        lax.psum_scatter(
            query_gain_grad.astype(jnp.bfloat16), "shard", scatter_dimension=0, tiled=True
        ).astype(jnp.float32),
        lax.psum_scatter(
            key_scale_gradient.astype(jnp.bfloat16), "shard", scatter_dimension=0, tiled=True
        ).astype(jnp.float32),
        lax.psum_scatter(
            out_w_grad.astype(jnp.bfloat16), "shard", scatter_dimension=0, tiled=True
        ).astype(jnp.float32),
    )
    totals = (
        lax.psum(attn_shards[0].astype(jnp.bfloat16), "rep").astype(jnp.float32),
        lax.psum(attn_shards[1].astype(jnp.bfloat16), "rep").astype(jnp.float32),
        lax.psum(attn_shards[2].astype(jnp.bfloat16), "rep").astype(jnp.float32),
        lax.psum(attn_shards[3].astype(jnp.bfloat16), "rep").astype(jnp.float32),
        lax.psum(attn_shards[4].astype(jnp.bfloat16), "rep").astype(jnp.float32),
        lax.psum(attn_shards[5].astype(jnp.bfloat16), "rep").astype(jnp.float32),
        lax.psum(attn_shards[6].astype(jnp.bfloat16), "rep").astype(jnp.float32),
        lax.psum(mlp_shards[0].astype(jnp.bfloat16), "rep").astype(jnp.float32),
        lax.psum(mlp_shards[1].astype(jnp.bfloat16), "rep").astype(jnp.float32),
        lax.psum(mlp_shards[2].astype(jnp.bfloat16), "rep").astype(jnp.float32),
        lax.psum(mlp_shards[3].astype(jnp.bfloat16), "rep").astype(jnp.float32),
    )
    return (
        layer_out,
        in_grad,
        totals[0],
        totals[1],
        totals[2],
        totals[3],
        totals[4],
        totals[5],
        totals[6],
        totals[7],
        totals[8],
        totals[9],
        totals[10],
    )


def solution(mesh):
    placed = (
        P("shard", "rep", None),
        P("shard", "rep", None),
        P("shard"),
        P("shard", None),
        P("shard", None),
        P("shard", None),
        P("shard"),
        P("shard"),
        P("shard", None),
        P("shard"),
        P("shard", None),
        P("shard", None),
        P("shard", None),
        P("shard", None),
        P("shard"),
    )
    return jax.shard_map(
        per_device,
        mesh=mesh,
        in_specs=placed,
        out_specs=(
            P("shard", "rep", None),
            P("shard", "rep", None),
            P("shard"),
            P("shard", None),
            P("shard", None),
            P("shard", None),
            P("shard"),
            P("shard"),
            P("shard", None),
            P("shard"),
            P("shard", None),
            P("shard", None),
            P("shard", None),
        ),
        check_vma=False,
    )
```

profile of v0, /device:TPU:0, one launch (start us, length us, event | category | flops | bytes accessed | tf_op | source)
XLA Modules:
  0.0 1095.8 jit_solution(11107517354061448778)
XLA Ops:
  8.7 13.5 %all-gather.1 = bf16[8,1,128]{2,1,0:T(2,128)(2,1)S(1)} all-gather(bf16[1,1,128]{2,1,0:T(2,128)(2,1)} %bitcast.372), channel_id=1, replica_groups=mesh['rep'=4,'shard'=8] {'shard'}, dimensions={0}, use_global_device_ids=true | all-gather | bytes 2304 | tf_op jit(solution)/shard_map/all_gather | solution.py:275
  24.0 17.4 %all-gather.13.cloned.1.call-done = bf16[1024,1024]{1,0:T(8,128)(2,1)} async-done(((bf16[128,1024]{1,0:T(8,128)(2,1)}), bf16[1024,1024]{1,0:T(8,128)(2,1)}) %all-gather.13.cloned.1.call-update) | async-done | bytes 2097168 | tf_op jit(solution)/shard_map/all_gather | solution.py:278
  41.5 3.3 convolution_convert_fusion.8
  46.7 15.7 %all-reduce.11 = (bf16[128]{0:T(256)(128)(2,1)S(1)}, bf16[128]{0:T(256)(128)(2,1)S(1)}) all-reduce(bf16[128]{0:T(256)(128)(2,1)S(1)} %dynamic-update-slice, bf16[128]{0:T(256)(128)(2,1)S(1)} %dynamic-update-slice.1), channel_id=1, replica_groups=mesh['rep'=4,'shard'=8] {'shard'}, use_global_device_ids=true, to_apply=%add.4 | all-reduce | flops 256 | bytes 1024
  62.8 9.2 all-gather.15.cloned.1.call-done
  72.0 2.9 copy.100
  82.5 10.5 all-gather.2
  94.2 15.0 %all-gather.29.cloned.1.call-done = bf16[1024,1024]{1,0:T(8,128)(2,1)} async-done(((bf16[256,1024]{1,0:T(8,128)(2,1)}), bf16[1024,1024]{1,0:T(8,128)(2,1)}) %all-gather.29.cloned.1.call-update) | async-done | bytes 2097168 | tf_op jit(solution)/shard_map/all_gather | solution.py:299
  109.2 3.6 copy.154
  112.8 34.0 %all-gather.17.cloned.1.call-done = bf16[1,1024,1024]{2,1,0:T(8,128)(2,1)} async-done(((bf16[1,256,1024]{2,1,0:T(8,128)(2,1)}), bf16[1,1024,1024]{2,1,0:T(8,128)(2,1)}) %all-gather.17.cloned.1.call-update) | async-done | bytes 2097168 | tf_op jit(solution)/shard_map/all_gather | solution.py:293
  152.3 43.1 %all-gather.19.cloned.1.call-done = bf16[1024,2048]{1,0:T(8,128)(2,1)} async-done(((bf16[128,2048]{1,0:T(8,128)(2,1)}), bf16[1024,2048]{1,0:T(8,128)(2,1)}) %all-gather.19.cloned.1.call-update) | async-done | bytes 4194320 | tf_op jit(solution)/shard_map/all_gather | solution.py:276
  195.4 6.4 copy.102
  201.8 3.9 multiply_reduce_fusion.2
  208.5 24.9 %while.52 = (s32[]{:T(128)}, f32[8,2,256]{2,1,0:T(2,128)S(1)}, f32[8,2,256]{2,1,0:T(2,128)}, pred[2,256,512]{1,2,0:T(8,128)(4,1)S(1)}, bf16[2,512,8,128]{3,1,2,0...) while((s32[]{:T(128)}, f32[8,2,256]{2,1,0:T(2,128)S(1)}, ...), condition=%wide.region_8.9_spmd.clone, body=%wide.region_5.8_spmd.clone.sunk | while | flops 553668608 | bytes 19742888 | solution.py:99
  208.5 6.5 fusion.189
  215.7 4.6 select_reduce_fusion.4
  220.9 6.5 fusion.189
  228.2 4.5 select_reduce_fusion.4
  234.7 21.4 %while.53 = (s32[]{:T(128)}, f32[256,8,2,128]{0,3,2,1:T(8,128)}, bf16[2,512,8,128]{3,2,1,0:T(8,128)(2,1)}, pred[2,256,512]{1,2,0:T(8,128)(4,1)S(1)}, bf16[2,512,...) while((s32[]{:T(128)}, f32[256,8,2,128]{0,3,2,1:T(8,128)}, ...), condition=%wide.region_10.11_spmd.clone, body=%wide.region_9.10_spmd.clone.sunk | while | flops 1083179008 | bytes 12009623 | solution.py:126
  239.4 5.2 bitcast_add_fusion.4
  249.3 6.3 bitcast_add_fusion.4
  256.1 2.7 convert_element_type.251
  258.8 4.0 multiply_reduce_fusion.7
  264.8 43.1 %all-gather.23.cloned.1.call-done = bf16[1024,3072]{1,0:T(8,128)(2,1)} async-done(((bf16[128,3072]{1,0:T(8,128)(2,1)}), bf16[1024,3072]{1,0:T(8,128)(2,1)}) %all-gather.23.cloned.1.call-update) | async-done | bytes 6291472 | tf_op jit(solution)/shard_map/all_gather | solution.py:285
  307.9 6.4 fusion.116
  314.3 58.7 %all-gather.25.cloned.1.call-done = bf16[1024,3072]{1,0:T(8,128)(2,1)} async-done(((bf16[128,3072]{1,0:T(8,128)(2,1)}), bf16[1024,3072]{1,0:T(8,128)(2,1)}) %all-gather.25.cloned.1.call-update) | async-done | bytes 6291472 | tf_op jit(solution)/shard_map/all_gather | solution.py:286
  373.0 6.4 fusion.117
  379.4 58.6 %all-gather.27.cloned.1.call-done = bf16[3072,1024]{1,0:T(8,128)(2,1)} async-done(((bf16[384,1024]{1,0:T(8,128)(2,1)}), bf16[3072,1024]{1,0:T(8,128)(2,1)}) %all-gather.27.cloned.1.call-update) | async-done | bytes 6291472 | tf_op jit(solution)/shard_map/all_gather | solution.py:287
  438.1 8.9 multiply_convert_fusion
  447.0 5.8 fusion.118
  462.1 3.6 copy.114
  468.2 12.1 %while.54 = (s32[]{:T(128)}, f32[8,2,256]{2,1,0:T(2,128)S(1)}, pred[2,256,512]{1,2,0:T(8,128)(4,1)S(1)}, bf16[2,512,8,128]{3,1,2,0:T(8,128)(2,1)S(1)}, bf16[256,...) while((s32[]{:T(128)}, f32[8,2,256]{2,1,0:T(2,128)S(1)}, ...), condition=%wide.region_15.16_spmd.clone, body=%wide.region_13.15_spmd.clone.sunk | while | flops 1084231680 | bytes 34029752 | solution.py:151
  470.9 3.3 fusion.201
  476.9 3.3 fusion.201
  480.3 54.1 %while.55 = (s32[]{:T(128)}, f32[256,8,2,128]{0,3,2,1:T(8,128)}, bf16[2,512,2048]{2,1,0:T(8,128)(2,1)}, bf16[2,512,8,128]{3,1,2,0:T(8,128)(2,1)S(1)}, pred[2,256...) while((s32[]{:T(128)}, f32[256,8,2,128]{0,3,2,1:T(8,128)}, ...), condition=%wide.region_17.18_spmd.clone, body=%wide.region_16.17_spmd.clone.sunk | while | flops 2712666112 | bytes 165331344 | solution.py:184
  481.6 3.3 copy-done.1
  484.9 4.3 fusion.213
  489.2 4.5 bitcast_add_fusion.5
  500.0 4.0 copy.159
  503.9 3.1 constant_dynamic-update-slice_fusion.2
  508.4 3.3 copy-done.1
  511.6 4.3 fusion.213
  516.0 5.1 bitcast_add_fusion.5
  527.3 4.0 copy.159
  531.3 3.1 constant_dynamic-update-slice_fusion.2
  539.2 3.4 convolution_convert_fusion.4
  544.2 3.2 convolution_convert_fusion.3
  547.5 38.4 %reduce-scatter.9.cloned.1.call-done = bf16[1,256,2048]{2,1,0:T(8,128)(2,1)} async-done(((bf16[1,1024,2048]{2,1,0:T(8,128)(2,1)}), bf16[1,256,2048]{2,1,0:T(8,128)(2,1)}) %reduce-scatter.9.cloned.1.call-update) | async-done | bytes 1048592 | tf_op jit(solution)/shard_map/reduce_scatter | solution.py:460
  595.0 3.2 convolution_convert_fusion.6
  598.3 5.9 convolution_convert_fusion.2
  604.3 5.9 convolution_convert_fusion.1
  611.2 6.0 convolution_convert_fusion
  617.3 21.1 %reduce-scatter.11.cloned.1.call-done = bf16[128,2048]{1,0:T(8,128)(2,1)} async-done(((bf16[1024,2048]{1,0:T(8,128)(2,1)}), bf16[128,2048]{1,0:T(8,128)(2,1)}) %reduce-scatter.11.cloned.1.call-update) | async-done | bytes 524304 | tf_op jit(solution)/shard_map/reduce_scatter | solution.py:509
  638.4 50.4 %reduce-scatter.17.cloned.1.call-done = bf16[256,1024]{1,0:T(8,128)(2,1)} async-done(((bf16[2048,1024]{1,0:T(8,128)(2,1)}), bf16[256,1024]{1,0:T(8,128)(2,1)}) %reduce-scatter.17.cloned.1.call-update) | async-done | bytes 524304 | tf_op jit(solution)/shard_map/reduce_scatter | solution.py:524
  688.8 36.3 %reduce-scatter.13.cloned.1.call-done = bf16[128,1024]{1,0:T(8,128)(2,1)} async-done(((bf16[1024,1024]{1,0:T(8,128)(2,1)}), bf16[128,1024]{1,0:T(8,128)(2,1)}) %reduce-scatter.13.cloned.1.call-update) | async-done | bytes 262160 | tf_op jit(solution)/shard_map/reduce_scatter | solution.py:512
  725.2 36.6 %reduce-scatter.15.cloned.1.call-done = bf16[128,1024]{1,0:T(8,128)(2,1)} async-done(((bf16[1024,1024]{1,0:T(8,128)(2,1)}), bf16[128,1024]{1,0:T(8,128)(2,1)}) %reduce-scatter.15.cloned.1.call-update) | async-done | bytes 262160 | tf_op jit(solution)/shard_map/reduce_scatter | solution.py:515
  761.8 70.8 %reduce-scatter.19.cloned.1.call-done = bf16[128,3072]{1,0:T(8,128)(2,1)} async-done(((bf16[1024,3072]{1,0:T(8,128)(2,1)}), bf16[128,3072]{1,0:T(8,128)(2,1)}) %reduce-scatter.19.cloned.1.call-update) | async-done | bytes 786448 | tf_op jit(solution)/shard_map/reduce_scatter | solution.py:422
  832.6 70.4 %reduce-scatter.21.cloned.1.call-done = bf16[128,3072]{1,0:T(8,128)(2,1)} async-done(((bf16[1024,3072]{1,0:T(8,128)(2,1)}), bf16[128,3072]{1,0:T(8,128)(2,1)}) %reduce-scatter.21.cloned.1.call-update) | async-done | bytes 786448 | tf_op jit(solution)/shard_map/reduce_scatter | solution.py:425
  903.0 70.5 %reduce-scatter.23.cloned.1.call-done = bf16[384,1024]{1,0:T(8,128)(2,1)} async-done(((bf16[3072,1024]{1,0:T(8,128)(2,1)}), bf16[384,1024]{1,0:T(8,128)(2,1)}) %reduce-scatter.23.cloned.1.call-update) | async-done | bytes 786448 | tf_op jit(solution)/shard_map/reduce_scatter | solution.py:428
  974.8 3.6 fusion.119
  978.5 5.6 fusion.76
  988.0 14.5 %all-reduce.10 = (bf16[1024]{0:T(1024)(128)(2,1)S(1)}, bf16[128]{0:T(256)(128)(2,1)S(1)}, bf16[128]{0:T(256)(128)(2,1)S(1)}, bf16[1024]{0:T(1024)(128)(2,1)S(1)}) all-reduce(bf16[1024]{0:T(1024)(128)(2,1)S(1)} %get-tuple-element.433, bf16[128]{0:T(256)(128)(2,1)S(1)} %get-tuple-element.427, ...), channel_id=4, replica_groups=mesh['rep'=4,'shard'=8] {'shard'}, use_global_device_ids=true, to_apply=%region_23.24.clone | all-reduce | flops 2304 | bytes 9216
  1002.7 10.2 all-reduce.12
  1017.3 60.5 %all-reduce.16.cloned.1.call-done = (bf16[128,2048]{1,0:T(8,128)(2,1)}, bf16[128,1024]{1,0:T(8,128)(2,1)}, bf16[128,1024]{1,0:T(8,128)(2,1)}, bf16[256,1024]{1,0...) async-done(((bf16[128,2048]{1,0:T(8,128)(2,1)}, bf16[128,1024]{1,0:T(8,128)(2,1)}, bf16[128,1024]{1,0:T(8,128)(2,1)}, ...) | async-done | bytes 3932176 | tf_op jit(solution)/shard_map/psum | solution.py:530
  (326 shorter events, 104.2 us)
Async XLA Ops:
  7.2 37.7 %copy-start.67 = (u32[32]{0:T(128)S(1)}, u32[32]{0:T(128)}, u32[]{:S(2)}) copy-start(u32[32]{0:T(128)} %constant.132) | copy-start | bytes 388
  7.2 39.0 %copy-start.74 = (bf16[16]{0:T(256)(128)(2,1)S(1)}, bf16[16]{0:T(256)(128)(2,1)}, u32[]{:S(2)}) copy-start(bf16[16]{0:T(256)(128)(2,1)} %param.30) | copy-start | bytes 100
  7.2 39.2 %copy-start.75 = (bf16[16]{0:T(256)(128)(2,1)S(1)}, bf16[16]{0:T(256)(128)(2,1)}, u32[]{:S(2)}) copy-start(bf16[16]{0:T(256)(128)(2,1)} %param.29) | copy-start | bytes 100
  7.2 34.3 %all-gather.13.cloned.1.call-start = ((), (), s32[]{:S(2)}) async-start(), calls=%async_computation.8 | async-start | bytes 2359296 | tf_op jit(solution)/shard_map/all_gather | solution.py:278
  7.9 64.0 %all-gather.15.cloned.1.call-start = ((), (), s32[]{:S(2)}) async-start(), calls=%async_computation.9 | async-start | bytes 2359296 | tf_op jit(solution)/shard_map/all_gather | solution.py:277
  8.7 100.5 %all-gather.29.cloned.1.call-start = ((), (), s32[]{:S(2)}) async-start(), calls=%async_computation.24 | async-start | bytes 2621440 | tf_op jit(solution)/shard_map/all_gather | solution.py:299
  22.3 52.5 %copy-start.43 = (f32[8,1,128]{2,1,0:T(1,128)}, f32[8,1,128]{2,1,0:T(1,128)S(1)}, u32[]{:S(2)}) copy-start(f32[8,1,128]{2,1,0:T(1,128)S(1)} %convert_element_type.292) | copy-start | bytes 12292
  24.0 50.8 %copy-start.52 = (f32[256]{0:T(256)}, f32[256]{0:T(256)S(1)}, u32[]{:S(2)}) copy-start(f32[256]{0:T(256)S(1)} %fusion.107) | copy-start | bytes 3076
  44.8 30.0 %copy-start.7 = (bf16[1,256,1024]{2,1,0:T(8,128)(2,1)S(1)}, bf16[1,256,1024]{2,1,0:T(8,128)(2,1)}, u32[]{:S(2)}) copy-start(bf16[1,256,1024]{2,1,0:T(8,128)(2,1)} %param.23) | copy-start | bytes 1572868
  44.8 102.0 %all-gather.17.cloned.1.call-start = ((), (), s32[]{:S(2)}) async-start(), calls=%async_computation.10 | async-start | bytes 2621440 | tf_op jit(solution)/shard_map/all_gather | solution.py:293
  62.4 13.3 %copy-start.63 = (f32[128]{0:T(128)}, f32[128]{0:T(128)S(1)}, u32[]{:S(2)}) copy-start(f32[128]{0:T(128)S(1)} %convert_element_type.247) | copy-start | bytes 1540
  62.8 143.4 %copy-start.26 = (f32[256,64]{0,1:T(8,128)}, f32[256,64]{0,1:T(8,128)S(1)}, u32[]{:S(2)}) copy-start(f32[256,64]{0,1:T(8,128)S(1)} %get-tuple-element.527) | copy-start | bytes 196612
  62.8 143.4 %copy-start.28 = (f32[256,64]{0,1:T(8,128)}, f32[256,64]{0,1:T(8,128)S(1)}, u32[]{:S(2)}) copy-start(f32[256,64]{0,1:T(8,128)S(1)} %get-tuple-element.528) | copy-start | bytes 196612
  77.0 5.3 copy-start.69
  77.0 5.4 copy-start.70
  78.1 117.3 %all-gather.19.cloned.1.call-start = ((), (), s32[]{:S(2)}) async-start(), calls=%async_computation.11 | async-start | bytes 4718592 | tf_op jit(solution)/shard_map/all_gather | solution.py:276
  78.7 180.1 %all-gather.21.cloned.1.call-start = ((), (), s32[]{:S(2)}) async-start(), calls=%async_computation.12 | async-start | bytes 4718592 | tf_op jit(solution)/shard_map/all_gather | solution.py:281
  79.3 228.6 %all-gather.23.cloned.1.call-start = ((), (), s32[]{:S(2)}) async-start(), calls=%async_computation.13 | async-start | bytes 7077888 | tf_op jit(solution)/shard_map/all_gather | solution.py:285
  80.1 292.9 %all-gather.25.cloned.1.call-start = ((), (), s32[]{:S(2)}) async-start(), calls=%async_computation.14 | async-start | bytes 7077888 | tf_op jit(solution)/shard_map/all_gather | solution.py:286
  80.8 357.3 %all-gather.27.cloned.1.call-start = ((), (), s32[]{:S(2)}) async-start(), calls=%async_computation.15 | async-start | bytes 7077888 | tf_op jit(solution)/shard_map/all_gather | solution.py:287
  81.5 504.4 %reduce-scatter.9.cloned.1.call-start = ((), (), s32[]{:S(2)}) async-start(), calls=%async_computation.16 | async-start | bytes 5242880 | tf_op jit(solution)/shard_map/reduce_scatter | solution.py:460
  82.5 123.3 %copy-start.65 = (f32[128]{0:T(128)}, f32[128]{0:T(128)S(1)}, u32[]{:S(2)}) copy-start(f32[128]{0:T(128)S(1)} %convert_element_type.250) | copy-start | bytes 1540
  195.4 6.4 copy-start.44
  195.4 6.4 copy-start.53
  215.7 4.6 copy-start.39
  228.2 4.6 copy-start.39
  234.7 4.7 copy-start.58
  244.6 4.7 copy-start.58
  258.8 5.1 copy-start.55
  447.0 5.8 copy-start.31
  447.0 5.8 copy-start.30
  447.0 5.8 copy-start.19
  447.0 6.0 copy-start.71
  459.5 8.7 copy-start.42
  480.3 4.6 copy-start.23
  480.3 4.6 copy-start.33
  480.3 4.6 copy-start.59
  489.2 5.4 copy-start.2
  489.2 5.6 copy-start.34
  489.2 5.6 copy-start.60
  507.1 4.6 copy-start.23
  507.1 4.6 copy-start.33
  507.1 4.6 copy-start.59
  516.0 6.0 copy-start.2
  516.0 6.2 copy-start.34
  516.0 6.2 copy-start.60
  534.5 103.9 %reduce-scatter.11.cloned.1.call-start = ((), (), s32[]{:S(2)}) async-start(), calls=%async_computation.17 | async-start | bytes 4718592 | tf_op jit(solution)/shard_map/reduce_scatter | solution.py:509
  542.7 146.1 %reduce-scatter.17.cloned.1.call-start = ((), (), s32[]{:S(2)}) async-start(), calls=%async_computation.20 | async-start | bytes 4718592 | tf_op jit(solution)/shard_map/reduce_scatter | solution.py:524
  547.5 44.5 %copy-start.10 = (f32[256,8,128]{0,2,1:T(8,128)S(1)}, f32[256,8,128]{0,2,1:T(8,128)}, u32[]{:S(2)}) copy-start(f32[256,8,128]{0,2,1:T(8,128)} %copy-done.9) | copy-start | bytes 3145732
  547.5 44.5 %copy-start.49 = (f32[256,8]{0,1:T(8,128)S(1)}, f32[256,8]{0,1:T(8,128)}, u32[]{:S(2)}) copy-start(f32[256,8]{0,1:T(8,128)} %copy-done.48) | copy-start | bytes 24580
  547.5 44.5 %copy-start.64 = (f32[128]{0:T(128)S(1)}, f32[128]{0:T(128)}, u32[]{:S(2)}) copy-start(f32[128]{0:T(128)} %copy-done.63) | copy-start | bytes 1540
  547.5 177.7 %reduce-scatter.13.cloned.1.call-start = ((), (), s32[]{:S(2)}) async-start(), calls=%async_computation.18 | async-start | bytes 2359296 | tf_op jit(solution)/shard_map/reduce_scatter | solution.py:512
  588.1 4.3 copy-start.57
  595.0 166.8 %reduce-scatter.15.cloned.1.call-start = ((), (), s32[]{:S(2)}) async-start(), calls=%async_computation.19 | async-start | bytes 2359296 | tf_op jit(solution)/shard_map/reduce_scatter | solution.py:515
  598.3 234.3 %reduce-scatter.19.cloned.1.call-start = ((), (), s32[]{:S(2)}) async-start(), calls=%async_computation.21 | async-start | bytes 7077888 | tf_op jit(solution)/shard_map/reduce_scatter | solution.py:422
  604.2 298.8 %reduce-scatter.21.cloned.1.call-start = ((), (), s32[]{:S(2)}) async-start(), calls=%async_computation.22 | async-start | bytes 7077888 | tf_op jit(solution)/shard_map/reduce_scatter | solution.py:425
  610.2 363.3 %reduce-scatter.23.cloned.1.call-start = ((), (), s32[]{:S(2)}) async-start(), calls=%async_computation.23 | async-start | bytes 7077888 | tf_op jit(solution)/shard_map/reduce_scatter | solution.py:428
  617.2 357.6 %copy-start.17 = (bf16[256,16,128]{0,2,1:T(8,128)(2,1)S(1)}, bf16[256,16,128]{0,2,1:T(8,128)(2,1)}, u32[]{:S(2)}) copy-start(bf16[256,16,128]{0,2,1:T(8,128)(2,1)} %copy-done.16) | copy-start | bytes 3145732
  617.2 460.6 %all-reduce.16.cloned.1.call-start = ((), (), s32[]{:S(2)}) async-start(), calls=%async_computation.25 | async-start | bytes 7864320 | tf_op jit(solution)/shard_map/psum | solution.py:530
  978.5 5.6 copy-start.13
  986.0 29.0 %copy-start.62 = (f32[256]{0:T(256)S(1)}, f32[256]{0:T(256)}, u32[]{:S(2)}) copy-start(f32[256]{0:T(256)} %copy-done.61) | copy-start | bytes 3076
  1077.8 5.9 copy-start.41
  1077.8 7.0 copy-start.38
  1080.1 6.1 copy-start.37
  (43 other events, 82.1 us)
Sparse Core Ops, SparseCore 0:
  9.6 31.7 all-gather.12
  43.1 28.8 all-gather.14
  74.4 34.7 all-gather.28
  111.4 35.2 all-gather.16
  148.2 47.1 all-gather.18
  196.9 45.8 all-gather.20
  244.4 63.4 all-gather.22
  309.6 63.3 all-gather.24
  374.6 63.3 all-gather.26
  534.6 51.3 reduce-scatter.8
  588.4 49.9 reduce-scatter.10
  640.7 48.1 reduce-scatter.16
  691.2 33.9 reduce-scatter.12
  727.4 34.2 reduce-scatter.14
  764.0 68.4 reduce-scatter.18
  834.8 68.1 reduce-scatter.20
  905.3 68.1 reduce-scatter.22
  977.7 100.0 all-reduce.15
where the time goes:
time: 1100 us
  waiting for transfers between devices  739 us (67%)
  matrix products  150 us (14%)
  local copies, waits for them, and re-layouts  78.1 us (7%)
  blocking collectives  64.5 us (6%)
  other arithmetic  44 us (4%)
  between operations  18 us (2%)
    reduce_scatter x1, waiting for transfers between devices, per_device(): lax.psum_scatter(gate_w_grad.astype(jnp.bfloat16), 'shard', scatter_dimen...  70.8 us
    reduce_scatter x1, waiting for transfers between devices, per_device(): lax.psum_scatter(down_w_grad.astype(jnp.bfloat16), 'shard', scatter_dimen...  70.5 us
    reduce_scatter x1, waiting for transfers between devices, per_device(): lax.psum_scatter(up_w_grad.astype(jnp.bfloat16), 'shard', scatter_dimensi...  70.4 us
    psum x1, waiting for transfers between devices, per_device(): lax.psum(attn_shards[1].astype(jnp.bfloat16), 'rep').astype(jnp.float32)  60.5 us
    all_gather x1, waiting for transfers between devices, per_device(): lax.all_gather(up_weight, 'shard', axis=0, tiled=True)  58.7 us
    all_gather x1, waiting for transfers between devices, per_device(): lax.all_gather(down_weight, 'shard', axis=0, tiled=True)  58.6 us
    reduce_scatter x1, waiting for transfers between devices, per_device(): lax.psum_scatter(out_w_grad.astype(jnp.bfloat16), 'shard', scatter_dimens...  50.4 us
    all_gather x1, waiting for transfers between devices, per_device(): lax.all_gather(gate_weight, 'shard', axis=0, tiled=True)  43.1 us
  transfers between devices with their start and end apart: 18, of which 17 were waited for; matrix products, arithmetic and copies ran while one was open for 14% of the time, Pallas kernels for 0%

commit v1 on v0

v1 whole, which is shorter than its diff:
```python
import jax
import jax.numpy as jnp
from jax import lax
from jax.experimental import pallas as pl
from jax.experimental.pallas import tpu as pltpu
from jax.sharding import PartitionSpec as P

MODEL_WIDTH = 1024
QUERY_HEADS = 16
KEY_VALUE_HEADS = 8
HEAD_SIZE = 128
GROUP = QUERY_HEADS // KEY_VALUE_HEADS
PIECE = 256

EPSILON = 1e-06
ROPE_BASE = 1000000.0
SCALE = HEAD_SIZE ** (-0.5)
LOG2E = 1.4426950408889634
BF = jnp.bfloat16
F32 = jnp.float32


def mm(a, b, dims=((1,), (0,))):
    return lax.dot_general(a, b, (dims, ((), ())), preferred_element_type=F32)


def flip(value, bit):
    count = lax.axis_size("rep")
    return lax.ppermute(value, "rep", [(i, i ^ bit) for i in range(count)])


def spread_blocks(value):
    count = lax.axis_size("rep")
    if count == 4:
        half = value.shape[0] // 2
        by_one, by_two = flip(value, 1), flip(value, 2)
        low, high = flip(by_one[:half], 2), flip(by_two[half:], 1)
        return jnp.stack([value, by_one, by_two, jnp.concatenate([low, high], axis=0)])
    blocks = value[None]
    bit = 1
    while bit < count:
        blocks = jnp.concatenate([blocks, flip(blocks, bit)], axis=0)
        bit *= 2
    return blocks


def sum_blocks(parts):
    count = lax.axis_size("rep")
    if count == 4:
        half = parts.shape[1] // 2
        a, b = parts[:, :half], parts[:, half:]
        a_in = flip(jnp.stack([a[1], a[3]]).astype(BF), 1).astype(F32)
        b_in = flip(jnp.stack([b[2], b[3]]).astype(BF), 2).astype(F32)
        a_last = flip((a[2] + a_in[1]).astype(BF), 2).astype(F32)
        b_last = flip((b[1] + b_in[1]).astype(BF), 1).astype(F32)
        return jnp.concatenate([a[0] + a_in[0] + a_last, b[0] + b_in[0] + b_last], axis=0)
    bit = count // 2
    while bit:
        parts = parts[:bit] + flip(parts[bit:].astype(BF), bit).astype(F32)
        bit //= 2
    return parts[0]


def ring_up(value):
    count = lax.axis_size("shard")
    return lax.ppermute(value, "shard", [(i, (i + 2) % count) for i in range(count)])


def other_core(value):
    count = lax.axis_size("shard")
    return lax.ppermute(value, "shard", [(i, i ^ 1) for i in range(count)])


def gather_rows(value):
    count = lax.axis_size("shard")
    chips = count // 2
    index = lax.axis_index("shard")
    chip, core = index // 2, index % 2
    full = jnp.zeros((count,) + value.shape, value.dtype)
    current = value
    for step in range(chips):
        if step:
            current = ring_up(current)
        place = 2 * ((chip + chips - step) % chips)
        full = lax.dynamic_update_index_in_dim(full, current, place + core, 0)
        full = lax.dynamic_update_index_in_dim(full, other_core(current), place + 1 - core, 0)
    return full, current


def scatter_rows(parts):
    count = lax.axis_size("shard")
    chips = count // 2
    index = lax.axis_index("shard")
    chip, core = index // 2, index % 2
    by_chip = parts.reshape((chips, 2) + parts.shape[1:])
    away = lax.dynamic_index_in_dim(by_chip, 1 - core, 1, keepdims=False).astype(BF)
    kept = lax.dynamic_index_in_dim(by_chip, core, 1, keepdims=False)
    paired = kept + other_core(away).astype(F32)

    def own(step):
        return lax.dynamic_index_in_dim(paired, (chip + 2 * chips - step) % chips, 0, keepdims=False)

    running = own(1)
    for step in range(1, chips):
        running = ring_up(running.astype(BF)).astype(F32) + own(step + 1)
    return running


def joint_move(value, pairs):
    shards = lax.axis_size("shard")
    joint = [
        (r0 * shards + 2 * z0 + c, r1 * shards + 2 * z1 + c)
        for (r0, z0), (r1, z1) in pairs
        for c in range(2)
    ]
    return lax.ppermute(value, ("rep", "shard"), joint)


def gather_heads(value):
    replicas, shards = lax.axis_size("rep"), lax.axis_size("shard")
    r, index = lax.axis_index("rep"), lax.axis_index("shard")
    if shards != 2 * replicas:
        full = lax.all_gather(value, "shard", axis=0, tiled=True)
        rows = full.shape[0] // replicas
        return lax.dynamic_slice_in_dim(full, r * rows, rows, 0)
    chip, core = index // 2, index % 2
    up = [((i, z), (i, z + 1)) for i in range(replicas) for z in range(i, replicas - 1)]
    down = [((i, z), (i, z - 1)) for i in range(replicas) for z in range(1, i + 1)]
    moved_up = joint_move(value, [p for p in up if p[0][1] == p[0][0]])
    moved_down = joint_move(value, [p for p in down if p[0][1] == p[0][0]])
    total = moved_up + moved_down
    result = jnp.where(chip == r, value, total)
    moved = total
    for hop in range(2, replicas):
        pairs = [p for p in up if p[0][1] - p[0][0] == hop - 1]
        pairs += [p for p in down if p[0][0] - p[0][1] == hop - 1]
        moved = joint_move(moved, pairs)
        result = result + moved
    other = other_core(result)
    first = jnp.where(core == 0, result, other)
    second = jnp.where(core == 0, other, result)
    return jnp.concatenate([first, second], axis=0)


def scatter_heads(parts):
    replicas, shards = lax.axis_size("rep"), lax.axis_size("shard")
    r, index = lax.axis_index("rep"), lax.axis_index("shard")
    if shards != 2 * replicas:
        rows = parts.shape[0]
        full = jnp.zeros((rows * replicas,) + parts.shape[1:], F32)
        full = lax.dynamic_update_slice_in_dim(full, parts, r * rows, 0)
        owned = lax.psum_scatter(full.astype(BF), "shard", scatter_dimension=0, tiled=True)
        return lax.psum(owned, "rep").astype(F32)
    chip, core = index // 2, index % 2
    halves = parts.reshape((2, -1) + parts.shape[1:])
    away = lax.dynamic_index_in_dim(halves, 1 - core, 0, keepdims=False).astype(BF)
    total = lax.dynamic_index_in_dim(halves, core, 0, keepdims=False) + other_core(away).astype(F32)
    low = total.astype(BF)
    for hop in range(1, replicas):
        pairs = [((i, (i + hop) % replicas), (i, i)) for i in range(replicas)]
        total = total + joint_move(low, pairs).astype(F32)
    low = total.astype(BF)
    if replicas == 4:
        half = low.shape[0] // 2
        one = joint_move(low, [((z, z), (z ^ 1, z)) for z in range(4)])
        two = joint_move(low, [((z, z), (z ^ 2, z)) for z in range(4)])
        top = joint_move(one[:half], [((z ^ 1, z), (z ^ 3, z)) for z in range(4)])
        bottom = joint_move(two[half:], [((z ^ 2, z), (z ^ 3, z)) for z in range(4)])
        rest = one + two + jnp.concatenate([top, bottom], axis=0)
    else:
        rest = jnp.zeros_like(low)
        for other in range(1, replicas):
            rest = rest + joint_move(low, [((z, z), ((z + other) % replicas, z)) for z in range(replicas)])
    return jnp.where(chip == r, low, rest).astype(F32)


def piece_mask(picture_flag, size, heads):
    key = lax.broadcasted_iota(jnp.int32, (size, size * heads), 0)
    query = lax.broadcasted_iota(jnp.int32, (size, size * heads), 1) % size
    return (key <= query) | (picture_flag > 0)


def attention_forward_kernel(info, q_ref, k_ref, v_ref, mixed_ref, lse_ref):
    blocks, size = k_ref.shape[0], k_ref.shape[1]
    own = info[0]
    for last in range(blocks):
        i = own ^ last
        query = jnp.concatenate(
            [q_ref[i, :, h * HEAD_SIZE : (h + 1) * HEAD_SIZE] for h in range(GROUP)], axis=0
        )
        total = jnp.zeros((1, GROUP * size), F32)
        mixed = jnp.zeros((HEAD_SIZE, GROUP * size), F32)
        for block in range(last + 1):
            j = own ^ block
            scores = mm(k_ref[j], query, ((1,), (1,)))
            weights = jnp.exp2(scores * (SCALE * LOG2E))
            if block == last:
                weights = jnp.where(piece_mask(info[1 + i], size, GROUP), weights, 0.0)
            total = total + jnp.sum(weights, axis=0, keepdims=True)
            mixed = mixed + mm(v_ref[j], weights.astype(BF), ((0,), (0,)))
        mixed = mixed * (1.0 / total)
        log_sum = jnp.log2(total)
        for h in range(GROUP):
            columns = slice(h * size, (h + 1) * size)
            mixed_ref[i, :, h * HEAD_SIZE : (h + 1) * HEAD_SIZE] = mixed[:, columns].T.astype(BF)
            lse_ref[i, h : h + 1, :] = log_sum[:, columns]


def attention_backward_kernel(
    info, q_ref, k_ref, v_ref, mixed_ref, lse_ref, grad_ref, dq_ref, dk_ref, dv_ref
):
    blocks, size = k_ref.shape[0], k_ref.shape[1]
    own = info[0]
    dk_ref[...] = jnp.zeros_like(dk_ref)
    dv_ref[...] = jnp.zeros_like(dv_ref)
    for last in range(blocks):
        i = own ^ last
        heads = [slice(h * HEAD_SIZE, (h + 1) * HEAD_SIZE) for h in range(GROUP)]
        query = jnp.concatenate([q_ref[i, :, h] for h in heads], axis=0)
        grad = jnp.concatenate([grad_ref[i, :, h] for h in heads], axis=0)
        mixed = jnp.concatenate([mixed_ref[i, :, h] for h in heads], axis=0)
        delta = jnp.sum((grad.astype(F32) * mixed.astype(F32)).T, axis=0, keepdims=True)
        log_sum = jnp.concatenate([lse_ref[i, h : h + 1, :] for h in range(GROUP)], axis=1)
        dquery = jnp.zeros((HEAD_SIZE, GROUP * size), F32)
        for block in range(last + 1):
            j = own ^ block
            scores = mm(k_ref[j], query, ((1,), (1,)))
            dprobs = mm(v_ref[j], grad, ((1,), (1,)))
            probs = jnp.exp2(scores * (SCALE * LOG2E) - log_sum)
            if block == last:
                probs = jnp.where(piece_mask(info[1 + i], size, GROUP), probs, 0.0)
            dscores = (probs * (dprobs - delta)).astype(BF)
            dv_ref[j] += mm(probs.astype(BF), grad)
            dk_ref[j] += mm(dscores, query)
            dquery = dquery + mm(k_ref[j], dscores, ((0,), (0,)))
        for h in range(GROUP):
            dq_ref[i, :, heads[h]] = dquery[:, h * size : (h + 1) * size].T * SCALE
    dk_ref[...] = dk_ref[...] * SCALE


def attention_specs(blocks, size):
    wide = pl.BlockSpec((blocks, size, GROUP * HEAD_SIZE), lambda g, info: (0, 0, g))
    thin = pl.BlockSpec((blocks, size, HEAD_SIZE), lambda g, info: (0, 0, g))
    rows = pl.BlockSpec((None, blocks, GROUP, size), lambda g, info: (g, 0, 0, 0))
    return wide, thin, rows


def attention_forward(info, query, key, value):
    blocks, size, width = key.shape
    groups = width // HEAD_SIZE
    wide, thin, rows = attention_specs(blocks, size)
    return pl.pallas_call(
        attention_forward_kernel,
        grid_spec=pltpu.PrefetchScalarGridSpec(
            num_scalar_prefetch=1,
            grid=(groups,),
            in_specs=[wide, thin, thin],
            out_specs=[wide, rows],
        ),
        out_shape=[
            jax.ShapeDtypeStruct(query.shape, BF),
            jax.ShapeDtypeStruct((groups, blocks, GROUP, size), F32),
        ],
        compiler_params=pltpu.CompilerParams(vmem_limit_bytes=48 << 20),
        name="attention_forward",
    )(info, query, key, value)


def attention_backward(info, query, key, value, mixed, lse, grad):
    blocks, size, width = key.shape
    groups = width // HEAD_SIZE
    wide, thin, rows = attention_specs(blocks, size)
    return pl.pallas_call(
        attention_backward_kernel,
        grid_spec=pltpu.PrefetchScalarGridSpec(
            num_scalar_prefetch=1,
            grid=(groups,),
            in_specs=[wide, thin, thin, wide, rows, wide],
            out_specs=[wide, thin, thin],
        ),
        out_shape=[
            jax.ShapeDtypeStruct(query.shape, F32),
            jax.ShapeDtypeStruct(key.shape, F32),
            jax.ShapeDtypeStruct(key.shape, F32),
        ],
        compiler_params=pltpu.CompilerParams(vmem_limit_bytes=48 << 20),
        name="attention_backward",
    )(info, query, key, value, mixed, lse, grad)


def inverse_root(values):
    return lax.rsqrt(jnp.mean(values * values, axis=-1, keepdims=True) + EPSILON)


def norm_back(values, inverse, gain, dy):
    weighted = dy * gain
    inner = jnp.mean(values * weighted, axis=-1, keepdims=True)
    return inverse * weighted - values * (inverse * inverse * inverse) * inner


def turn(values):
    return jnp.concatenate([values[..., HEAD_SIZE // 2 :], values[..., : HEAD_SIZE // 2]], axis=-1)


def per_device(
    layer_in,
    out_grad,
    attn_norm,
    query_weight,
    key_projection,
    value_projection,
    query_norm,
    key_norm,
    out_weight,
    mlp_norm,
    gate_weight,
    up_weight,
    down_weight,
    picture_starts,
    picture_count,
):
    replicas, shards = lax.axis_size("rep"), lax.axis_size("shard")
    r = lax.axis_index("rep")
    size = layer_in.shape[1]
    length = size * replicas
    rows = attn_norm.shape[0]
    q_width = QUERY_HEADS // replicas * HEAD_SIZE
    kv_width = KEY_VALUE_HEADS // replicas * HEAD_SIZE
    attn_width = q_width + 2 * kv_width
    ff_rows = down_weight.shape[0] // replicas
    ff = ff_rows * shards

    def columns_of(weight, width):
        return lax.dynamic_slice_in_dim(weight, r * width, width, 1)

    gains = jnp.concatenate([attn_norm, mlp_norm, query_norm, key_norm])
    head_rows = query_norm.shape[0]
    gain_rows = jnp.zeros((16, attn_width), BF).at[0, : gains.shape[0]].set(gains)
    attn_rows = jnp.concatenate(
        [
            jnp.concatenate(
                [
                    columns_of(query_weight, q_width),
                    columns_of(key_projection, kv_width),
                    columns_of(value_projection, kv_width),
                ],
                axis=1,
            ),
            gain_rows,
        ],
        axis=0,
    )

    def interleaved(weight):
        cut = weight.reshape(rows, shards, replicas, ff_rows)
        return lax.dynamic_index_in_dim(cut, r, 2, keepdims=False).reshape(rows, ff)

    gate_up_rows = jnp.concatenate([interleaved(gate_weight), interleaved(up_weight)], axis=1)
    down_rows = lax.dynamic_slice_in_dim(down_weight, r * ff_rows, ff_rows, 0)

    tokens = layer_in[0]
    all_tokens = spread_blocks(tokens)
    attn_all, attn_last = gather_rows(attn_rows)
    out_weight, _ = lax.optimization_barrier((out_weight, attn_last))
    out_matrix = gather_heads(out_weight)
    gate_up_rows, down_rows, _ = lax.optimization_barrier((gate_up_rows, down_rows, attn_last))
    gate_up_all, _ = gather_rows(gate_up_rows)
    down_all, _ = gather_rows(down_rows)
    cotangent_low, _ = lax.optimization_barrier((out_grad[0], all_tokens))
    all_cotangent = spread_blocks(cotangent_low).reshape(length, MODEL_WIDTH)

    attn_matrix = attn_all[:, :rows].reshape(MODEL_WIDTH, attn_width)
    gain_all = attn_all[:, rows].astype(F32)
    attn_gain = gain_all[:, :rows].reshape(MODEL_WIDTH)
    mlp_gain = gain_all[:, rows : 2 * rows].reshape(MODEL_WIDTH)
    query_gain = gain_all[:, 2 * rows : 2 * rows + head_rows].reshape(HEAD_SIZE)
    key_gain = gain_all[:, 2 * rows + head_rows : 2 * rows + 2 * head_rows].reshape(HEAD_SIZE)
    gate_up_matrix = gate_up_all.reshape(MODEL_WIDTH, 2 * ff)
    down_matrix = down_all.reshape(ff, MODEL_WIDTH)

    block_ids = r ^ jnp.arange(replicas, dtype=jnp.int32)
    positions = (block_ids[:, None] * size + jnp.arange(size, dtype=jnp.int32)[None, :]).reshape(-1)
    half = HEAD_SIZE // 2
    inv_freq = ROPE_BASE ** (-2.0 * jnp.arange(half, dtype=F32) / HEAD_SIZE)
    angles = positions.astype(F32)[:, None] * inv_freq[None, :]
    cosine, sine = jnp.cos(angles), jnp.sin(angles)
    cos_row = jnp.concatenate([cosine, cosine], axis=1)[:, None, :]
    sin_row = jnp.concatenate([-sine, sine], axis=1)[:, None, :]
    starts = picture_starts[0]
    held = (starts[None, :] == block_ids[:, None] * PIECE) & (
        jnp.arange(starts.shape[0], dtype=jnp.int32)[None, :] < picture_count[0]
    )
    info = jnp.concatenate([r[None].astype(jnp.int32), jnp.any(held, axis=1).astype(jnp.int32)])

    wide = all_tokens.reshape(length, MODEL_WIDTH).astype(F32)
    token_inverse = inverse_root(wide)
    normed = (wide * token_inverse * attn_gain).astype(BF)
    raw = mm(normed, attn_matrix)
    query_raw = raw[:, :q_width].reshape(length, -1, HEAD_SIZE)
    key_raw = raw[:, q_width : q_width + kv_width].reshape(length, -1, HEAD_SIZE)
    value = raw[:, q_width + kv_width :].astype(BF).reshape(replicas, size, kv_width)

    def rotated(values, gain):
        scaled = values * inverse_root(values) * gain
        return (scaled * cos_row + turn(scaled) * sin_row).astype(BF).reshape(replicas, size, -1)

    query, key = rotated(query_raw, query_gain), rotated(key_raw, key_gain)
    mixed, lse = attention_forward(info, query, key, value)
    mixed_rows = mixed.reshape(length, q_width)
    after_attn = tokens.astype(F32) + sum_blocks(
        mm(mixed_rows, out_matrix).reshape(replicas, size, MODEL_WIDTH)
    )
    after_inverse = inverse_root(after_attn)
    scaled_attn = after_attn * after_inverse
    mlp_in = spread_blocks((scaled_attn * mlp_gain).astype(BF)).reshape(length, MODEL_WIDTH)
    gate_up = mm(mlp_in, gate_up_matrix)
    gate_act, up_act = gate_up[:, :ff], gate_up[:, ff:]
    sigmoid = 1.0 / (1.0 + jnp.exp(-gate_act))
    silu = gate_act * sigmoid
    hidden = (silu * up_act).astype(BF)

    hidden_grad = mm(all_cotangent, down_matrix, ((1,), (1,)))
    gate_grad = (hidden_grad * up_act * sigmoid * (1.0 + gate_act * (1.0 - sigmoid))).astype(BF)
    up_grad = (hidden_grad * silu).astype(BF)
    gate_up_grad = jnp.concatenate([gate_grad, up_grad], axis=1)
    mlp_in_part = mm(gate_up_grad, gate_up_matrix, ((1,), (1,)))
    mlp_in_grad = sum_blocks(mlp_in_part.reshape(replicas, size, MODEL_WIDTH))
    residual_grad = out_grad[0].astype(F32) + norm_back(
        after_attn, after_inverse, mlp_gain, mlp_in_grad
    )
    mlp_gain_part = jnp.sum(mlp_in_grad * scaled_attn, axis=0)
    branch_grad = spread_blocks(residual_grad.astype(BF)).reshape(length, MODEL_WIDTH)

    layer_out = after_attn + sum_blocks(mm(hidden, down_matrix).reshape(replicas, size, MODEL_WIDTH))
    gate_up_w = scatter_rows(
        mm(mlp_in, gate_up_grad, ((0,), (0,))).reshape(shards, rows, 2 * ff)
    )
    down_w = scatter_rows(
        mm(hidden, all_cotangent, ((0,), (0,))).reshape(shards, ff_rows, MODEL_WIDTH)
    )

    out_w_grad = scatter_heads(mm(mixed_rows, branch_grad, ((0,), (0,))))
    mixed_grad = mm(branch_grad, out_matrix, ((1,), (1,))).astype(BF)
    dq, dk, dv = attention_backward(
        info, query, key, value, mixed, lse, mixed_grad.reshape(replicas, size, q_width)
    )

    def head_back(values, gain, dy):
        dy = dy.reshape(length, -1, HEAD_SIZE)
        dy = dy * cos_row - turn(dy) * sin_row
        inverse = inverse_root(values)
        gain_part = jnp.sum(dy * values * inverse, axis=(0, 1))
        return norm_back(values, inverse, gain, dy).astype(BF).reshape(length, -1), gain_part

    query_grad, query_gain_part = head_back(query_raw, query_gain, dq)
    key_grad, key_gain_part = head_back(key_raw, key_gain, dk)
    attn_grad = jnp.concatenate(
        [query_grad, key_grad, dv.reshape(length, kv_width).astype(BF)], axis=1
    )
    normed_part = mm(attn_grad, attn_matrix, ((1,), (1,)))
    normed_grad = sum_blocks(normed_part.reshape(replicas, size, MODEL_WIDTH))
    attn_gain_part = jnp.sum(normed_part * (wide * token_inverse), axis=0)
    own_tokens = tokens.astype(F32)
    in_grad = residual_grad + norm_back(own_tokens, inverse_root(own_tokens), attn_gain, normed_grad)

    gain_parts = jnp.concatenate(
        [
            attn_gain_part.reshape(shards, rows),
            mlp_gain_part.reshape(shards, rows),
            query_gain_part.reshape(shards, head_rows),
            key_gain_part.reshape(shards, head_rows),
        ],
        axis=1,
    )
    gain_block = jnp.zeros((shards, 16, attn_width), F32).at[:, 0, : gain_parts.shape[1]].set(gain_parts)
    attn_w_parts = mm(normed, attn_grad, ((0,), (0,))).reshape(shards, rows, attn_width)
    attn_w = scatter_rows(jnp.concatenate([attn_w_parts, gain_block], axis=1))

    def in_order(value):
        spread = spread_blocks(value.astype(BF))
        return jnp.stack(
            [lax.dynamic_index_in_dim(spread, r ^ a, 0, keepdims=False) for a in range(replicas)]
        ).astype(F32)

    attn_full = in_order(attn_w)
    gain_full = jnp.sum(attn_full[:, rows], axis=0)

    def beside(values):
        return jnp.concatenate([values[a] for a in range(replicas)], axis=1)

    query_w_grad = beside(attn_full[:, :rows, :q_width])
    key_w_grad = beside(attn_full[:, :rows, q_width : q_width + kv_width])
    value_w_grad = beside(attn_full[:, :rows, q_width + kv_width :])
    gate_up_full = in_order(gate_up_w)

    def woven(values):
        cut = values.reshape(replicas, rows, shards, ff_rows)
        return cut.transpose(1, 2, 0, 3).reshape(rows, shards * replicas * ff_rows)

    gate_w_grad = woven(gate_up_full[:, :, :ff])
    up_w_grad = woven(gate_up_full[:, :, ff:])
    down_w_grad = in_order(down_w).reshape(replicas * ff_rows, MODEL_WIDTH)

    return (
        layer_out.astype(BF)[None],
        in_grad.astype(BF)[None],
        gain_full[:rows],
        query_w_grad,
        key_w_grad,
        value_w_grad,
        gain_full[2 * rows : 2 * rows + head_rows],
        gain_full[2 * rows + head_rows : 2 * rows + 2 * head_rows],
        out_w_grad,
        gain_full[rows : 2 * rows],
        gate_w_grad,
        up_w_grad,
        down_w_grad,
    )


def solution(mesh):
    tokens, matrix, vector = P("shard", "rep", None), P("shard", None), P("shard")
    return jax.shard_map(
        per_device,
        mesh=mesh,
        in_specs=(tokens, tokens, vector, matrix, matrix, matrix, vector, vector, matrix, vector)
        + (matrix, matrix, matrix, matrix, vector),
        out_specs=(tokens, tokens, vector, matrix, matrix, matrix, vector, vector, matrix, vector)
        + (matrix, matrix, matrix),
        check_vma=False,
    )
```

time: 1100 us -> 514 us (0.47)
  waiting for transfers between devices: 739 us -> 153 us
  matrix products: 150 us -> 41.8 us
  starting transfers between devices: 1.19 us -> 101 us
  blocking collectives: 64.5 us -> 0 us
  local copies, waits for them, and re-layouts: 78.1 us -> 122 us
  other arithmetic: 44 us -> 67.9 us
  Pallas kernels: 0 us -> 15.8 us
  between operations: 18 us -> 4.25 us
    reduce_scatter x8 -> x0, waiting for transfers between devices: 395 us -> none  [the longest x1 70.8 us: per_device(): lax.psum_scatter(gate_w_grad.astype(jnp.bfloat16), 'shard', scatter_dimen...]
    all_gather x9 -> x0, waiting for transfers between devices: 279 us -> none  [the longest x1 58.7 us: per_device(): lax.all_gather(up_weight, 'shard', axis=0, tiled=True)]
    ppermute x0 -> x90, waiting for transfers between devices: none -> 153 us  [the longest x44 79.6 us: flip(): return lax.ppermute(value, 'rep', [(i, i ^ bit) for i in range(count)])]
    dot_general x39 -> x12, matrix products: 150 us -> 41.8 us  [mm(): return lax.dot_general(a, b, (dims, ((), ())), preferred_element_type=F32)]
    ppermute x0 -> x90, starting transfers between devices: none -> 101 us  [the longest x44 59.6 us: flip(): return lax.ppermute(value, 'rep', [(i, i ^ bit) for i in range(count)])]
    psum x1 -> x0, waiting for transfers between devices: 60.5 us -> none  [per_device(): lax.psum(attn_shards[1].astype(jnp.bfloat16), 'rep').astype(jnp.float32)]
    unnamed x2 -> x0, blocking collectives: 30.2 us -> none
    all_gather x2 -> x0, blocking collectives: 24.1 us -> none  [the longest x1 13.5 us: per_device(): lax.all_gather(attn_norm, 'shard', axis=0, tiled=True)]
  transfers between devices with their start and end apart: 18 -> 90, of which waited for: 17 -> 35; matrix products, arithmetic and copies ran while one was open for 14% -> 36% of each run, Pallas kernels for 0% -> 3%
where the time goes in v1:
time: 514 us; the launch traced here: 506 us
  waiting for transfers between devices  153 us (30%)
  local copies, waits for them, and re-layouts  122 us (24%)
  starting transfers between devices  101 us (20%)
  other arithmetic  67.9 us (13%)
  matrix products  41.8 us (8%)
  Pallas kernels  15.8 us (3%)
    ppermute x44, waiting for transfers between devices, flip(): return lax.ppermute(value, 'rep', [(i, i ^ bit) for i in range(count)])  79.6 us
    ppermute x44, starting transfers between devices, flip(): return lax.ppermute(value, 'rep', [(i, i ^ bit) for i in range(count)])  59.6 us
    dot_general x12, matrix products, mm(): return lax.dot_general(a, b, (dims, ((), ())), preferred_element_type=F32)  41.8 us
    ppermute x18, waiting for transfers between devices, ring_up(): lax.ppermute(value, 'shard', [(i, (i + 2) % count) for i in range(count)])  41.7 us
    ppermute x11, waiting for transfers between devices, joint_move(): return lax.ppermute(value, ('rep', 'shard'), joint)  31.6 us
    ppermute x18, starting transfers between devices, ring_up(): lax.ppermute(value, 'shard', [(i, (i + 2) % count) for i in range(count)])  24.4 us
    unnamed x185, local copies, waits for them, and re-layouts  23.4 us
    dynamic_update_slice x12, local copies, waits for them, and re-layouts, gather_rows(): full = lax.dynamic_update_index_in_dim(full, current, place + core, 0)  15.7 us
  transfers between devices with their start and end apart: 90, of which 35 were waited for; matrix products, arithmetic and copies ran while one was open for 36% of the time, Pallas kernels for 3%

profile of v1, /device:TPU:0, one launch (start us, length us, event | category | flops | bytes accessed | tf_op | source)
XLA Modules:
  0.0 505.7 jit_solution(8966792467634936649)
XLA Ops:
  4.1 3.0 collective-permute-start.5
  20.3 2.0 mul.648
  30.4 2.8 collective-permute-done.7
  34.7 2.4 collective-permute-done.2
  40.1 2.9 collective-permute-done.9
  43.5 2.1 broadcast_in_dim.120
  47.4 3.1 collective-permute-start.11
  51.0 9.9 %collective-permute-done.32 = bf16[96,1024]{1,0:T(8,128)(2,1)} collective-permute-done((bf16[96,1024]{1,0:T(8,128)(2,1)S(1)}, bf16[96,1024]{1,0:T(8,128)(2,1)}, u32[]{:S(2)}, u32[]{:S(2)}) %collective-permute-start.32) | collective-permute-done | bytes 196640 | tf_op jit(solution)/shard_map/ppermute | solution.py:66
  66.4 2.3 fusion.103
  74.8 2.4 multiply_multiply_fusion.1
  85.4 1.9 reshape.696
  89.0 2.4 multiply_multiply_fusion
  97.0 2.2 mul.637
  99.3 4.7 add_convert_fusion.q_ref
  105.6 5.6 %attention_forward.1 = (bf16[4,256,512]{2,1,0:T(8,128)(2,1)S(1)}, f32[2,4,2,256]{3,2,1,0:T(2,128)S(1)}) custom-call(s32[5]{0:T(128)S(1)} %pad_add_fusion.info, bf16[4,256,512]{2,1,0:T(8,128)(2,1)S(1)} %add_convert_fusion.q_ref, bf16[4,256,256]{2,1,0:T(8,128)(2,1)S(1)} %add_convert_fusion.3.k_ref, bf16[4,256,256]{2,1,0:T(8,128)(2,1)S(1)} %bitcast.449), custom_call_target="tpu_custom_call" | custom-call | tf_op jit(solution)/shard_map/attention_forward/pallas_call | solution.py:252
  115.0 3.4 collective-permute-start.34
  128.4 8.5 %collective-permute-start.36 = (bf16[96,1024]{1,0:T(8,128)(2,1)S(1)}, bf16[96,1024]{1,0:T(8,128)(2,1)S(1)}, u32[]{:S(2)}, u32[]{:S(2)}) collective-permute-start(bf16[96,1024]{1,0:T(8,128)(2,1)S(1)} %collective-permute-done.34), channel_id=1, source_target_pairs={{0,2},{1,3},{2,4},{3,5},{4,6},{5,7},{6,0},{7,1},{8,10},{9,11},{10,... | collective-permute-start | bytes 589832 | tf_op jit(solution)/shard_map/ppermute | solution.py:66
  138.5 6.9 %collective-permute-start.45 = (bf16[128,1024]{1,0:T(8,128)(2,1)S(1)}, bf16[128,1024]{1,0:T(8,128)(2,1)S(1)}, u32[]{:S(2)}, u32[]{:S(2)}) collective-permute-start(bf16[128,1024]{1,0:T(8,128)(2,1)S(1)} %slice.535), channel_id=1, source_target_pairs={{0,8},{8,0},{16,24},{24,16},{1,9},{9,1},{17,25},{25,17},{2,10},{10... | collective-permute-start | bytes 786440 | tf_op jit(solution)/shard_map/ppermute | solution.py:29
  148.5 2.8 collective-permute-done.45
  154.8 9.4 %collective-permute-start.18 = (bf16[2,128,1024]{2,1,0:T(8,128)(2,1)S(1)}, bf16[2,128,1024]{2,1,0:T(8,128)(2,1)S(1)}, u32[]{:S(2)}, u32[]{:S(2)}) collective-permute-start(bf16[2,128,1024]{2,1,0:T(8,128)(2,1)S(1)} %stack.190), channel_id=1, source_target_pairs={{0,16},{8,24},{16,0},{24,8},{1,17},{9,25},{17,1},{25,9},{2,18},{10... | collective-permute-start | bytes 1572872 | tf_op jit(solution)/shard_map/ppermute | solution.py:29
  166.8 7.7 %collective-permute-done.18 = bf16[2,128,1024]{2,1,0:T(8,128)(2,1)S(1)} collective-permute-done((bf16[2,128,1024]{2,1,0:T(8,128)(2,1)S(1)}, bf16[2,128,1024]{2,1,0:T(8,128)(2,1)S(1)}, u32[]{:S(2)}, u32[]{:S(2)}) %collective-permute-start.18) | collective-permute-done | bytes 524320 | tf_op jit(solution)/shard_map/ppermute | solution.py:29
  179.3 2.0 collective-permute-done.17
  188.0 4.8 copy.108
  196.4 3.5 collective-permute-start.22
  203.2 2.1 collective-permute-done.22
  205.3 2.5 collective-permute-done.23
  210.1 3.4 fusion.104
  213.5 4.1 multiply_convert_fusion.3
  219.3 5.1 %fusion.101 = (bf16[4,256,1024]{2,1,0:T(8,128)(2,1)S(1)}, f32[4,256,1024]{2,1,0:T(8,128)}) fusion(bf16[4,256,1536]{2,1,0:T(8,128)(2,1)S(1)} %bitcast.488, bf16[1024,1536,1]{1,0,2:T(8,128)(2,1)S(1)} %bitcast.487), kind=kOutput, calls=%fused_computation.312 | convolution fusion | flops 3222274048 | bytes 12582912 | tf_op jit(solution)/shard_map/dot_general | solution.py:24
  225.9 2.6 copy.126
  228.5 3.9 fusion.106
  235.1 4.3 copy.121
  239.5 6.1 %fusion = f32[4,2,128,1536]{3,2,1,0:T(8,128)S(1)} fusion(bf16[4,2,128,1024]{3,2,1,0:T(8,128)(2,1)} %bitcast.497, bf16[1024,768]{1,0:T(8,128)(2,1)} %copy-done.76, bf16[1024,768]{1,0:T(8,128)(2,1)} %copy-done.75), kind=kOutput, calls=%fused_computation.8 | convolution fusion | flops 3227516928 | bytes 11534336 | tf_op jit(solution)/shard_map/dot_general | solution.py:24
  252.0 8.5 %collective-permute-done.46 = bf16[2,128,1024]{2,1,0:T(8,128)(2,1)S(1)} collective-permute-done((bf16[2,128,1024]{2,1,0:T(8,128)(2,1)S(1)}, bf16[2,128,1024]{2,1,0:T(8,128)(2,1)S(1)}, u32[]{:S(2)}, u32[]{:S(2)}) %collective-permute-start.46) | collective-permute-done | bytes 524320 | tf_op jit(solution)/shard_map/ppermute | solution.py:29
  261.5 9.8 %collective-permute-done.38 = bf16[2,128,1024]{2,1,0:T(8,128)(2,1)S(1)} collective-permute-done((bf16[2,128,1024]{2,1,0:T(8,128)(2,1)S(1)}, bf16[2,128,1024]{2,1,0:T(8,128)(2,1)S(1)}, u32[]{:S(2)}, u32[]{:S(2)}) %collective-permute-start.38) | collective-permute-done | bytes 524320 | tf_op jit(solution)/shard_map/ppermute | solution.py:29
  272.7 4.8 collective-permute-done.47
  283.5 3.3 collective-permute-done.41
  287.1 3.9 collective-permute-done.83
  292.7 5.9 %collective-permute-done.84 = bf16[96,1024]{1,0:T(8,128)(2,1)S(1)} collective-permute-done((bf16[96,1024]{1,0:T(8,128)(2,1)S(1)}, bf16[96,1024]{1,0:T(8,128)(2,1)S(1)}, u32[]{:S(2)}, u32[]{:S(2)}) %collective-permute-start.84) | collective-permute-done | bytes 196640 | tf_op jit(solution)/shard_map/ppermute | solution.py:66
  302.0 4.1 collective-permute-done.85
  315.9 2.3 convolution_convert_fusion
  318.1 10.2 %attention_backward.1 = (f32[4,256,512]{2,1,0:T(8,128)}, f32[4,256,256]{2,1,0:T(8,128)S(1)}, f32[4,256,256]{2,1,0:T(8,128)S(1)}) custom-call(s32[5]{0:T(128)S(1)} %pad_add_fusion.info, bf16[4,256,512]{2,1,0:T(8,128)(2,1)S(1)} %add_convert_fusion.q_ref, bf16[4,256,256]{2,1,0:T(8,128)(2,1)S(1)} %add_convert_fusion.3.k_ref, bf16[4,256,256]{2,1,0:T(8,128)(2,1)S(1)} %bitcast.450, ...), custom_call_target="tpu_custom_call" | custom-call | tf_op jit(solution)/shard_map/attention_backward/pallas_call | solution.py:273
  334.0 4.5 multiply_reduce_fusion.2
  340.7 3.6 multiply_reduce_fusion.5
  347.9 2.0 fusion.5
  354.9 4.2 multiply_convert_fusion
  359.1 2.6 copy.132
  361.7 6.2 %fusion.6 = f32[8,128,1024]{2,1,0:T(8,128)} fusion(bf16[8,128,1024]{2,1,0:T(8,128)(2,1)} %bitcast.496, bf16[1024,256]{1,0:T(8,128)(2,1)} %bitcast.519, bf16[1024,256]{1,0:T(8,128)(2,1)} %copy-done.86, bf16[1024,512]{1,0:T(8,128)(2,1)S(1)} %get-tuple-element.119), kind=kOutput, calls=%fused_computation.35 | convolution fusion | flops 2153775104 | bytes 8388608 | tf_op jit(solution)/shard_map/dot_general | solution.py:24
  368.2 3.0 select_maximum_fusion
  375.2 3.0 collective-permute-done.88
  379.1 2.1 collective-permute-start.56
  384.5 6.9 %collective-permute-done.54 = bf16[2,128,1024]{2,1,0:T(8,128)(2,1)S(1)} collective-permute-done((bf16[2,128,1024]{2,1,0:T(8,128)(2,1)S(1)}, bf16[2,128,1024]{2,1,0:T(8,128)(2,1)S(1)}, u32[]{:S(2)}, u32[]{:S(2)}) %collective-permute-start.54) | collective-permute-done | bytes 524320 | tf_op jit(solution)/shard_map/ppermute | solution.py:29
  400.5 6.3 %collective-permute-done.57 = bf16[128,1024]{1,0:T(8,128)(2,1)S(1)} collective-permute-done((bf16[128,1024]{1,0:T(8,128)(2,1)S(1)}, bf16[128,1024]{1,0:T(8,128)(2,1)S(1)}, u32[]{:S(2)}, u32[]{:S(2)}) %collective-permute-start.57) | collective-permute-done | bytes 262176 | tf_op jit(solution)/shard_map/ppermute | solution.py:29
  408.7 31.6 %collective-permute-done.67 = bf16[256,1024]{1,0:T(8,128)(2,1)S(1)} collective-permute-done((bf16[256,1024]{1,0:T(8,128)(2,1)S(1)}, bf16[256,1024]{1,0:T(8,128)(2,1)S(1)}, u32[]{:S(2)}, u32[]{:S(2)}) %collective-permute-start.67) | collective-permute-done | bytes 524320 | tf_op jit(solution)/shard_map/ppermute | solution.py:116
  445.4 2.2 collective-permute-start.78
  447.6 6.2 %collective-permute-done.59 = bf16[144,1024]{1,0:T(8,128)(2,1)S(1)} collective-permute-done((bf16[144,1024]{1,0:T(8,128)(2,1)S(1)}, bf16[144,1024]{1,0:T(8,128)(2,1)S(1)}, u32[]{:S(2)}, u32[]{:S(2)}) %collective-permute-start.59) | collective-permute-done | bytes 294944 | tf_op jit(solution)/shard_map/ppermute | solution.py:66
  455.1 5.9 %collective-permute-done.78 = bf16[128,1536]{1,0:T(8,128)(2,1)S(1)} collective-permute-done((bf16[128,1536]{1,0:T(8,128)(2,1)S(1)}, bf16[128,1536]{1,0:T(8,128)(2,1)S(1)}, u32[]{:S(2)}, u32[]{:S(2)}) %collective-permute-start.78) | collective-permute-done | bytes 393248 | tf_op jit(solution)/shard_map/ppermute | solution.py:29
  461.0 3.3 collective-permute-done.79
  468.8 5.6 %collective-permute-start.61 = (bf16[144,1024]{1,0:T(8,128)(2,1)S(1)}, bf16[144,1024]{1,0:T(8,128)(2,1)S(1)}, u32[]{:S(2)}, u32[]{:S(2)}) collective-permute-start(bf16[144,1024]{1,0:T(8,128)(2,1)S(1)} %fusion.33), channel_id=1, source_target_pairs={{0,2},{1,3},{2,4},{3,5},{4,6},{5,7},{6,0},{7,1},{8,10},{9,11},{10,... | collective-permute-start | bytes 884744 | tf_op jit(solution)/shard_map/ppermute | solution.py:66
  475.1 3.6 collective-permute-done.61
  478.7 4.5 collective-permute-start.62
  491.5 2.0 collective-permute-start.64
  494.6 2.3 fusion.64
  497.0 2.7 collective-permute-done.65
  (548 shorter events, 201.7 us)
Async XLA Ops:
  4.1 18.1 %collective-permute-start.5 = (bf16[144,1024]{1,0:T(8,128)(2,1)}, bf16[144,1024]{1,0:T(8,128)(2,1)}, u32[]{:S(2)}, u32[]{:S(2)}) collective-permute-start(bf16[144,1024]{1,0:T(8,128)(2,1)} %fusion.69), channel_id=1, source_target_pairs={{0,2},{1,3},{2,4},{3,5},{4,6},{5,7},{6,0},{7,1},{8,10},{9,11},{10,... | collective-permute-start | bytes 884744 | tf_op jit(solution)/shard_map/ppermute | solution.py:66
  7.2 16.7 %collective-permute-start.4 = (bf16[144,1024]{1,0:T(8,128)(2,1)}, bf16[144,1024]{1,0:T(8,128)(2,1)}, u32[]{:S(2)}, u32[]{:S(2)}) collective-permute-start(bf16[144,1024]{1,0:T(8,128)(2,1)} %fusion.69), channel_id=1, source_target_pairs={{0,1},{1,0},{2,3},{3,2},{4,5},{5,4},{6,7},{7,6},{8,9},{9,8},{10,11... | collective-permute-start | bytes 884744 | tf_op jit(solution)/shard_map/ppermute | solution.py:71
  7.2 20.1 %collective-permute-start = (bf16[256,1024]{1,0:T(8,128)(2,1)}, bf16[256,1024]{1,0:T(8,128)(2,1)}, u32[]{:S(2)}, u32[]{:S(2)}) collective-permute-start(bf16[256,1024]{1,0:T(8,128)(2,1)} %bitcast.451), channel_id=1, source_target_pairs={{0,8},{8,0},{16,24},{24,16},{1,9},{9,1},{17,25},{25,17},{2,10},{10... | collective-permute-start | bytes 1572872 | tf_op jit(solution)/shard_map/ppermute | solution.py:29
  8.7 20.2 %collective-permute-start.1 = (bf16[256,1024]{1,0:T(8,128)(2,1)}, bf16[256,1024]{1,0:T(8,128)(2,1)}, u32[]{:S(2)}, u32[]{:S(2)}) collective-permute-start(bf16[256,1024]{1,0:T(8,128)(2,1)} %bitcast.452), channel_id=1, source_target_pairs={{0,16},{8,24},{16,0},{24,8},{1,17},{9,25},{17,1},{25,9},{2,18},{10... | collective-permute-start | bytes 1572872 | tf_op jit(solution)/shard_map/ppermute | solution.py:29
  22.3 10.9 %collective-permute-start.7 = (bf16[144,1024]{1,0:T(8,128)(2,1)}, bf16[144,1024]{1,0:T(8,128)(2,1)S(1)}, u32[]{:S(2)}, u32[]{:S(2)}) collective-permute-start(bf16[144,1024]{1,0:T(8,128)(2,1)} %collective-permute-done.5), channel_id=1, source_target_pairs={{0,2},{1,3},{2,4},{3,5},{4,6},{5,7},{6,0},{7,1},{8,10},{9,11},{10,... | collective-permute-start | bytes 884744 | tf_op jit(solution)/shard_map/ppermute | solution.py:66
  33.2 14.2 %collective-permute-start.8 = (bf16[144,1024]{1,0:T(8,128)(2,1)S(1)}, bf16[144,1024]{1,0:T(8,128)(2,1)S(1)}, u32[]{:S(2)}, u32[]{:S(2)}) collective-permute-start(bf16[144,1024]{1,0:T(8,128)(2,1)S(1)} %collective-permute-done.7), channel_id=1, source_target_pairs={{0,1},{1,0},{2,3},{3,2},{4,5},{5,4},{6,7},{7,6},{8,9},{9,8},{10,11... | collective-permute-start | bytes 884744 | tf_op jit(solution)/shard_map/ppermute | solution.py:71
  43.0 78.2 %collective-permute-start.24 = (bf16[128,1536]{0,1:T(8,128)(2,1)}, bf16[128,1536]{0,1:T(8,128)(2,1)}, u32[]{:S(2)}, u32[]{:S(2)}) collective-permute-start(bf16[128,1536]{0,1:T(8,128)(2,1)} %pad_maximum_fusion.25), channel_id=1, source_target_pairs={{0,1},{1,0},{2,3},{3,2},{4,5},{5,4},{6,7},{7,6},{8,9},{9,8},{10,11... | collective-permute-start | bytes 1179656 | tf_op jit(solution)/shard_map/ppermute | solution.py:71
  43.0 78.2 %collective-permute-start.25 = (bf16[128,1536]{0,1:T(8,128)(2,1)}, bf16[128,1536]{0,1:T(8,128)(2,1)}, u32[]{:S(2)}, u32[]{:S(2)}) collective-permute-start(bf16[128,1536]{0,1:T(8,128)(2,1)} %pad_maximum_fusion.25), channel_id=1, source_target_pairs={{0,2},{1,3},{2,4},{3,5},{4,6},{5,7},{6,0},{7,1},{8,10},{9,11},{10,... | collective-permute-start | bytes 1179656 | tf_op jit(solution)/shard_map/ppermute | solution.py:66
  43.5 17.3 %collective-permute-start.32 = (bf16[96,1024]{1,0:T(8,128)(2,1)S(1)}, bf16[96,1024]{1,0:T(8,128)(2,1)}, u32[]{:S(2)}, u32[]{:S(2)}) collective-permute-start(bf16[96,1024]{1,0:T(8,128)(2,1)S(1)} %constant_dynamic-slice_fusion.12), channel_id=1, source_target_pairs={{0,2},{1,3},{2,4},{3,5},{4,6},{5,7},{6,0},{7,1},{8,10},{9,11},{10,... | collective-permute-start | bytes 589832 | tf_op jit(solution)/shard_map/ppermute | solution.py:66
  47.4 67.2 %collective-permute-start.11 = (bf16[256,1024]{1,0:T(8,128)(2,1)}, bf16[256,1024]{1,0:T(8,128)(2,1)}, u32[]{:S(2)}, u32[]{:S(2)}) collective-permute-start(bf16[256,1024]{1,0:T(8,128)(2,1)} %param.27), channel_id=1, source_target_pairs={{0,2},{1,3},{10,12},{11,13},{20,22},{21,23}} | collective-permute-start | bytes 1572872 | tf_op jit(solution)/shard_map/ppermute | solution.py:116
  50.9 12.9 %collective-permute-start.10 = (bf16[144,1024]{1,0:T(8,128)(2,1)S(1)}, bf16[144,1024]{1,0:T(8,128)(2,1)S(1)}, u32[]{:S(2)}, u32[]{:S(2)}) collective-permute-start(bf16[144,1024]{1,0:T(8,128)(2,1)S(1)} %collective-permute-done.9), channel_id=1, source_target_pairs={{0,1},{1,0},{2,3},{3,2},{4,5},{5,4},{6,7},{7,6},{8,9},{9,8},{10,11... | collective-permute-start | bytes 884744 | tf_op jit(solution)/shard_map/ppermute | solution.py:71
  60.9 54.1 %collective-permute-start.12 = (bf16[256,1024]{1,0:T(8,128)(2,1)}, bf16[256,1024]{1,0:T(8,128)(2,1)}, u32[]{:S(2)}, u32[]{:S(2)}) collective-permute-start(bf16[256,1024]{1,0:T(8,128)(2,1)} %param.27), channel_id=1, source_target_pairs={{10,8},{11,9},{20,18},{21,19},{30,28},{31,29}} | collective-permute-start | bytes 1572872 | tf_op jit(solution)/shard_map/ppermute | solution.py:116
  63.7 56.1 %collective-permute-start.33 = (bf16[96,1024]{1,0:T(8,128)(2,1)}, bf16[96,1024]{1,0:T(8,128)(2,1)S(1)}, u32[]{:S(2)}, u32[]{:S(2)}) collective-permute-start(bf16[96,1024]{1,0:T(8,128)(2,1)} %collective-permute-done.32), channel_id=1, source_target_pairs={{0,1},{1,0},{2,3},{3,2},{4,5},{5,4},{6,7},{7,6},{8,9},{9,8},{10,11... | collective-permute-start | bytes 589832 | tf_op jit(solution)/shard_map/ppermute | solution.py:71
  114.6 13.8 %collective-permute-start.42 = (bf16[256,1024]{1,0:T(8,128)(2,1)}, bf16[256,1024]{1,0:T(8,128)(2,1)S(1)}, u32[]{:S(2)}, u32[]{:S(2)}) collective-permute-start(bf16[256,1024]{1,0:T(8,128)(2,1)} %bitcast.481), channel_id=1, source_target_pairs={{0,8},{8,0},{16,24},{24,16},{1,9},{9,1},{17,25},{25,17},{2,10},{10... | collective-permute-start | bytes 1572872 | tf_op jit(solution)/shard_map/ppermute | solution.py:29
  121.2 15.7 %collective-permute-start.43 = (bf16[256,1024]{1,0:T(8,128)(2,1)}, bf16[256,1024]{1,0:T(8,128)(2,1)S(1)}, u32[]{:S(2)}, u32[]{:S(2)}) collective-permute-start(bf16[256,1024]{1,0:T(8,128)(2,1)} %bitcast.482), channel_id=1, source_target_pairs={{0,16},{8,24},{16,0},{24,8},{1,17},{9,25},{17,1},{25,9},{2,18},{10... | collective-permute-start | bytes 1572872 | tf_op jit(solution)/shard_map/ppermute | solution.py:29
  121.2 44.6 %collective-permute-start.26 = (bf16[128,1536]{0,1:T(8,128)(2,1)}, bf16[128,1536]{0,1:T(8,128)(2,1)S(1)}, u32[]{:S(2)}, u32[]{:S(2)}) collective-permute-start(bf16[128,1536]{0,1:T(8,128)(2,1)} %collective-permute-done.25), channel_id=1, source_target_pairs={{0,1},{1,0},{2,3},{3,2},{4,5},{5,4},{6,7},{7,6},{8,9},{9,8},{10,11... | collective-permute-start | bytes 1179656 | tf_op jit(solution)/shard_map/ppermute | solution.py:71
  123.2 23.3 %collective-permute-start.35 = (bf16[96,1024]{1,0:T(8,128)(2,1)S(1)}, bf16[96,1024]{1,0:T(8,128)(2,1)S(1)}, u32[]{:S(2)}, u32[]{:S(2)}) collective-permute-start(bf16[96,1024]{1,0:T(8,128)(2,1)S(1)} %collective-permute-done.34), channel_id=1, source_target_pairs={{0,1},{1,0},{2,3},{3,2},{4,5},{5,4},{6,7},{7,6},{8,9},{9,8},{10,11... | collective-permute-start | bytes 589832 | tf_op jit(solution)/shard_map/ppermute | solution.py:71
  125.0 13.5 %collective-permute-start.14 = (bf16[256,1024]{1,0:T(8,128)(2,1)S(1)}, bf16[256,1024]{1,0:T(8,128)(2,1)S(1)}, u32[]{:S(2)}, u32[]{:S(2)}) collective-permute-start(bf16[256,1024]{1,0:T(8,128)(2,1)S(1)} %collective-permute-done.13), channel_id=1, source_target_pairs={{4,6},{5,7},{26,24},{27,25}} | collective-permute-start | bytes 1572872 | tf_op jit(solution)/shard_map/ppermute | solution.py:116
  128.4 19.0 %collective-permute-start.36 = (bf16[96,1024]{1,0:T(8,128)(2,1)S(1)}, bf16[96,1024]{1,0:T(8,128)(2,1)S(1)}, u32[]{:S(2)}, u32[]{:S(2)}) collective-permute-start(bf16[96,1024]{1,0:T(8,128)(2,1)S(1)} %collective-permute-done.34), channel_id=1, source_target_pairs={{0,2},{1,3},{2,4},{3,5},{4,6},{5,7},{6,0},{7,1},{8,10},{9,11},{10,... | collective-permute-start | bytes 589832 | tf_op jit(solution)/shard_map/ppermute | solution.py:66
  136.9 11.2 %collective-permute-start.44 = (bf16[128,1024]{1,0:T(8,128)(2,1)S(1)}, bf16[128,1024]{1,0:T(8,128)(2,1)S(1)}, u32[]{:S(2)}, u32[]{:S(2)}) collective-permute-start(bf16[128,1024]{1,0:T(8,128)(2,1)S(1)} %slice.534), channel_id=1, source_target_pairs={{0,16},{8,24},{16,0},{24,8},{1,17},{9,25},{17,1},{25,9},{2,18},{10... | collective-permute-start | bytes 786440 | tf_op jit(solution)/shard_map/ppermute | solution.py:29
  138.5 12.8 %collective-permute-start.45 = (bf16[128,1024]{1,0:T(8,128)(2,1)S(1)}, bf16[128,1024]{1,0:T(8,128)(2,1)S(1)}, u32[]{:S(2)}, u32[]{:S(2)}) collective-permute-start(bf16[128,1024]{1,0:T(8,128)(2,1)S(1)} %slice.535), channel_id=1, source_target_pairs={{0,8},{8,0},{16,24},{24,16},{1,9},{9,1},{17,25},{25,17},{2,10},{10... | collective-permute-start | bytes 786440 | tf_op jit(solution)/shard_map/ppermute | solution.py:29
  147.4 18.5 %collective-permute-start.27 = (bf16[128,1536]{0,1:T(8,128)(2,1)}, bf16[128,1536]{0,1:T(8,128)(2,1)S(1)}, u32[]{:S(2)}, u32[]{:S(2)}) collective-permute-start(bf16[128,1536]{0,1:T(8,128)(2,1)} %collective-permute-done.25), channel_id=1, source_target_pairs={{0,2},{1,3},{2,4},{3,5},{4,6},{5,7},{6,0},{7,1},{8,10},{9,11},{10,... | collective-permute-start | bytes 1179656 | tf_op jit(solution)/shard_map/ppermute | solution.py:66
  148.0 30.0 %collective-permute-start.37 = (bf16[96,1024]{1,0:T(8,128)(2,1)S(1)}, bf16[96,1024]{1,0:T(8,128)(2,1)S(1)}, u32[]{:S(2)}, u32[]{:S(2)}) collective-permute-start(bf16[96,1024]{1,0:T(8,128)(2,1)S(1)} %collective-permute-done.36), channel_id=1, source_target_pairs={{0,1},{1,0},{2,3},{3,2},{4,5},{5,4},{6,7},{7,6},{8,9},{9,8},{10,11... | collective-permute-start | bytes 589832 | tf_op jit(solution)/shard_map/ppermute | solution.py:71
  152.9 13.8 %collective-permute-start.16 = (bf16[2,128,1024]{2,1,0:T(8,128)(2,1)S(1)}, bf16[2,128,1024]{2,1,0:T(8,128)(2,1)S(1)}, u32[]{:S(2)}, u32[]{:S(2)}) collective-permute-start(bf16[2,128,1024]{2,1,0:T(8,128)(2,1)S(1)} %pad_maximum_fusion.19), channel_id=1, source_target_pairs={{0,8},{8,0},{16,24},{24,16},{1,9},{9,1},{17,25},{25,17},{2,10},{10... | collective-permute-start | bytes 1572872 | tf_op jit(solution)/shard_map/ppermute | solution.py:29
  154.8 19.8 %collective-permute-start.18 = (bf16[2,128,1024]{2,1,0:T(8,128)(2,1)S(1)}, bf16[2,128,1024]{2,1,0:T(8,128)(2,1)S(1)}, u32[]{:S(2)}, u32[]{:S(2)}) collective-permute-start(bf16[2,128,1024]{2,1,0:T(8,128)(2,1)S(1)} %stack.190), channel_id=1, source_target_pairs={{0,16},{8,24},{16,0},{24,8},{1,17},{9,25},{17,1},{25,9},{2,18},{10... | collective-permute-start | bytes 1572872 | tf_op jit(solution)/shard_map/ppermute | solution.py:29
  165.8 19.6 %collective-permute-start.28 = (bf16[128,1536]{0,1:T(8,128)(2,1)S(1)}, bf16[128,1536]{0,1:T(8,128)(2,1)S(1)}, u32[]{:S(2)}, u32[]{:S(2)}) collective-permute-start(bf16[128,1536]{0,1:T(8,128)(2,1)S(1)} %collective-permute-done.27), channel_id=1, source_target_pairs={{0,1},{1,0},{2,3},{3,2},{4,5},{5,4},{6,7},{7,6},{8,9},{9,8},{10,11... | collective-permute-start | bytes 1179656 | tf_op jit(solution)/shard_map/ppermute | solution.py:71
  165.8 13.4 %collective-permute-start.29 = (bf16[128,1536]{0,1:T(8,128)(2,1)S(1)}, bf16[128,1536]{0,1:T(8,128)(2,1)}, u32[]{:S(2)}, u32[]{:S(2)}) collective-permute-start(bf16[128,1536]{0,1:T(8,128)(2,1)S(1)} %collective-permute-done.27), channel_id=1, source_target_pairs={{0,2},{1,3},{2,4},{3,5},{4,6},{5,7},{6,0},{7,1},{8,10},{9,11},{10,... | collective-permute-start | bytes 1179656 | tf_op jit(solution)/shard_map/ppermute | solution.py:66
  179.3 13.5 %collective-permute-start.30 = (bf16[128,1536]{0,1:T(8,128)(2,1)}, bf16[128,1536]{0,1:T(8,128)(2,1)}, u32[]{:S(2)}, u32[]{:S(2)}) collective-permute-start(bf16[128,1536]{0,1:T(8,128)(2,1)} %collective-permute-done.29), channel_id=1, source_target_pairs={{0,1},{1,0},{2,3},{3,2},{4,5},{5,4},{6,7},{7,6},{8,9},{9,8},{10,11... | collective-permute-start | bytes 1179656 | tf_op jit(solution)/shard_map/ppermute | solution.py:71
  184.5 10.9 %collective-permute-start.20 = (bf16[256,1024]{1,0:T(8,128)(2,1)}, bf16[256,1024]{1,0:T(8,128)(2,1)}, u32[]{:S(2)}, u32[]{:S(2)}) collective-permute-start(bf16[256,1024]{1,0:T(8,128)(2,1)} %multiply_convert_fusion.5), channel_id=1, source_target_pairs={{0,8},{8,0},{16,24},{24,16},{1,9},{9,1},{17,25},{25,17},{2,10},{10... | collective-permute-start | bytes 1572872 | tf_op jit(solution)/shard_map/ppermute | solution.py:29
  185.1 14.7 %collective-permute-start.21 = (bf16[256,1024]{1,0:T(8,128)(2,1)}, bf16[256,1024]{1,0:T(8,128)(2,1)}, u32[]{:S(2)}, u32[]{:S(2)}) collective-permute-start(bf16[256,1024]{1,0:T(8,128)(2,1)} %multiply_convert_fusion.5), channel_id=1, source_target_pairs={{0,16},{8,24},{16,0},{24,8},{1,17},{9,25},{17,1},{25,9},{2,18},{10... | collective-permute-start | bytes 1572872 | tf_op jit(solution)/shard_map/ppermute | solution.py:29
  235.1 46.3 %collective-permute-start.82 = (bf16[4,96,1024]{2,1,0:T(8,128)(2,1)}, bf16[4,96,1024]{2,1,0:T(8,128)(2,1)}, u32[]{:S(2)}, u32[]{:S(2)}) collective-permute-start(bf16[4,96,1024]{2,1,0:T(8,128)(2,1)} %fusion.27), channel_id=1, source_target_pairs={{0,1},{1,0},{2,3},{3,2},{4,5},{5,4},{6,7},{7,6},{8,9},{9,8},{10,11... | collective-permute-start | bytes 2359304 | tf_op jit(solution)/shard_map/ppermute | solution.py:71
  245.6 14.8 %collective-permute-start.46 = (bf16[2,128,1024]{2,1,0:T(8,128)(2,1)S(1)}, bf16[2,128,1024]{2,1,0:T(8,128)(2,1)S(1)}, u32[]{:S(2)}, u32[]{:S(2)}) collective-permute-start(bf16[2,128,1024]{2,1,0:T(8,128)(2,1)S(1)} %pad_maximum_fusion.21), channel_id=1, source_target_pairs={{0,8},{8,0},{16,24},{24,16},{1,9},{9,1},{17,25},{25,17},{2,10},{10... | collective-permute-start | bytes 1572872 | tf_op jit(solution)/shard_map/ppermute | solution.py:29
  246.0 14.7 %collective-permute-start.48 = (bf16[2,128,1024]{2,1,0:T(8,128)(2,1)S(1)}, bf16[2,128,1024]{2,1,0:T(8,128)(2,1)S(1)}, u32[]{:S(2)}, u32[]{:S(2)}) collective-permute-start(bf16[2,128,1024]{2,1,0:T(8,128)(2,1)S(1)} %copy-done.87), channel_id=1, source_target_pairs={{0,16},{8,24},{16,0},{24,8},{1,17},{9,25},{17,1},{25,9},{2,18},{10... | collective-permute-start | bytes 1572872 | tf_op jit(solution)/shard_map/ppermute | solution.py:29
  248.3 23.0 %collective-permute-start.38 = (bf16[2,128,1024]{2,1,0:T(8,128)(2,1)S(1)}, bf16[2,128,1024]{2,1,0:T(8,128)(2,1)S(1)}, u32[]{:S(2)}, u32[]{:S(2)}) collective-permute-start(bf16[2,128,1024]{2,1,0:T(8,128)(2,1)S(1)} %pad_maximum_fusion.20), channel_id=1, source_target_pairs={{0,8},{8,0},{16,24},{24,16},{1,9},{9,1},{17,25},{25,17},{2,10},{10... | collective-permute-start | bytes 1572872 | tf_op jit(solution)/shard_map/ppermute | solution.py:29
  250.1 21.9 %collective-permute-start.40 = (bf16[2,128,1024]{2,1,0:T(8,128)(2,1)S(1)}, bf16[2,128,1024]{2,1,0:T(8,128)(2,1)S(1)}, u32[]{:S(2)}, u32[]{:S(2)}) collective-permute-start(bf16[2,128,1024]{2,1,0:T(8,128)(2,1)S(1)} %stack.191), channel_id=1, source_target_pairs={{0,16},{8,24},{16,0},{24,8},{1,17},{9,25},{17,1},{25,9},{2,18},{10... | collective-permute-start | bytes 1572872 | tf_op jit(solution)/shard_map/ppermute | solution.py:29
  260.4 49.0 %collective-permute-start.74 = (bf16[4,128,1536]{2,1,0:T(8,128)(2,1)S(1)}, bf16[4,128,1536]{2,1,0:T(8,128)(2,1)S(1)}, u32[]{:S(2)}, u32[]{:S(2)}) collective-permute-start(bf16[4,128,1536]{2,1,0:T(8,128)(2,1)S(1)} %fusion.8), channel_id=1, source_target_pairs={{0,1},{1,0},{2,3},{3,2},{4,5},{5,4},{6,7},{7,6},{8,9},{9,8},{10,11... | collective-permute-start | bytes 4718600 | tf_op jit(solution)/shard_map/ppermute | solution.py:71
  261.1 16.5 %collective-permute-start.47 = (bf16[128,1024]{1,0:T(8,128)(2,1)S(1)}, bf16[128,1024]{1,0:T(8,128)(2,1)S(1)}, u32[]{:S(2)}, u32[]{:S(2)}) collective-permute-start(bf16[128,1024]{1,0:T(8,128)(2,1)S(1)} %get-tuple-element.131), channel_id=1, source_target_pairs={{0,16},{8,24},{16,0},{24,8},{1,17},{9,25},{17,1},{25,9},{2,18},{10... | collective-permute-start | bytes 786440 | tf_op jit(solution)/shard_map/ppermute | solution.py:29
  272.3 11.2 %collective-permute-start.39 = (bf16[128,1024]{1,0:T(8,128)(2,1)S(1)}, bf16[128,1024]{1,0:T(8,128)(2,1)S(1)}, u32[]{:S(2)}, u32[]{:S(2)}) collective-permute-start(bf16[128,1024]{1,0:T(8,128)(2,1)S(1)} %get-tuple-element.135), channel_id=1, source_target_pairs={{0,16},{8,24},{16,0},{24,8},{1,17},{9,25},{17,1},{25,9},{2,18},{10... | collective-permute-start | bytes 786440 | tf_op jit(solution)/shard_map/ppermute | solution.py:29
  281.1 17.6 %collective-permute-start.50 = (bf16[256,1024]{1,0:T(8,128)(2,1)S(1)}, bf16[256,1024]{1,0:T(8,128)(2,1)S(1)}, u32[]{:S(2)}, u32[]{:S(2)}) collective-permute-start(bf16[256,1024]{1,0:T(8,128)(2,1)S(1)} %add_convert_fusion.2), channel_id=1, source_target_pairs={{0,8},{8,0},{16,24},{24,16},{1,9},{9,1},{17,25},{25,17},{2,10},{10... | collective-permute-start | bytes 1572872 | tf_op jit(solution)/shard_map/ppermute | solution.py:29
  281.4 18.8 %collective-permute-start.51 = (bf16[256,1024]{1,0:T(8,128)(2,1)S(1)}, bf16[256,1024]{1,0:T(8,128)(2,1)S(1)}, u32[]{:S(2)}, u32[]{:S(2)}) collective-permute-start(bf16[256,1024]{1,0:T(8,128)(2,1)S(1)} %add_convert_fusion.2), channel_id=1, source_target_pairs={{0,16},{8,24},{16,0},{24,8},{1,17},{9,25},{17,1},{25,9},{2,18},{10... | collective-permute-start | bytes 1572872 | tf_op jit(solution)/shard_map/ppermute | solution.py:29
  298.7 12.0 %collective-permute-start.52 = (bf16[128,1024]{1,0:T(8,128)(2,1)S(1)}, bf16[128,1024]{1,0:T(8,128)(2,1)S(1)}, u32[]{:S(2)}, u32[]{:S(2)}) collective-permute-start(bf16[128,1024]{1,0:T(8,128)(2,1)S(1)} %slice.546), channel_id=1, source_target_pairs={{0,16},{8,24},{16,0},{24,8},{1,17},{9,25},{17,1},{25,9},{2,18},{10... | collective-permute-start | bytes 786440 | tf_op jit(solution)/shard_map/ppermute | solution.py:29
  300.2 10.6 %collective-permute-start.53 = (bf16[128,1024]{1,0:T(8,128)(2,1)S(1)}, bf16[128,1024]{1,0:T(8,128)(2,1)S(1)}, u32[]{:S(2)}, u32[]{:S(2)}) collective-permute-start(bf16[128,1024]{1,0:T(8,128)(2,1)S(1)} %slice.547), channel_id=1, source_target_pairs={{0,8},{8,0},{16,24},{24,16},{1,9},{9,1},{17,25},{25,17},{2,10},{10... | collective-permute-start | bytes 786440 | tf_op jit(solution)/shard_map/ppermute | solution.py:29
  306.2 66.2 %collective-permute-start.86 = (bf16[96,1024]{1,0:T(8,128)(2,1)S(1)}, bf16[96,1024]{1,0:T(8,128)(2,1)}, u32[]{:S(2)}, u32[]{:S(2)}) collective-permute-start(bf16[96,1024]{1,0:T(8,128)(2,1)S(1)} %fusion.66), channel_id=1, source_target_pairs={{0,8},{8,0},{16,24},{24,16},{1,9},{9,1},{17,25},{25,17},{2,10},{10... | collective-permute-start | bytes 589832 | tf_op jit(solution)/shard_map/ppermute | solution.py:29
  307.7 66.0 %collective-permute-start.87 = (bf16[96,1024]{1,0:T(8,128)(2,1)S(1)}, bf16[96,1024]{1,0:T(8,128)(2,1)}, u32[]{:S(2)}, u32[]{:S(2)}) collective-permute-start(bf16[96,1024]{1,0:T(8,128)(2,1)S(1)} %fusion.66), channel_id=1, source_target_pairs={{0,16},{8,24},{16,0},{24,8},{1,17},{9,25},{17,1},{25,9},{2,18},{10... | collective-permute-start | bytes 589832 | tf_op jit(solution)/shard_map/ppermute | solution.py:29
  310.8 72.0 %collective-permute-start.75 = (bf16[128,1536]{1,0:T(8,128)(2,1)}, bf16[128,1536]{1,0:T(8,128)(2,1)}, u32[]{:S(2)}, u32[]{:S(2)}) collective-permute-start(bf16[128,1536]{1,0:T(8,128)(2,1)} %fusion.65), channel_id=1, source_target_pairs={{0,2},{1,3},{2,4},{3,5},{4,6},{5,7},{6,0},{7,1},{8,10},{9,11},{10,... | collective-permute-start | bytes 1179656 | tf_op jit(solution)/shard_map/ppermute | solution.py:66
  315.9 79.3 %collective-permute-start.66 = (bf16[256,1024]{1,0:T(8,128)(2,1)}, bf16[256,1024]{1,0:T(8,128)(2,1)}, u32[]{:S(2)}, u32[]{:S(2)}) collective-permute-start(bf16[256,1024]{1,0:T(8,128)(2,1)} %fusion.36), channel_id=1, source_target_pairs={{0,1},{1,0},{2,3},{3,2},{4,5},{5,4},{6,7},{7,6},{8,9},{9,8},{10,11... | collective-permute-start | bytes 1572872 | tf_op jit(solution)/shard_map/ppermute | solution.py:71
  371.4 73.1 %collective-permute-start.58 = (bf16[4,144,1024]{2,1,0:T(8,128)(2,1)S(1)}, bf16[4,144,1024]{2,1,0:T(8,128)(2,1)S(1)}, u32[]{:S(2)}, u32[]{:S(2)}) collective-permute-start(bf16[4,144,1024]{2,1,0:T(8,128)(2,1)S(1)} %fusion.9), channel_id=1, source_target_pairs={{0,1},{1,0},{2,3},{3,2},{4,5},{5,4},{6,7},{7,6},{8,9},{9,8},{10,11... | collective-permute-start | bytes 3538952 | tf_op jit(solution)/shard_map/ppermute | solution.py:71
  378.2 13.2 %collective-permute-start.54 = (bf16[2,128,1024]{2,1,0:T(8,128)(2,1)S(1)}, bf16[2,128,1024]{2,1,0:T(8,128)(2,1)S(1)}, u32[]{:S(2)}, u32[]{:S(2)}) collective-permute-start(bf16[2,128,1024]{2,1,0:T(8,128)(2,1)S(1)} %pad_maximum_fusion.22), channel_id=1, source_target_pairs={{0,8},{8,0},{16,24},{24,16},{1,9},{9,1},{17,25},{25,17},{2,10},{10... | collective-permute-start | bytes 1572872 | tf_op jit(solution)/shard_map/ppermute | solution.py:29
  379.1 12.9 %collective-permute-start.56 = (bf16[2,128,1024]{2,1,0:T(8,128)(2,1)S(1)}, bf16[2,128,1024]{2,1,0:T(8,128)(2,1)S(1)}, u32[]{:S(2)}, u32[]{:S(2)}) collective-permute-start(bf16[2,128,1024]{2,1,0:T(8,128)(2,1)S(1)} %stack.193), channel_id=1, source_target_pairs={{0,16},{8,24},{16,0},{24,8},{1,17},{9,25},{17,1},{25,9},{2,18},{10... | collective-permute-start | bytes 1572872 | tf_op jit(solution)/shard_map/ppermute | solution.py:29
  384.4 14.6 %collective-permute-start.76 = (bf16[128,1536]{1,0:T(8,128)(2,1)S(1)}, bf16[128,1536]{1,0:T(8,128)(2,1)S(1)}, u32[]{:S(2)}, u32[]{:S(2)}) collective-permute-start(bf16[128,1536]{1,0:T(8,128)(2,1)S(1)} %fusion.30), channel_id=1, source_target_pairs={{0,2},{1,3},{2,4},{3,5},{4,6},{5,7},{6,0},{7,1},{8,10},{9,11},{10,... | collective-permute-start | bytes 1179656 | tf_op jit(solution)/shard_map/ppermute | solution.py:66
  396.4 43.9 %collective-permute-start.67 = (bf16[256,1024]{1,0:T(8,128)(2,1)S(1)}, bf16[256,1024]{1,0:T(8,128)(2,1)S(1)}, u32[]{:S(2)}, u32[]{:S(2)}) collective-permute-start(bf16[256,1024]{1,0:T(8,128)(2,1)S(1)} %fusion.31), channel_id=1, source_target_pairs={{2,0},{3,1},{12,10},{13,11},{22,20},{23,21},{24,30},{25,31}} | collective-permute-start | bytes 1572872 | tf_op jit(solution)/shard_map/ppermute | solution.py:116
  397.7 42.6 %collective-permute-start.68 = (bf16[256,1024]{1,0:T(8,128)(2,1)S(1)}, bf16[256,1024]{1,0:T(8,128)(2,1)S(1)}, u32[]{:S(2)}, u32[]{:S(2)}) collective-permute-start(bf16[256,1024]{1,0:T(8,128)(2,1)S(1)} %fusion.31), channel_id=1, source_target_pairs={{4,0},{5,1},{14,10},{15,11},{16,20},{17,21},{26,30},{27,31}} | collective-permute-start | bytes 1572872 | tf_op jit(solution)/shard_map/ppermute | solution.py:116
  399.0 41.3 %collective-permute-start.69 = (bf16[256,1024]{1,0:T(8,128)(2,1)S(1)}, bf16[256,1024]{1,0:T(8,128)(2,1)S(1)}, u32[]{:S(2)}, u32[]{:S(2)}) collective-permute-start(bf16[256,1024]{1,0:T(8,128)(2,1)S(1)} %fusion.31), channel_id=1, source_target_pairs={{6,0},{7,1},{8,10},{9,11},{18,20},{19,21},{28,30},{29,31}} | collective-permute-start | bytes 1572872 | tf_op jit(solution)/shard_map/ppermute | solution.py:116
  406.7 38.5 %collective-permute-start.77 = (bf16[128,1536]{1,0:T(8,128)(2,1)S(1)}, bf16[128,1536]{1,0:T(8,128)(2,1)S(1)}, u32[]{:S(2)}, u32[]{:S(2)}) collective-permute-start(bf16[128,1536]{1,0:T(8,128)(2,1)S(1)} %fusion.29), channel_id=1, source_target_pairs={{0,2},{1,3},{2,4},{3,5},{4,6},{5,7},{6,0},{7,1},{8,10},{9,11},{10,... | collective-permute-start | bytes 1179656 | tf_op jit(solution)/shard_map/ppermute | solution.py:66
  441.8 22.6 %collective-permute-start.70 = (bf16[256,1024]{1,0:T(8,128)(2,1)S(1)}, bf16[256,1024]{1,0:T(8,128)(2,1)S(1)}, u32[]{:S(2)}, u32[]{:S(2)}) collective-permute-start(bf16[256,1024]{1,0:T(8,128)(2,1)S(1)} %add_convert_fusion.1), channel_id=1, source_target_pairs={{0,8},{1,9},{10,2},{11,3},{20,28},{21,29},{30,22},{31,23}} | collective-permute-start | bytes 1572872 | tf_op jit(solution)/shard_map/ppermute | solution.py:116
  443.2 23.4 %collective-permute-start.71 = (bf16[256,1024]{1,0:T(8,128)(2,1)S(1)}, bf16[256,1024]{1,0:T(8,128)(2,1)S(1)}, u32[]{:S(2)}, u32[]{:S(2)}) collective-permute-start(bf16[256,1024]{1,0:T(8,128)(2,1)S(1)} %add_convert_fusion.1), channel_id=1, source_target_pairs={{0,16},{1,17},{10,26},{11,27},{20,4},{21,5},{30,14},{31,15}} | collective-permute-start | bytes 1572872 | tf_op jit(solution)/shard_map/ppermute | solution.py:116
  445.4 15.6 %collective-permute-start.78 = (bf16[128,1536]{1,0:T(8,128)(2,1)S(1)}, bf16[128,1536]{1,0:T(8,128)(2,1)S(1)}, u32[]{:S(2)}, u32[]{:S(2)}) collective-permute-start(bf16[128,1536]{1,0:T(8,128)(2,1)S(1)} %fusion.28), channel_id=1, source_target_pairs={{0,8},{8,0},{16,24},{24,16},{1,9},{9,1},{17,25},{25,17},{2,10},{10... | collective-permute-start | bytes 1179656 | tf_op jit(solution)/shard_map/ppermute | solution.py:29
  447.6 16.8 %collective-permute-start.79 = (bf16[128,1536]{1,0:T(8,128)(2,1)S(1)}, bf16[128,1536]{1,0:T(8,128)(2,1)S(1)}, u32[]{:S(2)}, u32[]{:S(2)}) collective-permute-start(bf16[128,1536]{1,0:T(8,128)(2,1)S(1)} %fusion.28), channel_id=1, source_target_pairs={{0,16},{8,24},{16,0},{24,8},{1,17},{9,25},{17,1},{25,9},{2,18},{10... | collective-permute-start | bytes 1179656 | tf_op jit(solution)/shard_map/ppermute | solution.py:29
  453.8 14.8 %collective-permute-start.60 = (bf16[144,1024]{1,0:T(8,128)(2,1)S(1)}, bf16[144,1024]{1,0:T(8,128)(2,1)S(1)}, u32[]{:S(2)}, u32[]{:S(2)}) collective-permute-start(bf16[144,1024]{1,0:T(8,128)(2,1)S(1)} %fusion.34), channel_id=1, source_target_pairs={{0,2},{1,3},{2,4},{3,5},{4,6},{5,7},{6,0},{7,1},{8,10},{9,11},{10,... | collective-permute-start | bytes 884744 | tf_op jit(solution)/shard_map/ppermute | solution.py:66
  460.9 13.5 %collective-permute-start.80 = (bf16[64,1536]{1,0:T(8,128)(2,1)S(1)}, bf16[64,1536]{1,0:T(8,128)(2,1)S(1)}, u32[]{:S(2)}, u32[]{:S(2)}) collective-permute-start(bf16[64,1536]{1,0:T(8,128)(2,1)S(1)} %slice.570), channel_id=1, source_target_pairs={{0,16},{8,24},{16,0},{24,8},{1,17},{9,25},{17,1},{25,9},{2,18},{10... | collective-permute-start | bytes 589832 | tf_op jit(solution)/shard_map/ppermute | solution.py:29
  465.2 29.4 %collective-permute-start.72 = (bf16[128,1024]{1,0:T(8,128)(2,1)}, bf16[128,1024]{1,0:T(8,128)(2,1)}, u32[]{:S(2)}, u32[]{:S(2)}) collective-permute-start(bf16[128,1024]{1,0:T(8,128)(2,1)} %slice.568), channel_id=1, source_target_pairs={{8,24},{9,25},{2,18},{3,19},{28,12},{29,13},{22,6},{23,7}} | collective-permute-start | bytes 786440 | tf_op jit(solution)/shard_map/ppermute | solution.py:116
  467.3 27.3 %collective-permute-start.73 = (bf16[128,1024]{1,0:T(8,128)(2,1)}, bf16[128,1024]{1,0:T(8,128)(2,1)}, u32[]{:S(2)}, u32[]{:S(2)}) collective-permute-start(bf16[128,1024]{1,0:T(8,128)(2,1)} %slice.569), channel_id=1, source_target_pairs={{16,24},{17,25},{26,18},{27,19},{4,12},{5,13},{14,6},{15,7}} | collective-permute-start | bytes 786440 | tf_op jit(solution)/shard_map/ppermute | solution.py:116
  478.7 11.9 %collective-permute-start.62 = (bf16[144,1024]{1,0:T(8,128)(2,1)S(1)}, bf16[144,1024]{1,0:T(8,128)(2,1)}, u32[]{:S(2)}, u32[]{:S(2)}) collective-permute-start(bf16[144,1024]{1,0:T(8,128)(2,1)S(1)} %fusion.32), channel_id=1, source_target_pairs={{0,8},{8,0},{16,24},{24,16},{1,9},{9,1},{17,25},{25,17},{2,10},{10... | collective-permute-start | bytes 884744 | tf_op jit(solution)/shard_map/ppermute | solution.py:29
  483.2 10.4 %collective-permute-start.63 = (bf16[144,1024]{1,0:T(8,128)(2,1)S(1)}, bf16[144,1024]{1,0:T(8,128)(2,1)}, u32[]{:S(2)}, u32[]{:S(2)}) collective-permute-start(bf16[144,1024]{1,0:T(8,128)(2,1)S(1)} %fusion.32), channel_id=1, source_target_pairs={{0,16},{8,24},{16,0},{24,8},{1,17},{9,25},{17,1},{25,9},{2,18},{10... | collective-permute-start | bytes 884744 | tf_op jit(solution)/shard_map/ppermute | solution.py:29
  (115 other events, 667.2 us)

commit v2 on v1

--- a/solution.py
+++ b/solution.py
@@ -302,7 +302,7 @@
     return jnp.concatenate([values[..., HEAD_SIZE // 2 :], values[..., : HEAD_SIZE // 2]], axis=-1)
 
 
-def per_device(
+def per_device_any(
     layer_in,
     out_grad,
     attn_norm,
@@ -518,10 +518,727 @@
     )
 
 
+BLOCKS = 4
+CHIPS = 4
+ROWS = 128
+SIZE = 256
+HALF = SIZE // 2
+Q_WIDTH = QUERY_HEADS // BLOCKS * HEAD_SIZE
+KV_WIDTH = KEY_VALUE_HEADS // BLOCKS * HEAD_SIZE
+QK_WIDTH = Q_WIDTH + KV_WIDTH
+ATTN_WIDTH = Q_WIDTH + 2 * KV_WIDTH
+FF_ROWS = 96
+FF_PART = 768
+OUT_ROWS = 64
+PACKED = 3 * ROWS
+TURN = HEAD_SIZE // 2
+
+
+def shape(dims, dtype):
+    return jax.ShapeDtypeStruct(dims, dtype)
+
+
+def on_core(body, name, outs, scalars, args, flops=0, traffic=0):
+    return pl.pallas_call(
+        body,
+        name=name,
+        in_specs=[pl.BlockSpec(memory_space=pltpu.SMEM)] * len(scalars)
+        + [pl.BlockSpec(memory_space=pltpu.VMEM)] * len(args),
+        out_specs=[pl.BlockSpec(memory_space=pltpu.VMEM)] * len(outs),
+        out_shape=outs,
+        compiler_params=pltpu.CompilerParams(vmem_limit_bytes=50 << 20),
+        cost_estimate=pl.CostEstimate(flops=flops, bytes_accessed=traffic, transcendentals=0),
+    )(*scalars, *args)
+
+
+def partial_shapes():
+    return [
+        shape((SIZE, MODEL_WIDTH), BF),
+        shape((SIZE, MODEL_WIDTH), BF),
+        shape((HALF, MODEL_WIDTH), F32),
+        shape((HALF, MODEL_WIDTH), F32),
+        shape((SIZE, MODEL_WIDTH), F32),
+    ]
+
+
+def put_partial(refs, j, part):
+    by_one, by_two, keep_low, keep_high, keep = refs
+    if j == 0:
+        keep[...] = part
+    if j == 1:
+        by_one[:HALF] = part[:HALF].astype(BF)
+        keep_high[...] = part[HALF:]
+    if j == 2:
+        by_two[:HALF] = part[HALF:].astype(BF)
+        keep_low[...] = part[:HALF]
+    if j == 3:
+        by_one[HALF:] = part[:HALF].astype(BF)
+        by_two[HALF:] = part[HALF:].astype(BF)
+
+
+def move_partial(by_one, by_two, keep_low, keep_high, keep):
+    one, two = flip(by_one, 1), flip(by_two, 2)
+    low = flip((keep_low + one[HALF:].astype(F32)).astype(BF), 2)
+    high = flip((keep_high + two[HALF:].astype(F32)).astype(BF), 1)
+    return keep, one, two, low, high
+
+
+def joined(keep, one, two, low, high):
+    top = keep[:HALF] + one[:HALF].astype(F32) + low[...].astype(F32)
+    bottom = keep[HALF:] + two[:HALF].astype(F32) + high[...].astype(F32)
+    return jnp.concatenate([top, bottom], axis=0)
+
+
+def spread(value):
+    one, two = flip(value, 1), flip(value, 2)
+    return value, one, two, flip(one[:HALF], 2), flip(two[HALF:], 1)
+
+
+def spread_direct(value):
+    return value, flip(value, 1), flip(value, 2), flip(value, 3)
+
+
+def block_of(refs, j):
+    if j < 3:
+        return refs[j][...]
+    return jnp.concatenate([ref[...] for ref in refs[3:]], axis=0)
+
+
+def part_shard(info, t):
+    chip = lax.rem(info[1] + CHIPS - t % CHIPS, CHIPS)
+    return 2 * chip + (info[2] if t < CHIPS else 1 - info[2])
+
+
+def project_kernel(info, *refs):
+    tokens, (cos_ref, sin_ref), parts = refs[:5], refs[5:7], refs[7:15]
+    normed_ref, raw_ref, q_ref, k_ref, v_ref, w_ref, gain_ref = refs[15:]
+    gain_ref[...] = jnp.zeros_like(gain_ref)
+    for t in range(2 * CHIPS):
+        s = part_shard(info, t)
+        columns = pl.ds(pl.multiple_of(s * ROWS, ROWS), ROWS)
+        w_ref[columns, :] = parts[t][:ROWS]
+        row = parts[t][ROWS : ROWS + 16, : 4 * ROWS].astype(F32)[:1]
+        gain_ref[0:1, columns] = row[:, :ROWS]
+        gain_ref[1:2, columns] = row[:, ROWS : 2 * ROWS]
+        gain_ref[2:3, : 2 * HEAD_SIZE] += row[:, 2 * ROWS :]
+    for j in range(BLOCKS):
+        here = slice(j * SIZE, (j + 1) * SIZE)
+        wide = block_of(tokens, j).astype(F32)
+        normed = (wide * inverse_root(wide) * gain_ref[0:1, :]).astype(BF)
+        normed_ref[here, :] = normed
+        raw = mm(normed, w_ref[...])
+        raw_ref[here, :] = raw[:, :QK_WIDTH]
+        v_ref[j] = raw[:, QK_WIDTH:].astype(BF)
+        cosine, sine = cos_ref[here, :], sin_ref[here, :]
+        for h in range(QK_WIDTH // HEAD_SIZE):
+            one = raw[:, h * HEAD_SIZE : (h + 1) * HEAD_SIZE]
+            is_key = h * HEAD_SIZE >= Q_WIDTH
+            gain = gain_ref[2:3, HEAD_SIZE : 2 * HEAD_SIZE] if is_key else gain_ref[2:3, :HEAD_SIZE]
+            scaled = one * inverse_root(one) * gain
+            rotated = (scaled * cosine + pltpu.roll(scaled, TURN, 1) * sine).astype(BF)
+            at = h * HEAD_SIZE - (Q_WIDTH if is_key else 0)
+            (k_ref if is_key else q_ref)[j, :, at : at + HEAD_SIZE] = rotated
+
+
+def attend_kernel(info, q_ref, k_ref, v_ref, own_out, other_out, mixed_ref, lse_ref, out_ref, *partial):
+    own = info[0]
+    for core, rows in ((info[2], own_out), (1 - info[2], other_out)):
+        for q in range(BLOCKS):
+            at = pl.multiple_of(core * SIZE + (own ^ q) * OUT_ROWS, OUT_ROWS)
+            out_ref[pl.ds(at, OUT_ROWS), :] = rows[q * OUT_ROWS : (q + 1) * OUT_ROWS]
+    for last in range(BLOCKS - 1, -1, -1):
+        i = own ^ last
+        for g in range(KV_WIDTH // HEAD_SIZE):
+            heads = [
+                slice((g * GROUP + h) * HEAD_SIZE, (g * GROUP + h + 1) * HEAD_SIZE)
+                for h in range(GROUP)
+            ]
+            kv = slice(g * HEAD_SIZE, (g + 1) * HEAD_SIZE)
+            query = jnp.concatenate([q_ref[i, :, h] for h in heads], axis=0)
+            total = jnp.zeros((1, GROUP * SIZE), F32)
+            mixed = jnp.zeros((HEAD_SIZE, GROUP * SIZE), F32)
+            for block in range(last + 1):
+                j = own ^ block
+                scores = mm(k_ref[j, :, kv], query, ((1,), (1,)))
+                weights = jnp.exp2(scores * (SCALE * LOG2E))
+                if block == last:
+                    weights = jnp.where(piece_mask(info[3 + i], SIZE, GROUP), weights, 0.0)
+                total = total + jnp.sum(weights, axis=0, keepdims=True)
+                mixed = mixed + mm(v_ref[j, :, kv], weights.astype(BF), ((0,), (0,)))
+            mixed = mixed * (1.0 / total)
+            log_sum = jnp.log2(total)
+            for h in range(GROUP):
+                columns = slice(h * SIZE, (h + 1) * SIZE)
+                mixed_ref[i, :, heads[h]] = mixed[:, columns].T.astype(BF)
+                lse_ref[g, i, h : h + 1, :] = log_sum[:, columns]
+    for j in (3, 1, 2, 0):
+        put_partial(partial, j, mm(mixed_ref[j], out_ref[...]))
+
+
+def after_kernel(tokens, gain_ref, *refs):
+    after_ref, low_ref = refs[5:]
+    after = tokens[...].astype(F32) + joined(*refs[:5])
+    after_ref[...] = after
+    low_ref[...] = (after * inverse_root(after) * gain_ref[1:2, :]).astype(BF)
+
+
+def prepare_kernel(info, *refs):
+    parts, cotangent = refs[:8], refs[8:12]
+    gate_up_ref, down_ref = refs[12:14]
+    grads = refs[14:]
+    for t in range(2 * CHIPS):
+        s = part_shard(info, t)
+        at = pl.ds(pl.multiple_of(s * ROWS, ROWS), ROWS)
+        gate_up_ref[at, :FF_PART] = parts[t][:ROWS]
+        gate_up_ref[at, FF_PART:] = parts[t][ROWS : 2 * ROWS]
+        at = pl.ds(pl.multiple_of(s * FF_ROWS, 32), FF_ROWS)
+        down_ref[at, :FF_PART] = parts[t][2 * ROWS : 2 * ROWS + FF_ROWS]
+        for i in range(3):
+            at = pl.ds(pl.multiple_of(s * FF_ROWS + i * 32, 32), 32)
+            down_ref[at, FF_PART:] = parts[t][2 * ROWS + FF_ROWS :, i * 256 : (i + 1) * 256]
+    for j in range(BLOCKS):
+        grads[j][...] = mm(cotangent[j][...], down_ref[...], ((1,), (1,)))
+
+
+def feed_kernel(blocks, *refs):
+    count = len(blocks)
+    extra = 2 if blocks == (3,) else count
+    inputs, hidden_grads = refs[:extra], refs[extra : extra + count]
+    gate_up_ref = refs[extra + count]
+    outs = refs[extra + count + 1 :]
+    for n, j in enumerate(blocks):
+        if j == 3:
+            tokens = jnp.concatenate([inputs[0][...], inputs[1][...]], axis=0)
+        else:
+            tokens = inputs[n][...]
+        hidden_ref, both_ref = outs[2 * n : 2 * n + 2]
+        gate_up = mm(tokens, gate_up_ref[...])
+        gate, up = gate_up[:, :FF_PART], gate_up[:, FF_PART:]
+        sigmoid = 1.0 / (1.0 + jnp.exp(-gate))
+        silu = gate * sigmoid
+        hidden_ref[...] = (silu * up).astype(BF)
+        grad = hidden_grads[n][...]
+        both_ref[:, :FF_PART] = (grad * up * sigmoid * (1.0 + gate * (1.0 - sigmoid))).astype(BF)
+        both_ref[:, FF_PART:] = (grad * silu).astype(BF)
+        part = mm(both_ref[...], gate_up_ref[...], ((1,), (1,)))
+        first, second = outs[2 * count + 2 * n : 2 * count + 2 * n + 2]
+        first[...] = part[:HALF].astype(first.dtype)
+        second[...] = part[HALF:].astype(second.dtype)
+
+
+FEED_TYPES = {0: (F32, F32), 1: (BF, F32), 2: (F32, BF), 3: (BF, BF)}
+
+
+def feed(blocks, inputs, hidden_grads, gate_up):
+    outs = []
+    for _ in blocks:
+        outs += [shape((SIZE, FF_PART), BF), shape((SIZE, 2 * FF_PART), BF)]
+    for j in blocks:
+        outs += [shape((HALF, MODEL_WIDTH), dtype) for dtype in FEED_TYPES[j]]
+
+    def body(*refs):
+        feed_kernel(blocks, *refs)
+
+    result = on_core(
+        body,
+        "feed",
+        outs,
+        (),
+        (*inputs, *hidden_grads, gate_up),
+        flops=len(blocks) * 4 * SIZE * MODEL_WIDTH * 2 * FF_PART,
+    )
+    count = len(blocks)
+    hidden, both = result[0 : 2 * count : 2], result[1 : 2 * count : 2]
+    return hidden, both, result[2 * count :]
+
+
+def split_rows(info, kept, away, t, at, values):
+    half = values.shape[0] // 2
+    first, second = values[:half], values[half:]
+    is_first = info[2] == 0
+    kept[t, at : at + half, :] = jnp.where(is_first, first, second)
+    away[t, at : at + half, :] = jnp.where(is_first, second, first).astype(BF)
+
+
+def feed_weights_kernel(info, *refs):
+    mlp_in, cotangent, hidden, both = refs[:5], refs[5:9], refs[9:13], refs[13:17]
+    down_ref = refs[17]
+    kept, away = refs[18:20]
+    partial = refs[20:25]
+    down_grad = refs[25]
+    inputs = jnp.concatenate([block_of(mlp_in, j) for j in range(BLOCKS)], axis=0)
+    stored = refs[26]
+    stored[...] = inputs
+    both_all = jnp.concatenate([ref[...] for ref in both], axis=0)
+    hidden_all = jnp.concatenate([ref[...] for ref in hidden], axis=0)
+    cotangent_all = jnp.concatenate([ref[...] for ref in cotangent], axis=0)
+    down_grad[...] = mm(hidden_all, cotangent_all, ((0,), (0,)))
+    for t in range(CHIPS):
+        chip = lax.rem(info[1] + 2 * CHIPS - (t + 1), CHIPS)
+        columns = stored[:, pl.ds(pl.multiple_of(chip * 2 * ROWS, 2 * ROWS), 2 * ROWS)]
+        product = mm(columns, both_all, ((0,), (0,)))
+        split_rows(info, kept, away, t, 0, product[:, :FF_PART])
+        split_rows(info, kept, away, t, ROWS, product[:, FF_PART:])
+        for core, target in ((info[2], kept), (1 - info[2], away)):
+            at = pl.multiple_of((2 * chip + core) * FF_ROWS, 32)
+            rows = down_grad[pl.ds(at, FF_ROWS), :].astype(target.dtype)
+            target[t, 2 * ROWS : 2 * ROWS + FF_ROWS, :] = rows[:, :FF_PART]
+            for i in range(3):
+                target[t, 2 * ROWS + FF_ROWS :, i * 256 : (i + 1) * 256] = rows[
+                    i * 32 : (i + 1) * 32, FF_PART:
+                ]
+    for j in (3, 1, 2, 0):
+        put_partial(partial, j, mm(hidden[j][...], down_ref[...]))
+
+
+def residual_kernel(cotangent, after_ref, gain_ref, *refs):
+    grad_ref, low_ref, gain_part = refs[-3:]
+    keep_a, keep_b, one_a, one_b, two_a, two_b, low, high = refs[:8]
+    top = keep_a[...] + one_a[...].astype(F32) + low[...].astype(F32)
+    bottom = keep_b[...] + two_a[...].astype(F32) + high[...].astype(F32)
+    mlp_in_grad = jnp.concatenate([top, bottom], axis=0)
+    after = after_ref[...]
+    inverse = inverse_root(after)
+    gain_part[...] = jnp.sum(mlp_in_grad * (after * inverse), axis=0, keepdims=True)
+    grad = cotangent[...].astype(F32) + norm_back(after, inverse, gain_ref[1:2, :], mlp_in_grad)
+    grad_ref[...] = grad
+    low_ref[...] = grad.astype(BF)
+
+
+def mixed_grad_kernel(info, mixed_ref, out_ref, *refs):
+    branch, (grad_ref, kept, away, scratch) = refs[:5], refs[5:]
+    own = info[0]
+    for j in range(BLOCKS):
+        grad_ref[j] = mm(block_of(branch, j), out_ref[...], ((1,), (1,))).astype(BF)
+    branch_all = jnp.concatenate([block_of(branch, j) for j in range(BLOCKS)], axis=0)
+    mixed_all = jnp.concatenate([mixed_ref[j] for j in range(BLOCKS)], axis=0)
+    scratch[...] = mm(mixed_all, branch_all, ((0,), (0,)))
+    for core, target in ((info[2], kept), (1 - info[2], away)):
+        for q in range(BLOCKS):
+            at = pl.multiple_of(core * SIZE + (own ^ q) * OUT_ROWS, OUT_ROWS)
+            target[q] = scratch[pl.ds(at, OUT_ROWS), :].astype(target.dtype)
+
+
+def head_back(grad, cosine, sine, raw, gain):
+    dy = grad * cosine - pltpu.roll(grad, TURN, 1) * sine
+    inverse = inverse_root(raw)
+    gain_part = jnp.sum(dy * (raw * inverse), axis=0, keepdims=True)
+    return norm_back(raw, inverse, gain, dy).astype(BF), gain_part
+
+
+def attend_back_kernel(
+    info, q_ref, k_ref, v_ref, mixed_ref, lse_ref, grad_ref, raw_ref, cos_ref, sin_ref, gain_ref,
+    out_ref, gain_part, dk_ref, dv_ref,
+):
+    own = info[0]
+    query_part = jnp.zeros((1, HEAD_SIZE), F32)
+    key_part = jnp.zeros((1, HEAD_SIZE), F32)
+    for g in range(KV_WIDTH // HEAD_SIZE):
+        dk_ref[...] = jnp.zeros_like(dk_ref)
+        dv_ref[...] = jnp.zeros_like(dv_ref)
+        heads = [
+            slice((g * GROUP + h) * HEAD_SIZE, (g * GROUP + h + 1) * HEAD_SIZE) for h in range(GROUP)
+        ]
+        kv = slice(g * HEAD_SIZE, (g + 1) * HEAD_SIZE)
+        for last in range(BLOCKS):
+            i = own ^ last
+            rows = pl.ds(pl.multiple_of(i * SIZE, SIZE), SIZE)
+            query = jnp.concatenate([q_ref[i, :, h] for h in heads], axis=0)
+            grad = jnp.concatenate([grad_ref[i, :, h] for h in heads], axis=0)
+            mixed = jnp.concatenate([mixed_ref[i, :, h] for h in heads], axis=0)
+            delta = jnp.sum((grad.astype(F32) * mixed.astype(F32)).T, axis=0, keepdims=True)
+            log_sum = jnp.concatenate([lse_ref[g, i, h : h + 1, :] for h in range(GROUP)], axis=1)
+            dquery = jnp.zeros((HEAD_SIZE, GROUP * SIZE), F32)
+            for block in range(last + 1):
+                j = own ^ block
+                scores = mm(k_ref[j, :, kv], query, ((1,), (1,)))
+                dprobs = mm(v_ref[j, :, kv], grad, ((1,), (1,)))
+                probs = jnp.exp2(scores * (SCALE * LOG2E) - log_sum)
+                if block == last:
+                    probs = jnp.where(piece_mask(info[3 + i], SIZE, GROUP), probs, 0.0)
+                dscores = (probs * (dprobs - delta)).astype(BF)
+                dv_ref[j] += mm(probs.astype(BF), grad)
+                dk_ref[j] += mm(dscores, query)
+                dquery = dquery + mm(k_ref[j, :, kv], dscores, ((0,), (0,)))
+            for h in range(GROUP):
+                back, part = head_back(
+                    dquery[:, h * SIZE : (h + 1) * SIZE].T * SCALE,
+                    cos_ref[rows, :],
+                    sin_ref[rows, :],
+                    raw_ref[rows, heads[h]],
+                    gain_ref[2:3, :HEAD_SIZE],
+                )
+                out_ref[rows, heads[h]] = back
+                query_part = query_part + part
+        for j in range(BLOCKS):
+            rows = slice(j * SIZE, (j + 1) * SIZE)
+            at = Q_WIDTH + g * HEAD_SIZE
+            back, part = head_back(
+                dk_ref[j] * SCALE,
+                cos_ref[rows, :],
+                sin_ref[rows, :],
+                raw_ref[rows, at : at + HEAD_SIZE],
+                gain_ref[2:3, HEAD_SIZE : 2 * HEAD_SIZE],
+            )
+            out_ref[rows, at : at + HEAD_SIZE] = back
+            key_part = key_part + part
+            at += KV_WIDTH
+            out_ref[rows, at : at + HEAD_SIZE] = dv_ref[j].astype(BF)
+    gain_part[...] = jnp.concatenate([query_part, key_part], axis=1)
+
+
+def attend_weights_kernel(info, normed_ref, grad_ref, w_ref, mlp_part, head_part, *refs):
+    tokens, (kept, away), partial = refs[:5], refs[5:7], refs[7:12]
+    gain_part = jnp.zeros((1, MODEL_WIDTH), F32)
+    for j in (3, 1, 2, 0):
+        part = mm(grad_ref[j * SIZE : (j + 1) * SIZE, :], w_ref[...], ((1,), (1,)))
+        put_partial(partial, j, part)
+        wide = block_of(tokens, j).astype(F32)
+        gain_part = gain_part + jnp.sum(part * (wide * inverse_root(wide)), axis=0, keepdims=True)
+    heads = jnp.concatenate([head_part[...], jnp.zeros((1, MODEL_WIDTH - 2 * HEAD_SIZE), F32)], axis=1)
+    row = lax.broadcasted_iota(jnp.int32, (16, MODEL_WIDTH), 0)
+    gains = jnp.where(row == 0, gain_part, jnp.where(row == 1, mlp_part[...], jnp.where(row == 2, heads, 0.0)))
+    for t in range(CHIPS):
+        chip = lax.rem(info[1] + 2 * CHIPS - (t + 1), CHIPS)
+        columns = normed_ref[:, pl.ds(pl.multiple_of(chip * 2 * ROWS, 2 * ROWS), 2 * ROWS)]
+        split_rows(info, kept, away, t, 0, mm(columns, grad_ref[...], ((0,), (0,))))
+        kept[t, ROWS:, :] = gains
+        away[t, ROWS:, :] = gains.astype(BF)
+
+
+def final_kernel(tokens, gain_ref, residual, *refs):
+    grad_ref = refs[5]
+    wide = tokens[...].astype(F32)
+    dy = joined(*refs[:5])
+    back = norm_back(wide, inverse_root(wide), gain_ref[0:1, :], dy)
+    grad_ref[...] = (residual[...] + back).astype(BF)
+
+
+def output_kernel(after_ref, *refs):
+    refs[5][...] = (after_ref[...] + joined(*refs[:5])).astype(BF)
+
+
+def ring_parts(value):
+    own, other = [value], [other_core(value)]
+    for _ in range(CHIPS - 1):
+        own.append(ring_up(own[-1]))
+        other.append(other_core(own[-1]))
+    return own, other
+
+
+def ring_sum(kept, away):
+    crossed = other_core(away)
+    running = (kept[0] + crossed[0].astype(F32)).astype(BF)
+    for t in range(1, CHIPS):
+        running = (ring_up(running).astype(F32) + kept[t] + crossed[t].astype(F32)).astype(BF)
+    return running
+
+
+def per_device(
+    layer_in,
+    out_grad,
+    attn_norm,
+    query_weight,
+    key_projection,
+    value_projection,
+    query_norm,
+    key_norm,
+    out_weight,
+    mlp_norm,
+    gate_weight,
+    up_weight,
+    down_weight,
+    picture_starts,
+    picture_count,
+):
+    r, index = lax.axis_index("rep"), lax.axis_index("shard")
+    chip, core = index // 2, index % 2
+    length = BLOCKS * SIZE
+    tokens, cotangent_own = layer_in[0], out_grad[0]
+
+    def columns_of(weight, width):
+        return lax.dynamic_slice_in_dim(weight, r * width, width, 1)
+
+    def placed(gain):
+        return lax.dynamic_update_slice_in_dim(
+            jnp.zeros((HEAD_SIZE,), BF), gain, index * gain.shape[0], 0
+        )
+
+    gains = jnp.concatenate([attn_norm, mlp_norm, placed(query_norm), placed(key_norm)])
+    attn_rows = jnp.concatenate(
+        [
+            jnp.concatenate(
+                [
+                    columns_of(query_weight, Q_WIDTH),
+                    columns_of(key_projection, KV_WIDTH),
+                    columns_of(value_projection, KV_WIDTH),
+                ],
+                axis=1,
+            ),
+            jnp.pad(gains[None, :], ((0, 15), (0, ATTN_WIDTH - gains.shape[0]))),
+            lax.dynamic_slice_in_dim(out_weight, r * OUT_ROWS, OUT_ROWS, 0),
+        ],
+        axis=0,
+    )
+    attn_own, attn_other = ring_parts(attn_rows)
+    token_pieces = spread(tokens)
+
+    out_pieces = jnp.stack([part[ROWS + 16 :] for part in attn_own])
+
+    def out_piece(j):
+        step = (chip + CHIPS - (r ^ j)) % CHIPS
+        return lax.dynamic_index_in_dim(out_pieces, step, 0, keepdims=False)
+
+    out_own = jnp.concatenate([out_piece(0)] + [flip(out_piece(j), j) for j in (1, 2, 3)], axis=0)
+    out_other = other_core(out_own)
+
+    def interleaved(weight):
+        cut = weight.reshape(ROWS, 2 * CHIPS, BLOCKS, FF_ROWS)
+        return lax.dynamic_index_in_dim(cut, r, 2, keepdims=False).reshape(ROWS, FF_PART)
+
+    down_rows = lax.dynamic_slice_in_dim(down_weight, r * FF_ROWS, FF_ROWS, 0)
+    rest = down_rows[:, FF_PART:]
+    feed_rows = jnp.concatenate(
+        [
+            interleaved(gate_weight),
+            interleaved(up_weight),
+            down_rows[:, :FF_PART],
+            jnp.concatenate([rest[i * 32 : (i + 1) * 32] for i in range(3)], axis=1),
+        ],
+        axis=0,
+    )
+    feed_rows, _ = lax.optimization_barrier((feed_rows, attn_own[-1]))
+    feed_parts = sum(ring_parts(feed_rows), [])
+    cotangent_own, _ = lax.optimization_barrier((cotangent_own, out_own))
+    cotangent = spread_direct(cotangent_own)
+
+    block_ids = r ^ jnp.arange(BLOCKS, dtype=jnp.int32)
+    positions = (block_ids[:, None] * SIZE + jnp.arange(SIZE, dtype=jnp.int32)[None, :]).reshape(-1)
+    inv_freq = ROPE_BASE ** (-2.0 * jnp.arange(TURN, dtype=F32) / HEAD_SIZE)
+    angles = positions.astype(F32)[:, None] * inv_freq[None, :]
+    cosine, sine = jnp.cos(angles), jnp.sin(angles)
+    cos_rows = jnp.concatenate([cosine, cosine], axis=1)
+    sin_rows = jnp.concatenate([-sine, sine], axis=1)
+    starts = picture_starts[0]
+    held = (starts[None, :] == block_ids[:, None] * PIECE) & (
+        jnp.arange(starts.shape[0], dtype=jnp.int32)[None, :] < picture_count[0]
+    )
+    info = jnp.concatenate(
+        [jnp.stack([r, chip, core]).astype(jnp.int32), jnp.any(held, axis=1).astype(jnp.int32)]
+    )
+
+    normed, raw, query, key, value, attn_matrix, gain_rows = on_core(
+        project_kernel,
+        "project",
+        [
+            shape((length, MODEL_WIDTH), BF),
+            shape((length, QK_WIDTH), F32),
+            shape((BLOCKS, SIZE, Q_WIDTH), BF),
+            shape((BLOCKS, SIZE, KV_WIDTH), BF),
+            shape((BLOCKS, SIZE, KV_WIDTH), BF),
+            shape((MODEL_WIDTH, ATTN_WIDTH), BF),
+            shape((8, MODEL_WIDTH), F32),
+        ],
+        (info,),
+        (*token_pieces, cos_rows, sin_rows, *attn_own, *attn_other),
+        flops=2 * length * MODEL_WIDTH * ATTN_WIDTH,
+    )
+    mixed, lse, out_matrix, *partial = on_core(
+        attend_kernel,
+        "attend",
+        [
+            shape((BLOCKS, SIZE, Q_WIDTH), BF),
+            shape((KV_WIDTH // HEAD_SIZE, BLOCKS, GROUP, SIZE), F32),
+            shape((Q_WIDTH, MODEL_WIDTH), BF),
+        ]
+        + partial_shapes(),
+        (info,),
+        (query, key, value, out_own, out_other),
+        flops=4 * length * MODEL_WIDTH * Q_WIDTH,
+    )
+    after_attn, mlp_own = on_core(
+        after_kernel,
+        "after",
+        [shape((SIZE, MODEL_WIDTH), F32), shape((SIZE, MODEL_WIDTH), BF)],
+        (),
+        (tokens, gain_rows, *move_partial(*partial)),
+    )
+    mlp_in = spread(mlp_own)
+    gate_up, down, *hidden_grads = on_core(
+        prepare_kernel,
+        "prepare",
+        [shape((MODEL_WIDTH, 2 * FF_PART), BF), shape((FF_PART, MODEL_WIDTH), BF)]
+        + [shape((SIZE, FF_PART), F32)] * BLOCKS,
+        (info,),
+        (*feed_parts, *cotangent),
+        flops=2 * length * MODEL_WIDTH * FF_PART,
+    )
+    hidden_0, both_0, keep = feed((0,), mlp_in[:1], hidden_grads[:1], gate_up)
+    hidden_12, both_12, (one_a, keep_high, keep_low, two_a) = feed(
+        (1, 2), mlp_in[1:3], hidden_grads[1:3], gate_up
+    )
+    hidden_3, both_3, (one_b, two_b) = feed((3,), mlp_in[3:], hidden_grads[3:], gate_up)
+    hidden = [*hidden_0, *hidden_12, *hidden_3]
+    both = [*both_0, *both_12, *both_3]
+
+    one_b, two_b = flip(one_b, 1), flip(two_b, 2)
+    one_a, two_a = flip(one_a, 1), flip(two_a, 2)
+    low = flip((keep_low + one_b.astype(F32)).astype(BF), 2)
+    high = flip((keep_high + two_b.astype(F32)).astype(BF), 1)
+    residual_grad, branch_own, mlp_gain_part = on_core(
+        residual_kernel,
+        "residual",
+        [
+            shape((SIZE, MODEL_WIDTH), F32),
+            shape((SIZE, MODEL_WIDTH), BF),
+            shape((1, MODEL_WIDTH), F32),
+        ],
+        (),
+        (out_grad[0], after_attn, gain_rows, *keep, one_a, one_b, two_a, two_b, low, high),
+    )
+    branch = spread(branch_own)
+
+    feed_kept, feed_away, *partial = pl.pallas_call(
+        feed_weights_kernel,
+        name="feed_weights",
+        in_specs=[pl.BlockSpec(memory_space=pltpu.SMEM)]
+        + [pl.BlockSpec(memory_space=pltpu.VMEM)] * 18,
+        out_specs=[pl.BlockSpec(memory_space=pltpu.VMEM)] * 7,
+        out_shape=[
+            shape((CHIPS, PACKED, FF_PART), F32),
+            shape((CHIPS, PACKED, FF_PART), BF),
+        ]
+        + partial_shapes(),
+        scratch_shapes=[
+            pltpu.VMEM((FF_PART, MODEL_WIDTH), F32),
+            pltpu.VMEM((length, MODEL_WIDTH), BF),
+        ],
+        compiler_params=pltpu.CompilerParams(vmem_limit_bytes=56 << 20),
+        cost_estimate=pl.CostEstimate(
+            flops=8 * length * MODEL_WIDTH * FF_PART, bytes_accessed=0, transcendentals=0
+        ),
+    )(info, *mlp_in, *cotangent, *hidden, *both, down)
+    (layer_out,) = on_core(
+        output_kernel,
+        "output",
+        [shape((SIZE, MODEL_WIDTH), BF)],
+        (),
+        (after_attn, *move_partial(*partial)),
+    )
+    feed_sum = ring_sum(feed_kept, feed_away)
+
+    mixed_grad, out_kept, out_away = pl.pallas_call(
+        mixed_grad_kernel,
+        name="mixed_grad",
+        in_specs=[pl.BlockSpec(memory_space=pltpu.SMEM)]
+        + [pl.BlockSpec(memory_space=pltpu.VMEM)] * 7,
+        out_specs=[pl.BlockSpec(memory_space=pltpu.VMEM)] * 3,
+        out_shape=[
+            shape((BLOCKS, SIZE, Q_WIDTH), BF),
+            shape((BLOCKS, OUT_ROWS, MODEL_WIDTH), F32),
+            shape((BLOCKS, OUT_ROWS, MODEL_WIDTH), BF),
+        ],
+        scratch_shapes=[pltpu.VMEM((Q_WIDTH, MODEL_WIDTH), F32)],
+        compiler_params=pltpu.CompilerParams(vmem_limit_bytes=50 << 20),
+        cost_estimate=pl.CostEstimate(
+            flops=4 * length * MODEL_WIDTH * Q_WIDTH, bytes_accessed=0, transcendentals=0
+        ),
+    )(info, mixed, out_matrix, *branch)
+    out_pair = (out_kept + other_core(out_away).astype(F32)).astype(BF)
+    out_blocks = jnp.stack([out_pair[0]] + [flip(out_pair[j], j) for j in (1, 2, 3)])
+
+    def out_step(t):
+        return lax.dynamic_index_in_dim(
+            out_blocks, r ^ ((chip + 2 * CHIPS - t) % CHIPS), 0, keepdims=False
+        )
+
+    out_sum = out_step(1)
+    for t in range(1, CHIPS):
+        out_sum = (ring_up(out_sum).astype(F32) + out_step(t + 1).astype(F32)).astype(BF)
+
+    attn_grad, head_part = pl.pallas_call(
+        attend_back_kernel,
+        name="attend_back",
+        in_specs=[pl.BlockSpec(memory_space=pltpu.SMEM)]
+        + [pl.BlockSpec(memory_space=pltpu.VMEM)] * 10,
+        out_specs=[pl.BlockSpec(memory_space=pltpu.VMEM)] * 2,
+        out_shape=[shape((length, ATTN_WIDTH), BF), shape((1, 2 * HEAD_SIZE), F32)],
+        scratch_shapes=[pltpu.VMEM((BLOCKS, SIZE, HEAD_SIZE), F32)] * 2,
+        compiler_params=pltpu.CompilerParams(vmem_limit_bytes=50 << 20),
+        cost_estimate=pl.CostEstimate(
+            flops=20 * length * length * Q_WIDTH, bytes_accessed=0, transcendentals=0
+        ),
+    )(info, query, key, value, mixed, lse, mixed_grad, raw, cos_rows, sin_rows, gain_rows)
+    attn_kept, attn_away, *partial = on_core(
+        attend_weights_kernel,
+        "attend_weights",
+        [
+            shape((CHIPS, ROWS + 16, ATTN_WIDTH), F32),
+            shape((CHIPS, ROWS + 16, ATTN_WIDTH), BF),
+        ]
+        + partial_shapes(),
+        (info,),
+        (normed, attn_grad, attn_matrix, mlp_gain_part, head_part, *token_pieces),
+        flops=4 * length * MODEL_WIDTH * ATTN_WIDTH,
+    )
+    attn_sum = ring_sum(attn_kept, attn_away)
+    (in_grad,) = on_core(
+        final_kernel,
+        "final",
+        [shape((SIZE, MODEL_WIDTH), BF)],
+        (),
+        (tokens, gain_rows, residual_grad, *move_partial(*partial)),
+    )
+
+    def in_order(value):
+        pieces = jnp.stack(spread_direct(value))
+        return [lax.dynamic_index_in_dim(pieces, r ^ a, 0, keepdims=False) for a in range(BLOCKS)]
+
+    out_w_grad = jnp.concatenate(in_order(out_sum), axis=0).astype(F32)
+    attn_full = in_order(attn_sum)
+
+    def beside(start, stop):
+        return jnp.concatenate([one[:ROWS, start:stop] for one in attn_full], axis=1).astype(F32)
+
+    gain_full = sum(one[ROWS : ROWS + 3].astype(F32) for one in attn_full)
+
+    def slice_of(row, width, start=0):
+        return lax.dynamic_slice_in_dim(gain_full[row], start + index * width, width, 0)
+
+    feed_full = in_order(feed_sum)
+
+    def woven(first):
+        cut = jnp.stack([one[first : first + ROWS] for one in feed_full])
+        cut = cut.reshape(BLOCKS, ROWS, 2 * CHIPS, FF_ROWS).transpose(1, 2, 0, 3)
+        return cut.reshape(ROWS, 2 * CHIPS * BLOCKS * FF_ROWS).astype(F32)
+
+    def unpacked(one):
+        rest = one[2 * ROWS + FF_ROWS :]
+        side = jnp.concatenate([rest[:, i * 256 : (i + 1) * 256] for i in range(3)], axis=0)
+        return jnp.concatenate([one[2 * ROWS : 2 * ROWS + FF_ROWS], side], axis=1)
+
+    head_rows = query_norm.shape[0]
+    return (
+        layer_out[None],
+        in_grad[None],
+        slice_of(0, ROWS),
+        beside(0, Q_WIDTH),
+        beside(Q_WIDTH, QK_WIDTH),
+        beside(QK_WIDTH, ATTN_WIDTH),
+        slice_of(2, head_rows),
+        slice_of(2, head_rows, HEAD_SIZE),
+        out_w_grad,
+        slice_of(1, ROWS),
+        woven(0),
+        woven(ROWS),
+        jnp.concatenate([unpacked(one) for one in feed_full], axis=0).astype(F32),
+    )
+
+
 def solution(mesh):
     tokens, matrix, vector = P("shard", "rep", None), P("shard", None), P("shard")
     return jax.shard_map(
-        per_device,
+        per_device if dict(mesh.shape) == {"rep": 4, "shard": 8} else per_device_any,
         mesh=mesh,
         in_specs=(tokens, tokens, vector, matrix, matrix, matrix, vector, vector, matrix, vector)
         + (matrix, matrix, matrix, matrix, vector),

time: 514 us -> 401 us (0.78)
  local copies, waits for them, and re-layouts: 122 us -> 45.4 us
  Pallas kernels: 15.8 us -> 86 us
  matrix products: 41.8 us -> 0 us
  other arithmetic: 67.9 us -> 27.9 us
  starting transfers between devices: 101 us -> 61.9 us
  waiting for transfers between devices: 153 us -> 172 us
    pallas_call x2 -> x14, Pallas kernels: 15.8 us -> 86 us  [the longest x11 53.8 us: on_core(): pl.pallas_call(body, name=name, in_specs=[pl.BlockSpec(memory_space=pltpu...]
    dot_general x12 -> x0, matrix products: 41.8 us -> none  [mm(): return lax.dot_general(a, b, (dims, ((), ())), preferred_element_type=F32)]
    ppermute x11 -> x0, waiting for transfers between devices: 31.6 us -> none  [joint_move(): return lax.ppermute(value, ('rep', 'shard'), joint)]
    ppermute x18 -> x15, waiting for transfers between devices: 41.7 us -> 69.4 us  [ring_up(): lax.ppermute(value, 'shard', [(i, (i + 2) % count) for i in range(count)])]
    dynamic_update_slice x24 -> x2, local copies, waits for them, and re-layouts: 25.5 us -> 1.78 us  [placed(): lax.dynamic_update_slice_in_dim(jnp.zeros((HEAD_SIZE,), BF), gain, index...]
    ppermute x44 -> x48, waiting for transfers between devices: 79.6 us -> 103 us  [flip(): return lax.ppermute(value, 'rep', [(i, i ^ bit) for i in range(count)])]
    mul x21 -> x0, local copies, waits for them, and re-layouts: 22 us -> none  [the longest x6 7.21 us: norm_back(): return inverse * weighted - values * (inverse * inverse * inverse) * inner]
    ppermute x18 -> x15, starting transfers between devices: 24.4 us -> 6.44 us  [ring_up(): lax.ppermute(value, 'shard', [(i, (i + 2) % count) for i in range(count)])]
  transfers between devices with their start and end apart: 90 -> 75, of which waited for: 35 -> 30; matrix products, arithmetic and copies ran while one was open for 36% -> 10% of each run, Pallas kernels for 3% -> 20%
where the time goes in v2:
time: 401 us; the launch traced here: 396 us
  waiting for transfers between devices  172 us (43%)
  Pallas kernels  86 us (21%)
  starting transfers between devices  61.9 us (15%)
  local copies, waits for them, and re-layouts  45.4 us (11%)
  other arithmetic  27.9 us (7%)
    ppermute x48, waiting for transfers between devices, flip(): return lax.ppermute(value, 'rep', [(i, i ^ bit) for i in range(count)])  103 us
    ppermute x15, waiting for transfers between devices, ring_up(): lax.ppermute(value, 'shard', [(i, (i + 2) % count) for i in range(count)])  69.4 us
    ppermute x48, starting transfers between devices, flip(): return lax.ppermute(value, 'rep', [(i, i ^ bit) for i in range(count)])  53.8 us
    pallas_call x11, Pallas kernels, on_core(): pl.pallas_call(body, name=name, in_specs=[pl.BlockSpec(memory_space=pltpu...  53.8 us
    unnamed x141, local copies, waits for them, and re-layouts  27.1 us
    pallas_call x1, Pallas kernels, per_device(): pl.pallas_call(attend_back_kernel, name='attend_back', in_specs=[pl.Block...  13.5 us
    pallas_call x1, Pallas kernels, per_device(): pl.pallas_call(feed_weights_kernel, name='feed_weights', in_specs=[pl.Blo...  13.5 us
  transfers between devices with their start and end apart: 75, of which 30 were waited for; matrix products, arithmetic and copies ran while one was open for 10% of the time, Pallas kernels for 20%

profile of v2, /device:TPU:0, one launch (start us, length us, event | category | flops | bytes accessed | tf_op | source)
XLA Modules:
  0.0 395.7 jit_solution(11645138883264084241)
XLA Ops:
  5.6 2.6 collective-permute-start.4
  8.2 1.5 collective-permute-start.1
  9.7 1.5 collective-permute-start
  11.9 1.6 constant_dynamic-slice_fusion.12
  13.6 7.1 %collective-permute-done.4.refs_8_ = bf16[208,1024]{1,0:T(8,128)(2,1)S(1)} collective-permute-done((bf16[208,1024]{1,0:T(8,128)(2,1)S(1)}, bf16[208,1024]{1,0:T(8,128)(2,1)S(1)}, u32[]{:S(2)}, u32[]{:S(2)}) %collective-permute-start.4) | collective-permute-done | bytes 426016 | tf_op jit(solution)/shard_map/ppermute | solution.py:66
  20.8 2.3 copy.48
  23.1 2.3 copy.49
  25.4 1.8 constant_dynamic-slice_fusion.17
  27.2 3.1 fusion.15
  30.3 3.8 collective-permute-done.5.refs_9_
  34.1 12.5 %collective-permute-done.6.refs_10_ = bf16[208,1024]{1,0:T(8,128)(2,1)S(1)} collective-permute-done((bf16[208,1024]{1,0:T(8,128)(2,1)S(1)}, bf16[208,1024]{1,0:T(8,128)(2,1)S(1)}, u32[]{:S(2)}, u32[]{:S(2)}) %collective-permute-start.6) | collective-permute-done | bytes 426016 | tf_op jit(solution)/shard_map/ppermute | solution.py:66
  47.4 2.1 collective-permute-start.13
  51.1 1.7 slice.397
  54.8 1.7 copy.51
  56.5 1.7 copy.50
  60.6 1.6 collective-permute-start.2
  64.7 4.3 %collective-permute-done.2.refs_3_ = bf16[128,1024]{1,0:T(8,128)(2,1)S(1)} collective-permute-done((bf16[128,1024]{1,0:T(8,128)(2,1)S(1)}, bf16[128,1024]{1,0:T(8,128)(2,1)S(1)}, u32[]{:S(2)}, u32[]{:S(2)}) %collective-permute-start.2) | collective-permute-done | bytes 262176 | tf_op jit(solution)/shard_map/ppermute | solution.py:29
  69.5 7.3 %project.1 = (bf16[1024,1024]{1,0:T(8,128)(2,1)}, f32[1024,768]{1,0:T(8,128)}, bf16[4,256,512]{2,1,0:T(8,128)(2,1)}, bf16[4,256,256]{2,1,0:T(8,128)(2,1)}, bf16[...) custom-call(s32[7]{0:T(128)S(1)} %pad_add_fusion.info, bf16[256,1024]{1,0:T(8,128)(2,1)} %bitcast.177, ...), custom_call_target="tpu_custom_call" | custom-call | flops 2147483648 | tf_op jit(solution)/shard_map/project/pallas_call | solution.py:542
  79.7 8.1 %attend.1 = (bf16[4,256,512]{2,1,0:T(8,128)(2,1)}, f32[2,4,2,256]{3,2,1,0:T(2,128)S(1)}, bf16[512,1024]{1,0:T(8,128)(2,1)}, bf16[256,1024]{1,0:T(8,128)(2,1)S(1)...) custom-call(s32[7]{0:T(128)S(1)} %pad_add_fusion.info, ...), custom_call_target="tpu_custom_call" | custom-call | flops 2147483648 | tf_op jit(solution)/shard_map/attend/pallas_call | solution.py:542
  89.9 11.0 %collective-permute-done.15.refs_1_ = bf16[256,1024]{1,0:T(8,128)(2,1)S(1)} collective-permute-done((bf16[256,1024]{1,0:T(8,128)(2,1)S(1)}, bf16[256,1024]{1,0:T(8,128)(2,1)S(1)}, u32[]{:S(2)}, u32[]{:S(2)}) %collective-permute-start.15) | collective-permute-done | bytes 524320 | tf_op jit(solution)/shard_map/ppermute | solution.py:29
  101.0 1.6 collective-permute-start.17
  103.3 2.4 collective-permute-done.27.refs_2_
  105.8 1.5 collective-permute-start.25
  107.6 3.4 collective-permute-done.18.refs_4_
  111.0 1.6 after.1
  115.8 5.9 %collective-permute-done.25.refs_11_.refs_8_ = bf16[256,1024]{1,0:T(8,128)(2,1)S(1)} collective-permute-done((bf16[256,1024]{1,0:T(8,128)(2,1)S(1)}, bf16[256,1024]{1,0:T(8,128)(2,1)S(1)}, u32[]{:S(2)}, u32[]{:S(2)}) %collective-permute-start.25) | collective-permute-done | bytes 524320 | tf_op jit(solution)/shard_map/ppermute | solution.py:29
  123.2 8.4 %collective-permute-done.20.refs_1_.refs_2_ = bf16[256,1024]{1,0:T(8,128)(2,1)S(1)} collective-permute-done((bf16[256,1024]{1,0:T(8,128)(2,1)S(1)}, bf16[256,1024]{1,0:T(8,128)(2,1)S(1)}, u32[]{:S(2)}, u32[]{:S(2)}) %collective-permute-start.20) | collective-permute-done | bytes 524320 | tf_op jit(solution)/shard_map/ppermute | solution.py:29
  131.6 1.9 collective-permute-done.19.refs_0_.refs_1_
  133.5 9.2 %collective-permute-done.24.refs_10_.refs_7_ = bf16[256,1024]{1,0:T(8,128)(2,1)S(1)} collective-permute-done((bf16[256,1024]{1,0:T(8,128)(2,1)S(1)}, bf16[256,1024]{1,0:T(8,128)(2,1)S(1)}, u32[]{:S(2)}, u32[]{:S(2)}) %collective-permute-start.24) | collective-permute-done | bytes 524320 | tf_op jit(solution)/shard_map/ppermute | solution.py:29
  146.7 6.0 %prepare.1 = (bf16[1024,1536]{1,0:T(8,128)(2,1)}, bf16[768,1024]{1,0:T(8,128)(2,1)}, f32[256,768]{1,0:T(8,128)}, f32[256,768]{1,0:T(8,128)}, f32[256,768]{1,0:T(8,128)}, /*index=5*/f32[256,768]{1,0:T(8,128)}) custom-call(s32[7]{0:T(128)S(1)} %pad_add_fusion.info, bf16[384,768]{1,0:T(8,128)(2,1)S(1)} %maximum_maximum_fusion.refs_0_, ...), custom_call_target="tpu_custom_call" | custom-call | flops 1610612736 | tf_op jit(solution)/shard_map/prepare/pallas_call | solution.py:542
  154.1 3.8 feed.5
  161.5 6.1 %feed.4 = (bf16[256,768]{1,0:T(8,128)(2,1)S(1)}, bf16[256,1536]{1,0:T(8,128)(2,1)}, bf16[256,768]{1,0:T(8,128)(2,1)S(1)}, bf16[256,1536]{1,0:T(8,128)(2,1)}, bf1...) custom-call(bf16[256,1024]{1,0:T(8,128)(2,1)S(1)} %collective-permut, ...), custom_call_target="tpu_custom_call" | custom-call | flops 3221225472 | tf_op jit(solution)/shard_map/feed/pallas_call | solution.py:542
  173.5 3.8 feed.3
  179.6 2.3 collective-permute-done.42.refs_7_
  182.8 2.9 residual.1
  187.7 13.5 %feed_weights.1 = (f32[4,384,768]{2,1,0:T(8,128)}, bf16[4,384,768]{2,1,0:T(8,128)(2,1)}, bf16[256,1024]{1,0:T(8,128)(2,1)}, bf16[256,1024]{1,0:T(8,128)(2,1)}, f...) custom-call(s32[7]{0:T(128)} %copy-done.22, bf16[256,1024]{1,0:T(8,128)(2,1)} %copy-done.26, ...), custom_call_target="tpu_custom_call" | custom-call | flops 6442450944 | tf_op jit(solution)/shard_map/feed_weights/pallas_call | solution.py:1101
  206.1 8.9 %collective-permute-done.33.refs_1_ = bf16[256,1024]{1,0:T(8,128)(2,1)S(1)} collective-permute-done((bf16[256,1024]{1,0:T(8,128)(2,1)}, bf16[256,1024]{1,0:T(8,128)(2,1)S(1)}, u32[]{:S(2)}, u32[]{:S(2)}) %collective-permute-start.33) | collective-permute-done | bytes 524320 | tf_op jit(solution)/shard_map/ppermute | solution.py:29
  216.1 1.8 collective-permute-done.46.refs_4_
  220.6 5.3 %mixed_grad.1 = (bf16[4,256,512]{2,1,0:T(8,128)(2,1)S(1)}, f32[4,64,1024]{2,1,0:T(8,128)}, bf16[4,64,1024]{2,1,0:T(8,128)(2,1)S(1)}) custom-call(s32[7]{0:T(128)S(1)} %copy-done.23, bf16[4,256,512]{2,1,0:T(8,128)(2,1)} %get-tuple-element.118.mixed_ref, bf16[512,1024]{1,0:T(8,128)(2,1)} %get-tuple-element.120.out_ref, bf16[256,1024]{1,0:T(8,128)(2,1)S(1)} %copy-done.28, ...), custom_call_target="tpu_custom_call" | custom-call | flops 2147483648 | tf_op jit(solution)/shard_map/mixed_grad/pallas_call | solution.py:1130
  226.9 13.5 %attend_back.1 = (bf16[1024,1024]{1,0:T(8,128)(2,1)}, f32[1,256]{1,0:T(1,128)S(1)}) custom-call(s32[7]{0:T(128)S(1)} %copy-done.23, bf16[4,256,512]{2,1,0:T(8,128)(2,1)S(1)} %copy-done.35, bf16[4,256,256]{2,1,0:T(8,128)(2,1)S(1)} %copy-done.39, bf16[4,256,256]{2,1,0:T(8,128)(2,1)S(1)} %copy-done.41, bf16[4,256,512]{2,1,0:T(8,128)(2,1)} %get-tuple-element.118.mixed_ref, ...), custom_call_target="tpu_custom_call" | custom-call | flops 10737418240 | tf_op jit(solution)/shard_map/attend_back/pallas_call | solution.py:1159
  240.4 10.3 %attend_weights.1 = (f32[4,144,1024]{2,1,0:T(8,128)}, bf16[4,144,1024]{2,1,0:T(8,128)(2,1)}, bf16[256,1024]{1,0:T(8,128)(2,1)S(1)}, bf16[256,1024]{1,0:T(8,128)(...) custom-call(s32[7]{0:T(128)S(1)} %copy-done.23, ...), custom_call_target="tpu_custom_call" | custom-call | flops 4294967296 | tf_op jit(solution)/shard_map/attend_weights/pallas_call | solution.py:542
  255.8 13.1 %collective-permute-done.61 = bf16[64,1024]{1,0:T(8,128)(2,1)S(1)} collective-permute-done((bf16[64,1024]{1,0:T(8,128)(2,1)S(1)}, bf16[64,1024]{1,0:T(8,128)(2,1)S(1)}, u32[]{:S(2)}, u32[]{:S(2)}) %collective-permute-start.61) | collective-permute-done | bytes 131104 | tf_op jit(solution)/shard_map/ppermute | solution.py:29
  271.9 6.9 %collective-permute-done.62 = bf16[64,1024]{1,0:T(8,128)(2,1)S(1)} collective-permute-done((bf16[64,1024]{1,0:T(8,128)(2,1)S(1)}, bf16[64,1024]{1,0:T(8,128)(2,1)S(1)}, u32[]{:S(2)}, u32[]{:S(2)}) %collective-permute-start.62) | collective-permute-done | bytes 131104 | tf_op jit(solution)/shard_map/ppermute | solution.py:66
  280.0 7.6 %collective-permute-done.48.refs_2_ = bf16[256,1024]{1,0:T(8,128)(2,1)S(1)} collective-permute-done((bf16[256,1024]{1,0:T(8,128)(2,1)S(1)}, bf16[256,1024]{1,0:T(8,128)(2,1)S(1)}, u32[]{:S(2)}, u32[]{:S(2)}) %collective-permute-start.48) | collective-permute-done | bytes 524320 | tf_op jit(solution)/shard_map/ppermute | solution.py:29
  288.4 6.0 %collective-permute-done.63 = bf16[64,1024]{1,0:T(8,128)(2,1)S(1)} collective-permute-done((bf16[64,1024]{1,0:T(8,128)(2,1)S(1)}, bf16[64,1024]{1,0:T(8,128)(2,1)S(1)}, u32[]{:S(2)}, u32[]{:S(2)}) %collective-permute-start.63) | collective-permute-done | bytes 131104 | tf_op jit(solution)/shard_map/ppermute | solution.py:66
  297.2 2.3 fusion.5
  300.6 1.9 fusion.11
  303.1 1.7 collective-permute-start.52
  309.5 2.8 final.1
  313.3 1.7 collective-permute-start.67
  316.9 5.9 %collective-permute-done.52 = bf16[144,1024]{1,0:T(8,128)(2,1)} collective-permute-done((bf16[144,1024]{1,0:T(8,128)(2,1)}, bf16[144,1024]{1,0:T(8,128)(2,1)}, u32[]{:S(2)}, u32[]{:S(2)}) %collective-permute-start.52) | collective-permute-done | bytes 294944 | tf_op jit(solution)/shard_map/ppermute | solution.py:66
  323.9 1.7 fusion.2
  325.8 9.9 %collective-permute-done.53 = bf16[144,1024]{1,0:T(8,128)(2,1)S(1)} collective-permute-done((bf16[144,1024]{1,0:T(8,128)(2,1)S(1)}, bf16[144,1024]{1,0:T(8,128)(2,1)S(1)}, u32[]{:S(2)}, u32[]{:S(2)}) %collective-permute-start.53) | collective-permute-done | bytes 294944 | tf_op jit(solution)/shard_map/ppermute | solution.py:66
  337.3 12.1 %collective-permute-done.54 = bf16[144,1024]{1,0:T(8,128)(2,1)S(1)} collective-permute-done((bf16[144,1024]{1,0:T(8,128)(2,1)S(1)}, bf16[144,1024]{1,0:T(8,128)(2,1)S(1)}, u32[]{:S(2)}, u32[]{:S(2)}) %collective-permute-start.54) | collective-permute-done | bytes 294944 | tf_op jit(solution)/shard_map/ppermute | solution.py:66
  349.5 1.7 collective-permute-start.57
  353.3 4.2 %collective-permute-done.57 = bf16[144,1024]{1,0:T(8,128)(2,1)S(1)} collective-permute-done((bf16[144,1024]{1,0:T(8,128)(2,1)S(1)}, bf16[144,1024]{1,0:T(8,128)(2,1)S(1)}, u32[]{:S(2)}, u32[]{:S(2)}) %collective-permute-start.57) | collective-permute-done | bytes 294944 | tf_op jit(solution)/shard_map/ppermute | solution.py:29
  357.5 3.1 collective-permute-done.56
  362.2 2.8 collective-permute-done.71
  365.2 1.7 collective-permute-start.74
  372.0 8.7 %collective-permute-done.74 = bf16[384,768]{1,0:T(8,128)(2,1)S(1)} collective-permute-done((bf16[384,768]{1,0:T(8,128)(2,1)S(1)}, bf16[384,768]{1,0:T(8,128)(2,1)S(1)}, u32[]{:S(2)}, u32[]{:S(2)}) %collective-permute-start.74) | collective-permute-done | bytes 589856 | tf_op jit(solution)/shard_map/ppermute | solution.py:29
  380.7 6.2 %collective-permute-done.73 = bf16[384,768]{1,0:T(8,128)(2,1)S(1)} collective-permute-done((bf16[384,768]{1,0:T(8,128)(2,1)S(1)}, bf16[384,768]{1,0:T(8,128)(2,1)S(1)}, u32[]{:S(2)}, u32[]{:S(2)}) %collective-permute-start.73) | collective-permute-done | bytes 589856 | tf_op jit(solution)/shard_map/ppermute | solution.py:29
  389.1 1.6 copy.62
  391.0 1.6 copy.63
  392.6 3.0 maximum_convert_fusion
  (345 shorter events, 91.3 us)
Async XLA Ops:
  5.1 47.7 %collective-permute-start.7 = (bf16[208,1024]{1,0:T(8,128)(2,1)S(1)}, bf16[208,1024]{1,0:T(8,128)(2,1)S(1)}, u32[]{:S(2)}, u32[]{:S(2)}) collective-permute-start(bf16[208,1024]{1,0:T(8,128)(2,1)S(1)} %fusion.10.refs_7_), channel_id=1, source_target_pairs={{0,1},{1,0},{2,3},{3,2},{4,5},{5,4},{6,7},{7,6},{8,9},{9,8},{10,11... | collective-permute-start | bytes 1277960 | tf_op jit(solution)/shard_map/ppermute | solution.py:71
  5.6 15.1 %collective-permute-start.4 = (bf16[208,1024]{1,0:T(8,128)(2,1)S(1)}, bf16[208,1024]{1,0:T(8,128)(2,1)S(1)}, u32[]{:S(2)}, u32[]{:S(2)}) collective-permute-start(bf16[208,1024]{1,0:T(8,128)(2,1)S(1)} %fusion.10.refs_7_), channel_id=1, source_target_pairs={{0,2},{1,3},{2,4},{3,5},{4,6},{5,7},{6,0},{7,1},{8,10},{9,11},{10,... | collective-permute-start | bytes 1277960 | tf_op jit(solution)/shard_map/ppermute | solution.py:66
  8.2 41.9 %collective-permute-start.1 = (bf16[256,1024]{1,0:T(8,128)(2,1)S(1)}, bf16[256,1024]{1,0:T(8,128)(2,1)}, u32[]{:S(2)}, u32[]{:S(2)}) collective-permute-start(bf16[256,1024]{1,0:T(8,128)(2,1)S(1)} %bitcast.178), channel_id=1, source_target_pairs={{0,16},{8,24},{16,0},{24,8},{1,17},{9,25},{17,1},{25,9},{2,18},{10... | collective-permute-start | bytes 1572872 | tf_op jit(solution)/shard_map/ppermute | solution.py:29
  9.7 50.2 %collective-permute-start = (bf16[256,1024]{1,0:T(8,128)(2,1)S(1)}, bf16[256,1024]{1,0:T(8,128)(2,1)S(1)}, u32[]{:S(2)}, u32[]{:S(2)}) collective-permute-start(bf16[256,1024]{1,0:T(8,128)(2,1)S(1)} %bitcast.179), channel_id=1, source_target_pairs={{0,8},{8,0},{16,24},{24,16},{1,9},{9,1},{17,25},{25,17},{2,10},{10... | collective-permute-start | bytes 1572872 | tf_op jit(solution)/shard_map/ppermute | solution.py:29
  20.7 13.4 %collective-permute-start.5 = (bf16[208,1024]{1,0:T(8,128)(2,1)S(1)}, bf16[208,1024]{1,0:T(8,128)(2,1)S(1)}, u32[]{:S(2)}, u32[]{:S(2)}) collective-permute-start(bf16[208,1024]{1,0:T(8,128)(2,1)S(1)} %collective-permute-done.4.refs_8_), channel_id=1, source_target_pairs={{0,2},{1,3},{2,4},{3,5},{4,6},{5,7},{6,0},{7,1},{8,10},{9,11},{10,... | collective-permute-start | bytes 1277960 | tf_op jit(solution)/shard_map/ppermute | solution.py:66
  34.1 12.5 %collective-permute-start.6 = (bf16[208,1024]{1,0:T(8,128)(2,1)S(1)}, bf16[208,1024]{1,0:T(8,128)(2,1)S(1)}, u32[]{:S(2)}, u32[]{:S(2)}) collective-permute-start(bf16[208,1024]{1,0:T(8,128)(2,1)S(1)} %collective-permute-done.5.refs_9_), channel_id=1, source_target_pairs={{0,2},{1,3},{2,4},{3,5},{4,6},{5,7},{6,0},{7,1},{8,10},{9,11},{10,... | collective-permute-start | bytes 1277960 | tf_op jit(solution)/shard_map/ppermute | solution.py:66
  47.4 10.8 %collective-permute-start.13 = (bf16[64,1024]{1,0:T(8,128)(2,1)}, bf16[64,1024]{1,0:T(8,128)(2,1)}, u32[]{:S(2)}, u32[]{:S(2)}) collective-permute-start(bf16[64,1024]{1,0:T(8,128)(2,1)} %get-tuple-element.197), channel_id=1, source_target_pairs={{0,24},{8,16},{16,8},{24,0},{1,25},{9,17},{17,9},{25,1},{2,26},{10... | collective-permute-start | bytes 393224 | tf_op jit(solution)/shard_map/ppermute | solution.py:29
  58.2 11.2 %collective-permute-start.8 = (bf16[208,1024]{1,0:T(8,128)(2,1)S(1)}, bf16[208,1024]{1,0:T(8,128)(2,1)S(1)}, u32[]{:S(2)}, u32[]{:S(2)}) collective-permute-start(bf16[208,1024]{1,0:T(8,128)(2,1)S(1)} %collective-permute-done.4.refs_8_), channel_id=1, source_target_pairs={{0,1},{1,0},{2,3},{3,2},{4,5},{5,4},{6,7},{7,6},{8,9},{9,8},{10,11... | collective-permute-start | bytes 1277960 | tf_op jit(solution)/shard_map/ppermute | solution.py:71
  58.3 11.2 %collective-permute-start.9 = (bf16[208,1024]{1,0:T(8,128)(2,1)S(1)}, bf16[208,1024]{1,0:T(8,128)(2,1)S(1)}, u32[]{:S(2)}, u32[]{:S(2)}) collective-permute-start(bf16[208,1024]{1,0:T(8,128)(2,1)S(1)} %collective-permute-done.5.refs_9_), channel_id=1, source_target_pairs={{0,1},{1,0},{2,3},{3,2},{4,5},{5,4},{6,7},{7,6},{8,9},{9,8},{10,11... | collective-permute-start | bytes 1277960 | tf_op jit(solution)/shard_map/ppermute | solution.py:71
  58.8 10.7 %collective-permute-start.10 = (bf16[208,1024]{1,0:T(8,128)(2,1)S(1)}, bf16[208,1024]{1,0:T(8,128)(2,1)S(1)}, u32[]{:S(2)}, u32[]{:S(2)}) collective-permute-start(bf16[208,1024]{1,0:T(8,128)(2,1)S(1)} %collective-permute-done.6.refs_10_), channel_id=1, source_target_pairs={{0,1},{1,0},{2,3},{3,2},{4,5},{5,4},{6,7},{7,6},{8,9},{9,8},{10,11... | collective-permute-start | bytes 1277960 | tf_op jit(solution)/shard_map/ppermute | solution.py:71
  60.0 16.8 %collective-permute-start.14 = (bf16[256,1024]{1,0:T(8,128)(2,1)S(1)}, bf16[256,1024]{1,0:T(8,128)(2,1)S(1)}, u32[]{:S(2)}, u32[]{:S(2)}) collective-permute-start(bf16[256,1024]{1,0:T(8,128)(2,1)S(1)} %pad_maximum_fusion.5.own_out), channel_id=1, source_target_pairs={{0,1},{1,0},{2,3},{3,2},{4,5},{5,4},{6,7},{7,6},{8,9},{9,8},{10,11... | collective-permute-start | bytes 1572872 | tf_op jit(solution)/shard_map/ppermute | solution.py:71
  69.0 20.9 %collective-permute-start.26 = (bf16[384,768]{1,0:T(8,128)(2,1)S(1)}, bf16[384,768]{1,0:T(8,128)(2,1)S(1)}, u32[]{:S(2)}, u32[]{:S(2)}) collective-permute-start(bf16[384,768]{1,0:T(8,128)(2,1)S(1)} %maximum_maximum_fusion.refs_0_), channel_id=1, source_target_pairs={{0,2},{1,3},{2,4},{3,5},{4,6},{5,7},{6,0},{7,1},{8,10},{9,11},{10,... | collective-permute-start | bytes 1769480 | tf_op jit(solution)/shard_map/ppermute | solution.py:66
  87.8 13.1 %collective-permute-start.15 = (bf16[256,1024]{1,0:T(8,128)(2,1)S(1)}, bf16[256,1024]{1,0:T(8,128)(2,1)S(1)}, u32[]{:S(2)}, u32[]{:S(2)}) collective-permute-start(bf16[256,1024]{1,0:T(8,128)(2,1)S(1)} %get-tuple-element.81), channel_id=1, source_target_pairs={{0,8},{8,0},{16,24},{24,16},{1,9},{9,1},{17,25},{25,17},{2,10},{10... | collective-permute-start | bytes 1572872 | tf_op jit(solution)/shard_map/ppermute | solution.py:29
  88.7 13.9 %collective-permute-start.16 = (bf16[256,1024]{1,0:T(8,128)(2,1)S(1)}, bf16[256,1024]{1,0:T(8,128)(2,1)S(1)}, u32[]{:S(2)}, u32[]{:S(2)}) collective-permute-start(bf16[256,1024]{1,0:T(8,128)(2,1)S(1)} %get-tuple-element.82), channel_id=1, source_target_pairs={{0,16},{8,24},{16,0},{24,8},{1,17},{9,25},{17,1},{25,9},{2,18},{10... | collective-permute-start | bytes 1572872 | tf_op jit(solution)/shard_map/ppermute | solution.py:29
  89.9 15.7 %collective-permute-start.27 = (bf16[384,768]{1,0:T(8,128)(2,1)S(1)}, bf16[384,768]{1,0:T(8,128)(2,1)S(1)}, u32[]{:S(2)}, u32[]{:S(2)}) collective-permute-start(bf16[384,768]{1,0:T(8,128)(2,1)S(1)} %collective-permute-done.26.refs_1_), channel_id=1, source_target_pairs={{0,2},{1,3},{2,4},{3,5},{4,6},{5,7},{6,0},{7,1},{8,10},{9,11},{10,... | collective-permute-start | bytes 1769480 | tf_op jit(solution)/shard_map/ppermute | solution.py:66
  103.3 11.2 %collective-permute-start.29 = (bf16[384,768]{1,0:T(8,128)(2,1)S(1)}, bf16[384,768]{1,0:T(8,128)(2,1)S(1)}, u32[]{:S(2)}, u32[]{:S(2)}) collective-permute-start(bf16[384,768]{1,0:T(8,128)(2,1)S(1)} %maximum_maximum_fusion.refs_0_), channel_id=1, source_target_pairs={{0,1},{1,0},{2,3},{3,2},{4,5},{5,4},{6,7},{7,6},{8,9},{9,8},{10,11... | collective-permute-start | bytes 1769480 | tf_op jit(solution)/shard_map/ppermute | solution.py:71
  105.6 17.5 %collective-permute-start.28 = (bf16[384,768]{1,0:T(8,128)(2,1)S(1)}, bf16[384,768]{1,0:T(8,128)(2,1)S(1)}, u32[]{:S(2)}, u32[]{:S(2)}) collective-permute-start(bf16[384,768]{1,0:T(8,128)(2,1)S(1)} %collective-permute-done.27.refs_2_), channel_id=1, source_target_pairs={{0,2},{1,3},{2,4},{3,5},{4,6},{5,7},{6,0},{7,1},{8,10},{9,11},{10,... | collective-permute-start | bytes 1769480 | tf_op jit(solution)/shard_map/ppermute | solution.py:66
  105.8 15.9 %collective-permute-start.25 = (bf16[256,1024]{1,0:T(8,128)(2,1)S(1)}, bf16[256,1024]{1,0:T(8,128)(2,1)S(1)}, u32[]{:S(2)}, u32[]{:S(2)}) collective-permute-start(bf16[256,1024]{1,0:T(8,128)(2,1)S(1)} %bitcast.184), channel_id=1, source_target_pairs={{0,24},{8,16},{16,8},{24,0},{1,25},{9,17},{17,9},{25,1},{2,26},{10... | collective-permute-start | bytes 1572872 | tf_op jit(solution)/shard_map/ppermute | solution.py:29
  113.6 18.0 %collective-permute-start.20 = (bf16[256,1024]{1,0:T(8,128)(2,1)S(1)}, bf16[256,1024]{1,0:T(8,128)(2,1)S(1)}, u32[]{:S(2)}, u32[]{:S(2)}) collective-permute-start(bf16[256,1024]{1,0:T(8,128)(2,1)S(1)} %get-tuple-element.86.refs_0_), channel_id=1, source_target_pairs={{0,16},{8,24},{16,0},{24,8},{1,17},{9,25},{17,1},{25,9},{2,18},{10... | collective-permute-start | bytes 1572872 | tf_op jit(solution)/shard_map/ppermute | solution.py:29
  113.6 19.8 %collective-permute-start.19 = (bf16[256,1024]{1,0:T(8,128)(2,1)S(1)}, bf16[256,1024]{1,0:T(8,128)(2,1)S(1)}, u32[]{:S(2)}, u32[]{:S(2)}) collective-permute-start(bf16[256,1024]{1,0:T(8,128)(2,1)S(1)} %get-tuple-element.86.refs_0_), channel_id=1, source_target_pairs={{0,8},{8,0},{16,24},{24,16},{1,9},{9,1},{17,25},{25,17},{2,10},{10... | collective-permute-start | bytes 1572872 | tf_op jit(solution)/shard_map/ppermute | solution.py:29
  114.5 28.2 %collective-permute-start.24 = (bf16[256,1024]{1,0:T(8,128)(2,1)S(1)}, bf16[256,1024]{1,0:T(8,128)(2,1)S(1)}, u32[]{:S(2)}, u32[]{:S(2)}) collective-permute-start(bf16[256,1024]{1,0:T(8,128)(2,1)S(1)} %bitcast.185), channel_id=1, source_target_pairs={{0,16},{8,24},{16,0},{24,8},{1,17},{9,25},{17,1},{25,9},{2,18},{10... | collective-permute-start | bytes 1572872 | tf_op jit(solution)/shard_map/ppermute | solution.py:29
  121.8 22.1 %collective-permute-start.23 = (bf16[256,1024]{1,0:T(8,128)(2,1)S(1)}, bf16[256,1024]{1,0:T(8,128)(2,1)S(1)}, u32[]{:S(2)}, u32[]{:S(2)}) collective-permute-start(bf16[256,1024]{1,0:T(8,128)(2,1)S(1)} %bitcast.186), channel_id=1, source_target_pairs={{0,8},{8,0},{16,24},{24,16},{1,9},{9,1},{17,25},{25,17},{2,10},{10... | collective-permute-start | bytes 1572872 | tf_op jit(solution)/shard_map/ppermute | solution.py:29
  123.2 21.7 %collective-permute-start.30 = (bf16[384,768]{1,0:T(8,128)(2,1)S(1)}, bf16[384,768]{1,0:T(8,128)(2,1)S(1)}, u32[]{:S(2)}, u32[]{:S(2)}) collective-permute-start(bf16[384,768]{1,0:T(8,128)(2,1)S(1)} %collective-permute-done.26.refs_1_), channel_id=1, source_target_pairs={{0,1},{1,0},{2,3},{3,2},{4,5},{5,4},{6,7},{7,6},{8,9},{9,8},{10,11... | collective-permute-start | bytes 1769480 | tf_op jit(solution)/shard_map/ppermute | solution.py:71
  131.6 13.2 %collective-permute-start.31 = (bf16[384,768]{1,0:T(8,128)(2,1)S(1)}, bf16[384,768]{1,0:T(8,128)(2,1)S(1)}, u32[]{:S(2)}, u32[]{:S(2)}) collective-permute-start(bf16[384,768]{1,0:T(8,128)(2,1)S(1)} %collective-permute-done.27.refs_2_), channel_id=1, source_target_pairs={{0,1},{1,0},{2,3},{3,2},{4,5},{5,4},{6,7},{7,6},{8,9},{9,8},{10,11... | collective-permute-start | bytes 1769480 | tf_op jit(solution)/shard_map/ppermute | solution.py:71
  133.5 11.4 %collective-permute-start.32 = (bf16[384,768]{1,0:T(8,128)(2,1)S(1)}, bf16[384,768]{1,0:T(8,128)(2,1)S(1)}, u32[]{:S(2)}, u32[]{:S(2)}) collective-permute-start(bf16[384,768]{1,0:T(8,128)(2,1)S(1)} %collective-permute-done.28.refs_3_), channel_id=1, source_target_pairs={{0,1},{1,0},{2,3},{3,2},{4,5},{5,4},{6,7},{7,6},{8,9},{9,8},{10,11... | collective-permute-start | bytes 1769480 | tf_op jit(solution)/shard_map/ppermute | solution.py:71
  142.7 10.0 %collective-permute-start.22 = (bf16[128,1024]{1,0:T(8,128)(2,1)S(1)}, bf16[128,1024]{1,0:T(8,128)(2,1)S(1)}, u32[]{:S(2)}, u32[]{:S(2)}) collective-permute-start(bf16[128,1024]{1,0:T(8,128)(2,1)S(1)} %slice.404), channel_id=1, source_target_pairs={{0,8},{8,0},{16,24},{24,16},{1,9},{9,1},{17,25},{25,17},{2,10},{10... | collective-permute-start | bytes 786440 | tf_op jit(solution)/shard_map/ppermute | solution.py:29
  159.6 13.1 %collective-permute-start.38 = (bf16[128,1024]{1,0:T(8,128)(2,1)S(1)}, bf16[128,1024]{1,0:T(8,128)(2,1)S(1)}, u32[]{:S(2)}, u32[]{:S(2)}) collective-permute-start(bf16[128,1024]{1,0:T(8,128)(2,1)S(1)} %get-tuple-element.111), channel_id=1, source_target_pairs={{0,8},{8,0},{16,24},{24,16},{1,9},{9,1},{17,25},{25,17},{2,10},{10... | collective-permute-start | bytes 786440 | tf_op jit(solution)/shard_map/ppermute | solution.py:29
  160.8 10.5 %collective-permute-start.40 = (bf16[128,1024]{1,0:T(8,128)(2,1)S(1)}, bf16[128,1024]{1,0:T(8,128)(2,1)S(1)}, u32[]{:S(2)}, u32[]{:S(2)}) collective-permute-start(bf16[128,1024]{1,0:T(8,128)(2,1)S(1)} %get-tuple-element.113), channel_id=1, source_target_pairs={{0,16},{8,24},{16,0},{24,8},{1,17},{9,25},{17,1},{25,9},{2,18},{10... | collective-permute-start | bytes 786440 | tf_op jit(solution)/shard_map/ppermute | solution.py:29
  169.2 9.2 %collective-permute-start.37 = (bf16[128,1024]{1,0:T(8,128)(2,1)S(1)}, bf16[128,1024]{1,0:T(8,128)(2,1)S(1)}, u32[]{:S(2)}, u32[]{:S(2)}) collective-permute-start(bf16[128,1024]{1,0:T(8,128)(2,1)S(1)} %get-tuple-element.110), channel_id=1, source_target_pairs={{0,8},{8,0},{16,24},{24,16},{1,9},{9,1},{17,25},{25,17},{2,10},{10... | collective-permute-start | bytes 786440 | tf_op jit(solution)/shard_map/ppermute | solution.py:29
  170.4 9.2 %collective-permute-start.39 = (bf16[128,1024]{1,0:T(8,128)(2,1)S(1)}, bf16[128,1024]{1,0:T(8,128)(2,1)S(1)}, u32[]{:S(2)}, u32[]{:S(2)}) collective-permute-start(bf16[128,1024]{1,0:T(8,128)(2,1)S(1)} %get-tuple-element.112), channel_id=1, source_target_pairs={{0,16},{8,24},{16,0},{24,8},{1,17},{9,25},{17,1},{25,9},{2,18},{10... | collective-permute-start | bytes 786440 | tf_op jit(solution)/shard_map/ppermute | solution.py:29
  171.4 10.6 %collective-permute-start.42 = (bf16[128,1024]{1,0:T(8,128)(2,1)S(1)}, bf16[128,1024]{1,0:T(8,128)(2,1)S(1)}, u32[]{:S(2)}, u32[]{:S(2)}) collective-permute-start(bf16[128,1024]{1,0:T(8,128)(2,1)S(1)} %add_convert_fusion.5), channel_id=1, source_target_pairs={{0,8},{8,0},{16,24},{24,16},{1,9},{9,1},{17,25},{25,17},{2,10},{10... | collective-permute-start | bytes 786440 | tf_op jit(solution)/shard_map/ppermute | solution.py:29
  172.7 10.1 %collective-permute-start.41 = (bf16[128,1024]{1,0:T(8,128)(2,1)S(1)}, bf16[128,1024]{1,0:T(8,128)(2,1)S(1)}, u32[]{:S(2)}, u32[]{:S(2)}) collective-permute-start(bf16[128,1024]{1,0:T(8,128)(2,1)S(1)} %add_convert_fusion.6), channel_id=1, source_target_pairs={{0,16},{8,24},{16,0},{24,8},{1,17},{9,25},{17,1},{25,9},{2,18},{10... | collective-permute-start | bytes 786440 | tf_op jit(solution)/shard_map/ppermute | solution.py:29
  185.8 16.5 %collective-permute-start.44 = (bf16[256,1024]{1,0:T(8,128)(2,1)S(1)}, bf16[256,1024]{1,0:T(8,128)(2,1)S(1)}, u32[]{:S(2)}, u32[]{:S(2)}) collective-permute-start(bf16[256,1024]{1,0:T(8,128)(2,1)S(1)} %get-tuple-element.121.refs_0_), channel_id=1, source_target_pairs={{0,16},{8,24},{16,0},{24,8},{1,17},{9,25},{17,1},{25,9},{2,18},{10... | collective-permute-start | bytes 1572872 | tf_op jit(solution)/shard_map/ppermute | solution.py:29
  186.7 17.3 %collective-permute-start.43 = (bf16[256,1024]{1,0:T(8,128)(2,1)S(1)}, bf16[256,1024]{1,0:T(8,128)(2,1)S(1)}, u32[]{:S(2)}, u32[]{:S(2)}) collective-permute-start(bf16[256,1024]{1,0:T(8,128)(2,1)S(1)} %get-tuple-element.121.refs_0_), channel_id=1, source_target_pairs={{0,8},{8,0},{16,24},{24,16},{1,9},{9,1},{17,25},{25,17},{2,10},{10... | collective-permute-start | bytes 1572872 | tf_op jit(solution)/shard_map/ppermute | solution.py:29
  201.1 13.8 %collective-permute-start.33 = (bf16[256,1024]{1,0:T(8,128)(2,1)}, bf16[256,1024]{1,0:T(8,128)(2,1)S(1)}, u32[]{:S(2)}, u32[]{:S(2)}) collective-permute-start(bf16[256,1024]{1,0:T(8,128)(2,1)} %get-tuple-element.104), channel_id=1, source_target_pairs={{0,8},{8,0},{16,24},{24,16},{1,9},{9,1},{17,25},{25,17},{2,10},{10... | collective-permute-start | bytes 1572872 | tf_op jit(solution)/shard_map/ppermute | solution.py:29
  203.0 14.9 %collective-permute-start.46 = (bf16[128,1024]{1,0:T(8,128)(2,1)}, bf16[128,1024]{1,0:T(8,128)(2,1)}, u32[]{:S(2)}, u32[]{:S(2)}) collective-permute-start(bf16[128,1024]{1,0:T(8,128)(2,1)} %slice.408), channel_id=1, source_target_pairs={{0,8},{8,0},{16,24},{24,16},{1,9},{9,1},{17,25},{25,17},{2,10},{10... | collective-permute-start | bytes 786440 | tf_op jit(solution)/shard_map/ppermute | solution.py:29
  204.0 13.9 %collective-permute-start.45 = (bf16[128,1024]{1,0:T(8,128)(2,1)S(1)}, bf16[128,1024]{1,0:T(8,128)(2,1)S(1)}, u32[]{:S(2)}, u32[]{:S(2)}) collective-permute-start(bf16[128,1024]{1,0:T(8,128)(2,1)S(1)} %slice.407), channel_id=1, source_target_pairs={{0,16},{8,24},{16,0},{24,8},{1,17},{9,25},{17,1},{25,9},{2,18},{10... | collective-permute-start | bytes 786440 | tf_op jit(solution)/shard_map/ppermute | solution.py:29
  205.0 49.5 %collective-permute-start.34 = (bf16[256,1024]{1,0:T(8,128)(2,1)}, bf16[256,1024]{1,0:T(8,128)(2,1)S(1)}, u32[]{:S(2)}, u32[]{:S(2)}) collective-permute-start(bf16[256,1024]{1,0:T(8,128)(2,1)} %get-tuple-element.105), channel_id=1, source_target_pairs={{0,16},{8,24},{16,0},{24,8},{1,17},{9,25},{17,1},{25,9},{2,18},{10... | collective-permute-start | bytes 1572872 | tf_op jit(solution)/shard_map/ppermute | solution.py:29
  206.1 89.9 %collective-permute-start.68 = (bf16[4,384,768]{2,1,0:T(8,128)(2,1)}, bf16[4,384,768]{2,1,0:T(8,128)(2,1)S(1)}, u32[]{:S(2)}, u32[]{:S(2)}) collective-permute-start(bf16[4,384,768]{2,1,0:T(8,128)(2,1)} %get-tuple-element.138), channel_id=1, source_target_pairs={{0,1},{1,0},{2,3},{3,2},{4,5},{5,4},{6,7},{7,6},{8,9},{9,8},{10,11... | collective-permute-start | bytes 7077896 | tf_op jit(solution)/shard_map/ppermute | solution.py:71
  226.8 25.1 %collective-permute-start.58 = (bf16[4,64,1024]{2,1,0:T(8,128)(2,1)S(1)}, bf16[4,64,1024]{2,1,0:T(8,128)(2,1)S(1)}, u32[]{:S(2)}, u32[]{:S(2)}) collective-permute-start(bf16[4,64,1024]{2,1,0:T(8,128)(2,1)S(1)} %get-tuple-element.136), channel_id=1, source_target_pairs={{0,1},{1,0},{2,3},{3,2},{4,5},{5,4},{6,7},{7,6},{8,9},{9,8},{10,11... | collective-permute-start | bytes 1572872 | tf_op jit(solution)/shard_map/ppermute | solution.py:71
  250.7 20.3 %collective-permute-start.47 = (bf16[256,1024]{1,0:T(8,128)(2,1)S(1)}, bf16[256,1024]{1,0:T(8,128)(2,1)S(1)}, u32[]{:S(2)}, u32[]{:S(2)}) collective-permute-start(bf16[256,1024]{1,0:T(8,128)(2,1)S(1)} %get-tuple-element.129), channel_id=1, source_target_pairs={{0,8},{8,0},{16,24},{24,16},{1,9},{9,1},{17,25},{25,17},{2,10},{10... | collective-permute-start | bytes 1572872 | tf_op jit(solution)/shard_map/ppermute | solution.py:29
  252.2 16.7 %collective-permute-start.61 = (bf16[64,1024]{1,0:T(8,128)(2,1)S(1)}, bf16[64,1024]{1,0:T(8,128)(2,1)S(1)}, u32[]{:S(2)}, u32[]{:S(2)}) collective-permute-start(bf16[64,1024]{1,0:T(8,128)(2,1)S(1)} %get-tuple-element.193), channel_id=1, source_target_pairs={{0,24},{8,16},{16,8},{24,0},{1,25},{9,17},{17,9},{25,1},{2,26},{10... | collective-permute-start | bytes 393224 | tf_op jit(solution)/shard_map/ppermute | solution.py:29
  253.6 16.1 %collective-permute-start.60 = (bf16[64,1024]{1,0:T(8,128)(2,1)S(1)}, bf16[64,1024]{1,0:T(8,128)(2,1)S(1)}, u32[]{:S(2)}, u32[]{:S(2)}) collective-permute-start(bf16[64,1024]{1,0:T(8,128)(2,1)S(1)} %get-tuple-element.194), channel_id=1, source_target_pairs={{0,16},{8,24},{16,0},{24,8},{1,17},{9,25},{17,1},{25,9},{2,18},{10... | collective-permute-start | bytes 393224 | tf_op jit(solution)/shard_map/ppermute | solution.py:29
  254.5 16.4 %collective-permute-start.59 = (bf16[64,1024]{1,0:T(8,128)(2,1)S(1)}, bf16[64,1024]{1,0:T(8,128)(2,1)S(1)}, u32[]{:S(2)}, u32[]{:S(2)}) collective-permute-start(bf16[64,1024]{1,0:T(8,128)(2,1)S(1)} %get-tuple-element.195), channel_id=1, source_target_pairs={{0,8},{8,0},{16,24},{24,16},{1,9},{9,1},{17,25},{25,17},{2,10},{10... | collective-permute-start | bytes 393224 | tf_op jit(solution)/shard_map/ppermute | solution.py:29
  268.9 30.7 %collective-permute-start.35 = (bf16[128,1024]{1,0:T(8,128)(2,1)S(1)}, bf16[128,1024]{1,0:T(8,128)(2,1)S(1)}, u32[]{:S(2)}, u32[]{:S(2)}) collective-permute-start(bf16[128,1024]{1,0:T(8,128)(2,1)S(1)} %add_convert_fusion.8), channel_id=1, source_target_pairs={{0,16},{8,24},{16,0},{24,8},{1,17},{9,25},{17,1},{25,9},{2,18},{10... | collective-permute-start | bytes 786440 | tf_op jit(solution)/shard_map/ppermute | solution.py:29
  269.7 17.9 %collective-permute-start.48 = (bf16[256,1024]{1,0:T(8,128)(2,1)S(1)}, bf16[256,1024]{1,0:T(8,128)(2,1)S(1)}, u32[]{:S(2)}, u32[]{:S(2)}) collective-permute-start(bf16[256,1024]{1,0:T(8,128)(2,1)S(1)} %get-tuple-element.130), channel_id=1, source_target_pairs={{0,16},{8,24},{16,0},{24,8},{1,17},{9,25},{17,1},{25,9},{2,18},{10... | collective-permute-start | bytes 1572872 | tf_op jit(solution)/shard_map/ppermute | solution.py:29
  270.9 28.7 %collective-permute-start.51 = (bf16[4,144,1024]{2,1,0:T(8,128)(2,1)S(1)}, bf16[4,144,1024]{2,1,0:T(8,128)(2,1)S(1)}, u32[]{:S(2)}, u32[]{:S(2)}) collective-permute-start(bf16[4,144,1024]{2,1,0:T(8,128)(2,1)S(1)} %copy-done.64), channel_id=1, source_target_pairs={{0,1},{1,0},{2,3},{3,2},{4,5},{5,4},{6,7},{7,6},{8,9},{9,8},{10,11... | collective-permute-start | bytes 3538952 | tf_op jit(solution)/shard_map/ppermute | solution.py:71
  278.9 23.6 %collective-permute-start.36 = (bf16[128,1024]{1,0:T(8,128)(2,1)S(1)}, bf16[128,1024]{1,0:T(8,128)(2,1)S(1)}, u32[]{:S(2)}, u32[]{:S(2)}) collective-permute-start(bf16[128,1024]{1,0:T(8,128)(2,1)S(1)} %add_convert_fusion.7), channel_id=1, source_target_pairs={{0,8},{8,0},{16,24},{24,16},{1,9},{9,1},{17,25},{25,17},{2,10},{10... | collective-permute-start | bytes 786440 | tf_op jit(solution)/shard_map/ppermute | solution.py:29
  294.4 14.6 %collective-permute-start.49 = (bf16[128,1024]{1,0:T(8,128)(2,1)}, bf16[128,1024]{1,0:T(8,128)(2,1)}, u32[]{:S(2)}, u32[]{:S(2)}) collective-permute-start(bf16[128,1024]{1,0:T(8,128)(2,1)} %add_convert_fusion.4), channel_id=1, source_target_pairs={{0,16},{8,24},{16,0},{24,8},{1,17},{9,25},{17,1},{25,9},{2,18},{10... | collective-permute-start | bytes 786440 | tf_op jit(solution)/shard_map/ppermute | solution.py:29
  296.0 13.1 %collective-permute-start.50 = (bf16[128,1024]{1,0:T(8,128)(2,1)}, bf16[128,1024]{1,0:T(8,128)(2,1)}, u32[]{:S(2)}, u32[]{:S(2)}) collective-permute-start(bf16[128,1024]{1,0:T(8,128)(2,1)} %add_convert_fusion.3), channel_id=1, source_target_pairs={{0,8},{8,0},{16,24},{24,16},{1,9},{9,1},{17,25},{25,17},{2,10},{10... | collective-permute-start | bytes 786440 | tf_op jit(solution)/shard_map/ppermute | solution.py:29
  299.6 12.7 %collective-permute-start.64 = (bf16[64,1024]{1,0:T(8,128)(2,1)}, bf16[64,1024]{1,0:T(8,128)(2,1)}, u32[]{:S(2)}, u32[]{:S(2)}) collective-permute-start(bf16[64,1024]{1,0:T(8,128)(2,1)} %fusion.13), channel_id=1, source_target_pairs={{0,2},{1,3},{2,4},{3,5},{4,6},{5,7},{6,0},{7,1},{8,10},{9,11},{10,... | collective-permute-start | bytes 393224 | tf_op jit(solution)/shard_map/ppermute | solution.py:66
  299.6 24.3 %collective-permute-start.69 = (bf16[384,768]{1,0:T(8,128)(2,1)}, bf16[384,768]{1,0:T(8,128)(2,1)}, u32[]{:S(2)}, u32[]{:S(2)}) collective-permute-start(bf16[384,768]{1,0:T(8,128)(2,1)} %fusion.5), channel_id=1, source_target_pairs={{0,2},{1,3},{2,4},{3,5},{4,6},{5,7},{6,0},{7,1},{8,10},{9,11},{10,... | collective-permute-start | bytes 1769480 | tf_op jit(solution)/shard_map/ppermute | solution.py:66
  303.1 19.6 %collective-permute-start.52 = (bf16[144,1024]{1,0:T(8,128)(2,1)}, bf16[144,1024]{1,0:T(8,128)(2,1)}, u32[]{:S(2)}, u32[]{:S(2)}) collective-permute-start(bf16[144,1024]{1,0:T(8,128)(2,1)} %fusion.11), channel_id=1, source_target_pairs={{0,2},{1,3},{2,4},{3,5},{4,6},{5,7},{6,0},{7,1},{8,10},{9,11},{10,... | collective-permute-start | bytes 884744 | tf_op jit(solution)/shard_map/ppermute | solution.py:66
  313.3 22.7 %collective-permute-start.67 = (bf16[64,1024]{1,0:T(8,128)(2,1)S(1)}, bf16[64,1024]{1,0:T(8,128)(2,1)S(1)}, u32[]{:S(2)}, u32[]{:S(2)}) collective-permute-start(bf16[64,1024]{1,0:T(8,128)(2,1)S(1)} %fusion.12), channel_id=1, source_target_pairs={{0,24},{8,16},{16,8},{24,0},{1,25},{9,17},{17,9},{25,1},{2,26},{10... | collective-permute-start | bytes 393224 | tf_op jit(solution)/shard_map/ppermute | solution.py:29
  315.0 21.1 %collective-permute-start.66 = (bf16[64,1024]{1,0:T(8,128)(2,1)S(1)}, bf16[64,1024]{1,0:T(8,128)(2,1)S(1)}, u32[]{:S(2)}, u32[]{:S(2)}) collective-permute-start(bf16[64,1024]{1,0:T(8,128)(2,1)S(1)} %fusion.12), channel_id=1, source_target_pairs={{0,16},{8,24},{16,0},{24,8},{1,17},{9,25},{17,1},{25,9},{2,18},{10... | collective-permute-start | bytes 393224 | tf_op jit(solution)/shard_map/ppermute | solution.py:29
  316.1 19.9 %collective-permute-start.65 = (bf16[64,1024]{1,0:T(8,128)(2,1)S(1)}, bf16[64,1024]{1,0:T(8,128)(2,1)S(1)}, u32[]{:S(2)}, u32[]{:S(2)}) collective-permute-start(bf16[64,1024]{1,0:T(8,128)(2,1)S(1)} %fusion.12), channel_id=1, source_target_pairs={{0,8},{8,0},{16,24},{24,16},{1,9},{9,1},{17,25},{25,17},{2,10},{10... | collective-permute-start | bytes 393224 | tf_op jit(solution)/shard_map/ppermute | solution.py:29
  323.8 11.8 %collective-permute-start.53 = (bf16[144,1024]{1,0:T(8,128)(2,1)S(1)}, bf16[144,1024]{1,0:T(8,128)(2,1)S(1)}, u32[]{:S(2)}, u32[]{:S(2)}) collective-permute-start(bf16[144,1024]{1,0:T(8,128)(2,1)S(1)} %fusion.8), channel_id=1, source_target_pairs={{0,2},{1,3},{2,4},{3,5},{4,6},{5,7},{6,0},{7,1},{8,10},{9,11},{10,... | collective-permute-start | bytes 884744 | tf_op jit(solution)/shard_map/ppermute | solution.py:66
  325.7 27.4 %collective-permute-start.70 = (bf16[384,768]{1,0:T(8,128)(2,1)S(1)}, bf16[384,768]{1,0:T(8,128)(2,1)S(1)}, u32[]{:S(2)}, u32[]{:S(2)}) collective-permute-start(bf16[384,768]{1,0:T(8,128)(2,1)S(1)} %fusion.2), channel_id=1, source_target_pairs={{0,2},{1,3},{2,4},{3,5},{4,6},{5,7},{6,0},{7,1},{8,10},{9,11},{10,... | collective-permute-start | bytes 1769480 | tf_op jit(solution)/shard_map/ppermute | solution.py:66
  335.8 13.6 %collective-permute-start.54 = (bf16[144,1024]{1,0:T(8,128)(2,1)S(1)}, bf16[144,1024]{1,0:T(8,128)(2,1)S(1)}, u32[]{:S(2)}, u32[]{:S(2)}) collective-permute-start(bf16[144,1024]{1,0:T(8,128)(2,1)S(1)} %fusion.7), channel_id=1, source_target_pairs={{0,2},{1,3},{2,4},{3,5},{4,6},{5,7},{6,0},{7,1},{8,10},{9,11},{10,... | collective-permute-start | bytes 884744 | tf_op jit(solution)/shard_map/ppermute | solution.py:66
  351.2 9.4 %collective-permute-start.56 = (bf16[144,1024]{1,0:T(8,128)(2,1)S(1)}, bf16[144,1024]{1,0:T(8,128)(2,1)S(1)}, u32[]{:S(2)}, u32[]{:S(2)}) collective-permute-start(bf16[144,1024]{1,0:T(8,128)(2,1)S(1)} %fusion.6), channel_id=1, source_target_pairs={{0,16},{8,24},{16,0},{24,8},{1,17},{9,25},{17,1},{25,9},{2,18},{10... | collective-permute-start | bytes 884744 | tf_op jit(solution)/shard_map/ppermute | solution.py:29
  353.2 11.7 %collective-permute-start.71 = (bf16[384,768]{1,0:T(8,128)(2,1)S(1)}, bf16[384,768]{1,0:T(8,128)(2,1)S(1)}, u32[]{:S(2)}, u32[]{:S(2)}) collective-permute-start(bf16[384,768]{1,0:T(8,128)(2,1)S(1)} %fusion.1), channel_id=1, source_target_pairs={{0,2},{1,3},{2,4},{3,5},{4,6},{5,7},{6,0},{7,1},{8,10},{9,11},{10,... | collective-permute-start | bytes 1769480 | tf_op jit(solution)/shard_map/ppermute | solution.py:66
  365.2 15.5 %collective-permute-start.74 = (bf16[384,768]{1,0:T(8,128)(2,1)S(1)}, bf16[384,768]{1,0:T(8,128)(2,1)S(1)}, u32[]{:S(2)}, u32[]{:S(2)}) collective-permute-start(bf16[384,768]{1,0:T(8,128)(2,1)S(1)} %fusion), channel_id=1, source_target_pairs={{0,24},{8,16},{16,8},{24,0},{1,25},{9,17},{17,9},{25,1},{2,26},{10... | collective-permute-start | bytes 1769480 | tf_op jit(solution)/shard_map/ppermute | solution.py:29
  366.9 20.0 %collective-permute-start.73 = (bf16[384,768]{1,0:T(8,128)(2,1)S(1)}, bf16[384,768]{1,0:T(8,128)(2,1)S(1)}, u32[]{:S(2)}, u32[]{:S(2)}) collective-permute-start(bf16[384,768]{1,0:T(8,128)(2,1)S(1)} %fusion), channel_id=1, source_target_pairs={{0,16},{8,24},{16,0},{24,8},{1,17},{9,25},{17,1},{25,9},{2,18},{10... | collective-permute-start | bytes 1769480 | tf_op jit(solution)/shard_map/ppermute | solution.py:29
  368.0 18.9 %collective-permute-start.72 = (bf16[384,768]{1,0:T(8,128)(2,1)S(1)}, bf16[384,768]{1,0:T(8,128)(2,1)S(1)}, u32[]{:S(2)}, u32[]{:S(2)}) collective-permute-start(bf16[384,768]{1,0:T(8,128)(2,1)S(1)} %fusion), channel_id=1, source_target_pairs={{0,8},{8,0},{16,24},{24,16},{1,9},{9,1},{17,25},{25,17},{2,10},{10... | collective-permute-start | bytes 1769480 | tf_op jit(solution)/shard_map/ppermute | solution.py:29
  (79 other events, 831.0 us)

commit v3 on v1

--- a/solution.py
+++ b/solution.py
@@ -302,7 +302,7 @@
     return jnp.concatenate([values[..., HEAD_SIZE // 2 :], values[..., : HEAD_SIZE // 2]], axis=-1)
 
 
-def per_device(
+def per_device_any(
     layer_in,
     out_grad,
     attn_norm,
@@ -518,10 +518,929 @@
     )
 
 
+BLOCKS = 4
+CHIPS = 4
+ROWS = 128
+SIZE = 256
+HALF = SIZE // 2
+Q_WIDTH = QUERY_HEADS // BLOCKS * HEAD_SIZE
+KV_WIDTH = KEY_VALUE_HEADS // BLOCKS * HEAD_SIZE
+ATTN_WIDTH = Q_WIDTH + 2 * KV_WIDTH
+GROUPS = KV_WIDTH // HEAD_SIZE
+GROUP_Q = GROUP * HEAD_SIZE
+GROUP_WIDTH = GROUP_Q + 2 * HEAD_SIZE
+FF_ROWS = 96
+FF_PART = 768
+OUT_ROWS = 64
+PACKED = 3 * ROWS
+TURN = HEAD_SIZE // 2
+
+
+def shape(dims, dtype):
+    return jax.ShapeDtypeStruct(dims, dtype)
+
+
+def on_core(body, name, outs, scalars, args, far=(), scratch=(), limit=16):
+    return pl.pallas_call(
+        body,
+        name=name,
+        in_specs=[pl.BlockSpec(memory_space=pltpu.SMEM)] * len(scalars)
+        + [pl.BlockSpec(memory_space=pltpu.VMEM)] * len(args)
+        + [pl.BlockSpec(memory_space=pl.ANY)] * len(far),
+        out_specs=[pl.BlockSpec(memory_space=pltpu.VMEM)] * len(outs),
+        out_shape=outs,
+        scratch_shapes=list(scratch),
+        compiler_params=pltpu.CompilerParams(vmem_limit_bytes=limit << 20),
+    )(*scalars, *args, *far)
+
+
+class Loads:
+    def __init__(self, semaphores):
+        self.semaphores, self.used = semaphores, 0
+
+    def __call__(self, source, target):
+        copy = pltpu.make_async_copy(source, target, self.semaphores.at[self.used])
+        self.used += 1
+        copy.start()
+        return copy
+
+
+def partial_shapes():
+    return [
+        shape((SIZE, MODEL_WIDTH), BF),
+        shape((SIZE, MODEL_WIDTH), BF),
+        shape((HALF, MODEL_WIDTH), F32),
+        shape((HALF, MODEL_WIDTH), F32),
+        shape((SIZE, MODEL_WIDTH), F32),
+    ]
+
+
+def put_partial(refs, j, part):
+    by_one, by_two, keep_low, keep_high, keep = refs
+    if j == 0:
+        keep[...] = part
+    if j == 1:
+        by_one[:HALF] = part[:HALF].astype(BF)
+        keep_high[...] = part[HALF:]
+    if j == 2:
+        by_two[:HALF] = part[HALF:].astype(BF)
+        keep_low[...] = part[:HALF]
+    if j == 3:
+        by_one[HALF:] = part[:HALF].astype(BF)
+        by_two[HALF:] = part[HALF:].astype(BF)
+
+
+def move_partial(by_one, by_two, keep_low, keep_high, keep):
+    one, two = flip(by_one, 1), flip(by_two, 2)
+    low = flip((keep_low + one[HALF:].astype(F32)).astype(BF), 2)
+    high = flip((keep_high + two[HALF:].astype(F32)).astype(BF), 1)
+    return keep, one, two, low, high
+
+
+def joined(keep, one, two, low, high):
+    top = keep[:HALF] + one[:HALF].astype(F32) + low[...].astype(F32)
+    bottom = keep[HALF:] + two[:HALF].astype(F32) + high[...].astype(F32)
+    return jnp.concatenate([top, bottom], axis=0)
+
+
+def spread(value):
+    half = value.shape[0] // 2
+    one, two = flip(value, 1), flip(value, 2)
+    return value, one, two, flip(one[:half], 2), flip(two[half:], 1)
+
+
+def spread_direct(value):
+    return value, flip(value, 1), flip(value, 2), flip(value, 3)
+
+
+def tie(values, *others):
+    return lax.optimization_barrier((values, others))[0]
+
+
+def block_of(refs, j):
+    if j < 3 or len(refs) == 4:
+        return refs[j][...]
+    return jnp.concatenate([ref[...] for ref in refs[3:]], axis=0)
+
+
+def load_paired(loads, refs, which, target):
+    at = slice(which * HALF, (which + 1) * HALF)
+    return [
+        loads(refs[n].at[at, :], target.at[n * HALF : (n + 1) * HALF, :]) for n in range(2 * BLOCKS)
+    ]
+
+
+def part_shard(info, t):
+    chip = lax.rem(info[1] + CHIPS - t % CHIPS, CHIPS)
+    return 2 * chip + (info[2] if t < CHIPS else 1 - info[2])
+
+
+def pack_kernel(info, wq, wk, wv, wo, attn_gain, mlp_gain, query_gain, key_gain, out):
+    for g in range(GROUPS):
+        at = g * GROUP_WIDTH
+        head = info[0] * GROUPS + g
+        out[:ROWS, at : at + GROUP_Q] = wq[:, pl.ds(pl.multiple_of(head * GROUP_Q, GROUP_Q), GROUP_Q)]
+        for weight, start in ((wk, at + GROUP_Q), (wv, at + GROUP_Q + HEAD_SIZE)):
+            columns = pl.ds(pl.multiple_of(head * HEAD_SIZE, HEAD_SIZE), HEAD_SIZE)
+            out[:ROWS, start : start + HEAD_SIZE] = weight[:, columns]
+    tile = slice(ROWS, ROWS + 16)
+    out[tile, :] = jnp.zeros((16, ATTN_WIDTH), BF)
+    out[tile, :ROWS] = jnp.broadcast_to(attn_gain[...], (16, ROWS))
+    out[tile, ROWS : 2 * ROWS] = jnp.broadcast_to(mlp_gain[...], (16, ROWS))
+    out[tile, 2 * ROWS : 2 * ROWS + 16] = jnp.broadcast_to(query_gain[...], (16, 16))
+    out[tile, 3 * ROWS : 3 * ROWS + 16] = jnp.broadcast_to(key_gain[...], (16, 16))
+    out[ROWS + 16 :, :] = wo[pl.ds(pl.multiple_of(info[0] * OUT_ROWS, OUT_ROWS), OUT_ROWS), :]
+
+
+def pack_feed_kernel(info, gate, up, down, out):
+    for a in range(BLOCKS):
+
+        @pl.when(info[0] == a)
+        def _():
+            for weight, first in ((gate, 0), (up, ROWS)):
+                cut = []
+                for s in range(2 * CHIPS):
+                    start = (s * BLOCKS + a) * FF_ROWS
+                    cut.append(weight[:, start : start + FF_ROWS])
+                out[first : first + ROWS, :] = jnp.concatenate(cut, axis=1)
+            rows = slice(a * FF_ROWS, (a + 1) * FF_ROWS)
+            out[2 * ROWS : 2 * ROWS + FF_ROWS, :] = down[rows, :FF_PART]
+            for i in range(3):
+                rows = slice(a * FF_ROWS + i * 32, a * FF_ROWS + (i + 1) * 32)
+                out[2 * ROWS + FF_ROWS :, i * 256 : (i + 1) * 256] = down[rows, FF_PART:]
+
+
+def pick_kernel(info, *refs):
+    parts, outs, semaphores = refs[:CHIPS], refs[CHIPS:-1], refs[-1]
+    for j in range(BLOCKS):
+        step = lax.rem(info[1] + CHIPS - (info[0] ^ j), CHIPS)
+        for t in range(CHIPS):
+
+            @pl.when(step == t)
+            def _():
+                pltpu.make_async_copy(
+                    parts[t].at[ROWS + 16 :, :], outs[j], semaphores.at[j]
+                ).start()
+
+    for j in range(BLOCKS):
+        pltpu.make_async_copy(parts[0].at[ROWS + 16 :, :], outs[j], semaphores.at[j]).wait()
+
+
+def project_kernel(info, cos_ref, sin_ref, *refs):
+    parts, tokens = refs[:8], refs[8:16]
+    normed_ref, raw_ref, q_ref, k_ref, v_ref, w_ref, gain_ref = refs[16:23]
+    all_tokens, gain_rows, semaphores = refs[23:]
+    loads = Loads(semaphores)
+    gain_loads, part_loads = [], []
+    shards = [part_shard(info, t) for t in range(2 * CHIPS)]
+    for t in range(2 * CHIPS):
+        gain_loads.append(loads(parts[t].at[ROWS : ROWS + 16, :], gain_rows.at[t]))
+    token_loads = load_paired(loads, tokens, 0, all_tokens)
+    for t in range(2 * CHIPS):
+        at = pl.ds(pl.multiple_of(shards[t] * ROWS, ROWS), ROWS)
+        part_loads.append(loads(parts[t].at[:ROWS, :], w_ref.at[at, :]))
+    gain_ref[...] = jnp.zeros_like(gain_ref)
+    low_lane = lax.broadcasted_iota(jnp.int32, (8, HEAD_SIZE), 1) < 16
+    for t in range(2 * CHIPS):
+        gain_loads[t].wait()
+        columns = pl.ds(pl.multiple_of(shards[t] * ROWS, ROWS), ROWS)
+        row = gain_rows[t, :, : 4 * ROWS].astype(F32)[:8]
+        gain_ref[0:1, columns] = row[:1, :ROWS]
+        gain_ref[1:2, columns] = row[:1, ROWS : 2 * ROWS]
+        for start in (0, HEAD_SIZE):
+            mine = jnp.where(low_lane, row[:, 2 * ROWS + start : 3 * ROWS + start], 0.0)
+            gain_ref[2:3, start : start + HEAD_SIZE] += pltpu.roll(mine, shards[t] * 16, 1)[:1]
+    for j in range(BLOCKS):
+        here = slice(j * SIZE, (j + 1) * SIZE)
+        for copy in token_loads[2 * j : 2 * j + 2]:
+            copy.wait()
+        wide = all_tokens[here, :].astype(F32)
+        normed = (wide * inverse_root(wide) * gain_ref[0:1, :]).astype(BF)
+        normed_ref[here, :] = normed
+    for copy in part_loads:
+        copy.wait()
+    for j in range(BLOCKS):
+        here = slice(j * SIZE, (j + 1) * SIZE)
+        raw = mm(normed_ref[here, :], w_ref[...])
+        cosine, sine = cos_ref[here, :], sin_ref[here, :]
+        for g in range(GROUPS):
+            for h in range(GROUP + 1):
+                at = g * GROUP_WIDTH + h * HEAD_SIZE
+                one = raw[:, at : at + HEAD_SIZE]
+                raw_ref[g, here, h * HEAD_SIZE : (h + 1) * HEAD_SIZE] = one
+                gain_at = HEAD_SIZE if h == GROUP else 0
+                scaled = one * inverse_root(one) * gain_ref[2:3, gain_at : gain_at + HEAD_SIZE]
+                rotated = (scaled * cosine + pltpu.roll(scaled, TURN, 1) * sine).astype(BF)
+                if h == GROUP:
+                    k_ref[g, j] = rotated
+                else:
+                    q_ref[g, j, h * SIZE : (h + 1) * SIZE, :] = rotated
+            v_ref[g, j] = raw[:, (g + 1) * GROUP_WIDTH - HEAD_SIZE : (g + 1) * GROUP_WIDTH].astype(BF)
+
+
+def attend_kernel(info, q_ref, k_ref, v_ref, mixed_ref, lse_ref):
+    own = info[0]
+    for last in range(BLOCKS - 1, -1, -1):
+        i = own ^ last
+        for g in range(GROUPS):
+            query = q_ref[g, i]
+            total = jnp.zeros((1, GROUP * SIZE), F32)
+            mixed = jnp.zeros((HEAD_SIZE, GROUP * SIZE), F32)
+            for block in range(last + 1):
+                j = own ^ block
+                scores = mm(k_ref[g, j], query, ((1,), (1,)))
+                weights = jnp.exp2(scores * (SCALE * LOG2E))
+                if block == last:
+                    weights = jnp.where(piece_mask(info[3 + i], SIZE, GROUP), weights, 0.0)
+                total = total + jnp.sum(weights, axis=0, keepdims=True)
+                mixed = mixed + mm(v_ref[g, j], weights.astype(BF), ((0,), (0,)))
+            mixed = mixed * (1.0 / total)
+            for h in range(GROUP):
+                columns = slice(h * SIZE, (h + 1) * SIZE)
+                at = (g * GROUP + h) * HEAD_SIZE
+                mixed_ref[i, :, at : at + HEAD_SIZE] = mixed[:, columns].T.astype(BF)
+            lse_ref[g, i] = jnp.log2(total)
+
+
+def out_kernel(info, mixed_ref, *refs):
+    own_pieces, other_pieces, out_ref, partial = refs[:4], refs[4:8], refs[8], refs[9:]
+    own = info[0]
+    for core, rows in ((info[2], own_pieces), (1 - info[2], other_pieces)):
+        for q in range(BLOCKS):
+            at = pl.multiple_of(core * SIZE + (own ^ q) * OUT_ROWS, OUT_ROWS)
+            out_ref[pl.ds(at, OUT_ROWS), :] = rows[q][...]
+    for j in (3, 1, 2, 0):
+        put_partial(partial, j, mm(mixed_ref[j], out_ref[...]))
+
+
+def after_kernel(tokens, gain_ref, *refs):
+    after_ref, low_ref = refs[5:]
+    after = tokens[...].astype(F32) + joined(*refs[:5])
+    after_ref[...] = after
+    low_ref[...] = (after * inverse_root(after) * gain_ref[1:2, :]).astype(BF)
+
+
+def prepare_kernel(info, *refs):
+    parts, pieces = refs[:8], refs[8:16]
+    gate_up_ref, down_ref, cotangent = refs[16:19]
+    grads, semaphores = refs[19:23], refs[23]
+    loads = Loads(semaphores)
+    down_loads, gate_loads = [], []
+    cotangent_loads = load_paired(loads, pieces, 1, cotangent)
+    for t in range(2 * CHIPS):
+        s = part_shard(info, t)
+        at = pl.ds(pl.multiple_of(s * FF_ROWS, 32), FF_ROWS)
+        rows = slice(2 * ROWS, 2 * ROWS + FF_ROWS)
+        down_loads.append(loads(parts[t].at[rows, :], down_ref.at[at, :FF_PART]))
+        for i in range(3):
+            at = pl.ds(pl.multiple_of(s * FF_ROWS + i * 32, 32), 32)
+            rest = parts[t].at[2 * ROWS + FF_ROWS :, i * 256 : (i + 1) * 256]
+            down_loads.append(loads(rest, down_ref.at[at, FF_PART:]))
+    for t in range(2 * CHIPS):
+        at = pl.ds(pl.multiple_of(part_shard(info, t) * ROWS, ROWS), ROWS)
+        gate_loads.append(loads(parts[t].at[:ROWS, :], gate_up_ref.at[at, :FF_PART]))
+        gate_loads.append(loads(parts[t].at[ROWS : 2 * ROWS, :], gate_up_ref.at[at, FF_PART:]))
+    for copy in cotangent_loads + down_loads:
+        copy.wait()
+    for j in range(BLOCKS):
+        here = slice(j * SIZE, (j + 1) * SIZE)
+        grads[j][...] = mm(cotangent[here, :], down_ref[...], ((1,), (1,)))
+    for copy in gate_loads:
+        copy.wait()
+
+
+def feed_kernel(blocks, *refs):
+    count = len(blocks)
+    last = blocks == (3,)
+    extra = 2 if last else count
+    inputs, hidden_grads = refs[:extra], refs[extra : extra + count]
+    gate_up_ref = refs[extra + count]
+    if last:
+        first_a, second_b = refs[extra + count + 1 : extra + count + 3]
+    outs = refs[extra + count + (3 if last else 1) :]
+    for n, j in enumerate(blocks):
+        tokens = jnp.concatenate([inputs[0][...], inputs[1][...]], axis=0) if last else inputs[n][...]
+        hidden_ref, both_ref = outs[2 * n : 2 * n + 2]
+        gate_up = mm(tokens, gate_up_ref[...])
+        gate, up = gate_up[:, :FF_PART], gate_up[:, FF_PART:]
+        sigmoid = 1.0 / (1.0 + jnp.exp(-gate))
+        silu = gate * sigmoid
+        hidden_ref[...] = (silu * up).astype(BF)
+        grad = hidden_grads[n][...]
+        both_ref[:, :FF_PART] = (grad * up * sigmoid * (1.0 + gate * (1.0 - sigmoid))).astype(BF)
+        both_ref[:, FF_PART:] = (grad * silu).astype(BF)
+        part = mm(both_ref[...], gate_up_ref[...], ((1,), (1,)))
+        first, second = outs[2 * count + 2 * n : 2 * count + 2 * n + 2]
+        if last:
+            first[:HALF] = first_a[...]
+            first[HALF:] = part[:HALF].astype(BF)
+            second[:HALF] = second_b[...]
+            second[HALF:] = part[HALF:].astype(BF)
+        else:
+            first[...] = part[:HALF].astype(first.dtype)
+            second[...] = part[HALF:].astype(second.dtype)
+
+
+FEED_TYPES = {0: (F32, F32), 1: (BF, F32), 2: (F32, BF), 3: (BF, BF)}
+
+
+def feed(blocks, inputs, hidden_grads, gate_up, earlier=()):
+    outs = []
+    for _ in blocks:
+        outs += [shape((SIZE, FF_PART), BF), shape((SIZE, 2 * FF_PART), BF)]
+    for j in blocks:
+        outs += [shape((SIZE if j == 3 else HALF, MODEL_WIDTH), dtype) for dtype in FEED_TYPES[j]]
+
+    def body(*refs):
+        feed_kernel(blocks, *refs)
+
+    args = (*inputs, *hidden_grads, gate_up, *earlier)
+    result = on_core(body, "feed", outs, (), args)
+    count = len(blocks)
+    hidden, both = result[0 : 2 * count : 2], result[1 : 2 * count : 2]
+    return hidden, both, result[2 * count :]
+
+
+def split_rows(info, kept, away, t, at, values):
+    half = values.shape[0] // 2
+    first, second = values[:half], values[half:]
+    is_first = info[2] == 0
+    kept[t, at : at + half, :] = jnp.where(is_first, first, second)
+    away[t, at : at + half, :] = jnp.where(is_first, second, first).astype(BF)
+
+
+def feed_weights_kernel(info, cotangent, *refs):
+    hidden, both, mlp_in = refs[:4], refs[4:8], refs[8:13]
+    kept, away, down_grad, stored, semaphores = refs[13:]
+    loads = Loads(semaphores)
+    copies = [loads(mlp_in[j], stored.at[j * SIZE : (j + 1) * SIZE, :]) for j in range(3)]
+    copies += [
+        loads(mlp_in[3 + n], stored.at[3 * SIZE + n * HALF : 3 * SIZE + (n + 1) * HALF, :])
+        for n in range(2)
+    ]
+    both_all = jnp.concatenate([ref[...] for ref in both], axis=0)
+    hidden_all = jnp.concatenate([ref[...] for ref in hidden], axis=0)
+    down_grad[...] = mm(hidden_all, cotangent[...], ((0,), (0,)))
+    for copy in copies:
+        copy.wait()
+    for t in range(CHIPS):
+        chip = lax.rem(info[1] + 2 * CHIPS - (t + 1), CHIPS)
+        columns = stored[:, pl.ds(pl.multiple_of(chip * 2 * ROWS, 2 * ROWS), 2 * ROWS)]
+        product = mm(columns, both_all, ((0,), (0,)))
+        split_rows(info, kept, away, t, 0, product[:, :FF_PART])
+        split_rows(info, kept, away, t, ROWS, product[:, FF_PART:])
+        for core, target in ((info[2], kept), (1 - info[2], away)):
+            at = pl.multiple_of((2 * chip + core) * FF_ROWS, 32)
+            rows = down_grad[pl.ds(at, FF_ROWS), :].astype(target.dtype)
+            target[t, 2 * ROWS : 2 * ROWS + FF_ROWS, :] = rows[:, :FF_PART]
+            for i in range(3):
+                target[t, 2 * ROWS + FF_ROWS :, i * 256 : (i + 1) * 256] = rows[
+                    i * 32 : (i + 1) * 32, FF_PART:
+                ]
+
+
+def down_kernel(down_ref, *refs):
+    hidden, partial = refs[:4], refs[4:]
+    for j in (3, 1, 2, 0):
+        put_partial(partial, j, mm(hidden[j][...], down_ref[...]))
+
+
+def residual_kernel(cotangent, after_ref, gain_ref, *refs):
+    grad_ref, low_ref, gain_part = refs[-3:]
+    keep_a, keep_b, one, two, low, high = refs[:6]
+    top = keep_a[...] + one[:HALF].astype(F32) + low[...].astype(F32)
+    bottom = keep_b[...] + two[:HALF].astype(F32) + high[...].astype(F32)
+    mlp_in_grad = jnp.concatenate([top, bottom], axis=0)
+    after = after_ref[...]
+    inverse = inverse_root(after)
+    gain_part[...] = jnp.sum(mlp_in_grad * (after * inverse), axis=0, keepdims=True)
+    grad = cotangent[...].astype(F32) + norm_back(after, inverse, gain_ref[1:2, :], mlp_in_grad)
+    grad_ref[...] = grad
+    low_ref[...] = grad.astype(BF)
+
+
+def mixed_grad_kernel(info, mixed_ref, out_ref, *refs):
+    branch, (grad_ref, kept, away, scratch) = refs[:5], refs[5:]
+    own = info[0]
+    for j in range(BLOCKS):
+        grad_ref[j] = mm(block_of(branch, j), out_ref[...], ((1,), (1,))).astype(BF)
+    branch_all = jnp.concatenate([block_of(branch, j) for j in range(BLOCKS)], axis=0)
+    mixed_all = jnp.concatenate([mixed_ref[j] for j in range(BLOCKS)], axis=0)
+    scratch[...] = mm(mixed_all, branch_all, ((0,), (0,)))
+    for core, target in ((info[2], kept), (1 - info[2], away)):
+        for q in range(BLOCKS):
+            at = pl.multiple_of(core * SIZE + (own ^ q) * OUT_ROWS, OUT_ROWS)
+            target[q] = scratch[pl.ds(at, OUT_ROWS), :].astype(target.dtype)
+
+
+def head_back(grad, cosine, sine, raw, gain):
+    dy = grad * cosine - pltpu.roll(grad, TURN, 1) * sine
+    inverse = inverse_root(raw)
+    gain_part = jnp.sum(dy * (raw * inverse), axis=0, keepdims=True)
+    return norm_back(raw, inverse, gain, dy).astype(BF), gain_part
+
+
+def attend_back_kernel(g, info, lse_ref, mixed_ref, grad_ref, mlp_part, gain_ref, *refs):
+    far, (out_ref, kept, away) = refs[:8], refs[8:11]
+    dk_ref, dv_ref, q_ref, k_ref, v_ref, raw_ref, cos_ref, sin_ref, normed_ref, w_ref, semaphores = refs[11:]
+    loads = Loads(semaphores)
+    width = slice(g * GROUP_WIDTH, (g + 1) * GROUP_WIDTH)
+    first = [loads(far[n].at[g], near) for n, near in enumerate((q_ref, k_ref, v_ref))]
+    second = [loads(far[3].at[g], raw_ref), loads(far[4], cos_ref), loads(far[5], sin_ref)]
+    third = [loads(far[6], normed_ref), loads(far[7].at[:, width], w_ref)]
+    own = info[0]
+    query_part = jnp.zeros((1, HEAD_SIZE), F32)
+    key_part = jnp.zeros((1, HEAD_SIZE), F32)
+    dk_ref[...] = jnp.zeros_like(dk_ref)
+    dv_ref[...] = jnp.zeros_like(dv_ref)
+    for copy in first:
+        copy.wait()
+    for last in range(BLOCKS):
+        i = own ^ last
+        rows = pl.ds(pl.multiple_of(i * SIZE, SIZE), SIZE)
+        heads = [slice((g * GROUP + h) * HEAD_SIZE, (g * GROUP + h + 1) * HEAD_SIZE) for h in range(GROUP)]
+        query = q_ref[i]
+        grad = jnp.concatenate([grad_ref[i, :, h] for h in heads], axis=0)
+        mixed = jnp.concatenate([mixed_ref[i, :, h] for h in heads], axis=0)
+        delta = jnp.sum((grad.astype(F32) * mixed.astype(F32)).T, axis=0, keepdims=True)
+        log_sum = lse_ref[g, i]
+        dquery = jnp.zeros((HEAD_SIZE, GROUP * SIZE), F32)
+        for block in range(last + 1):
+            j = own ^ block
+            scores = mm(k_ref[j], query, ((1,), (1,)))
+            dprobs = mm(v_ref[j], grad, ((1,), (1,)))
+            probs = jnp.exp2(scores * (SCALE * LOG2E) - log_sum)
+            if block == last:
+                probs = jnp.where(piece_mask(info[3 + i], SIZE, GROUP), probs, 0.0)
+            dscores = (probs * (dprobs - delta)).astype(BF)
+            dv_ref[j] += mm(probs.astype(BF), grad)
+            dk_ref[j] += mm(dscores, query)
+            dquery = dquery + mm(k_ref[j], dscores, ((0,), (0,)))
+        if last == 0:
+            for copy in second:
+                copy.wait()
+        for h in range(GROUP):
+            at = slice(h * HEAD_SIZE, (h + 1) * HEAD_SIZE)
+            back, part = head_back(
+                dquery[:, h * SIZE : (h + 1) * SIZE].T * SCALE,
+                cos_ref[rows, :],
+                sin_ref[rows, :],
+                raw_ref[rows, at],
+                gain_ref[2:3, :HEAD_SIZE],
+            )
+            out_ref[rows, at] = back
+            query_part = query_part + part
+    for j in range(BLOCKS):
+        rows = slice(j * SIZE, (j + 1) * SIZE)
+        at = slice(GROUP_Q, GROUP_Q + HEAD_SIZE)
+        back, part = head_back(
+            dk_ref[j] * SCALE,
+            cos_ref[rows, :],
+            sin_ref[rows, :],
+            raw_ref[rows, at],
+            gain_ref[2:3, HEAD_SIZE : 2 * HEAD_SIZE],
+        )
+        out_ref[rows, at] = back
+        key_part = key_part + part
+        out_ref[rows, GROUP_Q + HEAD_SIZE :] = dv_ref[j].astype(BF)
+    for copy in third:
+        copy.wait()
+    row = lax.broadcasted_iota(jnp.int32, (16, GROUP_WIDTH), 0)
+    for t in range(CHIPS):
+        chip = lax.rem(info[1] + 2 * CHIPS - (t + 1), CHIPS)
+        at = pl.ds(pl.multiple_of(chip * 2 * ROWS, 2 * ROWS), 2 * ROWS)
+        product = mm(normed_ref[:, at], out_ref[...], ((0,), (0,)))
+        split_rows(info, kept, away, t, 0, product)
+        inner = jnp.sum(product * w_ref[at, :].astype(F32), axis=1, keepdims=True)
+        inner = jnp.broadcast_to(inner, (2 * ROWS, ROWS)).T[0:1] / gain_ref[0:1, at]
+        mlp = mlp_part[0:1, at] if g == 0 else jnp.zeros_like(inner)
+        for is_first, half in ((True, slice(0, ROWS)), (False, slice(ROWS, 2 * ROWS))):
+            values = jnp.concatenate([inner[:, half], mlp[:, half], query_part, key_part], axis=1)
+            values = jnp.where(row == 0, values, 0.0)
+
+            @pl.when((info[2] == 0) == is_first)
+            def _():
+                kept[t, ROWS:, :] = values
+
+            @pl.when((info[2] == 0) != is_first)
+            def _():
+                away[t, ROWS:, :] = values.astype(BF)
+
+
+def normed_grad_kernel(w_ref, *refs):
+    grads, partial = refs[:GROUPS], refs[GROUPS:]
+    for j in (3, 1, 2, 0):
+        here = slice(j * SIZE, (j + 1) * SIZE)
+        grad = jnp.concatenate([ref[here, :] for ref in grads], axis=1)
+        put_partial(partial, j, mm(grad, w_ref[...], ((1,), (1,))))
+
+
+def final_kernel(tokens, gain_ref, residual, *refs):
+    grad_ref = refs[5]
+    wide = tokens[...].astype(F32)
+    dy = joined(*refs[:5])
+    back = norm_back(wide, inverse_root(wide), gain_ref[0:1, :], dy)
+    grad_ref[...] = (residual[...] + back).astype(BF)
+
+
+def output_kernel(after_ref, *refs):
+    refs[5][...] = (after_ref[...] + joined(*refs[:5])).astype(BF)
+
+
+def unpack_feed_kernel(info, *refs):
+    pieces, (gate_ref, up_ref, down_ref, scratch) = refs[:5], refs[5:]
+    for j in range(BLOCKS):
+        scratch[info[0] ^ j] = block_of(pieces, j).astype(F32)
+    for first, target in ((0, gate_ref), (ROWS, up_ref)):
+        for s in range(0, 2 * CHIPS):
+            columns = slice(s * FF_ROWS, (s + 1) * FF_ROWS)
+            cut = [scratch[a, first : first + ROWS, columns] for a in range(BLOCKS)]
+            target[:, s * BLOCKS * FF_ROWS : (s + 1) * BLOCKS * FF_ROWS] = jnp.concatenate(cut, axis=1)
+    for a in range(BLOCKS):
+        at = slice(a * FF_ROWS, (a + 1) * FF_ROWS)
+        down_ref[at, :FF_PART] = scratch[a, 2 * ROWS : 2 * ROWS + FF_ROWS, :]
+        for i in range(3):
+            at = slice(a * FF_ROWS + i * 32, a * FF_ROWS + (i + 1) * 32)
+            down_ref[at, FF_PART:] = scratch[a, 2 * ROWS + FF_ROWS :, i * 256 : (i + 1) * 256]
+
+
+def unpack_attend_kernel(info, *refs):
+    pieces, (query_ref, key_ref, value_ref, out_ref, gain_ref) = (refs[:4], refs[4:8]), refs[8:]
+    gains = jnp.zeros((8, GROUP_WIDTH), F32)
+    for g in range(GROUPS):
+        for j in range(BLOCKS):
+            piece = pieces[g][j]
+            head = (info[0] ^ j) * GROUPS + g
+            values = piece[:ROWS, :].astype(F32)
+            wide = pl.ds(pl.multiple_of(head * GROUP_Q, GROUP_Q), GROUP_Q)
+            thin = pl.ds(pl.multiple_of(head * HEAD_SIZE, HEAD_SIZE), HEAD_SIZE)
+            query_ref[:, wide] = values[:, :GROUP_Q]
+            key_ref[:, thin] = values[:, GROUP_Q : GROUP_Q + HEAD_SIZE]
+            value_ref[:, thin] = values[:, GROUP_Q + HEAD_SIZE :]
+            gains = gains + piece[ROWS : ROWS + 16, :].astype(F32)[:8]
+            if g == 0:
+                rows = pl.ds(pl.multiple_of((info[0] ^ j) * OUT_ROWS, OUT_ROWS), OUT_ROWS)
+                top = piece[ROWS + 16 : ROWS + 16 + OUT_ROWS, :].astype(F32)
+                out_ref[rows, :GROUP_WIDTH] = top
+                out_ref[rows, GROUP_WIDTH:] = piece[ROWS + 16 + OUT_ROWS :, :].astype(F32)
+    gain_ref[...] = gains
+
+
+def ring_parts(value, then):
+    own, other = [value], [other_core(value)]
+    for t in range(1, CHIPS):
+        ready = then.get(t, ())
+        if t > 1:
+            ready = (ready, other[t - 2])
+        own.append(ring_up(tie(own[-1], ready)))
+        other.append(other_core(own[-1]))
+    return own, other
+
+
+def ring_sum(kept, away, then, beside=None):
+    crossed = other_core(away)
+
+    def term(t, moved):
+        value = kept[t] + crossed[t].astype(F32)
+        count = value.shape[0]
+        if moved is not None:
+            value = value + moved[:count].astype(F32)
+        value = value.astype(BF)
+        if beside is not None:
+            extra = beside(t + 1)
+            if moved is not None:
+                extra = (moved[count:].astype(F32) + extra.astype(F32)).astype(BF)
+            value = jnp.concatenate([value, extra], axis=0)
+        return value
+
+    running = [term(0, None)]
+    for t in range(1, CHIPS):
+        running.append(term(t, ring_up(tie(running[-1], then.get(t, ())))))
+    return running
+
+
+def per_device(
+    layer_in,
+    out_grad,
+    attn_norm,
+    query_weight,
+    key_projection,
+    value_projection,
+    query_norm,
+    key_norm,
+    out_weight,
+    mlp_norm,
+    gate_weight,
+    up_weight,
+    down_weight,
+    picture_starts,
+    picture_count,
+):
+    r, index = lax.axis_index("rep"), lax.axis_index("shard")
+    chip, core = index // 2, index % 2
+    length = BLOCKS * SIZE
+    tokens, cotangent_own = layer_in[0], out_grad[0]
+
+    block_ids = r ^ jnp.arange(BLOCKS, dtype=jnp.int32)
+    starts = picture_starts[0]
+    held = (starts[None, :] == block_ids[:, None] * PIECE) & (
+        jnp.arange(starts.shape[0], dtype=jnp.int32)[None, :] < picture_count[0]
+    )
+    place = jnp.stack([r, chip, core]).astype(jnp.int32)
+    info = jnp.concatenate([place, jnp.any(held, axis=1).astype(jnp.int32)])
+
+    (attn_rows,) = on_core(
+        pack_kernel,
+        "pack",
+        [shape((ROWS + 16 + OUT_ROWS, ATTN_WIDTH), BF)],
+        (place,),
+        (query_weight, key_projection, value_projection, out_weight)
+        + tuple(gain.reshape(1, -1) for gain in (attn_norm, mlp_norm, query_norm, key_norm)),
+    )
+    low_half, high_half = tie(
+        tuple(jnp.concatenate([tokens[at], cotangent_own[at]]) for at in (slice(0, HALF), slice(HALF, SIZE))),
+        attn_rows,
+    )
+    one = flip(low_half, 1), flip(high_half, 1)
+    two = flip(low_half, 2), flip(high_half, 2)
+    pieces = (low_half, high_half, *one, *two, flip(one[0], 2), flip(two[1], 1))
+    (feed_rows,) = on_core(
+        pack_feed_kernel,
+        "pack_feed",
+        [shape((PACKED, FF_PART), BF)],
+        (place,),
+        tie((gate_weight, up_weight, down_weight), attn_rows),
+    )
+
+    positions = (block_ids[:, None] * SIZE + jnp.arange(SIZE, dtype=jnp.int32)[None, :]).reshape(-1)
+    inv_freq = ROPE_BASE ** (-2.0 * jnp.arange(TURN, dtype=F32) / HEAD_SIZE)
+    angles = positions.astype(F32)[:, None] * inv_freq[None, :]
+    cosine, sine = jnp.cos(angles), jnp.sin(angles)
+    cos_rows = jnp.concatenate([cosine, cosine], axis=1)
+    sin_rows = jnp.concatenate([-sine, sine], axis=1)
+
+    attn_own, attn_other = ring_parts(
+        attn_rows, {2: (feed_rows, info), 3: (one, two, cos_rows, sin_rows)}
+    )
+
+    picked = on_core(
+        pick_kernel,
+        "pick",
+        [shape((OUT_ROWS, MODEL_WIDTH), BF)] * BLOCKS,
+        (place,),
+        (),
+        attn_own,
+        [pltpu.SemaphoreType.DMA((BLOCKS,))],
+    )
+    out_own = [picked[0]] + [flip(picked[j], j) for j in (1, 2, 3)]
+
+    normed, raw, query, key, value, attn_matrix, gain_rows = on_core(
+        project_kernel,
+        "project",
+        [
+            shape((length, MODEL_WIDTH), BF),
+            shape((GROUPS, length, GROUP_Q + HEAD_SIZE), F32),
+            shape((GROUPS, BLOCKS, GROUP * SIZE, HEAD_SIZE), BF),
+            shape((GROUPS, BLOCKS, SIZE, HEAD_SIZE), BF),
+            shape((GROUPS, BLOCKS, SIZE, HEAD_SIZE), BF),
+            shape((MODEL_WIDTH, ATTN_WIDTH), BF),
+            shape((8, MODEL_WIDTH), F32),
+        ],
+        (info,),
+        (cos_rows, sin_rows),
+        (*attn_own, *attn_other, *pieces),
+        [
+            pltpu.VMEM((length, MODEL_WIDTH), BF),
+            pltpu.VMEM((2 * CHIPS, 16, ATTN_WIDTH), BF),
+            pltpu.SemaphoreType.DMA((6 * CHIPS,)),
+        ],
+    )
+    mixed, lse = on_core(
+        attend_kernel,
+        "attend",
+        [
+            shape((BLOCKS, SIZE, Q_WIDTH), BF),
+            shape((GROUPS, BLOCKS, 1, GROUP * SIZE), F32),
+        ],
+        (info,),
+        (query, key, value),
+    )
+    out_own = tie(out_own, query)
+    out_other = other_core(jnp.concatenate(out_own, axis=0))
+    out_other = [out_other[j * OUT_ROWS : (j + 1) * OUT_ROWS] for j in range(BLOCKS)]
+    out_matrix, *partial = on_core(
+        out_kernel,
+        "out",
+        [shape((Q_WIDTH, MODEL_WIDTH), BF)] + partial_shapes(),
+        (info,),
+        (mixed, *out_own, *out_other),
+    )
+    feed_own, feed_other = ring_parts(tie(feed_rows, attn_own[-1]), {2: mixed, 3: partial[0]})
+    partial = move_partial(*partial)
+    after_attn, mlp_own = on_core(
+        after_kernel,
+        "after",
+        [shape((SIZE, MODEL_WIDTH), F32), shape((SIZE, MODEL_WIDTH), BF)],
+        (),
+        (tokens, gain_rows, *partial),
+    )
+    mlp_in = spread(mlp_own)
+    gate_up, down, cotangent, *hidden_grads = on_core(
+        prepare_kernel,
+        "prepare",
+        [
+            shape((MODEL_WIDTH, 2 * FF_PART), BF),
+            shape((FF_PART, MODEL_WIDTH), BF),
+            shape((length, MODEL_WIDTH), BF),
+        ]
+        + [shape((SIZE, FF_PART), F32)] * BLOCKS,
+        (info,),
+        (),
+        (*tie((*feed_own, *feed_other), mlp_own), *pieces),
+        [pltpu.SemaphoreType.DMA((14 * CHIPS,))],
+    )
+    hidden_0, both_0, keep = feed((0,), mlp_in[:1], hidden_grads[:1], gate_up)
+    hidden_12, both_12, (one_a, keep_high, keep_low, two_a) = feed(
+        (1, 2), tie(mlp_in[1:3], both_0), hidden_grads[1:3], gate_up
+    )
+    hidden_3, both_3, (one, two) = feed(
+        (3,), tie(mlp_in[3:], both_12), hidden_grads[3:], gate_up, (one_a, two_a)
+    )
+    hidden = [*hidden_0, *hidden_12, *hidden_3]
+    both = [*both_0, *both_12, *both_3]
+
+    feed_kept, feed_away = on_core(
+        feed_weights_kernel,
+        "feed_weights",
+        [
+            shape((CHIPS, PACKED, FF_PART), F32),
+            shape((CHIPS, PACKED, FF_PART), BF),
+        ],
+        (info,),
+        (cotangent, *hidden, *both),
+        mlp_in,
+        [
+            pltpu.VMEM((FF_PART, MODEL_WIDTH), F32),
+            pltpu.VMEM((length, MODEL_WIDTH), BF),
+            pltpu.SemaphoreType.DMA((5,)),
+        ],
+        24,
+    )
+    feed_ring = ring_sum(feed_kept, feed_away, {})
+    one, two = tie((flip(one, 1), flip(two, 2)), feed_kept)
+    low = flip((keep_low + one[HALF:].astype(F32)).astype(BF), 2)
+    high = flip((keep_high + two[HALF:].astype(F32)).astype(BF), 1)
+    residual_grad, branch_own, mlp_gain_part = on_core(
+        residual_kernel,
+        "residual",
+        [
+            shape((SIZE, MODEL_WIDTH), F32),
+            shape((SIZE, MODEL_WIDTH), BF),
+            shape((1, MODEL_WIDTH), F32),
+        ],
+        (),
+        (cotangent_own, after_attn, gain_rows, *tie((*keep, one, two, low, high), feed_ring[0])),
+    )
+    branch = spread(branch_own)
+    layer_partial = on_core(
+        down_kernel, "down", partial_shapes(), (), tie((down, *hidden), branch_own)
+    )
+
+    mixed_grad, out_kept, out_away = on_core(
+        mixed_grad_kernel,
+        "mixed_grad",
+        [
+            shape((BLOCKS, SIZE, Q_WIDTH), BF),
+            shape((BLOCKS, OUT_ROWS, MODEL_WIDTH), F32),
+            shape((BLOCKS, OUT_ROWS, MODEL_WIDTH), BF),
+        ],
+        (info,),
+        (mixed, out_matrix, *tie(branch, layer_partial, feed_ring[1])),
+        (),
+        [pltpu.VMEM((Q_WIDTH, MODEL_WIDTH), F32)],
+    )
+    out_pair = (out_kept + other_core(out_away).astype(F32)).astype(BF)
+    out_pair = [out_pair[j] for j in range(BLOCKS)]
+    out_moved = [out_pair[0]] + [flip(out_pair[j], j) for j in (1, 2, 3)]
+
+    def back(g, grad):
+        def body(*refs):
+            attend_back_kernel(g, *refs)
+
+        return on_core(
+            body,
+            "attend_back",
+            [
+                shape((length, GROUP_WIDTH), BF),
+                shape((CHIPS, ROWS + 16, GROUP_WIDTH), F32),
+                shape((CHIPS, ROWS + 16, GROUP_WIDTH), BF),
+            ],
+            (info,),
+            (lse, mixed, grad, mlp_gain_part, gain_rows),
+            (query, key, value, raw, cos_rows, sin_rows, normed, attn_matrix),
+            [
+                pltpu.VMEM((BLOCKS, SIZE, HEAD_SIZE), F32),
+                pltpu.VMEM((BLOCKS, SIZE, HEAD_SIZE), F32),
+                pltpu.VMEM((BLOCKS, GROUP * SIZE, HEAD_SIZE), BF),
+                pltpu.VMEM((BLOCKS, SIZE, HEAD_SIZE), BF),
+                pltpu.VMEM((BLOCKS, SIZE, HEAD_SIZE), BF),
+                pltpu.VMEM((length, GROUP_Q + HEAD_SIZE), F32),
+                pltpu.VMEM((length, HEAD_SIZE), F32),
+                pltpu.VMEM((length, HEAD_SIZE), F32),
+                pltpu.VMEM((length, MODEL_WIDTH), BF),
+                pltpu.VMEM((MODEL_WIDTH, GROUP_WIDTH), BF),
+                pltpu.SemaphoreType.DMA((8,)),
+            ],
+        )
+
+    grad_0, kept_0, away_0 = back(0, tie(mixed_grad, out_pair))
+    out_blocks = jnp.stack(tie(out_moved, grad_0))
+
+    def out_step(t):
+        block = lax.dynamic_index_in_dim(
+            out_blocks, r ^ ((chip + 2 * CHIPS - t) % CHIPS), 0, keepdims=False
+        )
+        return jnp.concatenate([block[:, :GROUP_WIDTH], block[:, GROUP_WIDTH:]], axis=0)
+
+    layer_pieces = move_partial(*tie(layer_partial, grad_0))
+    attn_first = ring_sum(kept_0, away_0, {}, out_step)
+    grad_1, kept_1, away_1 = back(1, tie(mixed_grad, attn_first[0], feed_ring[2]))
+    attn_second = ring_sum(kept_1, away_1, {})
+    partial = on_core(
+        normed_grad_kernel,
+        "normed_grad",
+        partial_shapes(),
+        (),
+        (attn_matrix, *tie((grad_0, grad_1), attn_second[0])),
+    )
+    (layer_out,) = on_core(
+        output_kernel,
+        "output",
+        [shape((SIZE, MODEL_WIDTH), BF)],
+        (),
+        (after_attn, *layer_pieces),
+    )
+    (in_grad,) = on_core(
+        final_kernel,
+        "final",
+        [shape((SIZE, MODEL_WIDTH), BF)],
+        (),
+        (tokens, gain_rows, residual_grad, *move_partial(*partial)),
+    )
+
+    gate_w_grad, up_w_grad, down_w_grad = on_core(
+        unpack_feed_kernel,
+        "unpack_feed",
+        [
+            shape((ROWS, 2 * CHIPS * BLOCKS * FF_ROWS), F32),
+            shape((ROWS, 2 * CHIPS * BLOCKS * FF_ROWS), F32),
+            shape((BLOCKS * FF_ROWS, MODEL_WIDTH), F32),
+        ],
+        (place,),
+        spread(feed_ring[-1]),
+        (),
+        [pltpu.VMEM((BLOCKS, PACKED, FF_PART), F32)],
+    )
+    query_w_grad, key_w_grad, value_w_grad, out_w_grad, gain_full = on_core(
+        unpack_attend_kernel,
+        "unpack_attend",
+        [
+            shape((ROWS, QUERY_HEADS * HEAD_SIZE), F32),
+            shape((ROWS, KEY_VALUE_HEADS * HEAD_SIZE), F32),
+            shape((ROWS, KEY_VALUE_HEADS * HEAD_SIZE), F32),
+            shape((SIZE, MODEL_WIDTH), F32),
+            shape((8, GROUP_WIDTH), F32),
+        ],
+        (place,),
+        (*spread_direct(attn_first[-1]), *spread_direct(attn_second[-1])),
+    )
+    gains = gain_full[0]
+    head_rows = query_norm.shape[0]
+
+    def slice_of(start, width):
+        return lax.dynamic_slice_in_dim(gains, start + index * width, width, 0)
+
+    return (
+        layer_out[None],
+        in_grad[None],
+        gains[:ROWS],
+        query_w_grad,
+        key_w_grad,
+        value_w_grad,
+        slice_of(2 * ROWS, head_rows),
+        slice_of(2 * ROWS + HEAD_SIZE, head_rows),
+        out_w_grad,
+        gains[ROWS : 2 * ROWS],
+        gate_w_grad,
+        up_w_grad,
+        down_w_grad,
+    )
+
+
 def solution(mesh):
     tokens, matrix, vector = P("shard", "rep", None), P("shard", None), P("shard")
     return jax.shard_map(
-        per_device,
+        per_device if dict(mesh.shape) == {"rep": 4, "shard": 8} else per_device_any,
         mesh=mesh,
         in_specs=(tokens, tokens, vector, matrix, matrix, matrix, vector, vector, matrix, vector)
         + (matrix, matrix, matrix, matrix, vector),

time: 514 us -> 304 us (0.59)
  local copies, waits for them, and re-layouts: 122 us -> 20.7 us
  other arithmetic: 67.9 us -> 10.1 us
  Pallas kernels: 15.8 us -> 69.1 us
  matrix products: 41.8 us -> 0 us
  starting transfers between devices: 101 us -> 59.7 us
  waiting for transfers between devices: 153 us -> 138 us
    pallas_call x2 -> x22, Pallas kernels: 15.8 us -> 69.1 us  [on_core(): pl.pallas_call(body, name=name, in_specs=[pl.BlockSpec(memory_space=pltpu...]
    dot_general x12 -> x0, matrix products: 41.8 us -> none  [mm(): return lax.dot_general(a, b, (dims, ((), ())), preferred_element_type=F32)]
    ppermute x11 -> x0, waiting for transfers between devices: 31.6 us -> none  [joint_move(): return lax.ppermute(value, ('rep', 'shard'), joint)]
    ppermute x18 -> x15, waiting for transfers between devices: 41.7 us -> 68.5 us  [ring_up(): lax.ppermute(value, 'shard', [(i, (i + 2) % count) for i in range(count)])]
    dynamic_update_slice x24 -> x0, local copies, waits for them, and re-layouts: 25.5 us -> none  [the longest x12 15.7 us: gather_rows(): full = lax.dynamic_update_index_in_dim(full, current, place + core, 0)]
    slice x34 -> x15, local copies, waits for them, and re-layouts: 22.9 us -> 0.78 us  [the longest x1 0.52 us: per_device(): gains[ROWS:2 * ROWS]]
    mul x21 -> x0, local copies, waits for them, and re-layouts: 22 us -> none  [the longest x6 7.21 us: norm_back(): return inverse * weighted - values * (inverse * inverse * inverse) * inner]
    ppermute x18 -> x15, starting transfers between devices: 24.4 us -> 4.31 us  [ring_up(): lax.ppermute(value, 'shard', [(i, (i + 2) % count) for i in range(count)])]
  transfers between devices with their start and end apart: 90 -> 74, of which waited for: 35 -> 30; matrix products, arithmetic and copies ran while one was open for 36% -> 4% of each run, Pallas kernels for 3% -> 18%
where the time goes in v3:
time: 304 us; the launch traced here: 300 us
  waiting for transfers between devices  138 us (45%)
  Pallas kernels  69.1 us (23%)
  starting transfers between devices  59.7 us (20%)
  local copies, waits for them, and re-layouts  20.7 us (7%)
  other arithmetic  10.1 us (3%)
    pallas_call x22, Pallas kernels, on_core(): pl.pallas_call(body, name=name, in_specs=[pl.BlockSpec(memory_space=pltpu...  69.1 us
    ppermute x15, waiting for transfers between devices, ring_up(): lax.ppermute(value, 'shard', [(i, (i + 2) % count) for i in range(count)])  68.5 us
    ppermute x46, waiting for transfers between devices, flip(): return lax.ppermute(value, 'rep', [(i, i ^ bit) for i in range(count)])  65.1 us
    ppermute x46, starting transfers between devices, flip(): return lax.ppermute(value, 'rep', [(i, i ^ bit) for i in range(count)])  54.3 us
    unnamed x101, local copies, waits for them, and re-layouts  19.2 us
  transfers between devices with their start and end apart: 74, of which 30 were waited for; matrix products, arithmetic and copies ran while one was open for 4% of the time, Pallas kernels for 18%

profile of v3, /device:TPU:0, one launch (start us, length us, event | category | flops | bytes accessed | tf_op | source)
XLA Modules:
  0.0 299.7 jit_solution(516160742546044725)
XLA Ops:
  8.8 2.8 collective-permute-start.3
  11.6 1.5 collective-permute-start.5
  13.1 1.6 collective-permute-start
  16.2 10.2 %collective-permute-done.refs_1_ = bf16[208,1024]{1,0:T(8,128)(2,1)S(1)} collective-permute-done((bf16[208,1024]{1,0:T(8,128)(2,1)S(1)}, bf16[208,1024]{1,0:T(8,128)(2,1)S(1)}, u32[]{:S(2)}, u32[]{:S(2)}) %collective-permute-start) | collective-permute-done | bytes 426016 | tf_op jit(solution)/shard_map/ppermute | solution.py:66
  27.9 1.9 fusion.10
  30.2 5.0 %collective-permute-done.4.refs_11_ = bf16[256,1024]{1,0:T(8,128)(2,1)S(1)} collective-permute-done((bf16[256,1024]{1,0:T(8,128)(2,1)S(1)}, bf16[256,1024]{1,0:T(8,128)(2,1)S(1)}, u32[]{:S(2)}, u32[]{:S(2)}) %collective-permute-start.4) | collective-permute-done | bytes 524320 | tf_op jit(solution)/shard_map/ppermute | solution.py:29
  35.2 3.9 %collective-permute-done.6.refs_13_ = bf16[256,1024]{1,0:T(8,128)(2,1)S(1)} collective-permute-done((bf16[256,1024]{1,0:T(8,128)(2,1)S(1)}, bf16[256,1024]{1,0:T(8,128)(2,1)S(1)}, u32[]{:S(2)}, u32[]{:S(2)}) %collective-permute-start.6) | collective-permute-done | bytes 524320 | tf_op jit(solution)/shard_map/ppermute | solution.py:29
  39.8 1.6 collective-permute-start.11
  41.9 9.1 %collective-permute-done.8.refs_3_ = bf16[208,1024]{1,0:T(8,128)(2,1)S(1)} collective-permute-done((bf16[208,1024]{1,0:T(8,128)(2,1)S(1)}, bf16[208,1024]{1,0:T(8,128)(2,1)S(1)}, u32[]{:S(2)}, u32[]{:S(2)}) %collective-permute-start.8) | collective-permute-done | bytes 426016 | tf_op jit(solution)/shard_map/ppermute | solution.py:66
  54.5 1.4 collective-permute-start.15
  56.5 5.7 %project.1 = (bf16[1024,1024]{1,0:T(8,128)(2,1)S(1)}, f32[2,1024,384]{2,1,0:T(8,128)S(1)}, bf16[2,4,512,128]{3,2,1,0:T(8,128)(2,1)S(1)}, bf16[2,4,256,128]{3,2,1...) custom-call(s32[7]{0:T(128)S(1)} %pad_add_fusion.info.refs_0_, ...), custom_call_target="tpu_custom_call" | custom-call | tf_op jit(solution)/shard_map/project/pallas_call | solution.py:544
  64.0 5.0 %attend.1 = (bf16[4,256,512]{2,1,0:T(8,128)(2,1)S(1)}, f32[2,4,1,512]{3,2,1,0:T(1,128)S(1)}) custom-call(s32[7]{0:T(128)S(1)} %pad_add_fusion.info.refs_0_, bf16[2,4,512,128]{3,2,1,0:T(8,128)(2,1)S(1)} %get-tuple-element.154.q_ref.refs_6_, bf16[2,4,256,128]{3,2,1,0:T(8,128)(2,1)S(1)} %get-tuple-element.155.k_ref.refs_7_, ...), custom_call_target="tpu_custom_call" | custom-call | tf_op jit(solution)/shard_map/attend/pallas_call | solution.py:544
  71.7 2.2 collective-permute-done.21.refs_1_
  74.0 1.9 out.1
  78.0 12.6 %collective-permute-done.23.refs_2_ = bf16[384,768]{1,0:T(8,128)(2,1)S(1)} collective-permute-done((bf16[384,768]{1,0:T(8,128)(2,1)S(1)}, bf16[384,768]{1,0:T(8,128)(2,1)S(1)}, u32[]{:S(2)}, u32[]{:S(2)}) %collective-permute-start.23) | collective-permute-done | bytes 589856 | tf_op jit(solution)/shard_map/ppermute | solution.py:66
  90.8 1.7 collective-permute-start.19
  93.1 5.2 %collective-permute-done.19.refs_3_ = bf16[128,1024]{1,0:T(8,128)(2,1)S(1)} collective-permute-done((bf16[128,1024]{1,0:T(8,128)(2,1)S(1)}, bf16[128,1024]{1,0:T(8,128)(2,1)S(1)}, u32[]{:S(2)}, u32[]{:S(2)}) %collective-permute-start.19) | collective-permute-done | bytes 262176 | tf_op jit(solution)/shard_map/ppermute | solution.py:29
  98.3 1.5 collective-permute-done.20.refs_4_
  101.8 4.7 %collective-permute-done.25.refs_3_ = bf16[384,768]{1,0:T(8,128)(2,1)S(1)} collective-permute-done((bf16[384,768]{1,0:T(8,128)(2,1)S(1)}, bf16[384,768]{1,0:T(8,128)(2,1)S(1)}, u32[]{:S(2)}, u32[]{:S(2)}) %collective-permute-start.25) | collective-permute-done | bytes 589856 | tf_op jit(solution)/shard_map/ppermute | solution.py:66
  106.6 5.5 %collective-permute-done.28.refs_0_.refs_9_ = bf16[256,1024]{1,0:T(8,128)(2,1)S(1)} collective-permute-done((bf16[256,1024]{1,0:T(8,128)(2,1)S(1)}, bf16[256,1024]{1,0:T(8,128)(2,1)S(1)}, u32[]{:S(2)}, u32[]{:S(2)}) %collective-permute-start.28) | collective-permute-done | bytes 524320 | tf_op jit(solution)/shard_map/ppermute | solution.py:29
  112.6 2.8 collective-permute-start.31
  115.4 3.9 %prepare.1 = (bf16[1024,1536]{1,0:T(8,128)(2,1)S(1)}, bf16[768,1024]{1,0:T(8,128)(2,1)S(1)}, bf16[1024,1024]{1,0:T(8,128)(2,1)S(1)}, f32[256,768]{1,0:T(8,128)S(...) custom-call(s32[7]{0:T(128)S(1)} %pad_add_fusion.info.refs_0_, ...), custom_call_target="tpu_custom_call" | custom-call | tf_op jit(solution)/shard_map/prepare/pallas_call | solution.py:544
  119.3 2.0 feed.3
  121.3 3.8 %feed.4 = (bf16[256,768]{1,0:T(8,128)(2,1)S(1)}, bf16[256,1536]{1,0:T(8,128)(2,1)S(1)}, bf16[256,768]{1,0:T(8,128)(2,1)S(1)}, bf16[256,1536]{1,0:T(8,128)(2,1)S(...) custom-call(bf16[256,1024]{1,0:T(8,128)(2,1)S(1)} %collective-permut, ...), custom_call_target="tpu_custom_call" | custom-call | tf_op jit(solution)/shard_map/feed/pallas_call | solution.py:544
  125.1 2.0 feed.5
  127.1 6.6 %feed_weights.1 = (f32[4,384,768]{2,1,0:T(8,128)S(1)}, bf16[4,384,768]{2,1,0:T(8,128)(2,1)S(1)}) custom-call(s32[7]{0:T(128)S(1)} %pad_add_fusion.info.refs_0_, bf16[1024,1024]{1,0:T(8,128)(2,1)S(1)} %get-tuple-element.207.cotangent, bf16[256,768]{1,0:T(8,128)(2,1)S(1)} %get-tuple-element.223.refs_0_, bf16[256,768]{1,0:T(8,128)(2,1)S(1)} %get-tuple-element.224.refs_1_, ...), custom_call_target="tpu_custom_call" | custom-call | tf_op jit(solution)/shard_map/feed_weights/pallas_call | solution.py:544
  135.0 13.1 %collective-permute-done.32.refs_2_ = bf16[256,1024]{1,0:T(8,128)(2,1)S(1)} collective-permute-done((bf16[256,1024]{1,0:T(8,128)(2,1)S(1)}, bf16[256,1024]{1,0:T(8,128)(2,1)S(1)}, u32[]{:S(2)}, u32[]{:S(2)}) %collective-permute-start.32) | collective-permute-done | bytes 524320 | tf_op jit(solution)/shard_map/ppermute | solution.py:29
  151.4 4.7 %collective-permute-done.34.refs_4_ = bf16[128,1024]{1,0:T(8,128)(2,1)S(1)} collective-permute-done((bf16[128,1024]{1,0:T(8,128)(2,1)S(1)}, bf16[128,1024]{1,0:T(8,128)(2,1)S(1)}, u32[]{:S(2)}, u32[]{:S(2)}) %collective-permute-start.34) | collective-permute-done | bytes 262176 | tf_op jit(solution)/shard_map/ppermute | solution.py:29
  158.3 1.5 collective-permute-start.37
  159.8 1.4 collective-permute-start.38
  161.2 1.8 down.2
  164.7 5.7 %collective-permute-done.37.refs_1_ = bf16[256,1024]{1,0:T(8,128)(2,1)S(1)} collective-permute-done((bf16[256,1024]{1,0:T(8,128)(2,1)S(1)}, bf16[256,1024]{1,0:T(8,128)(2,1)S(1)}, u32[]{:S(2)}, u32[]{:S(2)}) %collective-permute-start.37) | collective-permute-done | bytes 524320 | tf_op jit(solution)/shard_map/ppermute | solution.py:29
  170.5 1.6 collective-permute-start.39
  174.4 3.0 collective-permute-done.39.refs_3_
  177.4 1.9 collective-permute-done.40.refs_4_
  179.3 3.8 %mixed_grad.1 = (bf16[4,256,512]{2,1,0:T(8,128)(2,1)S(1)}, f32[4,64,1024]{2,1,0:T(8,128)S(1)}, bf16[4,64,1024]{2,1,0:T(8,128)(2,1)}) custom-call(s32[7]{0:T(128)S(1)} %pad_add_fusion.info.refs_0_, bf16[4,256,512]{2,1,0:T(8,128)(2,1)S(1)} %get-tuple-element.157.mixed_ref.refs_2_, bf16[512,1024]{1,0:T(8,128)(2,1)S(1)} %get-tuple-element.233.out_ref, ...), custom_call_target="tpu_custom_call" | custom-call | tf_op jit(solution)/shard_map/mixed_grad/pallas_call | solution.py:544
  185.2 2.2 collective-permute-done.42
  187.4 1.6 add_convert_fusion.1
  190.8 1.9 collective-permute-start.50
  192.6 10.6 %collective-permute-done.51 = bf16[384,768]{1,0:T(8,128)(2,1)} collective-permute-done((bf16[384,768]{1,0:T(8,128)(2,1)}, bf16[384,768]{1,0:T(8,128)(2,1)}, u32[]{:S(2)}, u32[]{:S(2)}) %collective-permute-start.51) | collective-permute-done | bytes 589856 | tf_op jit(solution)/shard_map/ppermute | solution.py:66
  203.3 1.8 fusion.1
  205.2 1.6 copy-done.9
  209.0 9.0 %attend_back.2 = (bf16[1024,512]{1,0:T(8,128)(2,1)S(1)}, f32[4,144,512]{2,1,0:T(8,128)S(1)}, bf16[4,144,512]{2,1,0:T(8,128)(2,1)S(1)}) custom-call(s32[7]{0:T(128)S(1)} %pad_add_fusion.info.refs_0_, f32[2,4,1,512]{3,2,1,0:T(1,128)S(1)} %get-tuple-element.232.refs_1_, bf16[4,256,512]{2,1,0:T(8,128)(2,1)S(1)} %get-tuple-element.157.mixed_ref.refs_2_, ...), custom_call_target="tpu_custom_call" | custom-call | tf_op jit(solution)/shard_map/attend_back/pallas_call | solution.py:544
  219.9 1.8 collective-permute-done.47
  222.2 1.6 fusion.refs_0_
  224.8 1.5 collective-permute-start.71
  226.3 6.3 %collective-permute-done.57 = bf16[272,512]{1,0:T(8,128)(2,1)S(1)} collective-permute-done((bf16[272,512]{1,0:T(8,128)(2,1)S(1)}, bf16[272,512]{1,0:T(8,128)(2,1)S(1)}, u32[]{:S(2)}, u32[]{:S(2)}) %collective-permute-start.57) | collective-permute-done | bytes 278560 | tf_op jit(solution)/shard_map/ppermute | solution.py:66
  233.8 1.7 collective-permute-start.46
  235.5 8.8 %attend_back.3 = (bf16[1024,512]{1,0:T(8,128)(2,1)S(1)}, f32[4,144,512]{2,1,0:T(8,128)S(1)}, bf16[4,144,512]{2,1,0:T(8,128)(2,1)S(1)}) custom-call(s32[7]{0:T(128)S(1)} %pad_add_fusion.info.refs_0_, f32[2,4,1,512]{3,2,1,0:T(1,128)S(1)} %get-tuple-element.232.refs_1_, bf16[4,256,512]{2,1,0:T(8,128)(2,1)S(1)} %get-tuple-element.157.mixed_ref.refs_2_, ...), custom_call_target="tpu_custom_call" | custom-call | tf_op jit(solution)/shard_map/attend_back/pallas_call | solution.py:544
  248.8 2.7 collective-permute-done.45.refs_3_
  252.6 2.5 normed_grad.1
  255.1 2.1 collective-permute-start.53
  257.2 4.3 %collective-permute-done.63 = bf16[144,512]{1,0:T(8,128)(2,1)S(1)} collective-permute-done((bf16[144,512]{1,0:T(8,128)(2,1)S(1)}, bf16[144,512]{1,0:T(8,128)(2,1)S(1)}, u32[]{:S(2)}, u32[]{:S(2)}) %collective-permute-start.63) | collective-permute-done | bytes 147488 | tf_op jit(solution)/shard_map/ppermute | solution.py:66
  262.2 3.8 %unpack_feed.1 = (f32[128,3072]{1,0:T(8,128)}, f32[128,3072]{1,0:T(8,128)}, f32[384,1024]{1,0:T(8,128)}) custom-call(s32[3]{0:T(128)S(1)} %pad_add_fusion.1.info, bf16[384,768]{1,0:T(8,128)(2,1)S(1)} %fusion.refs_0_, bf16[384,768]{1,0:T(8,128)(2,1)S(1)} %collective-permute-done.70.refs_1_, bf16[384,768]{1,0:T(8,128)(2,1)S(1)} %collective-permute-done.71.refs_2_, ...), custom_call_target="tpu_custom_call" | custom-call | tf_op jit(solution)/shard_map/unpack_feed/pallas_call | solution.py:544
  266.1 3.0 %collective-permute-done.64 = bf16[144,512]{1,0:T(8,128)(2,1)S(1)} collective-permute-done((bf16[144,512]{1,0:T(8,128)(2,1)S(1)}, bf16[144,512]{1,0:T(8,128)(2,1)S(1)}, u32[]{:S(2)}, u32[]{:S(2)}) %collective-permute-start.64) | collective-permute-done | bytes 147488 | tf_op jit(solution)/shard_map/ppermute | solution.py:66
  269.3 1.7 collective-permute-start.60
  271.6 4.6 %collective-permute-done.65 = bf16[144,512]{1,0:T(8,128)(2,1)S(1)} collective-permute-done((bf16[144,512]{1,0:T(8,128)(2,1)S(1)}, bf16[144,512]{1,0:T(8,128)(2,1)S(1)}, u32[]{:S(2)}, u32[]{:S(2)}) %collective-permute-start.65) | collective-permute-done | bytes 147488 | tf_op jit(solution)/shard_map/ppermute | solution.py:66
  276.2 1.6 collective-permute-start.62
  279.9 1.6 collective-permute-start.68
  281.6 8.2 %collective-permute-done.61.refs_2_ = bf16[272,512]{1,0:T(8,128)(2,1)S(1)} collective-permute-done((bf16[272,512]{1,0:T(8,128)(2,1)S(1)}, bf16[272,512]{1,0:T(8,128)(2,1)S(1)}, u32[]{:S(2)}, u32[]{:S(2)}) %collective-permute-start.61) | collective-permute-done | bytes 278560 | tf_op jit(solution)/shard_map/ppermute | solution.py:29
  290.7 2.1 collective-permute-start.56
  292.7 1.9 collective-permute-done.67.refs_6_
  294.6 2.4 unpack_attend.1
  298.1 1.4 final.1
  (266 shorter events, 58.3 us)
Async XLA Ops:
  8.0 19.7 %collective-permute-start.1 = (bf16[208,1024]{1,0:T(8,128)(2,1)S(1)}, bf16[208,1024]{1,0:T(8,128)(2,1)S(1)}, u32[]{:S(2)}, u32[]{:S(2)}) collective-permute-start(bf16[208,1024]{1,0:T(8,128)(2,1)S(1)} %pack.1.refs_0_), channel_id=1, source_target_pairs={{0,1},{1,0},{2,3},{3,2},{4,5},{5,4},{6,7},{7,6},{8,9},{9,8},{10,11... | collective-permute-start | bytes 1277960 | tf_op jit(solution)/shard_map/ppermute | solution.py:71
  8.8 19.0 %collective-permute-start.3 = (bf16[256,1024]{1,0:T(8,128)(2,1)S(1)}, bf16[256,1024]{1,0:T(8,128)(2,1)S(1)}, u32[]{:S(2)}, u32[]{:S(2)}) collective-permute-start(bf16[256,1024]{1,0:T(8,128)(2,1)S(1)} %get-tuple-element.150.refs_8_), channel_id=1, source_target_pairs={{0,8},{8,0},{16,24},{24,16},{1,9},{9,1},{17,25},{25,17},{2,10},{10... | collective-permute-start | bytes 1572872 | tf_op jit(solution)/shard_map/ppermute | solution.py:29
  11.6 23.5 %collective-permute-start.5 = (bf16[256,1024]{1,0:T(8,128)(2,1)S(1)}, bf16[256,1024]{1,0:T(8,128)(2,1)S(1)}, u32[]{:S(2)}, u32[]{:S(2)}) collective-permute-start(bf16[256,1024]{1,0:T(8,128)(2,1)S(1)} %get-tuple-element.150.refs_8_), channel_id=1, source_target_pairs={{0,16},{8,24},{16,0},{24,8},{1,17},{9,25},{17,1},{25,9},{2,18},{10... | collective-permute-start | bytes 1572872 | tf_op jit(solution)/shard_map/ppermute | solution.py:29
  13.1 13.2 %collective-permute-start = (bf16[208,1024]{1,0:T(8,128)(2,1)S(1)}, bf16[208,1024]{1,0:T(8,128)(2,1)S(1)}, u32[]{:S(2)}, u32[]{:S(2)}) collective-permute-start(bf16[208,1024]{1,0:T(8,128)(2,1)S(1)} %pack.1.refs_0_), channel_id=1, source_target_pairs={{0,2},{1,3},{2,4},{3,5},{4,6},{5,7},{6,0},{7,1},{8,10},{9,11},{10,... | collective-permute-start | bytes 1277960 | tf_op jit(solution)/shard_map/ppermute | solution.py:66
  14.7 20.4 %collective-permute-start.4 = (bf16[256,1024]{1,0:T(8,128)(2,1)S(1)}, bf16[256,1024]{1,0:T(8,128)(2,1)S(1)}, u32[]{:S(2)}, u32[]{:S(2)}) collective-permute-start(bf16[256,1024]{1,0:T(8,128)(2,1)S(1)} %get-tuple-element.151.refs_9_), channel_id=1, source_target_pairs={{0,8},{8,0},{16,24},{24,16},{1,9},{9,1},{17,25},{25,17},{2,10},{10... | collective-permute-start | bytes 1572872 | tf_op jit(solution)/shard_map/ppermute | solution.py:29
  26.4 12.7 %collective-permute-start.6 = (bf16[256,1024]{1,0:T(8,128)(2,1)S(1)}, bf16[256,1024]{1,0:T(8,128)(2,1)S(1)}, u32[]{:S(2)}, u32[]{:S(2)}) collective-permute-start(bf16[256,1024]{1,0:T(8,128)(2,1)S(1)} %get-tuple-element.151.refs_9_), channel_id=1, source_target_pairs={{0,16},{8,24},{16,0},{24,8},{1,17},{9,25},{17,1},{25,9},{2,18},{10... | collective-permute-start | bytes 1572872 | tf_op jit(solution)/shard_map/ppermute | solution.py:29
  27.7 12.1 %collective-permute-start.2 = (bf16[208,1024]{1,0:T(8,128)(2,1)S(1)}, bf16[208,1024]{1,0:T(8,128)(2,1)S(1)}, u32[]{:S(2)}, u32[]{:S(2)}) collective-permute-start(bf16[208,1024]{1,0:T(8,128)(2,1)S(1)} %collective-permute-done.refs_1_), channel_id=1, source_target_pairs={{0,2},{1,3},{2,4},{3,5},{4,6},{5,7},{6,0},{7,1},{8,10},{9,11},{10,... | collective-permute-start | bytes 1277960 | tf_op jit(solution)/shard_map/ppermute | solution.py:66
  27.8 12.0 %collective-permute-start.7 = (bf16[208,1024]{1,0:T(8,128)(2,1)S(1)}, bf16[208,1024]{1,0:T(8,128)(2,1)S(1)}, u32[]{:S(2)}, u32[]{:S(2)}) collective-permute-start(bf16[208,1024]{1,0:T(8,128)(2,1)S(1)} %collective-permute-done.refs_1_), channel_id=1, source_target_pairs={{0,1},{1,0},{2,3},{3,2},{4,5},{5,4},{6,7},{7,6},{8,9},{9,8},{10,11... | collective-permute-start | bytes 1277960 | tf_op jit(solution)/shard_map/ppermute | solution.py:71
  39.8 11.1 %collective-permute-start.8 = (bf16[208,1024]{1,0:T(8,128)(2,1)S(1)}, bf16[208,1024]{1,0:T(8,128)(2,1)S(1)}, u32[]{:S(2)}, u32[]{:S(2)}) collective-permute-start(bf16[208,1024]{1,0:T(8,128)(2,1)S(1)} %collective-permute-done.2.refs_2_), channel_id=1, source_target_pairs={{0,2},{1,3},{2,4},{3,5},{4,6},{5,7},{6,0},{7,1},{8,10},{9,11},{10,... | collective-permute-start | bytes 1277960 | tf_op jit(solution)/shard_map/ppermute | solution.py:66
  39.8 13.7 %collective-permute-start.11 = (bf16[256,1024]{1,0:T(8,128)(2,1)S(1)}, bf16[256,1024]{1,0:T(8,128)(2,1)S(1)}, u32[]{:S(2)}, u32[]{:S(2)}) collective-permute-start(bf16[256,1024]{1,0:T(8,128)(2,1)S(1)} %collective-permute-done.3.refs_10_), channel_id=1, source_target_pairs={{0,16},{8,24},{16,0},{24,8},{1,17},{9,25},{17,1},{25,9},{2,18},{10... | collective-permute-start | bytes 1572872 | tf_op jit(solution)/shard_map/ppermute | solution.py:29
  41.5 13.0 %collective-permute-start.12 = (bf16[256,1024]{1,0:T(8,128)(2,1)S(1)}, bf16[256,1024]{1,0:T(8,128)(2,1)S(1)}, u32[]{:S(2)}, u32[]{:S(2)}) collective-permute-start(bf16[256,1024]{1,0:T(8,128)(2,1)S(1)} %collective-permute-done.6.refs_13_), channel_id=1, source_target_pairs={{0,8},{8,0},{16,24},{24,16},{1,9},{9,1},{17,25},{25,17},{2,10},{10... | collective-permute-start | bytes 1572872 | tf_op jit(solution)/shard_map/ppermute | solution.py:29
  41.9 14.0 %collective-permute-start.9 = (bf16[208,1024]{1,0:T(8,128)(2,1)S(1)}, bf16[208,1024]{1,0:T(8,128)(2,1)S(1)}, u32[]{:S(2)}, u32[]{:S(2)}) collective-permute-start(bf16[208,1024]{1,0:T(8,128)(2,1)S(1)} %collective-permute-done.2.refs_2_), channel_id=1, source_target_pairs={{0,1},{1,0},{2,3},{3,2},{4,5},{5,4},{6,7},{7,6},{8,9},{9,8},{10,11... | collective-permute-start | bytes 1277960 | tf_op jit(solution)/shard_map/ppermute | solution.py:71
  52.3 11.1 %collective-permute-start.13 = (bf16[64,1024]{1,0:T(8,128)(2,1)S(1)}, bf16[64,1024]{1,0:T(8,128)(2,1)S(1)}, u32[]{:S(2)}, u32[]{:S(2)}) collective-permute-start(bf16[64,1024]{1,0:T(8,128)(2,1)S(1)} %get-tuple-element.159), channel_id=1, source_target_pairs={{0,8},{8,0},{16,24},{24,16},{1,9},{9,1},{17,25},{25,17},{2,10},{10... | collective-permute-start | bytes 393224 | tf_op jit(solution)/shard_map/ppermute | solution.py:29
  53.6 9.9 %collective-permute-start.14 = (bf16[64,1024]{1,0:T(8,128)(2,1)S(1)}, bf16[64,1024]{1,0:T(8,128)(2,1)S(1)}, u32[]{:S(2)}, u32[]{:S(2)}) collective-permute-start(bf16[64,1024]{1,0:T(8,128)(2,1)S(1)} %get-tuple-element.160), channel_id=1, source_target_pairs={{0,16},{8,24},{16,0},{24,8},{1,17},{9,25},{17,1},{25,9},{2,18},{10... | collective-permute-start | bytes 393224 | tf_op jit(solution)/shard_map/ppermute | solution.py:29
  54.5 9.0 %collective-permute-start.15 = (bf16[64,1024]{1,0:T(8,128)(2,1)S(1)}, bf16[64,1024]{1,0:T(8,128)(2,1)S(1)}, u32[]{:S(2)}, u32[]{:S(2)}) collective-permute-start(bf16[64,1024]{1,0:T(8,128)(2,1)S(1)} %get-tuple-element.161), channel_id=1, source_target_pairs={{0,24},{8,16},{16,8},{24,0},{1,25},{9,17},{17,9},{25,1},{2,26},{10... | collective-permute-start | bytes 393224 | tf_op jit(solution)/shard_map/ppermute | solution.py:29
  55.9 18.0 %collective-permute-start.22 = (bf16[384,768]{1,0:T(8,128)(2,1)S(1)}, bf16[384,768]{1,0:T(8,128)(2,1)S(1)}, u32[]{:S(2)}, u32[]{:S(2)}) collective-permute-start(bf16[384,768]{1,0:T(8,128)(2,1)S(1)} %pack_feed.1.refs_0_), channel_id=1, source_target_pairs={{0,1},{1,0},{2,3},{3,2},{4,5},{5,4},{6,7},{7,6},{8,9},{9,8},{10,11... | collective-permute-start | bytes 1769480 | tf_op jit(solution)/shard_map/ppermute | solution.py:71
  55.9 18.0 %collective-permute-start.21 = (bf16[384,768]{1,0:T(8,128)(2,1)S(1)}, bf16[384,768]{1,0:T(8,128)(2,1)S(1)}, u32[]{:S(2)}, u32[]{:S(2)}) collective-permute-start(bf16[384,768]{1,0:T(8,128)(2,1)S(1)} %pack_feed.1.refs_0_), channel_id=1, source_target_pairs={{0,2},{1,3},{2,4},{3,5},{4,6},{5,7},{6,0},{7,1},{8,10},{9,11},{10,... | collective-permute-start | bytes 1769480 | tf_op jit(solution)/shard_map/ppermute | solution.py:66
  63.5 10.4 %collective-permute-start.16 = (bf16[256,1024]{1,0:T(8,128)(2,1)S(1)}, bf16[256,1024]{1,0:T(8,128)(2,1)S(1)}, u32[]{:S(2)}, u32[]{:S(2)}) collective-permute-start(bf16[256,1024]{1,0:T(8,128)(2,1)S(1)} %pad_maximum_fusion.4), channel_id=1, source_target_pairs={{0,1},{1,0},{2,3},{3,2},{4,5},{5,4},{6,7},{7,6},{8,9},{9,8},{10,11... | collective-permute-start | bytes 1572872 | tf_op jit(solution)/shard_map/ppermute | solution.py:71
  73.9 16.7 %collective-permute-start.23 = (bf16[384,768]{1,0:T(8,128)(2,1)S(1)}, bf16[384,768]{1,0:T(8,128)(2,1)S(1)}, u32[]{:S(2)}, u32[]{:S(2)}) collective-permute-start(bf16[384,768]{1,0:T(8,128)(2,1)S(1)} %collective-permute-done.21.refs_1_), channel_id=1, source_target_pairs={{0,2},{1,3},{2,4},{3,5},{4,6},{5,7},{6,0},{7,1},{8,10},{9,11},{10,... | collective-permute-start | bytes 1769480 | tf_op jit(solution)/shard_map/ppermute | solution.py:66
  73.9 16.7 %collective-permute-start.24 = (bf16[384,768]{1,0:T(8,128)(2,1)S(1)}, bf16[384,768]{1,0:T(8,128)(2,1)S(1)}, u32[]{:S(2)}, u32[]{:S(2)}) collective-permute-start(bf16[384,768]{1,0:T(8,128)(2,1)S(1)} %collective-permute-done.21.refs_1_), channel_id=1, source_target_pairs={{0,1},{1,0},{2,3},{3,2},{4,5},{5,4},{6,7},{7,6},{8,9},{9,8},{10,11... | collective-permute-start | bytes 1769480 | tf_op jit(solution)/shard_map/ppermute | solution.py:71
  75.9 14.9 %collective-permute-start.17 = (bf16[256,1024]{1,0:T(8,128)(2,1)S(1)}, bf16[256,1024]{1,0:T(8,128)(2,1)S(1)}, u32[]{:S(2)}, u32[]{:S(2)}) collective-permute-start(bf16[256,1024]{1,0:T(8,128)(2,1)S(1)} %get-tuple-element.167), channel_id=1, source_target_pairs={{0,8},{8,0},{16,24},{24,16},{1,9},{9,1},{17,25},{25,17},{2,10},{10... | collective-permute-start | bytes 1572872 | tf_op jit(solution)/shard_map/ppermute | solution.py:29
  77.1 15.5 %collective-permute-start.18 = (bf16[256,1024]{1,0:T(8,128)(2,1)S(1)}, bf16[256,1024]{1,0:T(8,128)(2,1)S(1)}, u32[]{:S(2)}, u32[]{:S(2)}) collective-permute-start(bf16[256,1024]{1,0:T(8,128)(2,1)S(1)} %get-tuple-element.168), channel_id=1, source_target_pairs={{0,16},{8,24},{16,0},{24,8},{1,17},{9,25},{17,1},{25,9},{2,18},{10... | collective-permute-start | bytes 1572872 | tf_op jit(solution)/shard_map/ppermute | solution.py:29
  90.6 15.9 %collective-permute-start.25 = (bf16[384,768]{1,0:T(8,128)(2,1)S(1)}, bf16[384,768]{1,0:T(8,128)(2,1)S(1)}, u32[]{:S(2)}, u32[]{:S(2)}) collective-permute-start(bf16[384,768]{1,0:T(8,128)(2,1)S(1)} %collective-permute-done.23.refs_2_), channel_id=1, source_target_pairs={{0,2},{1,3},{2,4},{3,5},{4,6},{5,7},{6,0},{7,1},{8,10},{9,11},{10,... | collective-permute-start | bytes 1769480 | tf_op jit(solution)/shard_map/ppermute | solution.py:66
  90.8 7.4 %collective-permute-start.19 = (bf16[128,1024]{1,0:T(8,128)(2,1)S(1)}, bf16[128,1024]{1,0:T(8,128)(2,1)S(1)}, u32[]{:S(2)}, u32[]{:S(2)}) collective-permute-start(bf16[128,1024]{1,0:T(8,128)(2,1)S(1)} %add_convert_fusion.9), channel_id=1, source_target_pairs={{0,16},{8,24},{16,0},{24,8},{1,17},{9,25},{17,1},{25,9},{2,18},{10... | collective-permute-start | bytes 786440 | tf_op jit(solution)/shard_map/ppermute | solution.py:29
  100.2 11.9 %collective-permute-start.28 = (bf16[256,1024]{1,0:T(8,128)(2,1)S(1)}, bf16[256,1024]{1,0:T(8,128)(2,1)S(1)}, u32[]{:S(2)}, u32[]{:S(2)}) collective-permute-start(bf16[256,1024]{1,0:T(8,128)(2,1)S(1)} %get-tuple-element.175.refs_0_.refs_8_), channel_id=1, source_target_pairs={{0,8},{8,0},{16,24},{24,16},{1,9},{9,1},{17,25},{25,17},{2,10},{10... | collective-permute-start | bytes 1572872 | tf_op jit(solution)/shard_map/ppermute | solution.py:29
  100.7 11.9 %collective-permute-start.29 = (bf16[256,1024]{1,0:T(8,128)(2,1)S(1)}, bf16[256,1024]{1,0:T(8,128)(2,1)S(1)}, u32[]{:S(2)}, u32[]{:S(2)}) collective-permute-start(bf16[256,1024]{1,0:T(8,128)(2,1)S(1)} %get-tuple-element.175.refs_0_.refs_8_), channel_id=1, source_target_pairs={{0,16},{8,24},{16,0},{24,8},{1,17},{9,25},{17,1},{25,9},{2,18},{10... | collective-permute-start | bytes 1572872 | tf_op jit(solution)/shard_map/ppermute | solution.py:29
  101.8 13.6 %collective-permute-start.26 = (bf16[384,768]{1,0:T(8,128)(2,1)S(1)}, bf16[384,768]{1,0:T(8,128)(2,1)S(1)}, u32[]{:S(2)}, u32[]{:S(2)}) collective-permute-start(bf16[384,768]{1,0:T(8,128)(2,1)S(1)} %collective-permute-done.23.refs_2_), channel_id=1, source_target_pairs={{0,1},{1,0},{2,3},{3,2},{4,5},{5,4},{6,7},{7,6},{8,9},{9,8},{10,11... | collective-permute-start | bytes 1769480 | tf_op jit(solution)/shard_map/ppermute | solution.py:71
  106.6 8.8 %collective-permute-start.27 = (bf16[384,768]{1,0:T(8,128)(2,1)S(1)}, bf16[384,768]{1,0:T(8,128)(2,1)S(1)}, u32[]{:S(2)}, u32[]{:S(2)}) collective-permute-start(bf16[384,768]{1,0:T(8,128)(2,1)S(1)} %collective-permute-done.25.refs_3_), channel_id=1, source_target_pairs={{0,1},{1,0},{2,3},{3,2},{4,5},{5,4},{6,7},{7,6},{8,9},{9,8},{10,11... | collective-permute-start | bytes 1769480 | tf_op jit(solution)/shard_map/ppermute | solution.py:71
  112.0 13.0 %collective-permute-start.30 = (bf16[128,1024]{1,0:T(8,128)(2,1)S(1)}, bf16[128,1024]{1,0:T(8,128)(2,1)S(1)}, u32[]{:S(2)}, u32[]{:S(2)}) collective-permute-start(bf16[128,1024]{1,0:T(8,128)(2,1)S(1)} %slice.300), channel_id=1, source_target_pairs={{0,16},{8,24},{16,0},{24,8},{1,17},{9,25},{17,1},{25,9},{2,18},{10... | collective-permute-start | bytes 786440 | tf_op jit(solution)/shard_map/ppermute | solution.py:29
  112.6 12.5 %collective-permute-start.31 = (bf16[128,1024]{1,0:T(8,128)(2,1)S(1)}, bf16[128,1024]{1,0:T(8,128)(2,1)S(1)}, u32[]{:S(2)}, u32[]{:S(2)}) collective-permute-start(bf16[128,1024]{1,0:T(8,128)(2,1)S(1)} %slice.301), channel_id=1, source_target_pairs={{0,8},{8,0},{16,24},{24,16},{1,9},{9,1},{17,25},{25,17},{2,10},{10... | collective-permute-start | bytes 786440 | tf_op jit(solution)/shard_map/ppermute | solution.py:29
  133.7 16.7 %collective-permute-start.36 = (bf16[4,384,768]{2,1,0:T(8,128)(2,1)S(1)}, bf16[4,384,768]{2,1,0:T(8,128)(2,1)S(1)}, u32[]{:S(2)}, u32[]{:S(2)}) collective-permute-start(bf16[4,384,768]{2,1,0:T(8,128)(2,1)S(1)} %get-tuple-element.214), channel_id=1, source_target_pairs={{0,1},{1,0},{2,3},{3,2},{4,5},{5,4},{6,7},{7,6},{8,9},{9,8},{10,11... | collective-permute-start | bytes 7077896 | tf_op jit(solution)/shard_map/ppermute | solution.py:71
  133.8 14.3 %collective-permute-start.32 = (bf16[256,1024]{1,0:T(8,128)(2,1)S(1)}, bf16[256,1024]{1,0:T(8,128)(2,1)S(1)}, u32[]{:S(2)}, u32[]{:S(2)}) collective-permute-start(bf16[256,1024]{1,0:T(8,128)(2,1)S(1)} %get-tuple-element.205), channel_id=1, source_target_pairs={{0,8},{8,0},{16,24},{24,16},{1,9},{9,1},{17,25},{25,17},{2,10},{10... | collective-permute-start | bytes 1572872 | tf_op jit(solution)/shard_map/ppermute | solution.py:29
  133.9 14.2 %collective-permute-start.33 = (bf16[256,1024]{1,0:T(8,128)(2,1)S(1)}, bf16[256,1024]{1,0:T(8,128)(2,1)S(1)}, u32[]{:S(2)}, u32[]{:S(2)}) collective-permute-start(bf16[256,1024]{1,0:T(8,128)(2,1)S(1)} %get-tuple-element.206), channel_id=1, source_target_pairs={{0,16},{8,24},{16,0},{24,8},{1,17},{9,25},{17,1},{25,9},{2,18},{10... | collective-permute-start | bytes 1572872 | tf_op jit(solution)/shard_map/ppermute | solution.py:29
  148.2 7.9 %collective-permute-start.34 = (bf16[128,1024]{1,0:T(8,128)(2,1)S(1)}, bf16[128,1024]{1,0:T(8,128)(2,1)S(1)}, u32[]{:S(2)}, u32[]{:S(2)}) collective-permute-start(bf16[128,1024]{1,0:T(8,128)(2,1)S(1)} %add_convert_fusion.7), channel_id=1, source_target_pairs={{0,16},{8,24},{16,0},{24,8},{1,17},{9,25},{17,1},{25,9},{2,18},{10... | collective-permute-start | bytes 786440 | tf_op jit(solution)/shard_map/ppermute | solution.py:29
  150.6 22.8 %collective-permute-start.41 = (bf16[384,768]{1,0:T(8,128)(2,1)S(1)}, bf16[384,768]{1,0:T(8,128)(2,1)S(1)}, u32[]{:S(2)}, u32[]{:S(2)}) collective-permute-start(bf16[384,768]{1,0:T(8,128)(2,1)S(1)} %fusion.3), channel_id=1, source_target_pairs={{0,2},{1,3},{2,4},{3,5},{4,6},{5,7},{6,0},{7,1},{8,10},{9,11},{10,... | collective-permute-start | bytes 1769480 | tf_op jit(solution)/shard_map/ppermute | solution.py:66
  158.3 12.2 %collective-permute-start.37 = (bf16[256,1024]{1,0:T(8,128)(2,1)S(1)}, bf16[256,1024]{1,0:T(8,128)(2,1)S(1)}, u32[]{:S(2)}, u32[]{:S(2)}) collective-permute-start(bf16[256,1024]{1,0:T(8,128)(2,1)S(1)} %get-tuple-element.234.refs_0_), channel_id=1, source_target_pairs={{0,8},{8,0},{16,24},{24,16},{1,9},{9,1},{17,25},{25,17},{2,10},{10... | collective-permute-start | bytes 1572872 | tf_op jit(solution)/shard_map/ppermute | solution.py:29
  159.8 13.1 %collective-permute-start.38 = (bf16[256,1024]{1,0:T(8,128)(2,1)S(1)}, bf16[256,1024]{1,0:T(8,128)(2,1)S(1)}, u32[]{:S(2)}, u32[]{:S(2)}) collective-permute-start(bf16[256,1024]{1,0:T(8,128)(2,1)S(1)} %get-tuple-element.234.refs_0_), channel_id=1, source_target_pairs={{0,16},{8,24},{16,0},{24,8},{1,17},{9,25},{17,1},{25,9},{2,18},{10... | collective-permute-start | bytes 1572872 | tf_op jit(solution)/shard_map/ppermute | solution.py:29
  185.1 18.2 %collective-permute-start.51 = (bf16[384,768]{1,0:T(8,128)(2,1)}, bf16[384,768]{1,0:T(8,128)(2,1)}, u32[]{:S(2)}, u32[]{:S(2)}) collective-permute-start(bf16[384,768]{1,0:T(8,128)(2,1)} %fusion.2), channel_id=1, source_target_pairs={{0,2},{1,3},{2,4},{3,5},{4,6},{5,7},{6,0},{7,1},{8,10},{9,11},{10,... | collective-permute-start | bytes 1769480 | tf_op jit(solution)/shard_map/ppermute | solution.py:66
  189.1 29.4 %collective-permute-start.48 = (bf16[64,1024]{1,0:T(8,128)(2,1)S(1)}, bf16[64,1024]{1,0:T(8,128)(2,1)S(1)}, u32[]{:S(2)}, u32[]{:S(2)}) collective-permute-start(bf16[64,1024]{1,0:T(8,128)(2,1)S(1)} %get-tuple-element.285), channel_id=1, source_target_pairs={{0,8},{8,0},{16,24},{24,16},{1,9},{9,1},{17,25},{25,17},{2,10},{10... | collective-permute-start | bytes 393224 | tf_op jit(solution)/shard_map/ppermute | solution.py:29
  189.5 30.2 %collective-permute-start.49 = (bf16[64,1024]{1,0:T(8,128)(2,1)S(1)}, bf16[64,1024]{1,0:T(8,128)(2,1)S(1)}, u32[]{:S(2)}, u32[]{:S(2)}) collective-permute-start(bf16[64,1024]{1,0:T(8,128)(2,1)S(1)} %get-tuple-element.284), channel_id=1, source_target_pairs={{0,16},{8,24},{16,0},{24,8},{1,17},{9,25},{17,1},{25,9},{2,18},{10... | collective-permute-start | bytes 393224 | tf_op jit(solution)/shard_map/ppermute | solution.py:29
  190.8 29.0 %collective-permute-start.50 = (bf16[64,1024]{1,0:T(8,128)(2,1)S(1)}, bf16[64,1024]{1,0:T(8,128)(2,1)S(1)}, u32[]{:S(2)}, u32[]{:S(2)}) collective-permute-start(bf16[64,1024]{1,0:T(8,128)(2,1)S(1)} %get-tuple-element.283), channel_id=1, source_target_pairs={{0,24},{8,16},{16,8},{24,0},{1,25},{9,17},{17,9},{25,1},{2,26},{10... | collective-permute-start | bytes 393224 | tf_op jit(solution)/shard_map/ppermute | solution.py:29
  205.0 17.2 %collective-permute-start.69 = (bf16[384,768]{1,0:T(8,128)(2,1)S(1)}, bf16[384,768]{1,0:T(8,128)(2,1)S(1)}, u32[]{:S(2)}, u32[]{:S(2)}) collective-permute-start(bf16[384,768]{1,0:T(8,128)(2,1)S(1)} %fusion.1), channel_id=1, source_target_pairs={{0,2},{1,3},{2,4},{3,5},{4,6},{5,7},{6,0},{7,1},{8,10},{9,11},{10,... | collective-permute-start | bytes 1769480 | tf_op jit(solution)/shard_map/ppermute | solution.py:66
  218.0 14.9 %collective-permute-start.43 = (bf16[256,1024]{1,0:T(8,128)(2,1)S(1)}, bf16[256,1024]{1,0:T(8,128)(2,1)S(1)}, u32[]{:S(2)}, u32[]{:S(2)}) collective-permute-start(bf16[256,1024]{1,0:T(8,128)(2,1)S(1)} %copy-done.47), channel_id=1, source_target_pairs={{0,8},{8,0},{16,24},{24,16},{1,9},{9,1},{17,25},{25,17},{2,10},{10... | collective-permute-start | bytes 1572872 | tf_op jit(solution)/shard_map/ppermute | solution.py:29
  218.5 15.3 %collective-permute-start.44 = (bf16[256,1024]{1,0:T(8,128)(2,1)S(1)}, bf16[256,1024]{1,0:T(8,128)(2,1)S(1)}, u32[]{:S(2)}, u32[]{:S(2)}) collective-permute-start(bf16[256,1024]{1,0:T(8,128)(2,1)S(1)} %copy-done.45), channel_id=1, source_target_pairs={{0,16},{8,24},{16,0},{24,8},{1,17},{9,25},{17,1},{25,9},{2,18},{10... | collective-permute-start | bytes 1572872 | tf_op jit(solution)/shard_map/ppermute | solution.py:29
  221.8 10.8 %collective-permute-start.57 = (bf16[272,512]{1,0:T(8,128)(2,1)S(1)}, bf16[272,512]{1,0:T(8,128)(2,1)S(1)}, u32[]{:S(2)}, u32[]{:S(2)}) collective-permute-start(bf16[272,512]{1,0:T(8,128)(2,1)S(1)} %pad_maximum_fusion.6), channel_id=1, source_target_pairs={{0,2},{1,3},{2,4},{3,5},{4,6},{5,7},{6,0},{7,1},{8,10},{9,11},{10,... | collective-permute-start | bytes 835592 | tf_op jit(solution)/shard_map/ppermute | solution.py:66
  223.9 21.6 %collective-permute-start.70 = (bf16[384,768]{1,0:T(8,128)(2,1)S(1)}, bf16[384,768]{1,0:T(8,128)(2,1)S(1)}, u32[]{:S(2)}, u32[]{:S(2)}) collective-permute-start(bf16[384,768]{1,0:T(8,128)(2,1)S(1)} %fusion.refs_0_), channel_id=1, source_target_pairs={{0,8},{8,0},{16,24},{24,16},{1,9},{9,1},{17,25},{25,17},{2,10},{10... | collective-permute-start | bytes 1769480 | tf_op jit(solution)/shard_map/ppermute | solution.py:29
  224.8 21.1 %collective-permute-start.71 = (bf16[384,768]{1,0:T(8,128)(2,1)S(1)}, bf16[384,768]{1,0:T(8,128)(2,1)S(1)}, u32[]{:S(2)}, u32[]{:S(2)}) collective-permute-start(bf16[384,768]{1,0:T(8,128)(2,1)S(1)} %fusion.refs_0_), channel_id=1, source_target_pairs={{0,16},{8,24},{16,0},{24,8},{1,17},{9,25},{17,1},{25,9},{2,18},{10... | collective-permute-start | bytes 1769480 | tf_op jit(solution)/shard_map/ppermute | solution.py:29
  232.7 14.5 %collective-permute-start.58 = (bf16[272,512]{1,0:T(8,128)(2,1)S(1)}, bf16[272,512]{1,0:T(8,128)(2,1)S(1)}, u32[]{:S(2)}, u32[]{:S(2)}) collective-permute-start(bf16[272,512]{1,0:T(8,128)(2,1)S(1)} %pad_maximum_fusion.7), channel_id=1, source_target_pairs={{0,2},{1,3},{2,4},{3,5},{4,6},{5,7},{6,0},{7,1},{8,10},{9,11},{10,... | collective-permute-start | bytes 835592 | tf_op jit(solution)/shard_map/ppermute | solution.py:66
  232.9 18.6 %collective-permute-start.45 = (bf16[128,1024]{1,0:T(8,128)(2,1)S(1)}, bf16[128,1024]{1,0:T(8,128)(2,1)S(1)}, u32[]{:S(2)}, u32[]{:S(2)}) collective-permute-start(bf16[128,1024]{1,0:T(8,128)(2,1)S(1)} %add_convert_fusion.5), channel_id=1, source_target_pairs={{0,16},{8,24},{16,0},{24,8},{1,17},{9,25},{17,1},{25,9},{2,18},{10... | collective-permute-start | bytes 786440 | tf_op jit(solution)/shard_map/ppermute | solution.py:29
  233.8 17.7 %collective-permute-start.46 = (bf16[128,1024]{1,0:T(8,128)(2,1)S(1)}, bf16[128,1024]{1,0:T(8,128)(2,1)S(1)}, u32[]{:S(2)}, u32[]{:S(2)}) collective-permute-start(bf16[128,1024]{1,0:T(8,128)(2,1)S(1)} %add_convert_fusion.4), channel_id=1, source_target_pairs={{0,8},{8,0},{16,24},{24,16},{1,9},{9,1},{17,25},{25,17},{2,10},{10... | collective-permute-start | bytes 786440 | tf_op jit(solution)/shard_map/ppermute | solution.py:29
  245.9 16.2 %collective-permute-start.72 = (bf16[192,768]{1,0:T(8,128)(2,1)S(1)}, bf16[192,768]{1,0:T(8,128)(2,1)S(1)}, u32[]{:S(2)}, u32[]{:S(2)}) collective-permute-start(bf16[192,768]{1,0:T(8,128)(2,1)S(1)} %slice.338), channel_id=1, source_target_pairs={{0,16},{8,24},{16,0},{24,8},{1,17},{9,25},{17,1},{25,9},{2,18},{10... | collective-permute-start | bytes 884744 | tf_op jit(solution)/shard_map/ppermute | solution.py:29
  247.2 15.0 %collective-permute-start.73 = (bf16[192,768]{1,0:T(8,128)(2,1)S(1)}, bf16[192,768]{1,0:T(8,128)(2,1)S(1)}, u32[]{:S(2)}, u32[]{:S(2)}) collective-permute-start(bf16[192,768]{1,0:T(8,128)(2,1)S(1)} %slice.339), channel_id=1, source_target_pairs={{0,8},{8,0},{16,24},{24,16},{1,9},{9,1},{17,25},{25,17},{2,10},{10... | collective-permute-start | bytes 884744 | tf_op jit(solution)/shard_map/ppermute | solution.py:29
  248.4 17.7 %collective-permute-start.59 = (bf16[272,512]{1,0:T(8,128)(2,1)S(1)}, bf16[272,512]{1,0:T(8,128)(2,1)S(1)}, u32[]{:S(2)}, u32[]{:S(2)}) collective-permute-start(bf16[272,512]{1,0:T(8,128)(2,1)S(1)} %pad_maximum_fusion.8), channel_id=1, source_target_pairs={{0,2},{1,3},{2,4},{3,5},{4,6},{5,7},{6,0},{7,1},{8,10},{9,11},{10,... | collective-permute-start | bytes 835592 | tf_op jit(solution)/shard_map/ppermute | solution.py:66
  251.6 9.9 %collective-permute-start.63 = (bf16[144,512]{1,0:T(8,128)(2,1)S(1)}, bf16[144,512]{1,0:T(8,128)(2,1)S(1)}, u32[]{:S(2)}, u32[]{:S(2)}) collective-permute-start(bf16[144,512]{1,0:T(8,128)(2,1)S(1)} %fusion.12), channel_id=1, source_target_pairs={{0,2},{1,3},{2,4},{3,5},{4,6},{5,7},{6,0},{7,1},{8,10},{9,11},{10,... | collective-permute-start | bytes 442376 | tf_op jit(solution)/shard_map/ppermute | solution.py:66
  255.1 22.8 %collective-permute-start.53 = (bf16[256,1024]{1,0:T(8,128)(2,1)S(1)}, bf16[256,1024]{1,0:T(8,128)(2,1)S(1)}, u32[]{:S(2)}, u32[]{:S(2)}) collective-permute-start(bf16[256,1024]{1,0:T(8,128)(2,1)S(1)} %get-tuple-element.267), channel_id=1, source_target_pairs={{0,8},{8,0},{16,24},{24,16},{1,9},{9,1},{17,25},{25,17},{2,10},{10... | collective-permute-start | bytes 1572872 | tf_op jit(solution)/shard_map/ppermute | solution.py:29
  261.5 18.5 %collective-permute-start.54 = (bf16[256,1024]{1,0:T(8,128)(2,1)S(1)}, bf16[256,1024]{1,0:T(8,128)(2,1)S(1)}, u32[]{:S(2)}, u32[]{:S(2)}) collective-permute-start(bf16[256,1024]{1,0:T(8,128)(2,1)S(1)} %get-tuple-element.268), channel_id=1, source_target_pairs={{0,16},{8,24},{16,0},{24,8},{1,17},{9,25},{17,1},{25,9},{2,18},{10... | collective-permute-start | bytes 1572872 | tf_op jit(solution)/shard_map/ppermute | solution.py:29
  269.3 9.9 %collective-permute-start.60 = (bf16[272,512]{1,0:T(8,128)(2,1)S(1)}, bf16[272,512]{1,0:T(8,128)(2,1)S(1)}, u32[]{:S(2)}, u32[]{:S(2)}) collective-permute-start(bf16[272,512]{1,0:T(8,128)(2,1)S(1)} %pad_maximum_fusion.9.refs_0_), channel_id=1, source_target_pairs={{0,8},{8,0},{16,24},{24,16},{1,9},{9,1},{17,25},{25,17},{2,10},{10... | collective-permute-start | bytes 835592 | tf_op jit(solution)/shard_map/ppermute | solution.py:29
  271.0 18.8 %collective-permute-start.61 = (bf16[272,512]{1,0:T(8,128)(2,1)S(1)}, bf16[272,512]{1,0:T(8,128)(2,1)S(1)}, u32[]{:S(2)}, u32[]{:S(2)}) collective-permute-start(bf16[272,512]{1,0:T(8,128)(2,1)S(1)} %pad_maximum_fusion.9.refs_0_), channel_id=1, source_target_pairs={{0,16},{8,24},{16,0},{24,8},{1,17},{9,25},{17,1},{25,9},{2,18},{10... | collective-permute-start | bytes 835592 | tf_op jit(solution)/shard_map/ppermute | solution.py:29
  276.2 14.5 %collective-permute-start.62 = (bf16[272,512]{1,0:T(8,128)(2,1)S(1)}, bf16[272,512]{1,0:T(8,128)(2,1)S(1)}, u32[]{:S(2)}, u32[]{:S(2)}) collective-permute-start(bf16[272,512]{1,0:T(8,128)(2,1)S(1)} %pad_maximum_fusion.9.refs_0_), channel_id=1, source_target_pairs={{0,24},{8,16},{16,8},{24,0},{1,25},{9,17},{17,9},{25,1},{2,26},{10... | collective-permute-start | bytes 835592 | tf_op jit(solution)/shard_map/ppermute | solution.py:29
  277.9 14.9 %collective-permute-start.66 = (bf16[144,512]{1,0:T(8,128)(2,1)S(1)}, bf16[144,512]{1,0:T(8,128)(2,1)S(1)}, u32[]{:S(2)}, u32[]{:S(2)}) collective-permute-start(bf16[144,512]{1,0:T(8,128)(2,1)S(1)} %fusion.6.refs_4_), channel_id=1, source_target_pairs={{0,8},{8,0},{16,24},{24,16},{1,9},{9,1},{17,25},{25,17},{2,10},{10... | collective-permute-start | bytes 442376 | tf_op jit(solution)/shard_map/ppermute | solution.py:29
  279.3 15.3 %collective-permute-start.67 = (bf16[144,512]{1,0:T(8,128)(2,1)S(1)}, bf16[144,512]{1,0:T(8,128)(2,1)S(1)}, u32[]{:S(2)}, u32[]{:S(2)}) collective-permute-start(bf16[144,512]{1,0:T(8,128)(2,1)S(1)} %fusion.6.refs_4_), channel_id=1, source_target_pairs={{0,16},{8,24},{16,0},{24,8},{1,17},{9,25},{17,1},{25,9},{2,18},{10... | collective-permute-start | bytes 442376 | tf_op jit(solution)/shard_map/ppermute | solution.py:29
  279.9 14.6 %collective-permute-start.68 = (bf16[144,512]{1,0:T(8,128)(2,1)S(1)}, bf16[144,512]{1,0:T(8,128)(2,1)S(1)}, u32[]{:S(2)}, u32[]{:S(2)}) collective-permute-start(bf16[144,512]{1,0:T(8,128)(2,1)S(1)} %fusion.6.refs_4_), channel_id=1, source_target_pairs={{0,24},{8,16},{16,8},{24,0},{1,25},{9,17},{17,9},{25,1},{2,26},{10... | collective-permute-start | bytes 442376 | tf_op jit(solution)/shard_map/ppermute | solution.py:29
  289.8 8.3 %collective-permute-start.55 = (bf16[128,1024]{1,0:T(8,128)(2,1)S(1)}, bf16[128,1024]{1,0:T(8,128)(2,1)S(1)}, u32[]{:S(2)}, u32[]{:S(2)}) collective-permute-start(bf16[128,1024]{1,0:T(8,128)(2,1)S(1)} %add_convert_fusion.3), channel_id=1, source_target_pairs={{0,16},{8,24},{16,0},{24,8},{1,17},{9,25},{17,1},{25,9},{2,18},{10... | collective-permute-start | bytes 786440 | tf_op jit(solution)/shard_map/ppermute | solution.py:29
  290.7 7.5 %collective-permute-start.56 = (bf16[128,1024]{1,0:T(8,128)(2,1)S(1)}, bf16[128,1024]{1,0:T(8,128)(2,1)S(1)}, u32[]{:S(2)}, u32[]{:S(2)}) collective-permute-start(bf16[128,1024]{1,0:T(8,128)(2,1)S(1)} %add_convert_fusion.2), channel_id=1, source_target_pairs={{0,8},{8,0},{16,24},{24,16},{1,9},{9,1},{17,25},{25,17},{2,10},{10... | collective-permute-start | bytes 786440 | tf_op jit(solution)/shard_map/ppermute | solution.py:29
  (60 other events, 524.0 us)

commit v4 on v3

--- a/solution.py
+++ b/solution.py
@@ -534,22 +534,27 @@
 OUT_ROWS = 64
 PACKED = 3 * ROWS
 TURN = HEAD_SIZE // 2
+LENGTH = BLOCKS * SIZE
+STORE_ROWS = 32768
+RAW_WIDTH = GROUP_Q + HEAD_SIZE
 
 
 def shape(dims, dtype):
     return jax.ShapeDtypeStruct(dims, dtype)
 
 
-def on_core(body, name, outs, scalars, args, far=(), scratch=(), limit=16):
+def on_core(body, name, outs, scalars, args, far=(), scratch=(), limit=16, far_outs=(), aliases=None):
     return pl.pallas_call(
         body,
         name=name,
         in_specs=[pl.BlockSpec(memory_space=pltpu.SMEM)] * len(scalars)
         + [pl.BlockSpec(memory_space=pltpu.VMEM)] * len(args)
         + [pl.BlockSpec(memory_space=pl.ANY)] * len(far),
-        out_specs=[pl.BlockSpec(memory_space=pltpu.VMEM)] * len(outs),
-        out_shape=outs,
+        out_specs=[pl.BlockSpec(memory_space=pltpu.VMEM)] * len(outs)
+        + [pl.BlockSpec(memory_space=pl.ANY)] * len(far_outs),
+        out_shape=[*outs, *far_outs],
         scratch_shapes=list(scratch),
+        input_output_aliases=aliases or {},
         compiler_params=pltpu.CompilerParams(vmem_limit_bytes=limit << 20),
     )(*scalars, *args, *far)
 
@@ -623,6 +628,16 @@
     return jnp.concatenate([ref[...] for ref in refs[3:]], axis=0)
 
 
+def head_places(store, near, g):
+    places = []
+    for n, (ref, rows) in enumerate(zip(near, (GROUP * SIZE, SIZE, SIZE))):
+        columns = slice((n * GROUPS + g) * HEAD_SIZE, (n * GROUPS + g + 1) * HEAD_SIZE)
+        for j in range(BLOCKS):
+            at = 2 * LENGTH + j * rows
+            places.append((store.at[at : at + rows, columns], ref.at[j]))
+    return places
+
+
 def load_paired(loads, refs, which, target):
     at = slice(which * HALF, (which + 1) * HALF)
     return [
@@ -635,21 +650,30 @@
     return 2 * chip + (info[2] if t < CHIPS else 1 - info[2])
 
 
-def pack_kernel(info, wq, wk, wv, wo, attn_gain, mlp_gain, query_gain, key_gain, out):
+def pack_kernel(info, wq, wk, wv, wo, *refs):
+    gains, (out, *rows, semaphores) = refs[:4], refs[4:]
+    loads = Loads(semaphores)
+    gain_loads = [loads(gain, row) for gain, row in zip(gains, rows)]
+    copies = []
     for g in range(GROUPS):
         at = g * GROUP_WIDTH
         head = info[0] * GROUPS + g
-        out[:ROWS, at : at + GROUP_Q] = wq[:, pl.ds(pl.multiple_of(head * GROUP_Q, GROUP_Q), GROUP_Q)]
+        columns = pl.ds(pl.multiple_of(head * GROUP_Q, GROUP_Q), GROUP_Q)
+        copies.append(loads(wq.at[:, columns], out.at[:ROWS, at : at + GROUP_Q]))
+        columns = pl.ds(pl.multiple_of(head * HEAD_SIZE, HEAD_SIZE), HEAD_SIZE)
         for weight, start in ((wk, at + GROUP_Q), (wv, at + GROUP_Q + HEAD_SIZE)):
-            columns = pl.ds(pl.multiple_of(head * HEAD_SIZE, HEAD_SIZE), HEAD_SIZE)
-            out[:ROWS, start : start + HEAD_SIZE] = weight[:, columns]
+            copies.append(loads(weight.at[:, columns], out.at[:ROWS, start : start + HEAD_SIZE]))
+    own = pl.ds(pl.multiple_of(info[0] * OUT_ROWS, OUT_ROWS), OUT_ROWS)
+    copies.append(loads(wo.at[own, :], out.at[ROWS + 16 :, :]))
+    for copy in gain_loads:
+        copy.wait()
     tile = slice(ROWS, ROWS + 16)
     out[tile, :] = jnp.zeros((16, ATTN_WIDTH), BF)
-    out[tile, :ROWS] = jnp.broadcast_to(attn_gain[...], (16, ROWS))
-    out[tile, ROWS : 2 * ROWS] = jnp.broadcast_to(mlp_gain[...], (16, ROWS))
-    out[tile, 2 * ROWS : 2 * ROWS + 16] = jnp.broadcast_to(query_gain[...], (16, 16))
-    out[tile, 3 * ROWS : 3 * ROWS + 16] = jnp.broadcast_to(key_gain[...], (16, 16))
-    out[ROWS + 16 :, :] = wo[pl.ds(pl.multiple_of(info[0] * OUT_ROWS, OUT_ROWS), OUT_ROWS), :]
+    for start, row in enumerate(rows):
+        width = row.shape[1]
+        out[tile, start * ROWS : start * ROWS + width] = jnp.broadcast_to(row[...], (16, width))
+    for copy in copies:
+        copy.wait()
 
 
 def pack_feed_kernel(info, gate, up, down, out):
@@ -688,8 +712,8 @@
 
 def project_kernel(info, cos_ref, sin_ref, *refs):
     parts, tokens = refs[:8], refs[8:16]
-    normed_ref, raw_ref, q_ref, k_ref, v_ref, w_ref, gain_ref = refs[16:23]
-    all_tokens, gain_rows, semaphores = refs[23:]
+    q_ref, k_ref, v_ref, gain_ref, low_store, wide_store = refs[16:22]
+    normed_ref, raw_ref, w_ref, all_tokens, gain_rows, semaphores = refs[22:]
     loads = Loads(semaphores)
     gain_loads, part_loads = [], []
     shards = [part_shard(info, t) for t in range(2 * CHIPS)]
@@ -717,8 +741,13 @@
         wide = all_tokens[here, :].astype(F32)
         normed = (wide * inverse_root(wide) * gain_ref[0:1, :]).astype(BF)
         normed_ref[here, :] = normed
+    stores = [loads(normed_ref, low_store.at[:LENGTH, :])]
+    for n, table in enumerate((cos_ref, sin_ref)):
+        at = GROUPS * RAW_WIDTH + n * HEAD_SIZE
+        stores.append(loads(table, wide_store.at[:LENGTH, at : at + HEAD_SIZE]))
     for copy in part_loads:
         copy.wait()
+    stores.append(loads(w_ref, low_store.at[LENGTH : 2 * LENGTH, :]))
     for j in range(BLOCKS):
         here = slice(j * SIZE, (j + 1) * SIZE)
         raw = mm(normed_ref[here, :], w_ref[...])
@@ -736,10 +765,18 @@
                 else:
                     q_ref[g, j, h * SIZE : (h + 1) * SIZE, :] = rotated
             v_ref[g, j] = raw[:, (g + 1) * GROUP_WIDTH - HEAD_SIZE : (g + 1) * GROUP_WIDTH].astype(BF)
-
-
-def attend_kernel(info, q_ref, k_ref, v_ref, mixed_ref, lse_ref):
+            at = slice(g * RAW_WIDTH, (g + 1) * RAW_WIDTH)
+            stores.append(loads(raw_ref.at[g, here, :], wide_store.at[here, at]))
+            places = head_places(low_store, (q_ref.at[g], k_ref.at[g], v_ref.at[g]), g)
+            stores += [loads(near, far) for far, near in places[j::BLOCKS]]
+    for copy in stores:
+        copy.wait()
+
+
+def attend_kernel(info, q_ref, k_ref, v_ref, store_in, mixed_ref, lse_ref, store, semaphores):
     own = info[0]
+    loads = Loads(semaphores)
+    stores = []
     for last in range(BLOCKS - 1, -1, -1):
         i = own ^ last
         for g in range(GROUPS):
@@ -760,6 +797,10 @@
                 at = (g * GROUP + h) * HEAD_SIZE
                 mixed_ref[i, :, at : at + HEAD_SIZE] = mixed[:, columns].T.astype(BF)
             lse_ref[g, i] = jnp.log2(total)
+        at = pl.ds(pl.multiple_of(4 * LENGTH + i * SIZE, SIZE), SIZE)
+        stores.append(loads(mixed_ref.at[i], store.at[at, :Q_WIDTH]))
+    for copy in stores:
+        copy.wait()
 
 
 def out_kernel(info, mixed_ref, *refs):
@@ -906,7 +947,7 @@
 
 
 def residual_kernel(cotangent, after_ref, gain_ref, *refs):
-    grad_ref, low_ref, gain_part = refs[-3:]
+    low_ref, gain_part = refs[-2:]
     keep_a, keep_b, one, two, low, high = refs[:6]
     top = keep_a[...] + one[:HALF].astype(F32) + low[...].astype(F32)
     bottom = keep_b[...] + two[:HALF].astype(F32) + high[...].astype(F32)
@@ -915,22 +956,27 @@
     inverse = inverse_root(after)
     gain_part[...] = jnp.sum(mlp_in_grad * (after * inverse), axis=0, keepdims=True)
     grad = cotangent[...].astype(F32) + norm_back(after, inverse, gain_ref[1:2, :], mlp_in_grad)
-    grad_ref[...] = grad
     low_ref[...] = grad.astype(BF)
 
 
-def mixed_grad_kernel(info, mixed_ref, out_ref, *refs):
-    branch, (grad_ref, kept, away, scratch) = refs[:5], refs[5:]
+def mixed_grad_kernel(info, out_ref, *refs):
+    branch, store, (grad_ref, kept, away, scratch, mixed_ref, semaphores) = refs[:5], refs[5], refs[6:]
+    mixed_load = Loads(semaphores)(store.at[4 * LENGTH : 5 * LENGTH, :Q_WIDTH], mixed_ref)
     own = info[0]
     for j in range(BLOCKS):
         grad_ref[j] = mm(block_of(branch, j), out_ref[...], ((1,), (1,))).astype(BF)
     branch_all = jnp.concatenate([block_of(branch, j) for j in range(BLOCKS)], axis=0)
-    mixed_all = jnp.concatenate([mixed_ref[j] for j in range(BLOCKS)], axis=0)
-    scratch[...] = mm(mixed_all, branch_all, ((0,), (0,)))
+    mixed_load.wait()
+    scratch[...] = mm(mixed_ref[...], branch_all, ((0,), (0,)))
     for core, target in ((info[2], kept), (1 - info[2], away)):
         for q in range(BLOCKS):
             at = pl.multiple_of(core * SIZE + (own ^ q) * OUT_ROWS, OUT_ROWS)
             target[q] = scratch[pl.ds(at, OUT_ROWS), :].astype(target.dtype)
+
+
+def pair_kernel(kept, crossed, *outs):
+    for j, out in enumerate(outs):
+        out[...] = (kept[j] + crossed[j].astype(F32)).astype(BF)
 
 
 def head_back(grad, cosine, sine, raw, gain):
@@ -940,14 +986,25 @@
     return norm_back(raw, inverse, gain, dy).astype(BF), gain_part
 
 
-def attend_back_kernel(g, info, lse_ref, mixed_ref, grad_ref, mlp_part, gain_ref, *refs):
-    far, (out_ref, kept, away) = refs[:8], refs[8:11]
-    dk_ref, dv_ref, q_ref, k_ref, v_ref, raw_ref, cos_ref, sin_ref, normed_ref, w_ref, semaphores = refs[11:]
+def attend_back_kernel(g, info, lse_ref, grad_ref, mlp_part, gain_ref, *refs):
+    (store, wide_store), (out_ref, kept, away, dk_ref, dv_ref) = refs[:2], refs[2:7]
+    q_ref, k_ref, v_ref, mixed_ref, raw_ref, cos_ref, sin_ref, normed_ref, w_ref, semaphores = refs[7:]
     loads = Loads(semaphores)
-    width = slice(g * GROUP_WIDTH, (g + 1) * GROUP_WIDTH)
-    first = [loads(far[n].at[g], near) for n, near in enumerate((q_ref, k_ref, v_ref))]
-    second = [loads(far[3].at[g], raw_ref), loads(far[4], cos_ref), loads(far[5], sin_ref)]
-    third = [loads(far[6], normed_ref), loads(far[7].at[:, width], w_ref)]
+    first = [loads(far, near) for far, near in head_places(store, (q_ref, k_ref, v_ref), g)]
+    at = slice(g * GROUP_Q, (g + 1) * GROUP_Q)
+    first += [
+        loads(store.at[4 * LENGTH + j * SIZE : 4 * LENGTH + (j + 1) * SIZE, at], mixed_ref.at[j])
+        for j in range(BLOCKS)
+    ]
+    second = [loads(wide_store.at[:LENGTH, g * RAW_WIDTH : (g + 1) * RAW_WIDTH], raw_ref)]
+    for n, table in enumerate((cos_ref, sin_ref)):
+        at = GROUPS * RAW_WIDTH + n * HEAD_SIZE
+        second.append(loads(wide_store.at[:LENGTH, at : at + HEAD_SIZE], table))
+    at = slice(g * GROUP_WIDTH, (g + 1) * GROUP_WIDTH)
+    third = [
+        loads(store.at[:LENGTH, :], normed_ref),
+        loads(store.at[LENGTH : 2 * LENGTH, at], w_ref),
+    ]
     own = info[0]
     query_part = jnp.zeros((1, HEAD_SIZE), F32)
     key_part = jnp.zeros((1, HEAD_SIZE), F32)
@@ -961,7 +1018,9 @@
         heads = [slice((g * GROUP + h) * HEAD_SIZE, (g * GROUP + h + 1) * HEAD_SIZE) for h in range(GROUP)]
         query = q_ref[i]
         grad = jnp.concatenate([grad_ref[i, :, h] for h in heads], axis=0)
-        mixed = jnp.concatenate([mixed_ref[i, :, h] for h in heads], axis=0)
+        mixed = jnp.concatenate(
+            [mixed_ref[i, :, h * HEAD_SIZE : (h + 1) * HEAD_SIZE] for h in range(GROUP)], axis=0
+        )
         delta = jnp.sum((grad.astype(F32) * mixed.astype(F32)).T, axis=0, keepdims=True)
         log_sum = lse_ref[g, i]
         dquery = jnp.zeros((HEAD_SIZE, GROUP * SIZE), F32)
@@ -1027,8 +1086,9 @@
                 away[t, ROWS:, :] = values.astype(BF)
 
 
-def normed_grad_kernel(w_ref, *refs):
-    grads, partial = refs[:GROUPS], refs[GROUPS:]
+def normed_grad_kernel(*refs):
+    grads, store, partial, (w_ref, semaphores) = refs[:GROUPS], refs[GROUPS], refs[GROUPS + 1 : -2], refs[-2:]
+    Loads(semaphores)(store.at[LENGTH : 2 * LENGTH, :], w_ref).wait()
     for j in (3, 1, 2, 0):
         here = slice(j * SIZE, (j + 1) * SIZE)
         grad = jnp.concatenate([ref[here, :] for ref in grads], axis=1)
@@ -1040,7 +1100,7 @@
     wide = tokens[...].astype(F32)
     dy = joined(*refs[:5])
     back = norm_back(wide, inverse_root(wide), gain_ref[0:1, :], dy)
-    grad_ref[...] = (residual[...] + back).astype(BF)
+    grad_ref[...] = (residual[...].astype(F32) + back).astype(BF)
 
 
 def output_kernel(after_ref, *refs):
@@ -1086,8 +1146,8 @@
     gain_ref[...] = gains
 
 
-def ring_parts(value, then):
-    own, other = [value], [other_core(value)]
+def ring_parts(value, swapped, then):
+    own, other = [value], [swapped]
     for t in range(1, CHIPS):
         ready = then.get(t, ())
         if t > 1:
@@ -1097,25 +1157,25 @@
     return own, other
 
 
-def ring_sum(kept, away, then, beside=None):
-    crossed = other_core(away)
-
-    def term(t, moved):
-        value = kept[t] + crossed[t].astype(F32)
-        count = value.shape[0]
-        if moved is not None:
-            value = value + moved[:count].astype(F32)
-        value = value.astype(BF)
-        if beside is not None:
-            extra = beside(t + 1)
-            if moved is not None:
-                extra = (moved[count:].astype(F32) + extra.astype(F32)).astype(BF)
-            value = jnp.concatenate([value, extra], axis=0)
-        return value
-
-    running = [term(0, None)]
+def ring_term(kept, crossed, t, previous=None, beside=None, after=()):
+    value = kept[t] + crossed[t].astype(F32)
+    count = value.shape[0]
+    if t:
+        moved = tie(ring_up(previous), after)
+        value = value + moved[:count].astype(F32)
+    value = value.astype(BF)
+    if beside is not None:
+        extra = beside(t + 1)
+        if t:
+            extra = (moved[count:].astype(F32) + extra.astype(F32)).astype(BF)
+        value = jnp.concatenate([value, extra], axis=0)
+    return value
+
+
+def ring_sum(kept, crossed, beside=None):
+    running = [ring_term(kept, crossed, 0, None, beside)]
     for t in range(1, CHIPS):
-        running.append(term(t, ring_up(tie(running[-1], then.get(t, ())))))
+        running.append(ring_term(kept, crossed, t, running[-1], beside))
     return running
 
 
@@ -1149,14 +1209,18 @@
     place = jnp.stack([r, chip, core]).astype(jnp.int32)
     info = jnp.concatenate([place, jnp.any(held, axis=1).astype(jnp.int32)])
 
+    gains = tuple(gain.reshape(1, -1) for gain in (attn_norm, mlp_norm, query_norm, key_norm))
     (attn_rows,) = on_core(
         pack_kernel,
         "pack",
         [shape((ROWS + 16 + OUT_ROWS, ATTN_WIDTH), BF)],
         (place,),
-        (query_weight, key_projection, value_projection, out_weight)
-        + tuple(gain.reshape(1, -1) for gain in (attn_norm, mlp_norm, query_norm, key_norm)),
-    )
+        (),
+        (query_weight, key_projection, value_projection, out_weight, *gains),
+        [pltpu.VMEM(gain.shape, BF) for gain in gains] + [pltpu.SemaphoreType.DMA((11,))],
+        62,
+    )
+    attn_swap = other_core(attn_rows)
     low_half, high_half = tie(
         tuple(jnp.concatenate([tokens[at], cotangent_own[at]]) for at in (slice(0, HALF), slice(HALF, SIZE))),
         attn_rows,
@@ -1180,7 +1244,7 @@
     sin_rows = jnp.concatenate([-sine, sine], axis=1)
 
     attn_own, attn_other = ring_parts(
-        attn_rows, {2: (feed_rows, info), 3: (one, two, cos_rows, sin_rows)}
+        attn_rows, attn_swap, {2: (feed_rows, info), 3: (one, two, cos_rows, sin_rows)}
     )
 
     picked = on_core(
@@ -1194,28 +1258,31 @@
     )
     out_own = [picked[0]] + [flip(picked[j], j) for j in (1, 2, 3)]
 
-    normed, raw, query, key, value, attn_matrix, gain_rows = on_core(
+    heads = [
+        shape((GROUPS, BLOCKS, GROUP * SIZE, HEAD_SIZE), BF),
+        shape((GROUPS, BLOCKS, SIZE, HEAD_SIZE), BF),
+        shape((GROUPS, BLOCKS, SIZE, HEAD_SIZE), BF),
+    ]
+    store_shape = shape((STORE_ROWS, MODEL_WIDTH), BF)
+    query, key, value, gain_rows, store, wide_store = on_core(
         project_kernel,
         "project",
-        [
-            shape((length, MODEL_WIDTH), BF),
-            shape((GROUPS, length, GROUP_Q + HEAD_SIZE), F32),
-            shape((GROUPS, BLOCKS, GROUP * SIZE, HEAD_SIZE), BF),
-            shape((GROUPS, BLOCKS, SIZE, HEAD_SIZE), BF),
-            shape((GROUPS, BLOCKS, SIZE, HEAD_SIZE), BF),
-            shape((MODEL_WIDTH, ATTN_WIDTH), BF),
-            shape((8, MODEL_WIDTH), F32),
-        ],
+        heads + [shape((8, MODEL_WIDTH), F32)],
         (info,),
         (cos_rows, sin_rows),
         (*attn_own, *attn_other, *pieces),
         [
             pltpu.VMEM((length, MODEL_WIDTH), BF),
+            pltpu.VMEM((GROUPS, length, RAW_WIDTH), F32),
+            pltpu.VMEM((MODEL_WIDTH, ATTN_WIDTH), BF),
+            pltpu.VMEM((length, MODEL_WIDTH), BF),
             pltpu.VMEM((2 * CHIPS, 16, ATTN_WIDTH), BF),
-            pltpu.SemaphoreType.DMA((6 * CHIPS,)),
+            pltpu.SemaphoreType.DMA((14 * CHIPS + 4,)),
         ],
-    )
-    mixed, lse = on_core(
+        24,
+        [store_shape, shape((STORE_ROWS // 2, MODEL_WIDTH), F32)],
+    )
+    mixed, lse, store = on_core(
         attend_kernel,
         "attend",
         [
@@ -1224,6 +1291,11 @@
         ],
         (info,),
         (query, key, value),
+        (store,),
+        [pltpu.SemaphoreType.DMA((BLOCKS,))],
+        16,
+        [store_shape],
+        {4: 2},
     )
     out_own = tie(out_own, query)
     out_other = other_core(jnp.concatenate(out_own, axis=0))
@@ -1235,7 +1307,8 @@
         (info,),
         (mixed, *out_own, *out_other),
     )
-    feed_own, feed_other = ring_parts(tie(feed_rows, attn_own[-1]), {2: mixed, 3: partial[0]})
+    feed_start = tie(feed_rows, attn_own[-1])
+    feed_own, feed_other = ring_parts(feed_start, other_core(feed_start), {2: mixed, 3: partial[0]})
     partial = move_partial(*partial)
     after_attn, mlp_own = on_core(
         after_kernel,
@@ -1286,24 +1359,26 @@
         ],
         24,
     )
-    feed_ring = ring_sum(feed_kept, feed_away, {})
     one, two = tie((flip(one, 1), flip(two, 2)), feed_kept)
-    low = flip((keep_low + one[HALF:].astype(F32)).astype(BF), 2)
-    high = flip((keep_high + two[HALF:].astype(F32)).astype(BF), 1)
-    residual_grad, branch_own, mlp_gain_part = on_core(
+    low = (keep_low + one[HALF:].astype(F32)).astype(BF)
+    high = (keep_high + two[HALF:].astype(F32)).astype(BF)
+    crossed = other_core(tie(feed_away, low, high))
+    low, high = flip(low, 2), flip(high, 1)
+    branch_own, mlp_gain_part = on_core(
         residual_kernel,
         "residual",
         [
-            shape((SIZE, MODEL_WIDTH), F32),
             shape((SIZE, MODEL_WIDTH), BF),
             shape((1, MODEL_WIDTH), F32),
         ],
         (),
-        (cotangent_own, after_attn, gain_rows, *tie((*keep, one, two, low, high), feed_ring[0])),
+        (cotangent_own, after_attn, gain_rows, *tie((*keep, one, two, low, high), crossed)),
     )
     branch = spread(branch_own)
+    feed_ring = [ring_term(feed_kept, crossed, 0)]
+    feed_ring.append(ring_term(feed_kept, crossed, 1, feed_ring[0]))
     layer_partial = on_core(
-        down_kernel, "down", partial_shapes(), (), tie((down, *hidden), branch_own)
+        down_kernel, "down", partial_shapes(), (), tie((down, *hidden), branch_own, feed_ring[0])
     )
 
     mixed_grad, out_kept, out_away = on_core(
@@ -1315,12 +1390,21 @@
             shape((BLOCKS, OUT_ROWS, MODEL_WIDTH), BF),
         ],
         (info,),
-        (mixed, out_matrix, *tie(branch, layer_partial, feed_ring[1])),
+        (out_matrix, *tie(branch, layer_partial, feed_ring[1])),
+        (store,),
+        [
+            pltpu.VMEM((Q_WIDTH, MODEL_WIDTH), F32),
+            pltpu.VMEM((length, Q_WIDTH), BF),
+            pltpu.SemaphoreType.DMA((1,)),
+        ],
+    )
+    out_pair = on_core(
+        pair_kernel,
+        "pair",
+        [shape((OUT_ROWS, MODEL_WIDTH), BF)] * BLOCKS,
         (),
-        [pltpu.VMEM((Q_WIDTH, MODEL_WIDTH), F32)],
-    )
-    out_pair = (out_kept + other_core(out_away).astype(F32)).astype(BF)
-    out_pair = [out_pair[j] for j in range(BLOCKS)]
+        (out_kept, other_core(out_away)),
+    )
     out_moved = [out_pair[0]] + [flip(out_pair[j], j) for j in (1, 2, 3)]
 
     def back(g, grad):
@@ -1336,20 +1420,21 @@
                 shape((CHIPS, ROWS + 16, GROUP_WIDTH), BF),
             ],
             (info,),
-            (lse, mixed, grad, mlp_gain_part, gain_rows),
-            (query, key, value, raw, cos_rows, sin_rows, normed, attn_matrix),
+            (lse, grad, mlp_gain_part, gain_rows),
+            (store, wide_store),
             [
                 pltpu.VMEM((BLOCKS, SIZE, HEAD_SIZE), F32),
                 pltpu.VMEM((BLOCKS, SIZE, HEAD_SIZE), F32),
                 pltpu.VMEM((BLOCKS, GROUP * SIZE, HEAD_SIZE), BF),
                 pltpu.VMEM((BLOCKS, SIZE, HEAD_SIZE), BF),
                 pltpu.VMEM((BLOCKS, SIZE, HEAD_SIZE), BF),
-                pltpu.VMEM((length, GROUP_Q + HEAD_SIZE), F32),
+                pltpu.VMEM((BLOCKS, SIZE, GROUP_Q), BF),
+                pltpu.VMEM((length, RAW_WIDTH), F32),
                 pltpu.VMEM((length, HEAD_SIZE), F32),
                 pltpu.VMEM((length, HEAD_SIZE), F32),
                 pltpu.VMEM((length, MODEL_WIDTH), BF),
                 pltpu.VMEM((MODEL_WIDTH, GROUP_WIDTH), BF),
-                pltpu.SemaphoreType.DMA((8,)),
+                pltpu.SemaphoreType.DMA((4 * BLOCKS + 5,)),
             ],
         )
 
@@ -1362,30 +1447,41 @@
         )
         return jnp.concatenate([block[:, :GROUP_WIDTH], block[:, GROUP_WIDTH:]], axis=0)
 
-    layer_pieces = move_partial(*tie(layer_partial, grad_0))
-    attn_first = ring_sum(kept_0, away_0, {}, out_step)
+    kept = (kept_0, other_core(away_0))
+    attn_first = [ring_term(*kept, 0, None, out_step)]
+    feed_ring.append(ring_term(feed_kept, crossed, 2, feed_ring[1], None, grad_0))
+    layer_one, layer_two, layer_low, layer_high, layer_keep = tie(layer_partial, grad_0)
+    layer_one, layer_two = flip(layer_one, 1), flip(layer_two, 2)
     grad_1, kept_1, away_1 = back(1, tie(mixed_grad, attn_first[0], feed_ring[2]))
-    attn_second = ring_sum(kept_1, away_1, {})
+    layer_one, layer_two = tie((layer_one, layer_two), grad_1)
+    layer_low = flip((layer_low + layer_one[HALF:].astype(F32)).astype(BF), 2)
+    layer_high = flip((layer_high + layer_two[HALF:].astype(F32)).astype(BF), 1)
+    for t in range(1, CHIPS):
+        attn_first.append(ring_term(*kept, t, attn_first[-1], out_step, grad_1))
+    feed_ring.append(ring_term(feed_kept, crossed, 3, feed_ring[2], None, grad_1))
+    attn_second = ring_sum(kept_1, other_core(away_1))
     partial = on_core(
         normed_grad_kernel,
         "normed_grad",
         partial_shapes(),
         (),
-        (attn_matrix, *tie((grad_0, grad_1), attn_second[0])),
+        tie((grad_0, grad_1), out_blocks, attn_second[0]),
+        (store,),
+        [pltpu.VMEM((MODEL_WIDTH, ATTN_WIDTH), BF), pltpu.SemaphoreType.DMA((1,))],
     )
     (layer_out,) = on_core(
         output_kernel,
         "output",
         [shape((SIZE, MODEL_WIDTH), BF)],
         (),
-        (after_attn, *layer_pieces),
+        (after_attn, layer_keep, layer_one, layer_two, layer_low, layer_high),
     )
     (in_grad,) = on_core(
         final_kernel,
         "final",
         [shape((SIZE, MODEL_WIDTH), BF)],
         (),
-        (tokens, gain_rows, residual_grad, *move_partial(*partial)),
+        (tokens, gain_rows, branch_own, *move_partial(*partial)),
     )
 
     gate_w_grad, up_w_grad, down_w_grad = on_core(

time: 304 us -> 282 us (0.928)
  waiting for transfers between devices: 138 us -> 122 us
  local copies, waits for them, and re-layouts: 20.7 us -> 5.49 us
  Pallas kernels: 69.1 us -> 77 us
  starting transfers between devices: 59.7 us -> 64 us
  other arithmetic: 10.1 us -> 7.05 us
    unnamed x101 -> x57, local copies, waits for them, and re-layouts: 19.2 us -> 4.07 us
    ppermute x46, waiting for transfers between devices: 65.1 us -> 54.2 us  [flip(): return lax.ppermute(value, 'rep', [(i, i ^ bit) for i in range(count)])]
    pallas_call x22 -> x23, Pallas kernels: 69.1 us -> 77 us  [on_core(): pl.pallas_call(body, name=name, in_specs=[pl.BlockSpec(memory_space=pltpu...]
    ppermute x15, starting transfers between devices: 4.31 us -> 12 us  [ring_up(): lax.ppermute(value, 'shard', [(i, (i + 2) % count) for i in range(count)])]
    ppermute x15, waiting for transfers between devices: 68.5 us -> 63.2 us  [ring_up(): lax.ppermute(value, 'shard', [(i, (i + 2) % count) for i in range(count)])]
    convert_element_type x18 -> x19, other arithmetic: 6.83 us -> 3.32 us  [the longest x12 3 us: ring_term(): value = value.astype(BF)]
    ppermute x46, starting transfers between devices: 54.3 us -> 51 us  [flip(): return lax.ppermute(value, 'rep', [(i, i ^ bit) for i in range(count)])]
  transfers between devices with their start and end apart: 74 -> 74, of which waited for: 30 -> 31; matrix products, arithmetic and copies ran while one was open for 4% -> 3% of each run, Pallas kernels for 18% -> 26%
where the time goes in v4:
time: 282 us; the launch traced here: 278 us
  waiting for transfers between devices  122 us (43%)
  Pallas kernels  77 us (27%)
  starting transfers between devices  64 us (23%)
  other arithmetic  7.05 us (2%)
  local copies, waits for them, and re-layouts  5.49 us (2%)
    pallas_call x23, Pallas kernels, on_core(): pl.pallas_call(body, name=name, in_specs=[pl.BlockSpec(memory_space=pltpu...  77 us
    ppermute x15, waiting for transfers between devices, ring_up(): lax.ppermute(value, 'shard', [(i, (i + 2) % count) for i in range(count)])  63.2 us
    ppermute x46, waiting for transfers between devices, flip(): return lax.ppermute(value, 'rep', [(i, i ^ bit) for i in range(count)])  54.2 us
    ppermute x46, starting transfers between devices, flip(): return lax.ppermute(value, 'rep', [(i, i ^ bit) for i in range(count)])  51 us
    ppermute x15, starting transfers between devices, ring_up(): lax.ppermute(value, 'shard', [(i, (i + 2) % count) for i in range(count)])  12 us
  transfers between devices with their start and end apart: 74, of which 31 were waited for; matrix products, arithmetic and copies ran while one was open for 3% of the time, Pallas kernels for 26%

profile of v4, /device:TPU:0, one launch (start us, length us, event | category | flops | bytes accessed | tf_op | source)
XLA Modules:
  0.0 278.0 jit_solution(7863718335441445763)
XLA Ops:
  1.3 2.7 pack.1.refs_0_
  4.9 2.6 collective-permute-start.6
  7.5 1.5 collective-permute-start.4
  9.0 1.6 collective-permute-start
  12.0 10.4 %collective-permute-done.refs_1_ = bf16[208,1024]{1,0:T(8,128)(2,1)S(1)} collective-permute-done((bf16[208,1024]{1,0:T(8,128)(2,1)S(1)}, bf16[208,1024]{1,0:T(8,128)(2,1)S(1)}, u32[]{:S(2)}, u32[]{:S(2)}) %collective-permute-start) | collective-permute-done | bytes 426016 | tf_op jit(solution)/shard_map/ppermute | solution.py:66
  23.9 8.8 %collective-permute-done.3.refs_10_ = bf16[256,1024]{1,0:T(8,128)(2,1)S(1)} collective-permute-done((bf16[256,1024]{1,0:T(8,128)(2,1)S(1)}, bf16[256,1024]{1,0:T(8,128)(2,1)S(1)}, u32[]{:S(2)}, u32[]{:S(2)}) %collective-permute-start.3) | collective-permute-done | bytes 524320 | tf_op jit(solution)/shard_map/ppermute | solution.py:29
  32.8 1.9 fusion.10
  38.7 10.5 %collective-permute-done.8.refs_3_ = bf16[208,1024]{1,0:T(8,128)(2,1)S(1)} collective-permute-done((bf16[208,1024]{1,0:T(8,128)(2,1)S(1)}, bf16[208,1024]{1,0:T(8,128)(2,1)S(1)}, u32[]{:S(2)}, u32[]{:S(2)}) %collective-permute-start.8) | collective-permute-done | bytes 426016 | tf_op jit(solution)/shard_map/ppermute | solution.py:66
  50.6 1.6 collective-permute-start.13
  52.6 1.5 collective-permute-start.15
  54.1 1.7 collective-permute-start.21
  55.9 7.3 %project.1 = (bf16[2,4,512,128]{3,2,1,0:T(8,128)(2,1)S(1)}, bf16[2,4,256,128]{3,2,1,0:T(8,128)(2,1)S(1)}, bf16[2,4,256,128]{3,2,1,0:T(8,128)(2,1)S(1)}, f32[8,10...) custom-call(s32[7]{0:T(128)S(1)} %pad_add_fusion.info.refs_0_, ...), custom_call_target="tpu_custom_call" | custom-call | tf_op jit(solution)/shard_map/project/pallas_call | solution.py:547
  63.4 5.8 %attend.1 = (bf16[4,256,512]{2,1,0:T(8,128)(2,1)S(1)}, f32[2,4,1,512]{3,2,1,0:T(1,128)S(1)}, bf16[32768,1024]{1,0:T(8,128)(2,1)}) custom-call(s32[7]{0:T(128)S(1)} %pad_add_fusion.info.refs_0_, bf16[2,4,512,128]{3,2,1,0:T(8,128)(2,1)S(1)} %get-tuple-element.165.q_ref, ...), custom_call_target="tpu_custom_call", output_to_operand_aliasing={{2}: (4, {})} | custom-call | tf_op jit(solution)/shard_map/attend/pallas_call | solution.py:547
  69.3 2.9 %collective-permute-done.21.refs_1_ = bf16[384,768]{1,0:T(8,128)(2,1)S(1)} collective-permute-done((bf16[384,768]{1,0:T(8,128)(2,1)S(1)}, bf16[384,768]{1,0:T(8,128)(2,1)S(1)}, u32[]{:S(2)}, u32[]{:S(2)}) %collective-permute-start.21) | collective-permute-done | bytes 589856 | tf_op jit(solution)/shard_map/ppermute | solution.py:66
  72.3 1.9 out.1
  74.8 1.5 collective-permute-start.17
  76.3 12.6 %collective-permute-done.23.refs_2_ = bf16[384,768]{1,0:T(8,128)(2,1)S(1)} collective-permute-done((bf16[384,768]{1,0:T(8,128)(2,1)S(1)}, bf16[384,768]{1,0:T(8,128)(2,1)S(1)}, u32[]{:S(2)}, u32[]{:S(2)}) %collective-permute-start.23) | collective-permute-done | bytes 589856 | tf_op jit(solution)/shard_map/ppermute | solution.py:66
  89.1 1.6 collective-permute-start.20
  91.3 5.3 %collective-permute-done.20.refs_4_ = bf16[128,1024]{1,0:T(8,128)(2,1)S(1)} collective-permute-done((bf16[128,1024]{1,0:T(8,128)(2,1)S(1)}, bf16[128,1024]{1,0:T(8,128)(2,1)S(1)}, u32[]{:S(2)}, u32[]{:S(2)}) %collective-permute-start.20) | collective-permute-done | bytes 262176 | tf_op jit(solution)/shard_map/ppermute | solution.py:29
  100.0 4.8 %collective-permute-done.25.refs_3_ = bf16[384,768]{1,0:T(8,128)(2,1)S(1)} collective-permute-done((bf16[384,768]{1,0:T(8,128)(2,1)S(1)}, bf16[384,768]{1,0:T(8,128)(2,1)S(1)}, u32[]{:S(2)}, u32[]{:S(2)}) %collective-permute-start.25) | collective-permute-done | bytes 589856 | tf_op jit(solution)/shard_map/ppermute | solution.py:66
  104.9 5.4 %collective-permute-done.28.refs_0_.refs_9_ = bf16[256,1024]{1,0:T(8,128)(2,1)S(1)} collective-permute-done((bf16[256,1024]{1,0:T(8,128)(2,1)S(1)}, bf16[256,1024]{1,0:T(8,128)(2,1)S(1)}, u32[]{:S(2)}, u32[]{:S(2)}) %collective-permute-start.28) | collective-permute-done | bytes 524320 | tf_op jit(solution)/shard_map/ppermute | solution.py:29
  111.0 2.3 collective-permute-start.31
  113.3 4.0 %prepare.1 = (bf16[1024,1536]{1,0:T(8,128)(2,1)S(1)}, bf16[768,1024]{1,0:T(8,128)(2,1)S(1)}, bf16[1024,1024]{1,0:T(8,128)(2,1)S(1)}, f32[256,768]{1,0:T(8,128)S(...) custom-call(s32[7]{0:T(128)S(1)} %pad_add_fusion.info.refs_0_, ...), custom_call_target="tpu_custom_call" | custom-call | tf_op jit(solution)/shard_map/prepare/pallas_call | solution.py:547
  117.2 1.9 feed.3
  119.1 3.7 %feed.4 = (bf16[256,768]{1,0:T(8,128)(2,1)S(1)}, bf16[256,1536]{1,0:T(8,128)(2,1)S(1)}, bf16[256,768]{1,0:T(8,128)(2,1)S(1)}, bf16[256,1536]{1,0:T(8,128)(2,1)S(...) custom-call(bf16[256,1024]{1,0:T(8,128)(2,1)S(1)} %collective-permut, ...), custom_call_target="tpu_custom_call" | custom-call | tf_op jit(solution)/shard_map/feed/pallas_call | solution.py:547
  122.8 1.9 feed.5
  124.9 2.3 collective-permute-start.33
  127.2 6.6 %feed_weights.1 = (f32[4,384,768]{2,1,0:T(8,128)S(1)}, bf16[4,384,768]{2,1,0:T(8,128)(2,1)S(1)}) custom-call(s32[7]{0:T(128)S(1)} %pad_add_fusion.info.refs_0_, bf16[1024,1024]{1,0:T(8,128)(2,1)S(1)} %get-tuple-element.219.cotangent, bf16[256,768]{1,0:T(8,128)(2,1)S(1)} %get-tuple-element.236.refs_0_, bf16[256,768]{1,0:T(8,128)(2,1)S(1)} %get-tuple-element.237.refs_1_, ...), custom_call_target="tpu_custom_call" | custom-call | tf_op jit(solution)/shard_map/feed_weights/pallas_call | solution.py:547
  135.2 1.7 collective-permute-start.35
  137.2 2.5 collective-permute-done.36
  141.2 2.7 collective-permute-done.35.refs_5_
  143.9 1.4 collective-permute-done.34.refs_4_
  146.4 1.4 collective-permute-start.38
  147.8 11.4 %collective-permute-done.37.refs_1_ = bf16[256,1024]{1,0:T(8,128)(2,1)S(1)} collective-permute-done((bf16[256,1024]{1,0:T(8,128)(2,1)S(1)}, bf16[256,1024]{1,0:T(8,128)(2,1)S(1)}, u32[]{:S(2)}, u32[]{:S(2)}) %collective-permute-start.37) | collective-permute-done | bytes 524320 | tf_op jit(solution)/shard_map/ppermute | solution.py:29
  159.6 1.5 collective-permute-start.40
  163.4 1.8 down.2
  167.0 4.1 %mixed_grad.1 = (bf16[4,256,512]{2,1,0:T(8,128)(2,1)S(1)}, f32[4,64,1024]{2,1,0:T(8,128)S(1)}, bf16[4,64,1024]{2,1,0:T(8,128)(2,1)}) custom-call(s32[7]{0:T(128)S(1)} %pad_add_fusion.info.refs_0_, bf16[512,1024]{1,0:T(8,128)(2,1)S(1)} %get-tuple-element.246.out_ref, bf16[256,1024]{1,0:T(8,128)(2,1)S(1)} %get-tuple-element.247.refs_0_.residual, ...), custom_call_target="tpu_custom_call" | custom-call | tf_op jit(solution)/shard_map/mixed_grad/pallas_call | solution.py:547
  172.2 2.1 collective-permute-done.42.crossed
  175.6 1.5 collective-permute-start.46
  177.6 1.6 collective-permute-start.48
  179.2 9.8 %attend_back.2 = (bf16[1024,512]{1,0:T(8,128)(2,1)S(1)}, f32[4,144,512]{2,1,0:T(8,128)S(1)}, bf16[4,144,512]{2,1,0:T(8,128)(2,1)S(1)}) custom-call(s32[7]{0:T(128)S(1)} %pad_add_fusion.info.refs_0_, f32[2,4,1,512]{3,2,1,0:T(1,128)S(1)} %get-tuple-element.245.refs_1_, bf16[4,256,512]{2,1,0:T(8,128)(2,1)S(1)} %get-tuple-element.274.refs_2_, ...), custom_call_target="tpu_custom_call" | custom-call | tf_op jit(solution)/shard_map/attend_back/pallas_call | solution.py:547
  193.3 4.1 %collective-permute-start.57 = (bf16[272,512]{1,0:T(8,128)(2,1)S(1)}, bf16[272,512]{1,0:T(8,128)(2,1)S(1)}, u32[]{:S(2)}, u32[]{:S(2)}) collective-permute-start(bf16[272,512]{1,0:T(8,128)(2,1)S(1)} %pad_maximum_fusion.6), channel_id=1, source_target_pairs={{0,2},{1,3},{2,4},{3,5},{4,6},{5,7},{6,0},{7,1},{8,10},{9,11},{10,... | collective-permute-start | bytes 835592 | tf_op jit(solution)/shard_map/ppermute | solution.py:66
  197.4 9.6 %attend_back.3 = (bf16[1024,512]{1,0:T(8,128)(2,1)S(1)}, f32[4,144,512]{2,1,0:T(8,128)S(1)}, bf16[4,144,512]{2,1,0:T(8,128)(2,1)S(1)}) custom-call(s32[7]{0:T(128)S(1)} %pad_add_fusion.info.refs_0_, f32[2,4,1,512]{3,2,1,0:T(1,128)S(1)} %get-tuple-element.245.refs_1_, bf16[4,256,512]{2,1,0:T(8,128)(2,1)S(1)} %get-tuple-element.274.refs_2_, ...), custom_call_target="tpu_custom_call" | custom-call | tf_op jit(solution)/shard_map/attend_back/pallas_call | solution.py:547
  207.0 1.4 collective-permute-done.69
  208.7 1.4 collective-permute-start.70
  210.6 3.3 %collective-permute-done.57 = bf16[272,512]{1,0:T(8,128)(2,1)S(1)} collective-permute-done((bf16[272,512]{1,0:T(8,128)(2,1)S(1)}, bf16[272,512]{1,0:T(8,128)(2,1)S(1)}, u32[]{:S(2)}, u32[]{:S(2)}) %collective-permute-start.57) | collective-permute-done | bytes 278560 | tf_op jit(solution)/shard_map/ppermute | solution.py:66
  214.2 1.4 collective-permute-start.51
  215.8 8.4 %collective-permute-done.58 = bf16[272,512]{1,0:T(8,128)(2,1)S(1)} collective-permute-done((bf16[272,512]{1,0:T(8,128)(2,1)S(1)}, bf16[272,512]{1,0:T(8,128)(2,1)S(1)}, u32[]{:S(2)}, u32[]{:S(2)}) %collective-permute-start.58) | collective-permute-done | bytes 278560 | tf_op jit(solution)/shard_map/ppermute | solution.py:66
  225.5 3.3 %collective-permute-done.51.refs_4_ = bf16[128,1024]{1,0:T(8,128)(2,1)S(1)} collective-permute-done((bf16[128,1024]{1,0:T(8,128)(2,1)S(1)}, bf16[128,1024]{1,0:T(8,128)(2,1)S(1)}, u32[]{:S(2)}, u32[]{:S(2)}) %collective-permute-start.51) | collective-permute-done | bytes 262176 | tf_op jit(solution)/shard_map/ppermute | solution.py:29
  228.8 2.3 collective-permute-done.50.refs_3_
  234.2 4.0 %normed_grad.1 = (bf16[256,1024]{1,0:T(8,128)(2,1)S(1)}, bf16[256,1024]{1,0:T(8,128)(2,1)S(1)}, f32[128,1024]{1,0:T(8,128)S(1)}, f32[128,1024]{1,0:T(8,128)S(1)}, f32[256,1024]{1,0:T(8,128)S(1)}) custom-call(bf16[1024,512]{1,0:T(8,128)(2,1)S(1)} %get-tuple-element.282.refs_0_, bf16[1024,512]{1,0:T(8,128)(2,1)S(1)} %get-tuple-element.283.refs_1_, ...), custom_call_target="tpu_custom_call" | custom-call | tf_op jit(solution)/shard_map/normed_grad/pallas_call | solution.py:547
  238.1 1.6 collective-permute-start.54
  240.6 6.9 %collective-permute-done.64 = bf16[144,512]{1,0:T(8,128)(2,1)S(1)} collective-permute-done((bf16[144,512]{1,0:T(8,128)(2,1)S(1)}, bf16[144,512]{1,0:T(8,128)(2,1)S(1)}, u32[]{:S(2)}, u32[]{:S(2)}) %collective-permute-start.64) | collective-permute-done | bytes 147488 | tf_op jit(solution)/shard_map/ppermute | solution.py:66
  247.8 1.4 collective-permute-start.60
  249.8 3.8 %unpack_feed.1 = (f32[128,3072]{1,0:T(8,128)}, f32[128,3072]{1,0:T(8,128)}, f32[384,1024]{1,0:T(8,128)}) custom-call(s32[3]{0:T(128)S(1)} %copy-done.18, bf16[384,768]{1,0:T(8,128)(2,1)S(1)} %fusion.refs_0_, bf16[384,768]{1,0:T(8,128)(2,1)S(1)} %collective-permute-done.70.refs_1_, bf16[384,768]{1,0:T(8,128)(2,1)S(1)} %collective-permute-done.71.refs_2_, ...), custom_call_target="tpu_custom_call" | custom-call | tf_op jit(solution)/shard_map/unpack_feed/pallas_call | solution.py:547
  257.5 3.1 %collective-permute-done.60.refs_1_ = bf16[272,512]{1,0:T(8,128)(2,1)S(1)} collective-permute-done((bf16[272,512]{1,0:T(8,128)(2,1)S(1)}, bf16[272,512]{1,0:T(8,128)(2,1)S(1)}, u32[]{:S(2)}, u32[]{:S(2)}) %collective-permute-start.60) | collective-permute-done | bytes 278560 | tf_op jit(solution)/shard_map/ppermute | solution.py:29
  261.1 1.6 collective-permute-start.68
  262.7 1.5 collective-permute-start.56
  264.2 2.4 collective-permute-done.62.refs_3_
  266.5 1.5 collective-permute-start.55
  268.0 1.7 collective-permute-done.66.refs_5_
  270.3 2.6 collective-permute-done.68.refs_7_
  272.9 2.4 unpack_attend.1
  276.4 1.4 final.1
  (222 shorter events, 44.3 us)
Async XLA Ops:
  4.1 19.7 %collective-permute-start.1 = (bf16[208,1024]{1,0:T(8,128)(2,1)}, bf16[208,1024]{1,0:T(8,128)(2,1)S(1)}, u32[]{:S(2)}, u32[]{:S(2)}) collective-permute-start(bf16[208,1024]{1,0:T(8,128)(2,1)} %pack.1.refs_0_), channel_id=1, source_target_pairs={{0,1},{1,0},{2,3},{3,2},{4,5},{5,4},{6,7},{7,6},{8,9},{9,8},{10,11... | collective-permute-start | bytes 1277960 | tf_op jit(solution)/shard_map/ppermute | solution.py:71
  4.9 30.2 %collective-permute-start.6 = (bf16[256,1024]{1,0:T(8,128)(2,1)S(1)}, bf16[256,1024]{1,0:T(8,128)(2,1)S(1)}, u32[]{:S(2)}, u32[]{:S(2)}) collective-permute-start(bf16[256,1024]{1,0:T(8,128)(2,1)S(1)} %get-tuple-element.162.refs_9_), channel_id=1, source_target_pairs={{0,16},{8,24},{16,0},{24,8},{1,17},{9,25},{17,1},{25,9},{2,18},{10... | collective-permute-start | bytes 1572872 | tf_op jit(solution)/shard_map/ppermute | solution.py:29
  7.5 27.6 %collective-permute-start.4 = (bf16[256,1024]{1,0:T(8,128)(2,1)S(1)}, bf16[256,1024]{1,0:T(8,128)(2,1)S(1)}, u32[]{:S(2)}, u32[]{:S(2)}) collective-permute-start(bf16[256,1024]{1,0:T(8,128)(2,1)S(1)} %get-tuple-element.162.refs_9_), channel_id=1, source_target_pairs={{0,8},{8,0},{16,24},{24,16},{1,9},{9,1},{17,25},{25,17},{2,10},{10... | collective-permute-start | bytes 1572872 | tf_op jit(solution)/shard_map/ppermute | solution.py:29
  9.0 13.5 %collective-permute-start = (bf16[208,1024]{1,0:T(8,128)(2,1)S(1)}, bf16[208,1024]{1,0:T(8,128)(2,1)S(1)}, u32[]{:S(2)}, u32[]{:S(2)}) collective-permute-start(bf16[208,1024]{1,0:T(8,128)(2,1)S(1)} %copy-done.4), channel_id=1, source_target_pairs={{0,2},{1,3},{2,4},{3,5},{4,6},{5,7},{6,0},{7,1},{8,10},{9,11},{10,... | collective-permute-start | bytes 1277960 | tf_op jit(solution)/shard_map/ppermute | solution.py:66
  10.5 22.2 %collective-permute-start.3 = (bf16[256,1024]{1,0:T(8,128)(2,1)S(1)}, bf16[256,1024]{1,0:T(8,128)(2,1)S(1)}, u32[]{:S(2)}, u32[]{:S(2)}) collective-permute-start(bf16[256,1024]{1,0:T(8,128)(2,1)S(1)} %get-tuple-element.161.refs_8_), channel_id=1, source_target_pairs={{0,8},{8,0},{16,24},{24,16},{1,9},{9,1},{17,25},{25,17},{2,10},{10... | collective-permute-start | bytes 1572872 | tf_op jit(solution)/shard_map/ppermute | solution.py:29
  22.5 13.0 %collective-permute-start.5 = (bf16[256,1024]{1,0:T(8,128)(2,1)S(1)}, bf16[256,1024]{1,0:T(8,128)(2,1)S(1)}, u32[]{:S(2)}, u32[]{:S(2)}) collective-permute-start(bf16[256,1024]{1,0:T(8,128)(2,1)S(1)} %get-tuple-element.161.refs_8_), channel_id=1, source_target_pairs={{0,16},{8,24},{16,0},{24,8},{1,17},{9,25},{17,1},{25,9},{2,18},{10... | collective-permute-start | bytes 1572872 | tf_op jit(solution)/shard_map/ppermute | solution.py:29
  23.8 12.4 %collective-permute-start.2 = (bf16[208,1024]{1,0:T(8,128)(2,1)S(1)}, bf16[208,1024]{1,0:T(8,128)(2,1)S(1)}, u32[]{:S(2)}, u32[]{:S(2)}) collective-permute-start(bf16[208,1024]{1,0:T(8,128)(2,1)S(1)} %collective-permute-done.refs_1_), channel_id=1, source_target_pairs={{0,2},{1,3},{2,4},{3,5},{4,6},{5,7},{6,0},{7,1},{8,10},{9,11},{10,... | collective-permute-start | bytes 1277960 | tf_op jit(solution)/shard_map/ppermute | solution.py:66
  36.3 12.9 %collective-permute-start.8 = (bf16[208,1024]{1,0:T(8,128)(2,1)S(1)}, bf16[208,1024]{1,0:T(8,128)(2,1)S(1)}, u32[]{:S(2)}, u32[]{:S(2)}) collective-permute-start(bf16[208,1024]{1,0:T(8,128)(2,1)S(1)} %collective-permute-done.2.refs_2_), channel_id=1, source_target_pairs={{0,2},{1,3},{2,4},{3,5},{4,6},{5,7},{6,0},{7,1},{8,10},{9,11},{10,... | collective-permute-start | bytes 1277960 | tf_op jit(solution)/shard_map/ppermute | solution.py:66
  36.7 15.4 %collective-permute-start.11 = (bf16[256,1024]{1,0:T(8,128)(2,1)S(1)}, bf16[256,1024]{1,0:T(8,128)(2,1)S(1)}, u32[]{:S(2)}, u32[]{:S(2)}) collective-permute-start(bf16[256,1024]{1,0:T(8,128)(2,1)S(1)} %collective-permute-done.3.refs_10_), channel_id=1, source_target_pairs={{0,16},{8,24},{16,0},{24,8},{1,17},{9,25},{17,1},{25,9},{2,18},{10... | collective-permute-start | bytes 1572872 | tf_op jit(solution)/shard_map/ppermute | solution.py:29
  37.9 14.8 %collective-permute-start.12 = (bf16[256,1024]{1,0:T(8,128)(2,1)S(1)}, bf16[256,1024]{1,0:T(8,128)(2,1)S(1)}, u32[]{:S(2)}, u32[]{:S(2)}) collective-permute-start(bf16[256,1024]{1,0:T(8,128)(2,1)S(1)} %collective-permute-done.6.refs_13_), channel_id=1, source_target_pairs={{0,8},{8,0},{16,24},{24,16},{1,9},{9,1},{17,25},{25,17},{2,10},{10... | collective-permute-start | bytes 1572872 | tf_op jit(solution)/shard_map/ppermute | solution.py:29
  38.7 15.4 %collective-permute-start.9 = (bf16[208,1024]{1,0:T(8,128)(2,1)S(1)}, bf16[208,1024]{1,0:T(8,128)(2,1)S(1)}, u32[]{:S(2)}, u32[]{:S(2)}) collective-permute-start(bf16[208,1024]{1,0:T(8,128)(2,1)S(1)} %collective-permute-done.2.refs_2_), channel_id=1, source_target_pairs={{0,1},{1,0},{2,3},{3,2},{4,5},{5,4},{6,7},{7,6},{8,9},{9,8},{10,11... | collective-permute-start | bytes 1277960 | tf_op jit(solution)/shard_map/ppermute | solution.py:71
  50.6 12.6 %collective-permute-start.13 = (bf16[64,1024]{1,0:T(8,128)(2,1)S(1)}, bf16[64,1024]{1,0:T(8,128)(2,1)S(1)}, u32[]{:S(2)}, u32[]{:S(2)}) collective-permute-start(bf16[64,1024]{1,0:T(8,128)(2,1)S(1)} %get-tuple-element.171), channel_id=1, source_target_pairs={{0,8},{8,0},{16,24},{24,16},{1,9},{9,1},{17,25},{25,17},{2,10},{10... | collective-permute-start | bytes 393224 | tf_op jit(solution)/shard_map/ppermute | solution.py:29
  52.1 11.0 %collective-permute-start.14 = (bf16[64,1024]{1,0:T(8,128)(2,1)S(1)}, bf16[64,1024]{1,0:T(8,128)(2,1)S(1)}, u32[]{:S(2)}, u32[]{:S(2)}) collective-permute-start(bf16[64,1024]{1,0:T(8,128)(2,1)S(1)} %get-tuple-element.172), channel_id=1, source_target_pairs={{0,16},{8,24},{16,0},{24,8},{1,17},{9,25},{17,1},{25,9},{2,18},{10... | collective-permute-start | bytes 393224 | tf_op jit(solution)/shard_map/ppermute | solution.py:29
  52.6 10.5 %collective-permute-start.15 = (bf16[64,1024]{1,0:T(8,128)(2,1)S(1)}, bf16[64,1024]{1,0:T(8,128)(2,1)S(1)}, u32[]{:S(2)}, u32[]{:S(2)}) collective-permute-start(bf16[64,1024]{1,0:T(8,128)(2,1)S(1)} %get-tuple-element.173), channel_id=1, source_target_pairs={{0,24},{8,16},{16,8},{24,0},{1,25},{9,17},{17,9},{25,1},{2,26},{10... | collective-permute-start | bytes 393224 | tf_op jit(solution)/shard_map/ppermute | solution.py:29
  54.1 18.1 %collective-permute-start.22 = (bf16[384,768]{1,0:T(8,128)(2,1)S(1)}, bf16[384,768]{1,0:T(8,128)(2,1)S(1)}, u32[]{:S(2)}, u32[]{:S(2)}) collective-permute-start(bf16[384,768]{1,0:T(8,128)(2,1)S(1)} %pack_feed.1.refs_0_), channel_id=1, source_target_pairs={{0,1},{1,0},{2,3},{3,2},{4,5},{5,4},{6,7},{7,6},{8,9},{9,8},{10,11... | collective-permute-start | bytes 1769480 | tf_op jit(solution)/shard_map/ppermute | solution.py:71
  54.1 18.1 %collective-permute-start.21 = (bf16[384,768]{1,0:T(8,128)(2,1)S(1)}, bf16[384,768]{1,0:T(8,128)(2,1)S(1)}, u32[]{:S(2)}, u32[]{:S(2)}) collective-permute-start(bf16[384,768]{1,0:T(8,128)(2,1)S(1)} %pack_feed.1.refs_0_), channel_id=1, source_target_pairs={{0,2},{1,3},{2,4},{3,5},{4,6},{5,7},{6,0},{7,1},{8,10},{9,11},{10,... | collective-permute-start | bytes 1769480 | tf_op jit(solution)/shard_map/ppermute | solution.py:66
  63.2 9.0 %collective-permute-start.16 = (bf16[256,1024]{1,0:T(8,128)(2,1)S(1)}, bf16[256,1024]{1,0:T(8,128)(2,1)S(1)}, u32[]{:S(2)}, u32[]{:S(2)}) collective-permute-start(bf16[256,1024]{1,0:T(8,128)(2,1)S(1)} %pad_maximum_fusion.4), channel_id=1, source_target_pairs={{0,1},{1,0},{2,3},{3,2},{4,5},{5,4},{6,7},{7,6},{8,9},{9,8},{10,11... | collective-permute-start | bytes 1572872 | tf_op jit(solution)/shard_map/ppermute | solution.py:71
  72.2 16.7 %collective-permute-start.23 = (bf16[384,768]{1,0:T(8,128)(2,1)S(1)}, bf16[384,768]{1,0:T(8,128)(2,1)S(1)}, u32[]{:S(2)}, u32[]{:S(2)}) collective-permute-start(bf16[384,768]{1,0:T(8,128)(2,1)S(1)} %collective-permute-done.21.refs_1_), channel_id=1, source_target_pairs={{0,2},{1,3},{2,4},{3,5},{4,6},{5,7},{6,0},{7,1},{8,10},{9,11},{10,... | collective-permute-start | bytes 1769480 | tf_op jit(solution)/shard_map/ppermute | solution.py:66
  72.2 16.7 %collective-permute-start.24 = (bf16[384,768]{1,0:T(8,128)(2,1)S(1)}, bf16[384,768]{1,0:T(8,128)(2,1)S(1)}, u32[]{:S(2)}, u32[]{:S(2)}) collective-permute-start(bf16[384,768]{1,0:T(8,128)(2,1)S(1)} %collective-permute-done.21.refs_1_), channel_id=1, source_target_pairs={{0,1},{1,0},{2,3},{3,2},{4,5},{5,4},{6,7},{7,6},{8,9},{9,8},{10,11... | collective-permute-start | bytes 1769480 | tf_op jit(solution)/shard_map/ppermute | solution.py:71
  74.2 14.9 %collective-permute-start.18 = (bf16[256,1024]{1,0:T(8,128)(2,1)S(1)}, bf16[256,1024]{1,0:T(8,128)(2,1)S(1)}, u32[]{:S(2)}, u32[]{:S(2)}) collective-permute-start(bf16[256,1024]{1,0:T(8,128)(2,1)S(1)} %get-tuple-element.180), channel_id=1, source_target_pairs={{0,16},{8,24},{16,0},{24,8},{1,17},{9,25},{17,1},{25,9},{2,18},{10... | collective-permute-start | bytes 1572872 | tf_op jit(solution)/shard_map/ppermute | solution.py:29
  74.8 15.9 %collective-permute-start.17 = (bf16[256,1024]{1,0:T(8,128)(2,1)S(1)}, bf16[256,1024]{1,0:T(8,128)(2,1)S(1)}, u32[]{:S(2)}, u32[]{:S(2)}) collective-permute-start(bf16[256,1024]{1,0:T(8,128)(2,1)S(1)} %get-tuple-element.179), channel_id=1, source_target_pairs={{0,8},{8,0},{16,24},{24,16},{1,9},{9,1},{17,25},{25,17},{2,10},{10... | collective-permute-start | bytes 1572872 | tf_op jit(solution)/shard_map/ppermute | solution.py:29
  88.9 15.9 %collective-permute-start.25 = (bf16[384,768]{1,0:T(8,128)(2,1)S(1)}, bf16[384,768]{1,0:T(8,128)(2,1)S(1)}, u32[]{:S(2)}, u32[]{:S(2)}) collective-permute-start(bf16[384,768]{1,0:T(8,128)(2,1)S(1)} %collective-permute-done.23.refs_2_), channel_id=1, source_target_pairs={{0,2},{1,3},{2,4},{3,5},{4,6},{5,7},{6,0},{7,1},{8,10},{9,11},{10,... | collective-permute-start | bytes 1769480 | tf_op jit(solution)/shard_map/ppermute | solution.py:66
  89.1 7.5 %collective-permute-start.20 = (bf16[128,1024]{1,0:T(8,128)(2,1)S(1)}, bf16[128,1024]{1,0:T(8,128)(2,1)S(1)}, u32[]{:S(2)}, u32[]{:S(2)}) collective-permute-start(bf16[128,1024]{1,0:T(8,128)(2,1)S(1)} %add_convert_fusion.7), channel_id=1, source_target_pairs={{0,8},{8,0},{16,24},{24,16},{1,9},{9,1},{17,25},{25,17},{2,10},{10... | collective-permute-start | bytes 786440 | tf_op jit(solution)/shard_map/ppermute | solution.py:29
  98.4 11.9 %collective-permute-start.28 = (bf16[256,1024]{1,0:T(8,128)(2,1)S(1)}, bf16[256,1024]{1,0:T(8,128)(2,1)S(1)}, u32[]{:S(2)}, u32[]{:S(2)}) collective-permute-start(bf16[256,1024]{1,0:T(8,128)(2,1)S(1)} %get-tuple-element.187.refs_0_.refs_8_), channel_id=1, source_target_pairs={{0,8},{8,0},{16,24},{24,16},{1,9},{9,1},{17,25},{25,17},{2,10},{10... | collective-permute-start | bytes 1572872 | tf_op jit(solution)/shard_map/ppermute | solution.py:29
  99.0 12.0 %collective-permute-start.29 = (bf16[256,1024]{1,0:T(8,128)(2,1)S(1)}, bf16[256,1024]{1,0:T(8,128)(2,1)S(1)}, u32[]{:S(2)}, u32[]{:S(2)}) collective-permute-start(bf16[256,1024]{1,0:T(8,128)(2,1)S(1)} %get-tuple-element.187.refs_0_.refs_8_), channel_id=1, source_target_pairs={{0,16},{8,24},{16,0},{24,8},{1,17},{9,25},{17,1},{25,9},{2,18},{10... | collective-permute-start | bytes 1572872 | tf_op jit(solution)/shard_map/ppermute | solution.py:29
  100.0 13.2 %collective-permute-start.26 = (bf16[384,768]{1,0:T(8,128)(2,1)S(1)}, bf16[384,768]{1,0:T(8,128)(2,1)S(1)}, u32[]{:S(2)}, u32[]{:S(2)}) collective-permute-start(bf16[384,768]{1,0:T(8,128)(2,1)S(1)} %collective-permute-done.23.refs_2_), channel_id=1, source_target_pairs={{0,1},{1,0},{2,3},{3,2},{4,5},{5,4},{6,7},{7,6},{8,9},{9,8},{10,11... | collective-permute-start | bytes 1769480 | tf_op jit(solution)/shard_map/ppermute | solution.py:71
  104.8 8.4 %collective-permute-start.27 = (bf16[384,768]{1,0:T(8,128)(2,1)S(1)}, bf16[384,768]{1,0:T(8,128)(2,1)S(1)}, u32[]{:S(2)}, u32[]{:S(2)}) collective-permute-start(bf16[384,768]{1,0:T(8,128)(2,1)S(1)} %collective-permute-done.25.refs_3_), channel_id=1, source_target_pairs={{0,1},{1,0},{2,3},{3,2},{4,5},{5,4},{6,7},{7,6},{8,9},{9,8},{10,11... | collective-permute-start | bytes 1769480 | tf_op jit(solution)/shard_map/ppermute | solution.py:71
  110.3 12.5 %collective-permute-start.30 = (bf16[128,1024]{1,0:T(8,128)(2,1)S(1)}, bf16[128,1024]{1,0:T(8,128)(2,1)S(1)}, u32[]{:S(2)}, u32[]{:S(2)}) collective-permute-start(bf16[128,1024]{1,0:T(8,128)(2,1)S(1)} %slice.284), channel_id=1, source_target_pairs={{0,16},{8,24},{16,0},{24,8},{1,17},{9,25},{17,1},{25,9},{2,18},{10... | collective-permute-start | bytes 786440 | tf_op jit(solution)/shard_map/ppermute | solution.py:29
  111.0 11.9 %collective-permute-start.31 = (bf16[128,1024]{1,0:T(8,128)(2,1)S(1)}, bf16[128,1024]{1,0:T(8,128)(2,1)S(1)}, u32[]{:S(2)}, u32[]{:S(2)}) collective-permute-start(bf16[128,1024]{1,0:T(8,128)(2,1)S(1)} %slice.285), channel_id=1, source_target_pairs={{0,8},{8,0},{16,24},{24,16},{1,9},{9,1},{17,25},{25,17},{2,10},{10... | collective-permute-start | bytes 786440 | tf_op jit(solution)/shard_map/ppermute | solution.py:29
  124.8 10.1 %collective-permute-start.32 = (bf16[256,1024]{1,0:T(8,128)(2,1)S(1)}, bf16[256,1024]{1,0:T(8,128)(2,1)S(1)}, u32[]{:S(2)}, u32[]{:S(2)}) collective-permute-start(bf16[256,1024]{1,0:T(8,128)(2,1)S(1)} %get-tuple-element.217), channel_id=1, source_target_pairs={{0,8},{8,0},{16,24},{24,16},{1,9},{9,1},{17,25},{25,17},{2,10},{10... | collective-permute-start | bytes 1572872 | tf_op jit(solution)/shard_map/ppermute | solution.py:29
  124.9 10.1 %collective-permute-start.33 = (bf16[256,1024]{1,0:T(8,128)(2,1)S(1)}, bf16[256,1024]{1,0:T(8,128)(2,1)S(1)}, u32[]{:S(2)}, u32[]{:S(2)}) collective-permute-start(bf16[256,1024]{1,0:T(8,128)(2,1)S(1)} %get-tuple-element.218), channel_id=1, source_target_pairs={{0,16},{8,24},{16,0},{24,8},{1,17},{9,25},{17,1},{25,9},{2,18},{10... | collective-permute-start | bytes 1572872 | tf_op jit(solution)/shard_map/ppermute | solution.py:29
  135.2 8.7 %collective-permute-start.35 = (bf16[128,1024]{1,0:T(8,128)(2,1)S(1)}, bf16[128,1024]{1,0:T(8,128)(2,1)S(1)}, u32[]{:S(2)}, u32[]{:S(2)}) collective-permute-start(bf16[128,1024]{1,0:T(8,128)(2,1)S(1)} %add_convert_fusion.5), channel_id=1, source_target_pairs={{0,8},{8,0},{16,24},{24,16},{1,9},{9,1},{17,25},{25,17},{2,10},{10... | collective-permute-start | bytes 786440 | tf_op jit(solution)/shard_map/ppermute | solution.py:29
  136.9 8.4 %collective-permute-start.34 = (bf16[128,1024]{1,0:T(8,128)(2,1)S(1)}, bf16[128,1024]{1,0:T(8,128)(2,1)S(1)}, u32[]{:S(2)}, u32[]{:S(2)}) collective-permute-start(bf16[128,1024]{1,0:T(8,128)(2,1)S(1)} %add_convert_fusion.6), channel_id=1, source_target_pairs={{0,16},{8,24},{16,0},{24,8},{1,17},{9,25},{17,1},{25,9},{2,18},{10... | collective-permute-start | bytes 786440 | tf_op jit(solution)/shard_map/ppermute | solution.py:29
  139.8 21.3 %collective-permute-start.41 = (bf16[384,768]{1,0:T(8,128)(2,1)S(1)}, bf16[384,768]{1,0:T(8,128)(2,1)S(1)}, u32[]{:S(2)}, u32[]{:S(2)}) collective-permute-start(bf16[384,768]{1,0:T(8,128)(2,1)S(1)} %fusion.3), channel_id=1, source_target_pairs={{0,2},{1,3},{2,4},{3,5},{4,6},{5,7},{6,0},{7,1},{8,10},{9,11},{10,... | collective-permute-start | bytes 1769480 | tf_op jit(solution)/shard_map/ppermute | solution.py:66
  146.0 13.2 %collective-permute-start.37 = (bf16[256,1024]{1,0:T(8,128)(2,1)S(1)}, bf16[256,1024]{1,0:T(8,128)(2,1)S(1)}, u32[]{:S(2)}, u32[]{:S(2)}) collective-permute-start(bf16[256,1024]{1,0:T(8,128)(2,1)S(1)} %get-tuple-element.247.refs_0_.residual), channel_id=1, source_target_pairs={{0,8},{8,0},{16,24},{24,16},{1,9},{9,1},{17,25},{25,17},{2,10},{10... | collective-permute-start | bytes 1572872 | tf_op jit(solution)/shard_map/ppermute | solution.py:29
  146.4 13.2 %collective-permute-start.38 = (bf16[256,1024]{1,0:T(8,128)(2,1)S(1)}, bf16[256,1024]{1,0:T(8,128)(2,1)S(1)}, u32[]{:S(2)}, u32[]{:S(2)}) collective-permute-start(bf16[256,1024]{1,0:T(8,128)(2,1)S(1)} %get-tuple-element.247.refs_0_.residual), channel_id=1, source_target_pairs={{0,16},{8,24},{16,0},{24,8},{1,17},{9,25},{17,1},{25,9},{2,18},{10... | collective-permute-start | bytes 1572872 | tf_op jit(solution)/shard_map/ppermute | solution.py:29
  159.2 7.7 %collective-permute-start.39 = (bf16[128,1024]{1,0:T(8,128)(2,1)S(1)}, bf16[128,1024]{1,0:T(8,128)(2,1)S(1)}, u32[]{:S(2)}, u32[]{:S(2)}) collective-permute-start(bf16[128,1024]{1,0:T(8,128)(2,1)S(1)} %slice.287), channel_id=1, source_target_pairs={{0,16},{8,24},{16,0},{24,8},{1,17},{9,25},{17,1},{25,9},{2,18},{10... | collective-permute-start | bytes 786440 | tf_op jit(solution)/shard_map/ppermute | solution.py:29
  162.1 26.9 %collective-permute-start.49 = (bf16[384,768]{1,0:T(8,128)(2,1)}, bf16[384,768]{1,0:T(8,128)(2,1)}, u32[]{:S(2)}, u32[]{:S(2)}) collective-permute-start(bf16[384,768]{1,0:T(8,128)(2,1)} %fusion.2), channel_id=1, source_target_pairs={{0,2},{1,3},{2,4},{3,5},{4,6},{5,7},{6,0},{7,1},{8,10},{9,11},{10,... | collective-permute-start | bytes 1769480 | tf_op jit(solution)/shard_map/ppermute | solution.py:66
  175.6 15.8 %collective-permute-start.46 = (bf16[64,1024]{1,0:T(8,128)(2,1)S(1)}, bf16[64,1024]{1,0:T(8,128)(2,1)S(1)}, u32[]{:S(2)}, u32[]{:S(2)}) collective-permute-start(bf16[64,1024]{1,0:T(8,128)(2,1)S(1)} %get-tuple-element.257), channel_id=1, source_target_pairs={{0,8},{8,0},{16,24},{24,16},{1,9},{9,1},{17,25},{25,17},{2,10},{10... | collective-permute-start | bytes 393224 | tf_op jit(solution)/shard_map/ppermute | solution.py:29
  177.1 15.2 %collective-permute-start.47 = (bf16[64,1024]{1,0:T(8,128)(2,1)S(1)}, bf16[64,1024]{1,0:T(8,128)(2,1)S(1)}, u32[]{:S(2)}, u32[]{:S(2)}) collective-permute-start(bf16[64,1024]{1,0:T(8,128)(2,1)S(1)} %get-tuple-element.258), channel_id=1, source_target_pairs={{0,16},{8,24},{16,0},{24,8},{1,17},{9,25},{17,1},{25,9},{2,18},{10... | collective-permute-start | bytes 393224 | tf_op jit(solution)/shard_map/ppermute | solution.py:29
  177.6 15.5 %collective-permute-start.48 = (bf16[64,1024]{1,0:T(8,128)(2,1)S(1)}, bf16[64,1024]{1,0:T(8,128)(2,1)S(1)}, u32[]{:S(2)}, u32[]{:S(2)}) collective-permute-start(bf16[64,1024]{1,0:T(8,128)(2,1)S(1)} %get-tuple-element.259), channel_id=1, source_target_pairs={{0,24},{8,16},{16,8},{24,0},{1,25},{9,17},{17,9},{25,1},{2,26},{10... | collective-permute-start | bytes 393224 | tf_op jit(solution)/shard_map/ppermute | solution.py:29
  190.5 18.0 %collective-permute-start.69 = (bf16[384,768]{1,0:T(8,128)(2,1)S(1)}, bf16[384,768]{1,0:T(8,128)(2,1)S(1)}, u32[]{:S(2)}, u32[]{:S(2)}) collective-permute-start(bf16[384,768]{1,0:T(8,128)(2,1)S(1)} %fusion.1), channel_id=1, source_target_pairs={{0,2},{1,3},{2,4},{3,5},{4,6},{5,7},{6,0},{7,1},{8,10},{9,11},{10,... | collective-permute-start | bytes 1769480 | tf_op jit(solution)/shard_map/ppermute | solution.py:66
  191.4 19.3 %collective-permute-start.43 = (bf16[256,1024]{1,0:T(8,128)(2,1)S(1)}, bf16[256,1024]{1,0:T(8,128)(2,1)S(1)}, u32[]{:S(2)}, u32[]{:S(2)}) collective-permute-start(bf16[256,1024]{1,0:T(8,128)(2,1)S(1)} %copy-done.22), channel_id=1, source_target_pairs={{0,8},{8,0},{16,24},{24,16},{1,9},{9,1},{17,25},{25,17},{2,10},{10... | collective-permute-start | bytes 1572872 | tf_op jit(solution)/shard_map/ppermute | solution.py:29
  192.3 18.4 %collective-permute-start.44 = (bf16[256,1024]{1,0:T(8,128)(2,1)S(1)}, bf16[256,1024]{1,0:T(8,128)(2,1)S(1)}, u32[]{:S(2)}, u32[]{:S(2)}) collective-permute-start(bf16[256,1024]{1,0:T(8,128)(2,1)S(1)} %copy-done.20), channel_id=1, source_target_pairs={{0,16},{8,24},{16,0},{24,8},{1,17},{9,25},{17,1},{25,9},{2,18},{10... | collective-permute-start | bytes 1572872 | tf_op jit(solution)/shard_map/ppermute | solution.py:29
  193.3 20.6 %collective-permute-start.57 = (bf16[272,512]{1,0:T(8,128)(2,1)S(1)}, bf16[272,512]{1,0:T(8,128)(2,1)S(1)}, u32[]{:S(2)}, u32[]{:S(2)}) collective-permute-start(bf16[272,512]{1,0:T(8,128)(2,1)S(1)} %pad_maximum_fusion.6), channel_id=1, source_target_pairs={{0,2},{1,3},{2,4},{3,5},{4,6},{5,7},{6,0},{7,1},{8,10},{9,11},{10,... | collective-permute-start | bytes 835592 | tf_op jit(solution)/shard_map/ppermute | solution.py:66
  208.7 23.4 %collective-permute-start.70 = (bf16[384,768]{1,0:T(8,128)(2,1)S(1)}, bf16[384,768]{1,0:T(8,128)(2,1)S(1)}, u32[]{:S(2)}, u32[]{:S(2)}) collective-permute-start(bf16[384,768]{1,0:T(8,128)(2,1)S(1)} %fusion.refs_0_), channel_id=1, source_target_pairs={{0,8},{8,0},{16,24},{24,16},{1,9},{9,1},{17,25},{25,17},{2,10},{10... | collective-permute-start | bytes 1769480 | tf_op jit(solution)/shard_map/ppermute | solution.py:29
  210.1 23.2 %collective-permute-start.71 = (bf16[384,768]{1,0:T(8,128)(2,1)S(1)}, bf16[384,768]{1,0:T(8,128)(2,1)S(1)}, u32[]{:S(2)}, u32[]{:S(2)}) collective-permute-start(bf16[384,768]{1,0:T(8,128)(2,1)S(1)} %fusion.refs_0_), channel_id=1, source_target_pairs={{0,16},{8,24},{16,0},{24,8},{1,17},{9,25},{17,1},{25,9},{2,18},{10... | collective-permute-start | bytes 1769480 | tf_op jit(solution)/shard_map/ppermute | solution.py:29
  210.6 14.7 %collective-permute-start.52 = (bf16[4,144,512]{2,1,0:T(8,128)(2,1)S(1)}, bf16[4,144,512]{2,1,0:T(8,128)(2,1)S(1)}, u32[]{:S(2)}, u32[]{:S(2)}) collective-permute-start(bf16[4,144,512]{2,1,0:T(8,128)(2,1)S(1)} %get-tuple-element.281), channel_id=1, source_target_pairs={{0,1},{1,0},{2,3},{3,2},{4,5},{5,4},{6,7},{7,6},{8,9},{9,8},{10,11... | collective-permute-start | bytes 1769480 | tf_op jit(solution)/shard_map/ppermute | solution.py:71
  214.1 10.1 %collective-permute-start.58 = (bf16[272,512]{1,0:T(8,128)(2,1)S(1)}, bf16[272,512]{1,0:T(8,128)(2,1)S(1)}, u32[]{:S(2)}, u32[]{:S(2)}) collective-permute-start(bf16[272,512]{1,0:T(8,128)(2,1)S(1)} %pad_maximum_fusion.7), channel_id=1, source_target_pairs={{0,2},{1,3},{2,4},{3,5},{4,6},{5,7},{6,0},{7,1},{8,10},{9,11},{10,... | collective-permute-start | bytes 835592 | tf_op jit(solution)/shard_map/ppermute | solution.py:66
  214.2 14.5 %collective-permute-start.51 = (bf16[128,1024]{1,0:T(8,128)(2,1)S(1)}, bf16[128,1024]{1,0:T(8,128)(2,1)S(1)}, u32[]{:S(2)}, u32[]{:S(2)}) collective-permute-start(bf16[128,1024]{1,0:T(8,128)(2,1)S(1)} %add_convert_fusion.3), channel_id=1, source_target_pairs={{0,8},{8,0},{16,24},{24,16},{1,9},{9,1},{17,25},{25,17},{2,10},{10... | collective-permute-start | bytes 786440 | tf_op jit(solution)/shard_map/ppermute | solution.py:29
  225.3 15.1 %collective-permute-start.59 = (bf16[272,512]{1,0:T(8,128)(2,1)S(1)}, bf16[272,512]{1,0:T(8,128)(2,1)S(1)}, u32[]{:S(2)}, u32[]{:S(2)}) collective-permute-start(bf16[272,512]{1,0:T(8,128)(2,1)S(1)} %pad_maximum_fusion.8), channel_id=1, source_target_pairs={{0,2},{1,3},{2,4},{3,5},{4,6},{5,7},{6,0},{7,1},{8,10},{9,11},{10,... | collective-permute-start | bytes 835592 | tf_op jit(solution)/shard_map/ppermute | solution.py:66
  228.7 11.0 %collective-permute-start.63 = (bf16[144,512]{1,0:T(8,128)(2,1)S(1)}, bf16[144,512]{1,0:T(8,128)(2,1)S(1)}, u32[]{:S(2)}, u32[]{:S(2)}) collective-permute-start(bf16[144,512]{1,0:T(8,128)(2,1)S(1)} %fusion.12), channel_id=1, source_target_pairs={{0,2},{1,3},{2,4},{3,5},{4,6},{5,7},{6,0},{7,1},{8,10},{9,11},{10,... | collective-permute-start | bytes 442376 | tf_op jit(solution)/shard_map/ppermute | solution.py:66
  232.1 15.7 %collective-permute-start.72 = (bf16[192,768]{1,0:T(8,128)(2,1)S(1)}, bf16[192,768]{1,0:T(8,128)(2,1)S(1)}, u32[]{:S(2)}, u32[]{:S(2)}) collective-permute-start(bf16[192,768]{1,0:T(8,128)(2,1)S(1)} %slice.310), channel_id=1, source_target_pairs={{0,16},{8,24},{16,0},{24,8},{1,17},{9,25},{17,1},{25,9},{2,18},{10... | collective-permute-start | bytes 884744 | tf_op jit(solution)/shard_map/ppermute | solution.py:29
  233.3 16.0 %collective-permute-start.73 = (bf16[192,768]{1,0:T(8,128)(2,1)S(1)}, bf16[192,768]{1,0:T(8,128)(2,1)S(1)}, u32[]{:S(2)}, u32[]{:S(2)}) collective-permute-start(bf16[192,768]{1,0:T(8,128)(2,1)S(1)} %slice.311), channel_id=1, source_target_pairs={{0,8},{8,0},{16,24},{24,16},{1,9},{9,1},{17,25},{25,17},{2,10},{10... | collective-permute-start | bytes 884744 | tf_op jit(solution)/shard_map/ppermute | solution.py:29
  238.1 17.9 %collective-permute-start.54 = (bf16[256,1024]{1,0:T(8,128)(2,1)S(1)}, bf16[256,1024]{1,0:T(8,128)(2,1)S(1)}, u32[]{:S(2)}, u32[]{:S(2)}) collective-permute-start(bf16[256,1024]{1,0:T(8,128)(2,1)S(1)} %get-tuple-element.286), channel_id=1, source_target_pairs={{0,16},{8,24},{16,0},{24,8},{1,17},{9,25},{17,1},{25,9},{2,18},{10... | collective-permute-start | bytes 1572872 | tf_op jit(solution)/shard_map/ppermute | solution.py:29
  239.7 21.4 %collective-permute-start.53 = (bf16[256,1024]{1,0:T(8,128)(2,1)S(1)}, bf16[256,1024]{1,0:T(8,128)(2,1)S(1)}, u32[]{:S(2)}, u32[]{:S(2)}) collective-permute-start(bf16[256,1024]{1,0:T(8,128)(2,1)S(1)} %get-tuple-element.285), channel_id=1, source_target_pairs={{0,8},{8,0},{16,24},{24,16},{1,9},{9,1},{17,25},{25,17},{2,10},{10... | collective-permute-start | bytes 1572872 | tf_op jit(solution)/shard_map/ppermute | solution.py:29
  247.8 12.7 %collective-permute-start.60 = (bf16[272,512]{1,0:T(8,128)(2,1)S(1)}, bf16[272,512]{1,0:T(8,128)(2,1)S(1)}, u32[]{:S(2)}, u32[]{:S(2)}) collective-permute-start(bf16[272,512]{1,0:T(8,128)(2,1)S(1)} %pad_maximum_fusion.9.refs_0_), channel_id=1, source_target_pairs={{0,8},{8,0},{16,24},{24,16},{1,9},{9,1},{17,25},{25,17},{2,10},{10... | collective-permute-start | bytes 835592 | tf_op jit(solution)/shard_map/ppermute | solution.py:29
  249.3 13.4 %collective-permute-start.61 = (bf16[272,512]{1,0:T(8,128)(2,1)S(1)}, bf16[272,512]{1,0:T(8,128)(2,1)S(1)}, u32[]{:S(2)}, u32[]{:S(2)}) collective-permute-start(bf16[272,512]{1,0:T(8,128)(2,1)S(1)} %pad_maximum_fusion.9.refs_0_), channel_id=1, source_target_pairs={{0,16},{8,24},{16,0},{24,8},{1,17},{9,25},{17,1},{25,9},{2,18},{10... | collective-permute-start | bytes 835592 | tf_op jit(solution)/shard_map/ppermute | solution.py:29
  254.7 11.8 %collective-permute-start.62 = (bf16[272,512]{1,0:T(8,128)(2,1)S(1)}, bf16[272,512]{1,0:T(8,128)(2,1)S(1)}, u32[]{:S(2)}, u32[]{:S(2)}) collective-permute-start(bf16[272,512]{1,0:T(8,128)(2,1)S(1)} %pad_maximum_fusion.9.refs_0_), channel_id=1, source_target_pairs={{0,24},{8,16},{16,8},{24,0},{1,25},{9,17},{17,9},{25,1},{2,26},{10... | collective-permute-start | bytes 835592 | tf_op jit(solution)/shard_map/ppermute | solution.py:29
  256.1 13.6 %collective-permute-start.66 = (bf16[144,512]{1,0:T(8,128)(2,1)S(1)}, bf16[144,512]{1,0:T(8,128)(2,1)S(1)}, u32[]{:S(2)}, u32[]{:S(2)}) collective-permute-start(bf16[144,512]{1,0:T(8,128)(2,1)S(1)} %fusion.6.refs_4_), channel_id=1, source_target_pairs={{0,8},{8,0},{16,24},{24,16},{1,9},{9,1},{17,25},{25,17},{2,10},{10... | collective-permute-start | bytes 442376 | tf_op jit(solution)/shard_map/ppermute | solution.py:29
  260.6 9.7 %collective-permute-start.67 = (bf16[144,512]{1,0:T(8,128)(2,1)S(1)}, bf16[144,512]{1,0:T(8,128)(2,1)S(1)}, u32[]{:S(2)}, u32[]{:S(2)}) collective-permute-start(bf16[144,512]{1,0:T(8,128)(2,1)S(1)} %fusion.6.refs_4_), channel_id=1, source_target_pairs={{0,16},{8,24},{16,0},{24,8},{1,17},{9,25},{17,1},{25,9},{2,18},{10... | collective-permute-start | bytes 442376 | tf_op jit(solution)/shard_map/ppermute | solution.py:29
  261.1 11.8 %collective-permute-start.68 = (bf16[144,512]{1,0:T(8,128)(2,1)S(1)}, bf16[144,512]{1,0:T(8,128)(2,1)S(1)}, u32[]{:S(2)}, u32[]{:S(2)}) collective-permute-start(bf16[144,512]{1,0:T(8,128)(2,1)S(1)} %fusion.6.refs_4_), channel_id=1, source_target_pairs={{0,24},{8,16},{16,8},{24,0},{1,25},{9,17},{17,9},{25,1},{2,26},{10... | collective-permute-start | bytes 442376 | tf_op jit(solution)/shard_map/ppermute | solution.py:29
  262.7 13.7 %collective-permute-start.56 = (bf16[128,1024]{1,0:T(8,128)(2,1)S(1)}, bf16[128,1024]{1,0:T(8,128)(2,1)S(1)}, u32[]{:S(2)}, u32[]{:S(2)}) collective-permute-start(bf16[128,1024]{1,0:T(8,128)(2,1)S(1)} %add_convert_fusion.1), channel_id=1, source_target_pairs={{0,8},{8,0},{16,24},{24,16},{1,9},{9,1},{17,25},{25,17},{2,10},{10... | collective-permute-start | bytes 786440 | tf_op jit(solution)/shard_map/ppermute | solution.py:29
  266.5 9.9 %collective-permute-start.55 = (bf16[128,1024]{1,0:T(8,128)(2,1)S(1)}, bf16[128,1024]{1,0:T(8,128)(2,1)S(1)}, u32[]{:S(2)}, u32[]{:S(2)}) collective-permute-start(bf16[128,1024]{1,0:T(8,128)(2,1)S(1)} %add_convert_fusion.2), channel_id=1, source_target_pairs={{0,16},{8,24},{16,0},{24,8},{1,17},{9,25},{17,1},{25,9},{2,18},{10... | collective-permute-start | bytes 786440 | tf_op jit(solution)/shard_map/ppermute | solution.py:29
  (38 other events, 354.3 us)

commit v5 on v4

--- a/solution.py
+++ b/solution.py
@@ -1125,7 +1125,7 @@
 
 
 def unpack_attend_kernel(info, *refs):
-    pieces, (query_ref, key_ref, value_ref, out_ref, gain_ref) = (refs[:4], refs[4:8]), refs[8:]
+    pieces, (query_ref, key_ref, value_ref, out_ref, *gain_refs) = (refs[:4], refs[4:8]), refs[8:]
     gains = jnp.zeros((8, GROUP_WIDTH), F32)
     for g in range(GROUPS):
         for j in range(BLOCKS):
@@ -1143,7 +1143,14 @@
                 top = piece[ROWS + 16 : ROWS + 16 + OUT_ROWS, :].astype(F32)
                 out_ref[rows, :GROUP_WIDTH] = top
                 out_ref[rows, GROUP_WIDTH:] = piece[ROWS + 16 + OUT_ROWS :, :].astype(F32)
-    gain_ref[...] = gains
+    gain_refs[0][...] = gains[:1, :ROWS]
+    gain_refs[1][...] = gains[:1, ROWS : 2 * ROWS]
+    shard = 2 * info[1] + info[2]
+    for n, target in enumerate(gain_refs[2:]):
+        width = target.shape[1]
+        lanes = gains[:, 2 * ROWS + n * HEAD_SIZE : 2 * ROWS + (n + 1) * HEAD_SIZE]
+        turned = pltpu.roll(lanes, lax.rem(HEAD_SIZE - shard * width, HEAD_SIZE), 1)
+        target[...] = turned[:1, :width]
 
 
 def ring_parts(value, swapped, then):
@@ -1497,7 +1504,8 @@
         (),
         [pltpu.VMEM((BLOCKS, PACKED, FF_PART), F32)],
     )
-    query_w_grad, key_w_grad, value_w_grad, out_w_grad, gain_full = on_core(
+    head_rows = query_norm.shape[0]
+    query_w_grad, key_w_grad, value_w_grad, out_w_grad, *gains = on_core(
         unpack_attend_kernel,
         "unpack_attend",
         [
@@ -1505,28 +1513,27 @@
             shape((ROWS, KEY_VALUE_HEADS * HEAD_SIZE), F32),
             shape((ROWS, KEY_VALUE_HEADS * HEAD_SIZE), F32),
             shape((SIZE, MODEL_WIDTH), F32),
-            shape((8, GROUP_WIDTH), F32),
+            shape((1, ROWS), F32),
+            shape((1, ROWS), F32),
+            shape((1, head_rows), F32),
+            shape((1, head_rows), F32),
         ],
         (place,),
         (*spread_direct(attn_first[-1]), *spread_direct(attn_second[-1])),
     )
-    gains = gain_full[0]
-    head_rows = query_norm.shape[0]
-
-    def slice_of(start, width):
-        return lax.dynamic_slice_in_dim(gains, start + index * width, width, 0)
+    gains = [gain.reshape(-1) for gain in gains]
 
     return (
         layer_out[None],
         in_grad[None],
-        gains[:ROWS],
+        gains[0],
         query_w_grad,
         key_w_grad,
         value_w_grad,
-        slice_of(2 * ROWS, head_rows),
-        slice_of(2 * ROWS + HEAD_SIZE, head_rows),
+        gains[2],
+        gains[3],
         out_w_grad,
-        gains[ROWS : 2 * ROWS],
+        gains[1],
         gate_w_grad,
         up_w_grad,
         down_w_grad,

time: 282 us -> 290 us (1.028)
  waiting for transfers between devices: 122 us -> 132 us
    ppermute x15, waiting for transfers between devices: 63.2 us -> 73.1 us  [ring_up(): lax.ppermute(value, 'shard', [(i, (i + 2) % count) for i in range(count)])]
  transfers between devices with their start and end apart: 74 -> 74, of which waited for: 31 -> 29; matrix products, arithmetic and copies ran while one was open for 3% -> 2% of each run, Pallas kernels for 26% -> 25%
where the time goes in v5:
time: 290 us; the launch traced here: 286 us
  waiting for transfers between devices  132 us (46%)
  Pallas kernels  76.9 us (27%)
  starting transfers between devices  63.1 us (22%)
  other arithmetic  7.05 us (2%)
  local copies, waits for them, and re-layouts  4.38 us (2%)
    pallas_call x23, Pallas kernels, on_core(): pl.pallas_call(body, name=name, in_specs=[pl.BlockSpec(memory_space=pltpu...  76.9 us
    ppermute x15, waiting for transfers between devices, ring_up(): lax.ppermute(value, 'shard', [(i, (i + 2) % count) for i in range(count)])  73.1 us
    ppermute x46, waiting for transfers between devices, flip(): return lax.ppermute(value, 'rep', [(i, i ^ bit) for i in range(count)])  54 us
    ppermute x46, starting transfers between devices, flip(): return lax.ppermute(value, 'rep', [(i, i ^ bit) for i in range(count)])  49.7 us
    ppermute x15, starting transfers between devices, ring_up(): lax.ppermute(value, 'shard', [(i, (i + 2) % count) for i in range(count)])  12.5 us
  transfers between devices with their start and end apart: 74, of which 29 were waited for; matrix products, arithmetic and copies ran while one was open for 2% of the time, Pallas kernels for 25%

profile of v5, /device:TPU:0, one launch (start us, length us, event | category | flops | bytes accessed | tf_op | source)
XLA Modules:
  0.0 285.6 jit_solution(9053967125279556470)
XLA Ops:
  1.3 2.7 pack.1.refs_0_
  4.9 2.6 collective-permute-start.6
  7.5 1.5 collective-permute-start.4
  9.0 1.6 collective-permute-start
  12.0 10.4 %collective-permute-done.refs_1_ = bf16[208,1024]{1,0:T(8,128)(2,1)S(1)} collective-permute-done((bf16[208,1024]{1,0:T(8,128)(2,1)S(1)}, bf16[208,1024]{1,0:T(8,128)(2,1)S(1)}, u32[]{:S(2)}, u32[]{:S(2)}) %collective-permute-start) | collective-permute-done | bytes 426016 | tf_op jit(solution)/shard_map/ppermute | solution.py:66
  23.9 8.8 %collective-permute-done.3.refs_10_ = bf16[256,1024]{1,0:T(8,128)(2,1)S(1)} collective-permute-done((bf16[256,1024]{1,0:T(8,128)(2,1)S(1)}, bf16[256,1024]{1,0:T(8,128)(2,1)S(1)}, u32[]{:S(2)}, u32[]{:S(2)}) %collective-permute-start.3) | collective-permute-done | bytes 524320 | tf_op jit(solution)/shard_map/ppermute | solution.py:29
  32.8 1.9 fusion.10
  38.7 10.5 %collective-permute-done.8.refs_3_ = bf16[208,1024]{1,0:T(8,128)(2,1)S(1)} collective-permute-done((bf16[208,1024]{1,0:T(8,128)(2,1)S(1)}, bf16[208,1024]{1,0:T(8,128)(2,1)S(1)}, u32[]{:S(2)}, u32[]{:S(2)}) %collective-permute-start.8) | collective-permute-done | bytes 426016 | tf_op jit(solution)/shard_map/ppermute | solution.py:66
  49.2 1.4 pick.1
  50.6 1.6 collective-permute-start.13
  52.7 1.5 collective-permute-start.15
  54.2 1.7 collective-permute-start.21
  55.9 7.3 %project.1 = (bf16[2,4,512,128]{3,2,1,0:T(8,128)(2,1)S(1)}, bf16[2,4,256,128]{3,2,1,0:T(8,128)(2,1)S(1)}, bf16[2,4,256,128]{3,2,1,0:T(8,128)(2,1)S(1)}, f32[8,10...) custom-call(s32[7]{0:T(128)S(1)} %pad_add_fusion.info.refs_0_, ...), custom_call_target="tpu_custom_call" | custom-call | tf_op jit(solution)/shard_map/project/pallas_call | solution.py:547
  63.5 5.8 %attend.1 = (bf16[4,256,512]{2,1,0:T(8,128)(2,1)S(1)}, f32[2,4,1,512]{3,2,1,0:T(1,128)S(1)}, bf16[32768,1024]{1,0:T(8,128)(2,1)}) custom-call(s32[7]{0:T(128)S(1)} %pad_add_fusion.info.refs_0_, bf16[2,4,512,128]{3,2,1,0:T(8,128)(2,1)S(1)} %get-tuple-element.168.q_ref, ...), custom_call_target="tpu_custom_call", output_to_operand_aliasing={{2}: (4, {})} | custom-call | tf_op jit(solution)/shard_map/attend/pallas_call | solution.py:547
  69.3 2.9 %collective-permute-done.21.refs_1_ = bf16[384,768]{1,0:T(8,128)(2,1)S(1)} collective-permute-done((bf16[384,768]{1,0:T(8,128)(2,1)S(1)}, bf16[384,768]{1,0:T(8,128)(2,1)S(1)}, u32[]{:S(2)}, u32[]{:S(2)}) %collective-permute-start.21) | collective-permute-done | bytes 589856 | tf_op jit(solution)/shard_map/ppermute | solution.py:66
  72.3 1.9 out.1
  74.8 1.5 collective-permute-start.17
  76.3 12.6 %collective-permute-done.23.refs_2_ = bf16[384,768]{1,0:T(8,128)(2,1)S(1)} collective-permute-done((bf16[384,768]{1,0:T(8,128)(2,1)S(1)}, bf16[384,768]{1,0:T(8,128)(2,1)S(1)}, u32[]{:S(2)}, u32[]{:S(2)}) %collective-permute-start.23) | collective-permute-done | bytes 589856 | tf_op jit(solution)/shard_map/ppermute | solution.py:66
  89.1 1.6 collective-permute-start.20
  91.3 5.3 %collective-permute-done.20.refs_4_ = bf16[128,1024]{1,0:T(8,128)(2,1)S(1)} collective-permute-done((bf16[128,1024]{1,0:T(8,128)(2,1)S(1)}, bf16[128,1024]{1,0:T(8,128)(2,1)S(1)}, u32[]{:S(2)}, u32[]{:S(2)}) %collective-permute-start.20) | collective-permute-done | bytes 262176 | tf_op jit(solution)/shard_map/ppermute | solution.py:29
  96.6 1.3 collective-permute-done.19.refs_3_
  100.0 4.8 %collective-permute-done.25.refs_3_ = bf16[384,768]{1,0:T(8,128)(2,1)S(1)} collective-permute-done((bf16[384,768]{1,0:T(8,128)(2,1)S(1)}, bf16[384,768]{1,0:T(8,128)(2,1)S(1)}, u32[]{:S(2)}, u32[]{:S(2)}) %collective-permute-start.25) | collective-permute-done | bytes 589856 | tf_op jit(solution)/shard_map/ppermute | solution.py:66
  104.9 5.4 %collective-permute-done.28.refs_0_.refs_9_ = bf16[256,1024]{1,0:T(8,128)(2,1)S(1)} collective-permute-done((bf16[256,1024]{1,0:T(8,128)(2,1)S(1)}, bf16[256,1024]{1,0:T(8,128)(2,1)S(1)}, u32[]{:S(2)}, u32[]{:S(2)}) %collective-permute-start.28) | collective-permute-done | bytes 524320 | tf_op jit(solution)/shard_map/ppermute | solution.py:29
  111.0 2.3 collective-permute-start.31
  113.3 4.0 %prepare.1 = (bf16[1024,1536]{1,0:T(8,128)(2,1)S(1)}, bf16[768,1024]{1,0:T(8,128)(2,1)S(1)}, bf16[1024,1024]{1,0:T(8,128)(2,1)S(1)}, f32[256,768]{1,0:T(8,128)S(...) custom-call(s32[7]{0:T(128)S(1)} %pad_add_fusion.info.refs_0_, ...), custom_call_target="tpu_custom_call" | custom-call | tf_op jit(solution)/shard_map/prepare/pallas_call | solution.py:547
  117.2 1.9 feed.3
  119.1 3.7 %feed.4 = (bf16[256,768]{1,0:T(8,128)(2,1)S(1)}, bf16[256,1536]{1,0:T(8,128)(2,1)S(1)}, bf16[256,768]{1,0:T(8,128)(2,1)S(1)}, bf16[256,1536]{1,0:T(8,128)(2,1)S(...) custom-call(bf16[256,1024]{1,0:T(8,128)(2,1)S(1)} %collective-permut, ...), custom_call_target="tpu_custom_call" | custom-call | tf_op jit(solution)/shard_map/feed/pallas_call | solution.py:547
  122.8 1.9 feed.5
  124.9 2.3 collective-permute-start.33
  127.2 6.6 %feed_weights.1 = (f32[4,384,768]{2,1,0:T(8,128)S(1)}, bf16[4,384,768]{2,1,0:T(8,128)(2,1)S(1)}) custom-call(s32[7]{0:T(128)S(1)} %pad_add_fusion.info.refs_0_, bf16[1024,1024]{1,0:T(8,128)(2,1)S(1)} %get-tuple-element.222.cotangent, bf16[256,768]{1,0:T(8,128)(2,1)S(1)} %get-tuple-element.239.refs_0_, bf16[256,768]{1,0:T(8,128)(2,1)S(1)} %get-tuple-element.240.refs_1_, ...), custom_call_target="tpu_custom_call" | custom-call | tf_op jit(solution)/shard_map/feed_weights/pallas_call | solution.py:547
  135.2 1.7 collective-permute-start.35
  137.2 2.5 collective-permute-done.36
  139.8 1.3 collective-permute-start.41
  141.2 2.7 collective-permute-done.35.refs_5_
  143.9 1.4 collective-permute-done.34.refs_4_
  146.4 1.3 collective-permute-start.38
  147.8 11.5 %collective-permute-done.37.refs_1_ = bf16[256,1024]{1,0:T(8,128)(2,1)S(1)} collective-permute-done((bf16[256,1024]{1,0:T(8,128)(2,1)S(1)}, bf16[256,1024]{1,0:T(8,128)(2,1)S(1)}, u32[]{:S(2)}, u32[]{:S(2)}) %collective-permute-start.37) | collective-permute-done | bytes 524320 | tf_op jit(solution)/shard_map/ppermute | solution.py:29
  159.7 1.5 collective-permute-start.40
  163.4 1.8 down.2
  167.0 4.1 %mixed_grad.1 = (bf16[4,256,512]{2,1,0:T(8,128)(2,1)S(1)}, f32[4,64,1024]{2,1,0:T(8,128)S(1)}, bf16[4,64,1024]{2,1,0:T(8,128)(2,1)}) custom-call(s32[7]{0:T(128)S(1)} %pad_add_fusion.info.refs_0_, bf16[512,1024]{1,0:T(8,128)(2,1)S(1)} %get-tuple-element.249.out_ref, bf16[256,1024]{1,0:T(8,128)(2,1)S(1)} %get-tuple-element.250.refs_0_.residual, ...), custom_call_target="tpu_custom_call" | custom-call | tf_op jit(solution)/shard_map/mixed_grad/pallas_call | solution.py:547
  172.2 2.1 collective-permute-done.42.crossed
  175.6 1.5 collective-permute-start.46
  177.6 1.6 collective-permute-start.48
  179.2 9.8 %attend_back.2 = (bf16[1024,512]{1,0:T(8,128)(2,1)S(1)}, f32[4,144,512]{2,1,0:T(8,128)S(1)}, bf16[4,144,512]{2,1,0:T(8,128)(2,1)S(1)}) custom-call(s32[7]{0:T(128)S(1)} %pad_add_fusion.info.refs_0_, f32[2,4,1,512]{3,2,1,0:T(1,128)S(1)} %get-tuple-element.248.refs_1_, bf16[4,256,512]{2,1,0:T(8,128)(2,1)S(1)} %get-tuple-element.277.refs_2_, ...), custom_call_target="tpu_custom_call" | custom-call | tf_op jit(solution)/shard_map/attend_back/pallas_call | solution.py:547
  189.2 1.3 fusion.1
  193.3 4.1 %collective-permute-start.57 = (bf16[272,512]{1,0:T(8,128)(2,1)S(1)}, bf16[272,512]{1,0:T(8,128)(2,1)S(1)}, u32[]{:S(2)}, u32[]{:S(2)}) collective-permute-start(bf16[272,512]{1,0:T(8,128)(2,1)S(1)} %pad_maximum_fusion.6), channel_id=1, source_target_pairs={{0,2},{1,3},{2,4},{3,5},{4,6},{5,7},{6,0},{7,1},{8,10},{9,11},{10,... | collective-permute-start | bytes 835592 | tf_op jit(solution)/shard_map/ppermute | solution.py:66
  197.5 9.6 %attend_back.3 = (bf16[1024,512]{1,0:T(8,128)(2,1)S(1)}, f32[4,144,512]{2,1,0:T(8,128)S(1)}, bf16[4,144,512]{2,1,0:T(8,128)(2,1)S(1)}) custom-call(s32[7]{0:T(128)S(1)} %pad_add_fusion.info.refs_0_, f32[2,4,1,512]{3,2,1,0:T(1,128)S(1)} %get-tuple-element.248.refs_1_, bf16[4,256,512]{2,1,0:T(8,128)(2,1)S(1)} %get-tuple-element.277.refs_2_, ...), custom_call_target="tpu_custom_call" | custom-call | tf_op jit(solution)/shard_map/attend_back/pallas_call | solution.py:547
  207.1 1.4 collective-permute-done.69
  208.5 5.5 %collective-permute-done.57 = bf16[272,512]{1,0:T(8,128)(2,1)S(1)} collective-permute-done((bf16[272,512]{1,0:T(8,128)(2,1)S(1)}, bf16[272,512]{1,0:T(8,128)(2,1)S(1)}, u32[]{:S(2)}, u32[]{:S(2)}) %collective-permute-start.57) | collective-permute-done | bytes 278560 | tf_op jit(solution)/shard_map/ppermute | solution.py:66
  214.3 1.4 collective-permute-start.70
  217.6 6.5 %collective-permute-done.58 = bf16[272,512]{1,0:T(8,128)(2,1)S(1)} collective-permute-done((bf16[272,512]{1,0:T(8,128)(2,1)S(1)}, bf16[272,512]{1,0:T(8,128)(2,1)S(1)}, u32[]{:S(2)}, u32[]{:S(2)}) %collective-permute-start.58) | collective-permute-done | bytes 278560 | tf_op jit(solution)/shard_map/ppermute | solution.py:66
  224.9 4.0 %normed_grad.1 = (bf16[256,1024]{1,0:T(8,128)(2,1)S(1)}, bf16[256,1024]{1,0:T(8,128)(2,1)S(1)}, f32[128,1024]{1,0:T(8,128)S(1)}, f32[128,1024]{1,0:T(8,128)S(1)}, f32[256,1024]{1,0:T(8,128)S(1)}) custom-call(bf16[1024,512]{1,0:T(8,128)(2,1)S(1)} %get-tuple-element.285.refs_0_, bf16[1024,512]{1,0:T(8,128)(2,1)S(1)} %get-tuple-element.286.refs_1_, ...), custom_call_target="tpu_custom_call" | custom-call | tf_op jit(solution)/shard_map/normed_grad/pallas_call | solution.py:547
  228.9 1.7 collective-permute-done.70.refs_1_
  232.8 3.8 %collective-permute-done.63 = bf16[144,512]{1,0:T(8,128)(2,1)S(1)} collective-permute-done((bf16[144,512]{1,0:T(8,128)(2,1)S(1)}, bf16[144,512]{1,0:T(8,128)(2,1)S(1)}, u32[]{:S(2)}, u32[]{:S(2)}) %collective-permute-start.63) | collective-permute-done | bytes 147488 | tf_op jit(solution)/shard_map/ppermute | solution.py:66
  236.6 1.4 collective-permute-start.53
  238.2 6.9 %collective-permute-done.64 = bf16[144,512]{1,0:T(8,128)(2,1)S(1)} collective-permute-done((bf16[144,512]{1,0:T(8,128)(2,1)S(1)}, bf16[144,512]{1,0:T(8,128)(2,1)S(1)}, u32[]{:S(2)}, u32[]{:S(2)}) %collective-permute-start.64) | collective-permute-done | bytes 147488 | tf_op jit(solution)/shard_map/ppermute | solution.py:66
  245.4 6.9 %collective-permute-done.65 = bf16[144,512]{1,0:T(8,128)(2,1)S(1)} collective-permute-done((bf16[144,512]{1,0:T(8,128)(2,1)S(1)}, bf16[144,512]{1,0:T(8,128)(2,1)S(1)}, u32[]{:S(2)}, u32[]{:S(2)}) %collective-permute-start.65) | collective-permute-done | bytes 147488 | tf_op jit(solution)/shard_map/ppermute | solution.py:66
  255.0 1.5 collective-permute-start.61
  257.7 7.5 %collective-permute-done.72.refs_3_ = bf16[192,768]{1,0:T(8,128)(2,1)S(1)} collective-permute-done((bf16[192,768]{1,0:T(8,128)(2,1)S(1)}, bf16[192,768]{1,0:T(8,128)(2,1)S(1)}, u32[]{:S(2)}, u32[]{:S(2)}) %collective-permute-start.72) | collective-permute-done | bytes 294944 | tf_op jit(solution)/shard_map/ppermute | solution.py:29
  267.0 1.7 collective-permute-done.60.refs_1_
  270.9 4.8 %collective-permute-done.62.refs_3_ = bf16[272,512]{1,0:T(8,128)(2,1)S(1)} collective-permute-done((bf16[272,512]{1,0:T(8,128)(2,1)S(1)}, bf16[272,512]{1,0:T(8,128)(2,1)S(1)}, u32[]{:S(2)}, u32[]{:S(2)}) %collective-permute-start.62) | collective-permute-done | bytes 278560 | tf_op jit(solution)/shard_map/ppermute | solution.py:29
  277.9 3.8 %unpack_feed.1 = (f32[128,3072]{1,0:T(8,128)}, f32[128,3072]{1,0:T(8,128)}, f32[384,1024]{1,0:T(8,128)}) custom-call(s32[3]{0:T(128)S(1)} %copy-done.18, bf16[384,768]{1,0:T(8,128)(2,1)S(1)} %fusion.refs_0_, bf16[384,768]{1,0:T(8,128)(2,1)S(1)} %collective-permute-done.70.refs_1_, bf16[384,768]{1,0:T(8,128)(2,1)S(1)} %collective-permute-done.71.refs_2_, ...), custom_call_target="tpu_custom_call" | custom-call | tf_op jit(solution)/shard_map/unpack_feed/pallas_call | solution.py:547
  281.7 2.3 unpack_attend.1
  284.0 1.4 final.1
  (219 shorter events, 41.5 us)
Async XLA Ops:
  4.1 19.7 %collective-permute-start.1 = (bf16[208,1024]{1,0:T(8,128)(2,1)}, bf16[208,1024]{1,0:T(8,128)(2,1)S(1)}, u32[]{:S(2)}, u32[]{:S(2)}) collective-permute-start(bf16[208,1024]{1,0:T(8,128)(2,1)} %pack.1.refs_0_), channel_id=1, source_target_pairs={{0,1},{1,0},{2,3},{3,2},{4,5},{5,4},{6,7},{7,6},{8,9},{9,8},{10,11... | collective-permute-start | bytes 1277960 | tf_op jit(solution)/shard_map/ppermute | solution.py:71
  4.9 30.2 %collective-permute-start.6 = (bf16[256,1024]{1,0:T(8,128)(2,1)S(1)}, bf16[256,1024]{1,0:T(8,128)(2,1)S(1)}, u32[]{:S(2)}, u32[]{:S(2)}) collective-permute-start(bf16[256,1024]{1,0:T(8,128)(2,1)S(1)} %get-tuple-element.165.refs_9_), channel_id=1, source_target_pairs={{0,16},{8,24},{16,0},{24,8},{1,17},{9,25},{17,1},{25,9},{2,18},{10... | collective-permute-start | bytes 1572872 | tf_op jit(solution)/shard_map/ppermute | solution.py:29
  7.5 27.6 %collective-permute-start.4 = (bf16[256,1024]{1,0:T(8,128)(2,1)S(1)}, bf16[256,1024]{1,0:T(8,128)(2,1)S(1)}, u32[]{:S(2)}, u32[]{:S(2)}) collective-permute-start(bf16[256,1024]{1,0:T(8,128)(2,1)S(1)} %get-tuple-element.165.refs_9_), channel_id=1, source_target_pairs={{0,8},{8,0},{16,24},{24,16},{1,9},{9,1},{17,25},{25,17},{2,10},{10... | collective-permute-start | bytes 1572872 | tf_op jit(solution)/shard_map/ppermute | solution.py:29
  9.0 13.5 %collective-permute-start = (bf16[208,1024]{1,0:T(8,128)(2,1)S(1)}, bf16[208,1024]{1,0:T(8,128)(2,1)S(1)}, u32[]{:S(2)}, u32[]{:S(2)}) collective-permute-start(bf16[208,1024]{1,0:T(8,128)(2,1)S(1)} %copy-done.4), channel_id=1, source_target_pairs={{0,2},{1,3},{2,4},{3,5},{4,6},{5,7},{6,0},{7,1},{8,10},{9,11},{10,... | collective-permute-start | bytes 1277960 | tf_op jit(solution)/shard_map/ppermute | solution.py:66
  10.5 22.2 %collective-permute-start.3 = (bf16[256,1024]{1,0:T(8,128)(2,1)S(1)}, bf16[256,1024]{1,0:T(8,128)(2,1)S(1)}, u32[]{:S(2)}, u32[]{:S(2)}) collective-permute-start(bf16[256,1024]{1,0:T(8,128)(2,1)S(1)} %get-tuple-element.164.refs_8_), channel_id=1, source_target_pairs={{0,8},{8,0},{16,24},{24,16},{1,9},{9,1},{17,25},{25,17},{2,10},{10... | collective-permute-start | bytes 1572872 | tf_op jit(solution)/shard_map/ppermute | solution.py:29
  22.5 13.0 %collective-permute-start.5 = (bf16[256,1024]{1,0:T(8,128)(2,1)S(1)}, bf16[256,1024]{1,0:T(8,128)(2,1)S(1)}, u32[]{:S(2)}, u32[]{:S(2)}) collective-permute-start(bf16[256,1024]{1,0:T(8,128)(2,1)S(1)} %get-tuple-element.164.refs_8_), channel_id=1, source_target_pairs={{0,16},{8,24},{16,0},{24,8},{1,17},{9,25},{17,1},{25,9},{2,18},{10... | collective-permute-start | bytes 1572872 | tf_op jit(solution)/shard_map/ppermute | solution.py:29
  23.8 12.4 %collective-permute-start.2 = (bf16[208,1024]{1,0:T(8,128)(2,1)S(1)}, bf16[208,1024]{1,0:T(8,128)(2,1)S(1)}, u32[]{:S(2)}, u32[]{:S(2)}) collective-permute-start(bf16[208,1024]{1,0:T(8,128)(2,1)S(1)} %collective-permute-done.refs_1_), channel_id=1, source_target_pairs={{0,2},{1,3},{2,4},{3,5},{4,6},{5,7},{6,0},{7,1},{8,10},{9,11},{10,... | collective-permute-start | bytes 1277960 | tf_op jit(solution)/shard_map/ppermute | solution.py:66
  36.3 12.9 %collective-permute-start.8 = (bf16[208,1024]{1,0:T(8,128)(2,1)S(1)}, bf16[208,1024]{1,0:T(8,128)(2,1)S(1)}, u32[]{:S(2)}, u32[]{:S(2)}) collective-permute-start(bf16[208,1024]{1,0:T(8,128)(2,1)S(1)} %collective-permute-done.2.refs_2_), channel_id=1, source_target_pairs={{0,2},{1,3},{2,4},{3,5},{4,6},{5,7},{6,0},{7,1},{8,10},{9,11},{10,... | collective-permute-start | bytes 1277960 | tf_op jit(solution)/shard_map/ppermute | solution.py:66
  36.7 15.4 %collective-permute-start.11 = (bf16[256,1024]{1,0:T(8,128)(2,1)S(1)}, bf16[256,1024]{1,0:T(8,128)(2,1)S(1)}, u32[]{:S(2)}, u32[]{:S(2)}) collective-permute-start(bf16[256,1024]{1,0:T(8,128)(2,1)S(1)} %collective-permute-done.3.refs_10_), channel_id=1, source_target_pairs={{0,16},{8,24},{16,0},{24,8},{1,17},{9,25},{17,1},{25,9},{2,18},{10... | collective-permute-start | bytes 1572872 | tf_op jit(solution)/shard_map/ppermute | solution.py:29
  37.9 14.8 %collective-permute-start.12 = (bf16[256,1024]{1,0:T(8,128)(2,1)S(1)}, bf16[256,1024]{1,0:T(8,128)(2,1)S(1)}, u32[]{:S(2)}, u32[]{:S(2)}) collective-permute-start(bf16[256,1024]{1,0:T(8,128)(2,1)S(1)} %collective-permute-done.6.refs_13_), channel_id=1, source_target_pairs={{0,8},{8,0},{16,24},{24,16},{1,9},{9,1},{17,25},{25,17},{2,10},{10... | collective-permute-start | bytes 1572872 | tf_op jit(solution)/shard_map/ppermute | solution.py:29
  38.7 15.4 %collective-permute-start.9 = (bf16[208,1024]{1,0:T(8,128)(2,1)S(1)}, bf16[208,1024]{1,0:T(8,128)(2,1)S(1)}, u32[]{:S(2)}, u32[]{:S(2)}) collective-permute-start(bf16[208,1024]{1,0:T(8,128)(2,1)S(1)} %collective-permute-done.2.refs_2_), channel_id=1, source_target_pairs={{0,1},{1,0},{2,3},{3,2},{4,5},{5,4},{6,7},{7,6},{8,9},{9,8},{10,11... | collective-permute-start | bytes 1277960 | tf_op jit(solution)/shard_map/ppermute | solution.py:71
  50.6 12.6 %collective-permute-start.13 = (bf16[64,1024]{1,0:T(8,128)(2,1)S(1)}, bf16[64,1024]{1,0:T(8,128)(2,1)S(1)}, u32[]{:S(2)}, u32[]{:S(2)}) collective-permute-start(bf16[64,1024]{1,0:T(8,128)(2,1)S(1)} %get-tuple-element.174), channel_id=1, source_target_pairs={{0,8},{8,0},{16,24},{24,16},{1,9},{9,1},{17,25},{25,17},{2,10},{10... | collective-permute-start | bytes 393224 | tf_op jit(solution)/shard_map/ppermute | solution.py:29
  52.1 11.0 %collective-permute-start.14 = (bf16[64,1024]{1,0:T(8,128)(2,1)S(1)}, bf16[64,1024]{1,0:T(8,128)(2,1)S(1)}, u32[]{:S(2)}, u32[]{:S(2)}) collective-permute-start(bf16[64,1024]{1,0:T(8,128)(2,1)S(1)} %get-tuple-element.175), channel_id=1, source_target_pairs={{0,16},{8,24},{16,0},{24,8},{1,17},{9,25},{17,1},{25,9},{2,18},{10... | collective-permute-start | bytes 393224 | tf_op jit(solution)/shard_map/ppermute | solution.py:29
  52.7 10.5 %collective-permute-start.15 = (bf16[64,1024]{1,0:T(8,128)(2,1)S(1)}, bf16[64,1024]{1,0:T(8,128)(2,1)S(1)}, u32[]{:S(2)}, u32[]{:S(2)}) collective-permute-start(bf16[64,1024]{1,0:T(8,128)(2,1)S(1)} %get-tuple-element.176), channel_id=1, source_target_pairs={{0,24},{8,16},{16,8},{24,0},{1,25},{9,17},{17,9},{25,1},{2,26},{10... | collective-permute-start | bytes 393224 | tf_op jit(solution)/shard_map/ppermute | solution.py:29
  54.1 18.1 %collective-permute-start.22 = (bf16[384,768]{1,0:T(8,128)(2,1)S(1)}, bf16[384,768]{1,0:T(8,128)(2,1)S(1)}, u32[]{:S(2)}, u32[]{:S(2)}) collective-permute-start(bf16[384,768]{1,0:T(8,128)(2,1)S(1)} %pack_feed.1.refs_0_), channel_id=1, source_target_pairs={{0,1},{1,0},{2,3},{3,2},{4,5},{5,4},{6,7},{7,6},{8,9},{9,8},{10,11... | collective-permute-start | bytes 1769480 | tf_op jit(solution)/shard_map/ppermute | solution.py:71
  54.2 18.1 %collective-permute-start.21 = (bf16[384,768]{1,0:T(8,128)(2,1)S(1)}, bf16[384,768]{1,0:T(8,128)(2,1)S(1)}, u32[]{:S(2)}, u32[]{:S(2)}) collective-permute-start(bf16[384,768]{1,0:T(8,128)(2,1)S(1)} %pack_feed.1.refs_0_), channel_id=1, source_target_pairs={{0,2},{1,3},{2,4},{3,5},{4,6},{5,7},{6,0},{7,1},{8,10},{9,11},{10,... | collective-permute-start | bytes 1769480 | tf_op jit(solution)/shard_map/ppermute | solution.py:66
  63.2 9.0 %collective-permute-start.16 = (bf16[256,1024]{1,0:T(8,128)(2,1)S(1)}, bf16[256,1024]{1,0:T(8,128)(2,1)S(1)}, u32[]{:S(2)}, u32[]{:S(2)}) collective-permute-start(bf16[256,1024]{1,0:T(8,128)(2,1)S(1)} %pad_maximum_fusion.4), channel_id=1, source_target_pairs={{0,1},{1,0},{2,3},{3,2},{4,5},{5,4},{6,7},{7,6},{8,9},{9,8},{10,11... | collective-permute-start | bytes 1572872 | tf_op jit(solution)/shard_map/ppermute | solution.py:71
  72.2 16.7 %collective-permute-start.23 = (bf16[384,768]{1,0:T(8,128)(2,1)S(1)}, bf16[384,768]{1,0:T(8,128)(2,1)S(1)}, u32[]{:S(2)}, u32[]{:S(2)}) collective-permute-start(bf16[384,768]{1,0:T(8,128)(2,1)S(1)} %collective-permute-done.21.refs_1_), channel_id=1, source_target_pairs={{0,2},{1,3},{2,4},{3,5},{4,6},{5,7},{6,0},{7,1},{8,10},{9,11},{10,... | collective-permute-start | bytes 1769480 | tf_op jit(solution)/shard_map/ppermute | solution.py:66
  72.2 16.7 %collective-permute-start.24 = (bf16[384,768]{1,0:T(8,128)(2,1)S(1)}, bf16[384,768]{1,0:T(8,128)(2,1)S(1)}, u32[]{:S(2)}, u32[]{:S(2)}) collective-permute-start(bf16[384,768]{1,0:T(8,128)(2,1)S(1)} %collective-permute-done.21.refs_1_), channel_id=1, source_target_pairs={{0,1},{1,0},{2,3},{3,2},{4,5},{5,4},{6,7},{7,6},{8,9},{9,8},{10,11... | collective-permute-start | bytes 1769480 | tf_op jit(solution)/shard_map/ppermute | solution.py:71
  74.2 14.9 %collective-permute-start.18 = (bf16[256,1024]{1,0:T(8,128)(2,1)S(1)}, bf16[256,1024]{1,0:T(8,128)(2,1)S(1)}, u32[]{:S(2)}, u32[]{:S(2)}) collective-permute-start(bf16[256,1024]{1,0:T(8,128)(2,1)S(1)} %get-tuple-element.183), channel_id=1, source_target_pairs={{0,16},{8,24},{16,0},{24,8},{1,17},{9,25},{17,1},{25,9},{2,18},{10... | collective-permute-start | bytes 1572872 | tf_op jit(solution)/shard_map/ppermute | solution.py:29
  74.8 15.9 %collective-permute-start.17 = (bf16[256,1024]{1,0:T(8,128)(2,1)S(1)}, bf16[256,1024]{1,0:T(8,128)(2,1)S(1)}, u32[]{:S(2)}, u32[]{:S(2)}) collective-permute-start(bf16[256,1024]{1,0:T(8,128)(2,1)S(1)} %get-tuple-element.182), channel_id=1, source_target_pairs={{0,8},{8,0},{16,24},{24,16},{1,9},{9,1},{17,25},{25,17},{2,10},{10... | collective-permute-start | bytes 1572872 | tf_op jit(solution)/shard_map/ppermute | solution.py:29
  88.9 15.9 %collective-permute-start.25 = (bf16[384,768]{1,0:T(8,128)(2,1)S(1)}, bf16[384,768]{1,0:T(8,128)(2,1)S(1)}, u32[]{:S(2)}, u32[]{:S(2)}) collective-permute-start(bf16[384,768]{1,0:T(8,128)(2,1)S(1)} %collective-permute-done.23.refs_2_), channel_id=1, source_target_pairs={{0,2},{1,3},{2,4},{3,5},{4,6},{5,7},{6,0},{7,1},{8,10},{9,11},{10,... | collective-permute-start | bytes 1769480 | tf_op jit(solution)/shard_map/ppermute | solution.py:66
  89.1 7.5 %collective-permute-start.20 = (bf16[128,1024]{1,0:T(8,128)(2,1)S(1)}, bf16[128,1024]{1,0:T(8,128)(2,1)S(1)}, u32[]{:S(2)}, u32[]{:S(2)}) collective-permute-start(bf16[128,1024]{1,0:T(8,128)(2,1)S(1)} %add_convert_fusion.7), channel_id=1, source_target_pairs={{0,8},{8,0},{16,24},{24,16},{1,9},{9,1},{17,25},{25,17},{2,10},{10... | collective-permute-start | bytes 786440 | tf_op jit(solution)/shard_map/ppermute | solution.py:29
  98.4 11.9 %collective-permute-start.28 = (bf16[256,1024]{1,0:T(8,128)(2,1)S(1)}, bf16[256,1024]{1,0:T(8,128)(2,1)S(1)}, u32[]{:S(2)}, u32[]{:S(2)}) collective-permute-start(bf16[256,1024]{1,0:T(8,128)(2,1)S(1)} %get-tuple-element.190.refs_0_.refs_8_), channel_id=1, source_target_pairs={{0,8},{8,0},{16,24},{24,16},{1,9},{9,1},{17,25},{25,17},{2,10},{10... | collective-permute-start | bytes 1572872 | tf_op jit(solution)/shard_map/ppermute | solution.py:29
  99.0 12.0 %collective-permute-start.29 = (bf16[256,1024]{1,0:T(8,128)(2,1)S(1)}, bf16[256,1024]{1,0:T(8,128)(2,1)S(1)}, u32[]{:S(2)}, u32[]{:S(2)}) collective-permute-start(bf16[256,1024]{1,0:T(8,128)(2,1)S(1)} %get-tuple-element.190.refs_0_.refs_8_), channel_id=1, source_target_pairs={{0,16},{8,24},{16,0},{24,8},{1,17},{9,25},{17,1},{25,9},{2,18},{10... | collective-permute-start | bytes 1572872 | tf_op jit(solution)/shard_map/ppermute | solution.py:29
  100.0 13.2 %collective-permute-start.26 = (bf16[384,768]{1,0:T(8,128)(2,1)S(1)}, bf16[384,768]{1,0:T(8,128)(2,1)S(1)}, u32[]{:S(2)}, u32[]{:S(2)}) collective-permute-start(bf16[384,768]{1,0:T(8,128)(2,1)S(1)} %collective-permute-done.23.refs_2_), channel_id=1, source_target_pairs={{0,1},{1,0},{2,3},{3,2},{4,5},{5,4},{6,7},{7,6},{8,9},{9,8},{10,11... | collective-permute-start | bytes 1769480 | tf_op jit(solution)/shard_map/ppermute | solution.py:71
  104.9 8.4 %collective-permute-start.27 = (bf16[384,768]{1,0:T(8,128)(2,1)S(1)}, bf16[384,768]{1,0:T(8,128)(2,1)S(1)}, u32[]{:S(2)}, u32[]{:S(2)}) collective-permute-start(bf16[384,768]{1,0:T(8,128)(2,1)S(1)} %collective-permute-done.25.refs_3_), channel_id=1, source_target_pairs={{0,1},{1,0},{2,3},{3,2},{4,5},{5,4},{6,7},{7,6},{8,9},{9,8},{10,11... | collective-permute-start | bytes 1769480 | tf_op jit(solution)/shard_map/ppermute | solution.py:71
  110.3 12.5 %collective-permute-start.30 = (bf16[128,1024]{1,0:T(8,128)(2,1)S(1)}, bf16[128,1024]{1,0:T(8,128)(2,1)S(1)}, u32[]{:S(2)}, u32[]{:S(2)}) collective-permute-start(bf16[128,1024]{1,0:T(8,128)(2,1)S(1)} %slice.262), channel_id=1, source_target_pairs={{0,16},{8,24},{16,0},{24,8},{1,17},{9,25},{17,1},{25,9},{2,18},{10... | collective-permute-start | bytes 786440 | tf_op jit(solution)/shard_map/ppermute | solution.py:29
  111.0 11.9 %collective-permute-start.31 = (bf16[128,1024]{1,0:T(8,128)(2,1)S(1)}, bf16[128,1024]{1,0:T(8,128)(2,1)S(1)}, u32[]{:S(2)}, u32[]{:S(2)}) collective-permute-start(bf16[128,1024]{1,0:T(8,128)(2,1)S(1)} %slice.263), channel_id=1, source_target_pairs={{0,8},{8,0},{16,24},{24,16},{1,9},{9,1},{17,25},{25,17},{2,10},{10... | collective-permute-start | bytes 786440 | tf_op jit(solution)/shard_map/ppermute | solution.py:29
  124.8 10.1 %collective-permute-start.32 = (bf16[256,1024]{1,0:T(8,128)(2,1)S(1)}, bf16[256,1024]{1,0:T(8,128)(2,1)S(1)}, u32[]{:S(2)}, u32[]{:S(2)}) collective-permute-start(bf16[256,1024]{1,0:T(8,128)(2,1)S(1)} %get-tuple-element.220), channel_id=1, source_target_pairs={{0,8},{8,0},{16,24},{24,16},{1,9},{9,1},{17,25},{25,17},{2,10},{10... | collective-permute-start | bytes 1572872 | tf_op jit(solution)/shard_map/ppermute | solution.py:29
  124.9 10.1 %collective-permute-start.33 = (bf16[256,1024]{1,0:T(8,128)(2,1)S(1)}, bf16[256,1024]{1,0:T(8,128)(2,1)S(1)}, u32[]{:S(2)}, u32[]{:S(2)}) collective-permute-start(bf16[256,1024]{1,0:T(8,128)(2,1)S(1)} %get-tuple-element.221), channel_id=1, source_target_pairs={{0,16},{8,24},{16,0},{24,8},{1,17},{9,25},{17,1},{25,9},{2,18},{10... | collective-permute-start | bytes 1572872 | tf_op jit(solution)/shard_map/ppermute | solution.py:29
  135.2 8.7 %collective-permute-start.35 = (bf16[128,1024]{1,0:T(8,128)(2,1)S(1)}, bf16[128,1024]{1,0:T(8,128)(2,1)S(1)}, u32[]{:S(2)}, u32[]{:S(2)}) collective-permute-start(bf16[128,1024]{1,0:T(8,128)(2,1)S(1)} %add_convert_fusion.5), channel_id=1, source_target_pairs={{0,8},{8,0},{16,24},{24,16},{1,9},{9,1},{17,25},{25,17},{2,10},{10... | collective-permute-start | bytes 786440 | tf_op jit(solution)/shard_map/ppermute | solution.py:29
  136.9 8.4 %collective-permute-start.34 = (bf16[128,1024]{1,0:T(8,128)(2,1)S(1)}, bf16[128,1024]{1,0:T(8,128)(2,1)S(1)}, u32[]{:S(2)}, u32[]{:S(2)}) collective-permute-start(bf16[128,1024]{1,0:T(8,128)(2,1)S(1)} %add_convert_fusion.6), channel_id=1, source_target_pairs={{0,16},{8,24},{16,0},{24,8},{1,17},{9,25},{17,1},{25,9},{2,18},{10... | collective-permute-start | bytes 786440 | tf_op jit(solution)/shard_map/ppermute | solution.py:29
  139.8 21.3 %collective-permute-start.41 = (bf16[384,768]{1,0:T(8,128)(2,1)S(1)}, bf16[384,768]{1,0:T(8,128)(2,1)S(1)}, u32[]{:S(2)}, u32[]{:S(2)}) collective-permute-start(bf16[384,768]{1,0:T(8,128)(2,1)S(1)} %fusion.3), channel_id=1, source_target_pairs={{0,2},{1,3},{2,4},{3,5},{4,6},{5,7},{6,0},{7,1},{8,10},{9,11},{10,... | collective-permute-start | bytes 1769480 | tf_op jit(solution)/shard_map/ppermute | solution.py:66
  146.0 13.2 %collective-permute-start.37 = (bf16[256,1024]{1,0:T(8,128)(2,1)S(1)}, bf16[256,1024]{1,0:T(8,128)(2,1)S(1)}, u32[]{:S(2)}, u32[]{:S(2)}) collective-permute-start(bf16[256,1024]{1,0:T(8,128)(2,1)S(1)} %get-tuple-element.250.refs_0_.residual), channel_id=1, source_target_pairs={{0,8},{8,0},{16,24},{24,16},{1,9},{9,1},{17,25},{25,17},{2,10},{10... | collective-permute-start | bytes 1572872 | tf_op jit(solution)/shard_map/ppermute | solution.py:29
  146.4 13.2 %collective-permute-start.38 = (bf16[256,1024]{1,0:T(8,128)(2,1)S(1)}, bf16[256,1024]{1,0:T(8,128)(2,1)S(1)}, u32[]{:S(2)}, u32[]{:S(2)}) collective-permute-start(bf16[256,1024]{1,0:T(8,128)(2,1)S(1)} %get-tuple-element.250.refs_0_.residual), channel_id=1, source_target_pairs={{0,16},{8,24},{16,0},{24,8},{1,17},{9,25},{17,1},{25,9},{2,18},{10... | collective-permute-start | bytes 1572872 | tf_op jit(solution)/shard_map/ppermute | solution.py:29
  159.3 7.7 %collective-permute-start.39 = (bf16[128,1024]{1,0:T(8,128)(2,1)S(1)}, bf16[128,1024]{1,0:T(8,128)(2,1)S(1)}, u32[]{:S(2)}, u32[]{:S(2)}) collective-permute-start(bf16[128,1024]{1,0:T(8,128)(2,1)S(1)} %slice.265), channel_id=1, source_target_pairs={{0,16},{8,24},{16,0},{24,8},{1,17},{9,25},{17,1},{25,9},{2,18},{10... | collective-permute-start | bytes 786440 | tf_op jit(solution)/shard_map/ppermute | solution.py:29
  162.1 26.9 %collective-permute-start.49 = (bf16[384,768]{1,0:T(8,128)(2,1)}, bf16[384,768]{1,0:T(8,128)(2,1)}, u32[]{:S(2)}, u32[]{:S(2)}) collective-permute-start(bf16[384,768]{1,0:T(8,128)(2,1)} %fusion.2), channel_id=1, source_target_pairs={{0,2},{1,3},{2,4},{3,5},{4,6},{5,7},{6,0},{7,1},{8,10},{9,11},{10,... | collective-permute-start | bytes 1769480 | tf_op jit(solution)/shard_map/ppermute | solution.py:66
  175.6 15.8 %collective-permute-start.46 = (bf16[64,1024]{1,0:T(8,128)(2,1)S(1)}, bf16[64,1024]{1,0:T(8,128)(2,1)S(1)}, u32[]{:S(2)}, u32[]{:S(2)}) collective-permute-start(bf16[64,1024]{1,0:T(8,128)(2,1)S(1)} %get-tuple-element.260), channel_id=1, source_target_pairs={{0,8},{8,0},{16,24},{24,16},{1,9},{9,1},{17,25},{25,17},{2,10},{10... | collective-permute-start | bytes 393224 | tf_op jit(solution)/shard_map/ppermute | solution.py:29
  177.1 15.2 %collective-permute-start.47 = (bf16[64,1024]{1,0:T(8,128)(2,1)S(1)}, bf16[64,1024]{1,0:T(8,128)(2,1)S(1)}, u32[]{:S(2)}, u32[]{:S(2)}) collective-permute-start(bf16[64,1024]{1,0:T(8,128)(2,1)S(1)} %get-tuple-element.261), channel_id=1, source_target_pairs={{0,16},{8,24},{16,0},{24,8},{1,17},{9,25},{17,1},{25,9},{2,18},{10... | collective-permute-start | bytes 393224 | tf_op jit(solution)/shard_map/ppermute | solution.py:29
  177.6 15.5 %collective-permute-start.48 = (bf16[64,1024]{1,0:T(8,128)(2,1)S(1)}, bf16[64,1024]{1,0:T(8,128)(2,1)S(1)}, u32[]{:S(2)}, u32[]{:S(2)}) collective-permute-start(bf16[64,1024]{1,0:T(8,128)(2,1)S(1)} %get-tuple-element.262), channel_id=1, source_target_pairs={{0,24},{8,16},{16,8},{24,0},{1,25},{9,17},{17,9},{25,1},{2,26},{10... | collective-permute-start | bytes 393224 | tf_op jit(solution)/shard_map/ppermute | solution.py:29
  190.5 18.0 %collective-permute-start.69 = (bf16[384,768]{1,0:T(8,128)(2,1)S(1)}, bf16[384,768]{1,0:T(8,128)(2,1)S(1)}, u32[]{:S(2)}, u32[]{:S(2)}) collective-permute-start(bf16[384,768]{1,0:T(8,128)(2,1)S(1)} %fusion.1), channel_id=1, source_target_pairs={{0,2},{1,3},{2,4},{3,5},{4,6},{5,7},{6,0},{7,1},{8,10},{9,11},{10,... | collective-permute-start | bytes 1769480 | tf_op jit(solution)/shard_map/ppermute | solution.py:66
  191.4 25.2 %collective-permute-start.43 = (bf16[256,1024]{1,0:T(8,128)(2,1)S(1)}, bf16[256,1024]{1,0:T(8,128)(2,1)S(1)}, u32[]{:S(2)}, u32[]{:S(2)}) collective-permute-start(bf16[256,1024]{1,0:T(8,128)(2,1)S(1)} %copy-done.22), channel_id=1, source_target_pairs={{0,8},{8,0},{16,24},{24,16},{1,9},{9,1},{17,25},{25,17},{2,10},{10... | collective-permute-start | bytes 1572872 | tf_op jit(solution)/shard_map/ppermute | solution.py:29
  192.3 24.2 %collective-permute-start.44 = (bf16[256,1024]{1,0:T(8,128)(2,1)S(1)}, bf16[256,1024]{1,0:T(8,128)(2,1)S(1)}, u32[]{:S(2)}, u32[]{:S(2)}) collective-permute-start(bf16[256,1024]{1,0:T(8,128)(2,1)S(1)} %copy-done.20), channel_id=1, source_target_pairs={{0,16},{8,24},{16,0},{24,8},{1,17},{9,25},{17,1},{25,9},{2,18},{10... | collective-permute-start | bytes 1572872 | tf_op jit(solution)/shard_map/ppermute | solution.py:29
  193.3 20.6 %collective-permute-start.57 = (bf16[272,512]{1,0:T(8,128)(2,1)S(1)}, bf16[272,512]{1,0:T(8,128)(2,1)S(1)}, u32[]{:S(2)}, u32[]{:S(2)}) collective-permute-start(bf16[272,512]{1,0:T(8,128)(2,1)S(1)} %pad_maximum_fusion.6), channel_id=1, source_target_pairs={{0,2},{1,3},{2,4},{3,5},{4,6},{5,7},{6,0},{7,1},{8,10},{9,11},{10,... | collective-permute-start | bytes 835592 | tf_op jit(solution)/shard_map/ppermute | solution.py:66
  214.1 10.1 %collective-permute-start.58 = (bf16[272,512]{1,0:T(8,128)(2,1)S(1)}, bf16[272,512]{1,0:T(8,128)(2,1)S(1)}, u32[]{:S(2)}, u32[]{:S(2)}) collective-permute-start(bf16[272,512]{1,0:T(8,128)(2,1)S(1)} %pad_maximum_fusion.7), channel_id=1, source_target_pairs={{0,2},{1,3},{2,4},{3,5},{4,6},{5,7},{6,0},{7,1},{8,10},{9,11},{10,... | collective-permute-start | bytes 835592 | tf_op jit(solution)/shard_map/ppermute | solution.py:66
  214.3 16.3 %collective-permute-start.70 = (bf16[384,768]{1,0:T(8,128)(2,1)S(1)}, bf16[384,768]{1,0:T(8,128)(2,1)S(1)}, u32[]{:S(2)}, u32[]{:S(2)}) collective-permute-start(bf16[384,768]{1,0:T(8,128)(2,1)S(1)} %fusion.refs_0_), channel_id=1, source_target_pairs={{0,8},{8,0},{16,24},{24,16},{1,9},{9,1},{17,25},{25,17},{2,10},{10... | collective-permute-start | bytes 1769480 | tf_op jit(solution)/shard_map/ppermute | solution.py:29
  215.8 15.9 %collective-permute-start.71 = (bf16[384,768]{1,0:T(8,128)(2,1)S(1)}, bf16[384,768]{1,0:T(8,128)(2,1)S(1)}, u32[]{:S(2)}, u32[]{:S(2)}) collective-permute-start(bf16[384,768]{1,0:T(8,128)(2,1)S(1)} %fusion.refs_0_), channel_id=1, source_target_pairs={{0,16},{8,24},{16,0},{24,8},{1,17},{9,25},{17,1},{25,9},{2,18},{10... | collective-permute-start | bytes 1769480 | tf_op jit(solution)/shard_map/ppermute | solution.py:29
  216.5 7.8 %collective-permute-start.52 = (bf16[4,144,512]{2,1,0:T(8,128)(2,1)S(1)}, bf16[4,144,512]{2,1,0:T(8,128)(2,1)S(1)}, u32[]{:S(2)}, u32[]{:S(2)}) collective-permute-start(bf16[4,144,512]{2,1,0:T(8,128)(2,1)S(1)} %get-tuple-element.284), channel_id=1, source_target_pairs={{0,1},{1,0},{2,3},{3,2},{4,5},{5,4},{6,7},{7,6},{8,9},{9,8},{10,11... | collective-permute-start | bytes 1769480 | tf_op jit(solution)/shard_map/ppermute | solution.py:71
  216.6 37.5 %collective-permute-start.51 = (bf16[128,1024]{1,0:T(8,128)(2,1)S(1)}, bf16[128,1024]{1,0:T(8,128)(2,1)S(1)}, u32[]{:S(2)}, u32[]{:S(2)}) collective-permute-start(bf16[128,1024]{1,0:T(8,128)(2,1)S(1)} %add_convert_fusion.3), channel_id=1, source_target_pairs={{0,8},{8,0},{16,24},{24,16},{1,9},{9,1},{17,25},{25,17},{2,10},{10... | collective-permute-start | bytes 786440 | tf_op jit(solution)/shard_map/ppermute | solution.py:29
  224.3 13.8 %collective-permute-start.59 = (bf16[272,512]{1,0:T(8,128)(2,1)S(1)}, bf16[272,512]{1,0:T(8,128)(2,1)S(1)}, u32[]{:S(2)}, u32[]{:S(2)}) collective-permute-start(bf16[272,512]{1,0:T(8,128)(2,1)S(1)} %pad_maximum_fusion.8), channel_id=1, source_target_pairs={{0,2},{1,3},{2,4},{3,5},{4,6},{5,7},{6,0},{7,1},{8,10},{9,11},{10,... | collective-permute-start | bytes 835592 | tf_op jit(solution)/shard_map/ppermute | solution.py:66
  224.4 12.2 %collective-permute-start.63 = (bf16[144,512]{1,0:T(8,128)(2,1)S(1)}, bf16[144,512]{1,0:T(8,128)(2,1)S(1)}, u32[]{:S(2)}, u32[]{:S(2)}) collective-permute-start(bf16[144,512]{1,0:T(8,128)(2,1)S(1)} %fusion.12), channel_id=1, source_target_pairs={{0,2},{1,3},{2,4},{3,5},{4,6},{5,7},{6,0},{7,1},{8,10},{9,11},{10,... | collective-permute-start | bytes 442376 | tf_op jit(solution)/shard_map/ppermute | solution.py:66
  230.7 24.3 %collective-permute-start.50 = (bf16[128,1024]{1,0:T(8,128)(2,1)S(1)}, bf16[128,1024]{1,0:T(8,128)(2,1)S(1)}, u32[]{:S(2)}, u32[]{:S(2)}) collective-permute-start(bf16[128,1024]{1,0:T(8,128)(2,1)S(1)} %add_convert_fusion.4), channel_id=1, source_target_pairs={{0,16},{8,24},{16,0},{24,8},{1,17},{9,25},{17,1},{25,9},{2,18},{10... | collective-permute-start | bytes 786440 | tf_op jit(solution)/shard_map/ppermute | solution.py:29
  231.7 21.1 %collective-permute-start.54 = (bf16[256,1024]{1,0:T(8,128)(2,1)S(1)}, bf16[256,1024]{1,0:T(8,128)(2,1)S(1)}, u32[]{:S(2)}, u32[]{:S(2)}) collective-permute-start(bf16[256,1024]{1,0:T(8,128)(2,1)S(1)} %get-tuple-element.289), channel_id=1, source_target_pairs={{0,16},{8,24},{16,0},{24,8},{1,17},{9,25},{17,1},{25,9},{2,18},{10... | collective-permute-start | bytes 1572872 | tf_op jit(solution)/shard_map/ppermute | solution.py:29
  236.6 19.9 %collective-permute-start.53 = (bf16[256,1024]{1,0:T(8,128)(2,1)S(1)}, bf16[256,1024]{1,0:T(8,128)(2,1)S(1)}, u32[]{:S(2)}, u32[]{:S(2)}) collective-permute-start(bf16[256,1024]{1,0:T(8,128)(2,1)S(1)} %get-tuple-element.288), channel_id=1, source_target_pairs={{0,8},{8,0},{16,24},{24,16},{1,9},{9,1},{17,25},{25,17},{2,10},{10... | collective-permute-start | bytes 1572872 | tf_op jit(solution)/shard_map/ppermute | solution.py:29
  252.3 12.9 %collective-permute-start.72 = (bf16[192,768]{1,0:T(8,128)(2,1)S(1)}, bf16[192,768]{1,0:T(8,128)(2,1)S(1)}, u32[]{:S(2)}, u32[]{:S(2)}) collective-permute-start(bf16[192,768]{1,0:T(8,128)(2,1)S(1)} %slice.288), channel_id=1, source_target_pairs={{0,16},{8,24},{16,0},{24,8},{1,17},{9,25},{17,1},{25,9},{2,18},{10... | collective-permute-start | bytes 884744 | tf_op jit(solution)/shard_map/ppermute | solution.py:29
  252.8 12.9 %collective-permute-start.73 = (bf16[192,768]{1,0:T(8,128)(2,1)S(1)}, bf16[192,768]{1,0:T(8,128)(2,1)S(1)}, u32[]{:S(2)}, u32[]{:S(2)}) collective-permute-start(bf16[192,768]{1,0:T(8,128)(2,1)S(1)} %slice.289), channel_id=1, source_target_pairs={{0,8},{8,0},{16,24},{24,16},{1,9},{9,1},{17,25},{25,17},{2,10},{10... | collective-permute-start | bytes 884744 | tf_op jit(solution)/shard_map/ppermute | solution.py:29
  254.1 14.6 %collective-permute-start.60 = (bf16[272,512]{1,0:T(8,128)(2,1)S(1)}, bf16[272,512]{1,0:T(8,128)(2,1)S(1)}, u32[]{:S(2)}, u32[]{:S(2)}) collective-permute-start(bf16[272,512]{1,0:T(8,128)(2,1)S(1)} %pad_maximum_fusion.9.refs_0_), channel_id=1, source_target_pairs={{0,8},{8,0},{16,24},{24,16},{1,9},{9,1},{17,25},{25,17},{2,10},{10... | collective-permute-start | bytes 835592 | tf_op jit(solution)/shard_map/ppermute | solution.py:29
  255.0 14.9 %collective-permute-start.61 = (bf16[272,512]{1,0:T(8,128)(2,1)S(1)}, bf16[272,512]{1,0:T(8,128)(2,1)S(1)}, u32[]{:S(2)}, u32[]{:S(2)}) collective-permute-start(bf16[272,512]{1,0:T(8,128)(2,1)S(1)} %pad_maximum_fusion.9.refs_0_), channel_id=1, source_target_pairs={{0,16},{8,24},{16,0},{24,8},{1,17},{9,25},{17,1},{25,9},{2,18},{10... | collective-permute-start | bytes 835592 | tf_op jit(solution)/shard_map/ppermute | solution.py:29
  256.5 19.1 %collective-permute-start.62 = (bf16[272,512]{1,0:T(8,128)(2,1)S(1)}, bf16[272,512]{1,0:T(8,128)(2,1)S(1)}, u32[]{:S(2)}, u32[]{:S(2)}) collective-permute-start(bf16[272,512]{1,0:T(8,128)(2,1)S(1)} %pad_maximum_fusion.9.refs_0_), channel_id=1, source_target_pairs={{0,24},{8,16},{16,8},{24,0},{1,25},{9,17},{17,9},{25,1},{2,26},{10... | collective-permute-start | bytes 835592 | tf_op jit(solution)/shard_map/ppermute | solution.py:29
  265.2 18.8 %collective-permute-start.56 = (bf16[128,1024]{1,0:T(8,128)(2,1)S(1)}, bf16[128,1024]{1,0:T(8,128)(2,1)S(1)}, u32[]{:S(2)}, u32[]{:S(2)}) collective-permute-start(bf16[128,1024]{1,0:T(8,128)(2,1)S(1)} %add_convert_fusion.1), channel_id=1, source_target_pairs={{0,8},{8,0},{16,24},{24,16},{1,9},{9,1},{17,25},{25,17},{2,10},{10... | collective-permute-start | bytes 786440 | tf_op jit(solution)/shard_map/ppermute | solution.py:29
  265.7 18.3 %collective-permute-start.55 = (bf16[128,1024]{1,0:T(8,128)(2,1)S(1)}, bf16[128,1024]{1,0:T(8,128)(2,1)S(1)}, u32[]{:S(2)}, u32[]{:S(2)}) collective-permute-start(bf16[128,1024]{1,0:T(8,128)(2,1)S(1)} %add_convert_fusion.2), channel_id=1, source_target_pairs={{0,16},{8,24},{16,0},{24,8},{1,17},{9,25},{17,1},{25,9},{2,18},{10... | collective-permute-start | bytes 786440 | tf_op jit(solution)/shard_map/ppermute | solution.py:29
  268.7 13.0 %collective-permute-start.66 = (bf16[144,512]{1,0:T(8,128)(2,1)S(1)}, bf16[144,512]{1,0:T(8,128)(2,1)S(1)}, u32[]{:S(2)}, u32[]{:S(2)}) collective-permute-start(bf16[144,512]{1,0:T(8,128)(2,1)S(1)} %fusion.6.refs_4_), channel_id=1, source_target_pairs={{0,8},{8,0},{16,24},{24,16},{1,9},{9,1},{17,25},{25,17},{2,10},{10... | collective-permute-start | bytes 442376 | tf_op jit(solution)/shard_map/ppermute | solution.py:29
  270.0 11.7 %collective-permute-start.67 = (bf16[144,512]{1,0:T(8,128)(2,1)S(1)}, bf16[144,512]{1,0:T(8,128)(2,1)S(1)}, u32[]{:S(2)}, u32[]{:S(2)}) collective-permute-start(bf16[144,512]{1,0:T(8,128)(2,1)S(1)} %fusion.6.refs_4_), channel_id=1, source_target_pairs={{0,16},{8,24},{16,0},{24,8},{1,17},{9,25},{17,1},{25,9},{2,18},{10... | collective-permute-start | bytes 442376 | tf_op jit(solution)/shard_map/ppermute | solution.py:29
  (38 other events, 373.2 us)
